TPU v7x, 32 devices: a whole 2x2x4 slice. The times are simulated.
32 devices in a mesh: groups: 2 (over y), tile: 4 (over z), tm: 4 (over x, core).
Axes of the slice: x: 2, y: 2, z: 4, core: 2. Of those that a mesh axis runs over, the one named last changes fastest.
Arguments:
- multiplier: float32 [8, 8, 64, 512], P(('groups', 'tm'), None, 'tile'), parts along dimension 0, may hold values from -6 to 6
- increment: float32 [8, 8, 64, 512], P(('groups', 'tm'), None, 'tile'), parts along dimension 0, may hold values from -6 to 6
- obs_dual: float32 [8, 2048], P(('groups', 'tm'), 'tile'), parts along dimension 0, may hold values from -6 to 6
- rhs_model: float32 [8, 8, 64, 512], P(('groups', 'tm'), None, 'tile'), parts along dimension 0, may hold values from -6 to 6
- rhs_obs: float32 [8, 2048], P(('groups', 'tm'), 'tile'), parts along dimension 0, may hold values from -6 to 6
- model_err: float32 [8, 8, 64, 512], P(('groups', 'tm'), None, 'tile'), parts along dimension 0, may hold values from 0.2 to 2
- obs_err: float32 [8, 2048], P(('groups', 'tm'), 'tile'), parts along dimension 0, may hold values from 0.25 to 4
- drift_east: float32 [8, 8, 64, 512], P(('groups', 'tm'), None, 'tile'), parts along dimension 0, may hold values from -0.1 to 0.1
- drift_north: float32 [8, 8, 64, 512], P(('groups', 'tm'), None, 'tile'), parts along dimension 0, may hold values from -0.1 to 0.1
- diffusion: float32 [8, 8, 64, 512], P(('groups', 'tm'), None, 'tile'), parts along dimension 0, may hold values from 0.02 to 0.12
- obs_cell: int32 [8, 2048], P(('groups', 'tm'), 'tile'), parts along dimension 0, may hold values from 0 to 65535
- obs_count: int32 [8, 4], P(('groups', 'tm'), 'tile'), parts along dimension 0, may hold values from 256 to 512, as said below
Outputs:
- new_multiplier: float32 [8, 8, 64, 512], P(('groups', 'tm'), None, 'tile'), parts along dimension 0
- new_increment: float32 [8, 8, 64, 512], P(('groups', 'tm'), None, 'tile'), parts along dimension 0
- new_obs_dual: float32 [8, 2048], P(('groups', 'tm'), 'tile'), parts along dimension 0
There are 2 independent parts, one for each index of `groups`. A program takes and returns all parts, laid end to end along the dimension named above; each array names one. Nothing has to cross between parts.
Inputs may be any that keep to these rules, and one draw needn't show every extreme that they name: `obs_count`: every tile and sub-window has between 256 and 512 live slots; the live ones come first; some tile and sub-window has all 512 live.
All inputs are finite; a program needn't handle non-finite values.
Results may differ from a plain program's by a relative error of at most 0.000027.
Values sent between devices are 32-bit elements; how exact they have to be, the bound alone decides.
No kernel may reach another device: no remote copies, remote signals or barrier semaphores. Data moves between devices by JAX's collectives and lax.ppermute only.
A program may use at most 64 MiB of HBM per device.

v0:
```python
import jax
import jax.numpy as jnp
from jax import lax
from jax.sharding import PartitionSpec as P


def with_halo(block, sides, width):
    for axis, dim in sides:
        count = lax.axis_size(axis)
        forward = [(i, i + 1) for i in range(count - 1)]
        backward = [(target, source) for source, target in forward]
        low = lax.ppermute(
            lax.slice_in_dim(block, block.shape[dim] - width, None, axis=dim), axis, forward
        )
        high = lax.ppermute(lax.slice_in_dim(block, 0, width, axis=dim), axis, backward)
        block = jnp.concatenate([low, block, high], axis=dim)
    return block


def passed_along(value, axis, steps):
    count = lax.axis_size(axis)
    initial, last = (max(0, -steps), min(count, count - steps))
    return lax.ppermute(value, axis, [(source, source + steps) for source in range(initial, last)])


def prefix(array, axis, combine, identity, reverse):
    peers, position = (lax.axis_size(axis), lax.axis_index(axis))
    everything = lax.all_gather(array, axis)
    start = jnp.broadcast_to(jnp.asarray(identity, array.dtype), array.shape)

    def lap(k, before):
        at = peers - 1 - k if reverse else k
        reached = at > position if reverse else at < position
        new = combine(before, everything[at])
        return jnp.where(reached, new, before)

    return lax.fori_loop(0, peers, lap, start)


def shift_north(field, before, after):
    padded = jnp.pad(field, ((0, 0), (0, 0), (before, after)))
    return padded


def forward_step(state, drift_e, drift_n, diffuse):
    padded = with_halo(state, (("tile", 1),), 1)
    along_y = shift_north(state, 1, 1)
    return (
        (1.0 - 4.0 * diffuse) * state
        + (diffuse - drift_e) * padded[:, 2:, :]
        + (diffuse + drift_e) * padded[:, :-2, :]
        + (diffuse - drift_n) * along_y[:, :, 2:]
        + (diffuse + drift_n) * along_y[:, :, :-2]
    )


def adjoint_step(state, rim_drift, rim_diffuse, drift_n, diffuse):
    padded = with_halo(state, (("tile", 1),), 1)
    plus_x = ((rim_diffuse - rim_drift) * padded)[:, :-2, :]
    minus_x = ((rim_diffuse + rim_drift) * padded)[:, 2:, :]
    plus_y = shift_north((diffuse - drift_n) * state, 1, 0)[:, :, :-1]
    minus_y = shift_north((diffuse + drift_n) * state, 0, 1)[:, :, 1:]
    return (1.0 - 4.0 * diffuse) * state + plus_x + minus_x + plus_y + minus_y


def add_fields(earlier, later):
    return earlier + later


def shards(
    multiplier,
    increment,
    obs_dual,
    rhs_model,
    rhs_obs,
    model_err,
    obs_err,
    drift_east,
    drift_north,
    diffusion,
    obs_cell,
    obs_count,
):
    mult_here = multiplier[0]
    incr_here = increment[0]
    drift_e = drift_east[0]
    drift_n = drift_north[0]
    diffuse = diffusion[0]
    slots = obs_cell.shape[1]
    later = passed_along(mult_here, "tm", -1)
    coeff_pair = jnp.stack([drift_e, diffuse])
    coeff_rims = with_halo(coeff_pair, (("tile", 2),), 1)
    rim_drift = coeff_rims[0]
    rim_diffuse = coeff_rims[1]
    moved = forward_step(
        forward_step(incr_here, drift_e, drift_n, diffuse), drift_e, drift_n, diffuse
    )
    back = adjoint_step(
        adjoint_step(later, rim_drift, rim_diffuse, drift_n, diffuse),
        rim_drift,
        rim_diffuse,
        drift_n,
        diffuse,
    )
    arrived = passed_along(moved, "tm", 1)
    valid = (jnp.arange(slots, dtype=jnp.int32)[None, :] < obs_count).astype(jnp.float32)
    cells = obs_cell[0]
    flat_incr = incr_here.reshape(-1)
    hx = flat_incr[cells][None, :] * valid
    spread = jnp.zeros(flat_incr.shape, jnp.float32).at[cells].add((valid * obs_dual)[0])
    ht = spread.reshape(incr_here.shape)
    lx = incr_here - arrived
    lt = mult_here - back
    res_model = rhs_model[0] - (model_err[0] * mult_here + lx)
    res_obs = valid * (rhs_obs - (obs_err * obs_dual + hx))
    res_incr = -(lt + ht)
    empty = jnp.zeros_like(res_model)
    before = prefix(res_model, "tm", add_fields, empty, False)
    after = prefix(res_incr, "tm", add_fields, empty, True)
    dir_model = before + res_model
    dir_incr = after + res_incr
    dir_obs = res_obs / obs_err
    numer_part = (
        jnp.sum(res_model * dir_model) + jnp.sum(res_incr * dir_incr) + jnp.sum(res_obs * dir_obs)
    )
    denom_part = (
        jnp.sum(dir_model * dir_model) + jnp.sum(dir_incr * dir_incr) + jnp.sum(dir_obs * dir_obs)
    )
    numer, denom = lax.psum((numer_part, denom_part), ("tile", "tm"))
    step_size = numer / denom
    return (
        multiplier + step_size * dir_model[None],
        increment + step_size * dir_incr[None],
        obs_dual + step_size * dir_obs,
    )


def solution(mesh):
    return jax.shard_map(
        shards,
        mesh=mesh,
        in_specs=(
            P(("groups", "tm"), None, "tile", None),
            P(("groups", "tm"), None, "tile", None),
            P(("groups", "tm"), "tile"),
            P(("groups", "tm"), None, "tile", None),
            P(("groups", "tm"), "tile"),
            P(("groups", "tm"), None, "tile", None),
            P(("groups", "tm"), "tile"),
            P(("groups", "tm"), None, "tile", None),
            P(("groups", "tm"), None, "tile", None),
            P(("groups", "tm"), None, "tile", None),
            P(("groups", "tm"), "tile"),
            P(("groups", "tm"), "tile"),
        ),
        out_specs=(
            P(("groups", "tm"), None, "tile", None),
            P(("groups", "tm"), None, "tile", None),
            P(("groups", "tm"), "tile"),
        ),
        check_vma=False,
    )
```

profile of v0, /device:TPU:0, one launch (start us, length us, event | category | flops | bytes accessed | tf_op | source)
XLA Modules:
  0.0 151.4 jit_solution(6181419421452236517)
XLA Ops:
  7.2 0.0 all-gather.5.cloned.1.call-start
  7.2 1.3 collective-permute-start.5
  8.5 1.0 fusion.36
  9.5 1.3 collective-permute-start
  10.8 0.0 copy-start
  10.8 5.7 %collective-permute-start.1 = (f32[8,1,512]{2,1,0:T(1,128)S(1)}, f32[8,1,512]{2,1,0:T(1,128)S(1)}, u32[]{:S(2)}, u32[]{:S(2)}) collective-permute-start(f32[8,1,512]{2,1,0:T(1,128)S(1)} %get-tuple-element.273), channel_id=1, source_target_pairs={{0,4},{4,8},{8,12},{1,5},{5,9},{9,13},{2,6},{6,10},{10,14},{3,7},{... | collective-permute-start | bytes 49160 | tf_op jit(solution)/shard_map/ppermute | solution.py:12
  16.5 1.0 constant_dynamic-update-slice_fusion.1
  17.5 0.0 copy-start.1
  17.5 0.1 fusion.32
  17.6 0.0 copy-start.12
  17.6 3.9 %collective-permute-start.6 = (f32[2,8,1,512]{3,2,1,0:T(1,128)S(1)}, f32[2,8,1,512]{3,2,1,0:T(1,128)S(1)}, u32[]{:S(2)}, u32[]{:S(2)}) collective-permute-start(f32[2,8,1,512]{3,2,1,0:T(1,128)S(1)} %get-tuple-element.262), channel_id=1, source_target_pairs={{0,4},{4,8},{8,12},{1,5},{5,9},{9,13},{2,6},{6,10},{10,14},{3,7},{... | collective-permute-start | bytes 98312 | tf_op jit(solution)/shard_map/ppermute | solution.py:12
  21.5 1.3 collective-permute-start.7
  22.9 0.1 copy.15
  23.6 0.0 copy-start.10
  23.6 0.0 copy-start.11
  23.6 3.1 %gather_fusion = f32[512]{0:T(512)S(1)} fusion(f32[65536]{0:T(1024)S(1)} %bitcast.70, s32[1024]{0:T(1024)S(1)} %pad_clamp_fusion), kind=kCustom, calls=%fused_computation | custom fusion | bytes 6144 | tf_op jit(solution)/shard_map/gather | solution.py:109
  26.8 0.0 copy-start.9
  26.8 0.7 copy-done.9
  27.5 3.3 %scatter_custom_fusion = f32[65536]{0:T(1024)S(1)} fusion(s32[512]{0:T(512)S(1)} %bitcast.78, f32[512]{0:T(512)S(1)} %bitcast.80, f32[]{:T(128)} %constant.81.clone.1), kind=kCustom, calls=%fused_computation.70 | custom fusion | flops 512 | bytes 262148 | tf_op jit(solution)/shard_map/scatter-add | solution.py:110
  30.9 0.0 collective-permute-done.6
  30.9 0.1 pad_maximum_fusion
  31.0 0.0 copy-start.6
  31.0 0.1 subtract_bitcast_fusion
  31.2 4.5 %collective-permute-start.8 = (f32[8,1,512]{2,1,0:T(1,128)S(1)}, f32[8,1,512]{2,1,0:T(1,128)S(1)}, u32[]{:S(2)}, u32[]{:S(2)}) collective-permute-start(f32[8,1,512]{2,1,0:T(1,128)S(1)} %get-tuple-element.268), channel_id=1, source_target_pairs={{0,4},{4,8},{8,12},{1,5},{5,9},{9,13},{2,6},{6,10},{10,14},{3,7},{... | collective-permute-start | bytes 49160 | tf_op jit(solution)/shard_map/ppermute | solution.py:12
  35.7 0.0 copy-start.4
  35.7 1.4 collective-permute-start.9
  37.2 0.1 bitcast_multiply_fusion.3
  37.3 0.0 collective-permute-done.1
  37.3 0.2 fusion.9
  37.6 1.3 collective-permute-start.2
  38.9 5.2 %collective-permute-start.3 = (f32[8,1,512]{2,1,0:T(1,128)S(1)}, f32[8,1,512]{2,1,0:T(1,128)S(1)}, u32[]{:S(2)}, u32[]{:S(2)}) collective-permute-start(f32[8,1,512]{2,1,0:T(1,128)S(1)} %get-tuple-element.271), channel_id=1, source_target_pairs={{0,4},{4,8},{8,12},{1,5},{5,9},{9,13},{2,6},{6,10},{10,14},{3,7},{... | collective-permute-start | bytes 49160 | tf_op jit(solution)/shard_map/ppermute | solution.py:12
  44.1 0.1 pad_maximum_fusion.1
  44.2 1.3 collective-permute-done.3
  45.5 0.5 bitcast_multiply_fusion
  46.0 4.2 %collective-permute-start.10 = (f32[8,1,512]{2,1,0:T(1,128)S(1)}, f32[8,1,512]{2,1,0:T(1,128)S(1)}, u32[]{:S(2)}, u32[]{:S(2)}) collective-permute-start(f32[8,1,512]{2,1,0:T(1,128)S(1)} %get-tuple-element.266), channel_id=1, source_target_pairs={{0,4},{4,8},{8,12},{1,5},{5,9},{9,13},{2,6},{6,10},{10,14},{3,7},{... | collective-permute-start | bytes 49160 | tf_op jit(solution)/shard_map/ppermute | solution.py:12
  50.3 1.3 collective-permute-start.11
  51.6 1.3 collective-permute-start.4
  52.9 0.0 copy-start.8
  52.9 0.0 copy-start.5
  52.9 0.0 copy-start.7
  53.0 2.9 %collective-permute-done.11 = f32[8,1,512]{2,1,0:T(1,128)S(1)} collective-permute-done((f32[8,1,512]{2,1,0:T(1,128)S(1)}, f32[8,1,512]{2,1,0:T(1,128)S(1)}, u32[]{:S(2)}, u32[]{:S(2)}) %collective-permute-start.11) | collective-permute-done | bytes 16416 | tf_op jit(solution)/shard_map/ppermute | solution.py:15
  55.9 0.1 pad_maximum_fusion.2
  56.0 1.2 fusion.6
  57.2 0.0 all-gather.5.cloned.1.call-update
  57.2 0.0 all-gather.7.cloned.1.call-start
  57.3 0.7 all-gather.7.cloned.1.call-update
  58.0 0.7 multiply_reduce_fusion.4
  58.7 22.1 %all-gather.5.cloned.1.call-done = f32[32,16,512]{2,1,0:T(8,128)} async-done(((f32[8,16,512]{2,1,0:T(8,128)}), f32[32,16,512]{2,1,0:T(8,128)}) %all-gather.5.cloned.1.call-update) | async-done | bytes 1048592 | tf_op jit(solution)/shard_map/all_gather | solution.py:28
  80.8 4.3 %while.30 = (s32[]{:T(128)}, f32[8,16,512]{2,1,0:T(8,128)S(1)}, s32[]{:T(128)}, f32[4,8,16,512]{3,2,1,0:T(8,128)}, s32[]{:T(128)}, /*index=5*/s32[]{:T(128)}) while((s32[]{:T(128)}, f32[8,16,512]{2,1,0:T(8,128)S(1)}, s32[]{:T(128)}, f32[4,8,16,512]{3,2,1,0:T(8,128)}, s32[]{:T(128)}, /*index=5*/s32[]{:T(128)}) %tuple.103), condition=%wide.region_1.2_spmd.clone, body=%wide.region_0.1_spmd.clone.sunk | while | flops 196612 | bytes 786525 | solution.py:37
  80.8 1.1 add_select_fusion.4
  81.9 1.0 add_select_fusion.4
  83.0 1.0 add_select_fusion.4
  84.0 1.0 add_select_fusion.4
  85.1 0.8 multiply_reduce_fusion.1
  85.9 13.8 %all-gather.7.cloned.1.call-done = f32[32,16,512]{2,1,0:T(8,128)} async-done(((f32[8,16,512]{2,1,0:T(8,128)}), f32[32,16,512]{2,1,0:T(8,128)}) %all-gather.7.cloned.1.call-update) | async-done | bytes 1048592 | tf_op jit(solution)/shard_map/all_gather | solution.py:28
  99.7 4.3 %while.31 = (s32[]{:T(128)}, f32[8,16,512]{2,1,0:T(8,128)S(1)}, s32[]{:T(128)}, f32[4,8,16,512]{3,2,1,0:T(8,128)}, s32[]{:T(128)}, /*index=5*/s32[]{:T(128)}, s32[]{:T(128)}, s32[]{:T(128)}) while((s32[]{:T(128)}, f32[8,16,512]{2,1,0:T(8,128)S(1)}, s32[]{:T(128)}, f32[4,8,16,512]{3,2,1,0:T(8,128)}, s32[]{:T(128)}, ...), condition=%wide.region_5.6_spmd.clone, body=%wide.region_4.5_spmd.clone.sunk | while | flops 196616 | bytes 786587 | solution.py:37
  99.7 1.1 add_select_fusion.5
  100.8 1.0 add_select_fusion.5
  101.9 1.0 add_select_fusion.5
  102.9 1.0 add_select_fusion.5
  104.0 0.7 multiply_reduce_fusion
  108.6 33.1 %all-reduce.6 = (f32[]{:T(128)}, f32[]{:T(128)}) all-reduce(f32[]{:T(128)S(6)} %add.233, f32[]{:T(128)S(6)} %add.235), channel_id=1, replica_groups=mesh['groups'=2,'tile'=4,'tm'=4] {'tile','tm'}, use_global_device_ids=true, to_apply=%region_8.9 | all-reduce | flops 2 | bytes 16 | tf_op jit(solution)/shard_map/psum | solution.py:129
  143.1 0.6 multiply_add_fusion
  143.7 0.9 bitcast_add_fusion
  (33 shorter events, 0.3 us)
Async XLA Ops:
  7.2 73.6 %all-gather.5.cloned.1.call-start = ((), (), s32[]{:S(2)}) async-start(), calls=%async_computation | async-start | bytes 1310720 | tf_op jit(solution)/shard_map/all_gather | solution.py:28
  7.2 23.9 %collective-permute-start.5 = (f32[8,16,512]{2,1,0:T(8,128)}, f32[8,16,512]{2,1,0:T(8,128)S(1)}, u32[]{:S(2)}, u32[]{:S(2)}) collective-permute-start(f32[8,16,512]{2,1,0:T(8,128)} %bitcast.76), channel_id=1, source_target_pairs={{1,0},{2,1},{3,2},{5,4},{6,5},{7,6},{9,8},{10,9},{11,10},{13,12},{... | collective-permute-start | bytes 786440 | tf_op jit(solution)/shard_map/ppermute | solution.py:23
  9.5 27.8 %collective-permute-start = (f32[8,1,512]{2,1,0:T(1,128)S(1)}, f32[8,1,512]{2,1,0:T(1,128)S(1)}, u32[]{:S(2)}, u32[]{:S(2)}) collective-permute-start(f32[8,1,512]{2,1,0:T(1,128)S(1)} %get-tuple-element.272), channel_id=1, source_target_pairs={{4,0},{8,4},{12,8},{5,1},{9,5},{13,9},{6,2},{10,6},{14,10},{7,3},{... | collective-permute-start | bytes 49160 | tf_op jit(solution)/shard_map/ppermute | solution.py:15
  10.8 6.7 %copy-start = (f32[1,8,16,512]{3,2,1,0:T(8,128)S(1)}, f32[1,8,16,512]{3,2,1,0:T(8,128)}, u32[]{:S(2)}) copy-start(f32[1,8,16,512]{3,2,1,0:T(8,128)} %param.25) | copy-start | bytes 786436
  10.8 26.5 %collective-permute-start.1 = (f32[8,1,512]{2,1,0:T(1,128)S(1)}, f32[8,1,512]{2,1,0:T(1,128)S(1)}, u32[]{:S(2)}, u32[]{:S(2)}) collective-permute-start(f32[8,1,512]{2,1,0:T(1,128)S(1)} %get-tuple-element.273), channel_id=1, source_target_pairs={{0,4},{4,8},{8,12},{1,5},{5,9},{9,13},{2,6},{6,10},{10,14},{3,7},{... | collective-permute-start | bytes 49160 | tf_op jit(solution)/shard_map/ppermute | solution.py:12
  17.5 5.4 %copy-start.1 = (f32[1,8,16,512]{3,2,1,0:T(8,128)S(1)}, f32[1,8,16,512]{3,2,1,0:T(8,128)}, u32[]{:S(2)}) copy-start(f32[1,8,16,512]{3,2,1,0:T(8,128)} %param.17) | copy-start | bytes 786436
  17.6 5.2 %copy-start.12 = (s32[1,512]{1,0:T(1,128)S(1)}, s32[1,512]{1,0:T(1,128)}, u32[]{:S(2)}) copy-start(s32[1,512]{1,0:T(1,128)} %param.26) | copy-start | bytes 6148
  17.6 13.3 %collective-permute-start.6 = (f32[2,8,1,512]{3,2,1,0:T(1,128)S(1)}, f32[2,8,1,512]{3,2,1,0:T(1,128)S(1)}, u32[]{:S(2)}, u32[]{:S(2)}) collective-permute-start(f32[2,8,1,512]{3,2,1,0:T(1,128)S(1)} %get-tuple-element.262), channel_id=1, source_target_pairs={{0,4},{4,8},{8,12},{1,5},{5,9},{9,13},{2,6},{6,10},{10,14},{3,7},{... | collective-permute-start | bytes 98312 | tf_op jit(solution)/shard_map/ppermute | solution.py:12
  21.5 9.3 %collective-permute-start.7 = (f32[2,8,1,512]{3,2,1,0:T(1,128)S(1)}, f32[2,8,1,512]{3,2,1,0:T(1,128)S(1)}, u32[]{:S(2)}, u32[]{:S(2)}) collective-permute-start(f32[2,8,1,512]{3,2,1,0:T(1,128)S(1)} %get-tuple-element.263), channel_id=1, source_target_pairs={{4,0},{8,4},{12,8},{5,1},{9,5},{13,9},{6,2},{10,6},{14,10},{7,3},{... | collective-permute-start | bytes 98312 | tf_op jit(solution)/shard_map/ppermute | solution.py:15
  23.6 3.2 %copy-start.10 = (f32[1,512]{1,0:T(1,128)S(1)}, f32[1,512]{1,0:T(1,128)}, u32[]{:S(2)}) copy-start(f32[1,512]{1,0:T(1,128)} %param.18) | copy-start | bytes 6148
  23.6 3.2 %copy-start.11 = (f32[1,512]{1,0:T(1,128)S(1)}, f32[1,512]{1,0:T(1,128)}, u32[]{:S(2)}) copy-start(f32[1,512]{1,0:T(1,128)} %param.20) | copy-start | bytes 6148
  26.8 0.7 copy-start.9
  31.0 6.1 %copy-start.6 = (f32[1,8,16,512]{3,2,1,0:T(8,128)S(1)}, f32[1,8,16,512]{3,2,1,0:T(8,128)}, u32[]{:S(2)}) copy-start(f32[1,8,16,512]{3,2,1,0:T(8,128)} %param.24) | copy-start | bytes 786436
  31.2 12.9 %collective-permute-start.8 = (f32[8,1,512]{2,1,0:T(1,128)S(1)}, f32[8,1,512]{2,1,0:T(1,128)S(1)}, u32[]{:S(2)}, u32[]{:S(2)}) collective-permute-start(f32[8,1,512]{2,1,0:T(1,128)S(1)} %get-tuple-element.268), channel_id=1, source_target_pairs={{0,4},{4,8},{8,12},{1,5},{5,9},{9,13},{2,6},{6,10},{10,14},{3,7},{... | collective-permute-start | bytes 49160 | tf_op jit(solution)/shard_map/ppermute | solution.py:12
  35.7 1.6 %copy-start.4 = (f32[1,8,16,512]{3,2,1,0:T(8,128)S(1)}, f32[1,8,16,512]{3,2,1,0:T(8,128)}, u32[]{:S(2)}) copy-start(f32[1,8,16,512]{3,2,1,0:T(8,128)} %param.23) | copy-start | bytes 786436
  35.7 8.4 %collective-permute-start.9 = (f32[8,1,512]{2,1,0:T(1,128)S(1)}, f32[8,1,512]{2,1,0:T(1,128)S(1)}, u32[]{:S(2)}, u32[]{:S(2)}) collective-permute-start(f32[8,1,512]{2,1,0:T(1,128)S(1)} %get-tuple-element.269), channel_id=1, source_target_pairs={{4,0},{8,4},{12,8},{5,1},{9,5},{13,9},{6,2},{10,6},{14,10},{7,3},{... | collective-permute-start | bytes 49160 | tf_op jit(solution)/shard_map/ppermute | solution.py:15
  37.6 6.6 %collective-permute-start.2 = (f32[8,1,512]{2,1,0:T(1,128)S(1)}, f32[8,1,512]{2,1,0:T(1,128)S(1)}, u32[]{:S(2)}, u32[]{:S(2)}) collective-permute-start(f32[8,1,512]{2,1,0:T(1,128)S(1)} %get-tuple-element.270), channel_id=1, source_target_pairs={{4,0},{8,4},{12,8},{5,1},{9,5},{13,9},{6,2},{10,6},{14,10},{7,3},{... | collective-permute-start | bytes 49160 | tf_op jit(solution)/shard_map/ppermute | solution.py:15
  38.9 6.6 %collective-permute-start.3 = (f32[8,1,512]{2,1,0:T(1,128)S(1)}, f32[8,1,512]{2,1,0:T(1,128)S(1)}, u32[]{:S(2)}, u32[]{:S(2)}) collective-permute-start(f32[8,1,512]{2,1,0:T(1,128)S(1)} %get-tuple-element.271), channel_id=1, source_target_pairs={{0,4},{4,8},{8,12},{1,5},{5,9},{9,13},{2,6},{6,10},{10,14},{3,7},{... | collective-permute-start | bytes 49160 | tf_op jit(solution)/shard_map/ppermute | solution.py:12
  46.0 6.9 %collective-permute-start.10 = (f32[8,1,512]{2,1,0:T(1,128)S(1)}, f32[8,1,512]{2,1,0:T(1,128)S(1)}, u32[]{:S(2)}, u32[]{:S(2)}) collective-permute-start(f32[8,1,512]{2,1,0:T(1,128)S(1)} %get-tuple-element.266), channel_id=1, source_target_pairs={{0,4},{4,8},{8,12},{1,5},{5,9},{9,13},{2,6},{6,10},{10,14},{3,7},{... | collective-permute-start | bytes 49160 | tf_op jit(solution)/shard_map/ppermute | solution.py:12
  50.3 5.6 %collective-permute-start.11 = (f32[8,1,512]{2,1,0:T(1,128)S(1)}, f32[8,1,512]{2,1,0:T(1,128)S(1)}, u32[]{:S(2)}, u32[]{:S(2)}) collective-permute-start(f32[8,1,512]{2,1,0:T(1,128)S(1)} %get-tuple-element.267), channel_id=1, source_target_pairs={{4,0},{8,4},{12,8},{5,1},{9,5},{13,9},{6,2},{10,6},{14,10},{7,3},{... | collective-permute-start | bytes 49160 | tf_op jit(solution)/shard_map/ppermute | solution.py:15
  51.6 4.4 %collective-permute-start.4 = (f32[8,16,512]{2,1,0:T(8,128)S(1)}, f32[8,16,512]{2,1,0:T(8,128)S(1)}, u32[]{:S(2)}, u32[]{:S(2)}) collective-permute-start(f32[8,16,512]{2,1,0:T(8,128)S(1)} %get-tuple-element.261), channel_id=1, source_target_pairs={{0,1},{1,2},{2,3},{4,5},{5,6},{6,7},{8,9},{9,10},{10,11},{12,13},{... | collective-permute-start | bytes 786440 | tf_op jit(solution)/shard_map/ppermute | solution.py:23
  52.9 3.1 %copy-start.8 = (f32[1,8,16,512]{3,2,1,0:T(8,128)S(1)}, f32[1,8,16,512]{3,2,1,0:T(8,128)}, u32[]{:S(2)}) copy-start(f32[1,8,16,512]{3,2,1,0:T(8,128)} %param.19) | copy-start | bytes 786436
  52.9 3.1 %copy-start.5 = (f32[1,8,16,512]{3,2,1,0:T(8,128)S(1)}, f32[1,8,16,512]{3,2,1,0:T(8,128)}, u32[]{:S(2)}) copy-start(f32[1,8,16,512]{3,2,1,0:T(8,128)} %param.16) | copy-start | bytes 786436
  52.9 3.1 %copy-start.7 = (f32[1,8,16,512]{3,2,1,0:T(8,128)S(1)}, f32[1,8,16,512]{3,2,1,0:T(8,128)}, u32[]{:S(2)}) copy-start(f32[1,8,16,512]{3,2,1,0:T(8,128)} %param.21) | copy-start | bytes 786436
  57.2 42.4 %all-gather.7.cloned.1.call-start = ((), (), s32[]{:S(2)}) async-start(), calls=%async_computation.1 | async-start | bytes 1310720 | tf_op jit(solution)/shard_map/all_gather | solution.py:28
  80.8 4.3 %copy-start.3 = (f32[8,16,512]{2,1,0:T(8,128)S(1)}, f32[8,16,512]{2,1,0:T(8,128)}, u32[]{:S(2)}) copy-start(f32[8,16,512]{2,1,0:T(8,128)} %get-tuple-element.265) | copy-start | bytes 786436
  99.7 4.3 %copy-start.2 = (f32[8,16,512]{2,1,0:T(8,128)S(1)}, f32[8,16,512]{2,1,0:T(8,128)}, u32[]{:S(2)}) copy-start(f32[8,16,512]{2,1,0:T(8,128)} %get-tuple-element.264) | copy-start | bytes 786436
Sparse Core Ops, SparseCore 0:
  57.3 23.3 all-gather.4
  82.9 16.7 all-gather.6
where the time goes:
time: 152 us; the launch traced here: 151 us
  waiting for transfers between devices  40.9 us (27%)
  blocking collectives  33.1 us (22%)
  starting transfers between devices  32.8 us (22%)
  between operations  20.5 us (13%)
  other arithmetic  17.8 us (12%)
  local copies, waits for them, and re-layouts  6.1 us (4%)
    all_gather x2, waiting for transfers between devices, prefix(): everything = lax.all_gather(array, axis)  35.9 us
    psum x1, blocking collectives, shards(): numer, denom = lax.psum((numer_part, denom_part), ('tile', 'tm'))  33.1 us
    ppermute x5, starting transfers between devices, with_halo(): lax.ppermute(lax.slice_in_dim(block, block.shape[dim] - width, None, axis...  23.5 us
    select_n x8, other arithmetic, lap(): return jnp.where(reached, new, before)  8.47 us
    ppermute x5, starting transfers between devices, with_halo(): lax.ppermute(lax.slice_in_dim(block, 0, width, axis=dim), axis, backward)  6.59 us
    scatter-add x1, other arithmetic, shards(): jnp.zeros(flat_incr.shape, jnp.float32).at[cells].add((valid * obs_dual)[0])  3.33 us
    gather x1, local copies, waits for them, and re-layouts, shards(): hx = flat_incr[cells][None, :] * valid  3.14 us
  transfers between devices with their start and end apart: 14, of which 4 were waited for; matrix products, arithmetic and copies ran while one was open for 10% of the time, Pallas kernels for 0%

commit v1 on v0

v1 whole, which is shorter than its diff:
```python
import jax
import jax.numpy as jnp
from jax import lax
from jax.experimental import pallas as pl
from jax.experimental.pallas import tpu as pltpu
from jax.sharding import PartitionSpec as P

F32 = jnp.float32
VMEM = pltpu.VMEM
GRANT = 24 * 1024 * 1024


def kernel_call(body, name, inputs, outputs):
    arrays, in_specs = [], []
    for array, home in inputs:
        if home == "scalar":
            in_specs.append(pl.BlockSpec(memory_space=pltpu.SMEM))
        else:
            in_specs.append(pl.BlockSpec(memory_space=VMEM))
            if home == "near":
                array = pltpu.with_memory_space_constraint(array, VMEM)
        arrays.append(array)
    out_shape = [
        VMEM(shape, F32) if home == "near" else jax.ShapeDtypeStruct(shape, F32)
        for shape, home in outputs
    ]
    return pl.pallas_call(
        body,
        name=name,
        out_shape=out_shape,
        in_specs=in_specs,
        out_specs=[pl.BlockSpec(memory_space=VMEM)] * len(outputs),
        compiler_params=pltpu.CompilerParams(vmem_limit_bytes=GRANT),
    )(*arrays)


def iotas(shape):
    return (
        lax.broadcasted_iota(jnp.int32, shape, 0),
        lax.broadcasted_iota(jnp.int32, shape, 1),
    )


def up(field, axis):
    return pltpu.roll(field, field.shape[axis] - 1, axis)


def down(field, axis):
    return pltpu.roll(field, 1, axis)


def taps(a, b, c):
    i, y = iotas(a.shape)
    rows, cols = a.shape
    return (
        1.0 - 4.0 * c,
        jnp.where(i < rows - 1, c - a, 0.0),
        jnp.where(i > 0, c + a, 0.0),
        jnp.where(y < cols - 1, c - b, 0.0),
        jnp.where(y > 0, c + b, 0.0),
    )


def forward(state, coeffs):
    mid, east, west, north, south = coeffs
    return (
        mid * state
        + east * up(state, 0)
        + west * down(state, 0)
        + north * up(state, 1)
        + south * down(state, 1)
    )


def adjoint(state, coeffs):
    mid, east, west, north, south = coeffs
    return (
        mid * state
        + down(east * state, 0)
        + up(west * state, 0)
        + down(north * state, 1)
        + up(south * state, 1)
    )


EDGE = ("mid_low", "mid_high", "north_low", "north_high", "south_low", "south_high")
EDGE += ("west_low", "west_next", "east_high", "east_next", "east_low", "west_high")


def forward_body(s_ref, a_ref, b_ref, c_ref, moved_ref, high_ref, low_ref, edge_ref):
    levels, rows, _ = s_ref.shape
    last = rows - 1
    for lev in range(levels):
        s, a, b, c = s_ref[lev], a_ref[lev], b_ref[lev], c_ref[lev]
        coeffs = taps(a, b, c)
        once = forward(s, coeffs)
        moved_ref[lev] = forward(once, coeffs)
        mid, east, west, north, south = coeffs
        at = pl.ds(lev, 1)
        open_east = c[last : last + 1] - a[last : last + 1]
        open_west = c[0:1] + a[0:1]
        high_ref[0, at] = s[last : last + 1]
        high_ref[1, at] = once[last : last + 1]
        high_ref[2, at] = open_east
        low_ref[0, at] = s[0:1]
        low_ref[1, at] = once[0:1]
        low_ref[2, at] = open_west
        rows_of = {
            "mid_low": mid[0:1],
            "mid_high": mid[last : last + 1],
            "north_low": north[0:1],
            "north_high": north[last : last + 1],
            "south_low": south[0:1],
            "south_high": south[last : last + 1],
            "west_low": open_west,
            "west_next": west[1:2],
            "east_high": open_east,
            "east_next": east[last - 1 : last],
            "east_low": east[0:1],
            "west_high": west[last : last + 1],
        }
        for n, key in enumerate(EDGE):
            edge_ref[n, at] = rows_of[key]


def adjoint_body(
    a_ref, b_ref, c_ref, inner_ref, outer_ref, high_ref, low_ref, back_ref, first_ref, second_ref
):
    levels, rows, _ = a_ref.shape
    last = rows - 1
    position, peers = lax.axis_index("tm"), lax.axis_size("tm")
    odd = lax.rem(lax.axis_index("tile"), 2)
    for n in range(3):
        first_ref[n] = jnp.where(odd == 0, high_ref[n], low_ref[n])
        second_ref[n] = jnp.where(odd == 0, low_ref[n], high_ref[n])
    for lev in range(levels):
        a, b, c = a_ref[lev], b_ref[lev], c_ref[lev]
        later = jnp.where(lax.rem(position, 2) == 0, inner_ref[lev], outer_ref[lev])
        later = jnp.where(position < peers - 1, later, 0.0)
        coeffs = taps(a, b, c)
        once = adjoint(later, coeffs)
        back_ref[lev] = adjoint(once, coeffs)
        at = pl.ds(lev, 1)
        east = c[last : last + 1] - a[last : last + 1]
        west = c[0:1] + a[0:1]
        highs = (east * later[last : last + 1], east * once[last : last + 1])
        lows = (west * later[0:1], west * once[0:1])
        for n in range(2):
            first_ref[3 + n, at] = jnp.where(odd == 0, highs[n], lows[n])
            second_ref[3 + n, at] = jnp.where(odd == 0, lows[n], highs[n])


def edges_body(
    first_ref, second_ref, got_first_ref, got_second_ref, edge_ref, moved_ref, back_ref
):
    tile, tiles = lax.axis_index("tile"), lax.axis_size("tile")
    odd = lax.rem(tile, 2)
    has_low, has_high = tile > 0, tile < tiles - 1

    def sides(n):
        below = jnp.where(odd == 0, got_second_ref[n], got_first_ref[n])
        above = jnp.where(odd == 0, got_first_ref[n], got_second_ref[n])
        return jnp.where(has_low, below, 0.0), jnp.where(has_high, above, 0.0)

    def own(n):
        one, two = first_ref[n], second_ref[n]
        return jnp.where(odd == 0, two, one), jnp.where(odd == 0, one, two)

    k = {key: edge_ref[n] for n, key in enumerate(EDGE)}
    (s_low, s_high), (w_low, w_high), (east_below, west_above) = sides(0), sides(1), sides(2)
    (p_low, p_high), (q_low, q_high) = sides(3), sides(4)
    (my_s_low, my_s_high), (my_p_low, my_p_high) = own(0), own(3)

    def along(x, mid, north, south):
        return mid * x + north * up(x, 1) + south * down(x, 1)

    def across(x, mid, north, south):
        return mid * x + down(north * x, 1) + up(south * x, 1)

    new_low = k["west_low"] * s_low
    new_high = k["east_high"] * s_high
    low = (k["mid_low"], k["north_low"], k["south_low"])
    high = (k["mid_high"], k["north_high"], k["south_high"])
    moved_ref[0] = along(new_low, *low) + k["west_low"] * (w_low + east_below * my_s_low)
    moved_ref[1] = k["west_next"] * new_low
    moved_ref[2] = k["east_next"] * new_high
    moved_ref[3] = along(new_high, *high) + k["east_high"] * (w_high + west_above * my_s_high)
    back_ref[0] = across(p_low, *low) + (q_low + east_below * my_p_low)
    back_ref[1] = k["east_low"] * p_low
    back_ref[2] = k["west_high"] * p_high
    back_ref[3] = across(p_high, *high) + (q_high + west_above * my_p_high)


def thirds(x):
    one = x.astype(jnp.bfloat16)
    rest = x - one.astype(F32)
    two = rest.astype(jnp.bfloat16)
    return one, two, (rest - two.astype(F32)).astype(jnp.bfloat16)


def observe_body(
    incr_ref, mult_ref, rhs_ref, err_ref, cell_ref, dual_ref, want_ref, var_ref, count_ref,
    local_ref, held_ref, dir_ref, sums_ref,
):
    levels, rows, cols = incr_ref.shape
    slots = cell_ref.shape[1]
    lines = levels * rows
    cell = cell_ref[...]
    _, slot = iotas(cell.shape)
    valid = jnp.where(slot < count_ref[0, 0], 1.0, 0.0)
    dual = dual_ref[...]
    line, col = cell // cols, lax.rem(cell, cols)
    at_line = iotas((lines, slots))[0] == line
    at_col = jnp.where(iotas((cols, slots))[0] == col, 1.0, 0.0).astype(jnp.bfloat16)
    weights = thirds(jnp.where(at_line, valid * dual, 0.0))
    spread = lax.dot_general(
        jnp.concatenate(weights, 0), at_col, (((1,), (1,)), ((), ())), preferred_element_type=F32
    )
    fields = thirds(incr_ref[...].reshape(lines, cols))
    picked = jnp.dot(jnp.concatenate(fields, 0), at_col, preferred_element_type=F32)
    picked = picked[:lines] + picked[lines : 2 * lines] + picked[2 * lines :]
    hx = jnp.sum(jnp.where(at_line, picked, 0.0), axis=0, keepdims=True) * valid
    var = var_ref[...]
    res = valid * (want_ref[...] - (var * dual + hx))
    direction = res / var
    dir_ref[...] = direction
    sums_ref[0] = res * direction
    sums_ref[1] = direction * direction
    ht = spread[:lines] + spread[lines : 2 * lines] + spread[2 * lines :]
    mult = mult_ref[...]
    held_ref[...] = mult + ht.reshape(levels, rows, cols)
    local_ref[...] = rhs_ref[...] - (err_ref[...] * mult + incr_ref[...])


def share_body(local_ref, moved_ref, held_ref, back_ref, out_ref):
    half = out_ref.shape[1]
    away = pl.ds((1 - lax.rem(lax.axis_index("tm"), 2)) * half, half)
    out_ref[0] = local_ref[away]
    out_ref[1] = moved_ref[away]
    out_ref[2] = held_ref[away] - back_ref[away]


def corrected(field, fix):
    rows = field.shape[0]
    i, _ = iotas(field.shape)
    for n, row in enumerate((0, 1, rows - 2, rows - 1)):
        field = field + jnp.where(i == row, fix[n], 0.0)
    return field


def pairs_body(
    local_ref, moved_ref, held_ref, back_ref, fix_ref, got_ref, got_fix_ref, terms_ref, send_ref
):
    half = got_ref.shape[1]
    position = lax.axis_index("tm")
    side = lax.rem(position, 2)
    low_pair = position < 2

    def pick(i, lev):
        fix_m = [fix_ref[0, n, pl.ds(lev, 1)] for n in range(4)]
        fix_b = [fix_ref[1, n, pl.ds(lev, 1)] for n in range(4)]
        got_m = [got_fix_ref[0, n, pl.ds(lev, 1)] for n in range(4)]
        got_b = [got_fix_ref[1, n, pl.ds(lev, 1)] for n in range(4)]
        mine = (
            local_ref[lev],
            corrected(moved_ref[lev], fix_m),
            corrected(held_ref[lev] - back_ref[lev], [-x for x in fix_b]),
        )
        other = (
            got_ref[0, i],
            corrected(got_ref[1, i], got_m),
            corrected(got_ref[2, i], [-x for x in got_b]),
        )
        even = [jnp.where(side == 0, x, y) for x, y in zip(mine, other)]
        odd = [jnp.where(side == 0, y, x) for x, y in zip(mine, other)]
        return even, odd

    for i in range(half):
        (l0, m0, t0), (l1, m1, t1) = pick(i, side * half + i)
        model1 = l1 + m0
        terms_ref[0, i] = jnp.where(low_pair, l0, t1)
        terms_ref[1, i] = jnp.where(low_pair, model1, t0)
        terms_ref[2, i] = jnp.where(low_pair, t1, l0)
        terms_ref[3, i] = jnp.where(low_pair, t0, model1)
        send_ref[0, i] = jnp.where(low_pair, l0 + model1, t1 + t0)
        send_ref[1, i] = jnp.where(low_pair, m1, 0.0)


def dots_body(terms_ref, got_ref, obs_ref, keep_ref, send_ref, sums_ref):
    half, rows, cols = terms_ref.shape[1:]
    position = lax.axis_index("tm")
    low_pair = position < 2
    inner = (position == 1) | (position == 2)
    numer, denom = jnp.zeros((8, 128), F32), jnp.zeros((8, 128), F32)

    def folded(x):
        total = None
        for r in range(0, rows, 8):
            for col in range(0, cols, 128):
                part = x[r : r + 8, col : col + 128]
                total = part if total is None else total + part
        return total

    for i in range(half):
        y0, y1, z0, z1 = (terms_ref[n, i] for n in range(4))
        z0 = z0 + got_ref[1, i]
        one = y0 + y1
        two = got_ref[0, i] + z0
        three = two + z1
        numer = numer + folded(y0 * y0 + y1 * one + z0 * two + z1 * three)
        denom = denom + folded(y0 * y0 + one * one + two * two + three * three)
        here = (jnp.where(inner, one, y0), jnp.where(inner, two, three))
        there = (jnp.where(inner, y0, one), jnp.where(inner, three, two))
        for ref, (own_side, far_side) in ((keep_ref, here), (send_ref, there)):
            ref[0, i] = jnp.where(low_pair, own_side, far_side)
            ref[1, i] = jnp.where(low_pair, far_side, own_side)
    slots = obs_ref.shape[2]
    for n, total in enumerate((numer, denom)):
        obs = obs_ref[n]
        row = obs[:, 0:128]
        for col in range(128, slots, 128):
            row = row + obs[:, col : col + 128]
        sums_ref[n] = total
        sums_ref[n, 0:1] = total[0:1] + row


def update_body(
    mult_ref, incr_ref, dual_ref, dir_ref, keep_ref, got_ref, sums_ref, new_m_ref, new_i_ref, new_o_ref
):
    half = keep_ref.shape[1]
    side = lax.rem(lax.axis_index("tm"), 2)
    total = [
        jnp.sum(jnp.sum(sums_ref[n], axis=0, keepdims=True), axis=1, keepdims=True)
        for n in range(2)
    ]
    step = total[0] / total[1]
    for i in range(half):
        for ref, place in ((keep_ref, side), (got_ref, 1 - side)):
            lev = place * half + i
            new_m_ref[lev] = mult_ref[lev] + step * ref[0, i]
            new_i_ref[lev] = incr_ref[lev] - step * ref[1, i]
    new_o_ref[...] = dual_ref[...] + step * dir_ref[...]


def flat_pairs(tiles, peers, partner):
    pairs = []
    for t in range(tiles):
        for k in range(peers):
            to_t, to_k = partner(t, k)
            pairs.append((t * peers + k, to_t * peers + to_k))
    return pairs


def swap(value, axis, distance):
    return lax.ppermute(value, axis, [(i, i ^ distance) for i in range(lax.axis_size(axis))])


def shifted(value, steps):
    count = lax.axis_size("tm")
    pairs = [(i, i + steps) for i in range(count) if 0 <= i + steps < count]
    return lax.ppermute(value, "tm", pairs)


def scanned(value, direction):
    reach = 1
    while reach < lax.axis_size("tm"):
        value = value + shifted(value, direction * reach)
        reach *= 2
    return value


def shards(
    multiplier, increment, obs_dual, rhs_model, rhs_obs, model_err, obs_err,
    drift_east, drift_north, diffusion, obs_cell, obs_count,
):
    tiles, peers = lax.axis_size("tile"), lax.axis_size("tm")
    mult, incr = multiplier[0], increment[0]
    coeffs = [drift_east[0], drift_north[0], diffusion[0]]
    levels, rows, cols = mult.shape
    field, half = mult.shape, levels // 2
    both = ("tile", "tm")

    def across(t, k):
        if 0 < k < peers - 1:
            return t, (k - 1 if k % 2 == 0 else k + 1)
        return t ^ 1, k

    def second_side(t, k):
        if 0 < t < tiles - 1:
            return (t - 1 if t % 2 == 0 else t + 1), k
        return t, k ^ 1

    outer = lax.ppermute(mult, both, flat_pairs(tiles, peers, across))
    inner = swap(mult, "tm", 1)
    moved, high, low, edge = kernel_call(
        forward_body,
        "forward",
        [(x, "far") for x in (incr, *coeffs)],
        [(field, "near")] + [((3, levels, cols), "near")] * 2 + [((len(EDGE), levels, cols), "near")],
    )
    back, first, second = kernel_call(
        adjoint_body,
        "adjoint",
        [(x, "far") for x in coeffs] + [(x, "near") for x in (inner, outer, high, low)],
        [(field, "near")] + [((5, levels, cols), "near")] * 2,
    )
    got_first = swap(first, "tile", 1)
    got_second = lax.ppermute(second, both, flat_pairs(tiles, peers, second_side))
    local, held, dir_obs, obs_sums = kernel_call(
        observe_body,
        "observe",
        [(x, "far") for x in (incr, mult, rhs_model[0], model_err[0])]
        + [(x, "far") for x in (obs_cell, obs_dual, rhs_obs, obs_err)]
        + [(obs_count, "scalar")],
        [(field, "near")] * 2 + [(obs_dual.shape, "near"), ((2, *obs_dual.shape), "near")],
    )
    near = lambda *arrays: [(x, "near") for x in arrays]
    fix_shape = ((4, levels, cols), "near")
    fix_moved, fix_back = kernel_call(
        edges_body, "edges", near(first, second, got_first, got_second, edge), [fix_shape] * 2
    )
    fix = jnp.stack([fix_moved, fix_back])
    if peers != 4:
        return scan_path(
            multiplier, increment, obs_dual, local, moved, held, back, fix, dir_obs, obs_sums
        )
    share = kernel_call(
        share_body, "share", near(local, moved, held, back), [((3, half, rows, cols), "near")]
    )[0]
    got_share = swap(share, "tm", 1)
    got_fix = swap(fix, "tm", 1)
    part = (half, rows, cols)
    terms, send = kernel_call(
        pairs_body,
        "pairs",
        near(local, moved, held, back, fix, got_share, got_fix),
        [((4, *part), "near"), ((2, *part), "near")],
    )
    got = swap(send, "tm", 2)
    keep, give, sums = kernel_call(
        dots_body,
        "dots",
        near(terms, got, obs_sums),
        [((2, *part), "near"), ((2, *part), "near"), ((2, 8, 128), "near")],
    )
    sums = sums + swap(sums, "tm", 1)
    got_dirs = swap(give, "tm", 1)
    sums = sums + swap(sums, "tm", 2)
    sums = reduced(sums, "tile")
    new_m, new_i, new_o = kernel_call(
        update_body,
        "update",
        [(mult, "near"), (incr, "near"), (obs_dual, "far")] + near(dir_obs, keep, got_dirs, sums),
        [(field, "far"), (field, "far"), (obs_dual.shape, "far")],
    )
    return new_m[None], new_i[None], new_o


def reduced(value, axis):
    distance = 1
    while distance < lax.axis_size(axis):
        value = value + swap(value, axis, distance)
        distance *= 2
    return value


def scan_path(multiplier, increment, obs_dual, local, moved, held, back, fix, dir_obs, obs_sums):
    rows = local.shape[1]
    fix = jnp.moveaxis(fix, 1, 2)
    at = jnp.array([0, 1, rows - 2, rows - 1])
    moved = moved.at[:, at].add(fix[0])
    res_incr = -(held - back.at[:, at].add(fix[1]))
    res_model = local + shifted(moved, 1)
    dir_model, dir_incr = scanned(res_model, 1), scanned(res_incr, -1)
    numer = jnp.sum(res_model * dir_model) + jnp.sum(res_incr * dir_incr) + jnp.sum(obs_sums[0])
    denom = jnp.sum(dir_model**2) + jnp.sum(dir_incr**2) + jnp.sum(obs_sums[1])
    sums = reduced(reduced(jnp.stack([numer, denom]), "tm"), "tile")
    step = sums[0] / sums[1]
    return (
        multiplier + step * dir_model[None],
        increment + step * dir_incr[None],
        obs_dual + step * dir_obs,
    )


def solution(mesh):
    grid = P(("groups", "tm"), None, "tile", None)
    line = P(("groups", "tm"), "tile")
    return jax.shard_map(
        shards,
        mesh=mesh,
        in_specs=(grid, grid, line, grid, line, grid, line, grid, grid, grid, line, line),
        out_specs=(grid, grid, line),
        check_vma=False,
    )
```

time: 152 us -> 42.4 us (0.28)
  blocking collectives: 33.1 us -> 0 us
  waiting for transfers between devices: 40.9 us -> 18.8 us
  starting transfers between devices: 32.8 us -> 13.5 us
  between operations: 20.5 us -> 1.43 us
  other arithmetic: 17.8 us -> 0.02 us
  Pallas kernels: 0 us -> 3.42 us
    all_gather x2 -> x0, waiting for transfers between devices: 35.9 us -> none  [prefix(): everything = lax.all_gather(array, axis)]
    psum x1 -> x0, blocking collectives: 33.1 us -> none  [shards(): numer, denom = lax.psum((numer_part, denom_part), ('tile', 'tm'))]
    ppermute x12, starting transfers between devices: 32.7 us -> 13.5 us  [the longest x10 10.2 us: swap(): lax.ppermute(value, axis, [(i, i ^ distance) for i in range(lax.axis_size...]
    ppermute x12, waiting for transfers between devices: 4.28 us -> 18.8 us  [the longest x10 18.8 us: swap(): lax.ppermute(value, axis, [(i, i ^ distance) for i in range(lax.axis_size...]
    select_n x9 -> x0, other arithmetic: 8.48 us -> none  [the longest x8 8.47 us: lap(): return jnp.where(reached, new, before)]
    pallas_call x0 -> x8, Pallas kernels: none -> 3.42 us  [kernel_call(): pl.pallas_call(body, name=name, out_shape=out_shape, in_specs=in_specs, o...]
    scatter-add x1 -> x0, other arithmetic: 3.33 us -> none  [shards(): jnp.zeros(flat_incr.shape, jnp.float32).at[cells].add((valid * obs_dual)[0])]
    unnamed x28 -> x30, local copies, waits for them, and re-layouts: 1.77 us -> 4.93 us
  transfers between devices with their start and end apart: 14 -> 12, of which waited for: 4 -> 7; matrix products, arithmetic and copies ran while one was open for 10% -> 0% of each run, Pallas kernels for 0% -> 4%
where the time goes in v1:
time: 42.4 us; the launch traced here: 42.1 us
  waiting for transfers between devices  18.8 us (44%)
  starting transfers between devices  13.5 us (32%)
  local copies, waits for them, and re-layouts  4.93 us (12%)
  Pallas kernels  3.42 us (8%)
  between operations  1.43 us (3%)
    ppermute x10, waiting for transfers between devices, swap(): lax.ppermute(value, axis, [(i, i ^ distance) for i in range(lax.axis_size...  18.8 us
    ppermute x10, starting transfers between devices, swap(): lax.ppermute(value, axis, [(i, i ^ distance) for i in range(lax.axis_size...  10.2 us
    unnamed x30, local copies, waits for them, and re-layouts  4.93 us
    pallas_call x8, Pallas kernels, kernel_call(): pl.pallas_call(body, name=name, out_shape=out_shape, in_specs=in_specs, o...  3.42 us
    ppermute x1, starting transfers between devices, shards(): outer = lax.ppermute(mult, both, flat_pairs(tiles, peers, across))  3.09 us
  transfers between devices with their start and end apart: 12, of which 7 were waited for; matrix products, arithmetic and copies ran while one was open for 0% of the time, Pallas kernels for 4%

profile of v1, /device:TPU:0, one launch (start us, length us, event | category | flops | bytes accessed | tf_op | source)
XLA Modules:
  0.0 42.1 jit_solution(5193977107558273879)
XLA Ops:
  0.6 3.1 %collective-permute-start.1 = (f32[8,16,512]{2,1,0:T(8,128)}, f32[8,16,512]{2,1,0:T(8,128)S(1)}, u32[]{:S(2)}, u32[]{:S(2)}) collective-permute-start(f32[8,16,512]{2,1,0:T(8,128)} %bitcast.20), channel_id=1, source_target_pairs={{0,4},{1,2},{2,1},{3,7},{4,0},{5,6},{6,5},{7,3},{8,12},{9,10},{10,... | collective-permute-start | bytes 786440 | tf_op jit(solution)/shard_map/ppermute | solution.py:393
  3.7 0.0 collective-permute-start
  4.4 0.0 copy-start
  4.4 0.9 %copy-done = f32[1,8,16,512]{3,2,1,0:T(8,128)S(1)} copy-done((f32[1,8,16,512]{3,2,1,0:T(8,128)S(1)}, f32[1,8,16,512]{3,2,1,0:T(8,128)}, u32[]{:S(2)}) %copy-start) | copy-done | bytes 262168
  5.4 0.0 copy-start.2
  5.4 0.9 %copy-done.2 = f32[1,8,16,512]{3,2,1,0:T(8,128)S(1)} copy-done((f32[1,8,16,512]{3,2,1,0:T(8,128)S(1)}, f32[1,8,16,512]{3,2,1,0:T(8,128)}, u32[]{:S(2)}) %copy-start.2) | copy-done | bytes 262168
  6.3 0.0 copy-start.4
  6.3 0.9 %copy-done.4 = f32[1,8,16,512]{3,2,1,0:T(8,128)S(1)} copy-done((f32[1,8,16,512]{3,2,1,0:T(8,128)S(1)}, f32[1,8,16,512]{3,2,1,0:T(8,128)}, u32[]{:S(2)}) %copy-start.4) | copy-done | bytes 262168
  7.3 0.0 copy-start.6
  7.3 0.9 %copy-done.6 = f32[1,8,16,512]{3,2,1,0:T(8,128)S(1)} copy-done((f32[1,8,16,512]{3,2,1,0:T(8,128)S(1)}, f32[1,8,16,512]{3,2,1,0:T(8,128)}, u32[]{:S(2)}) %copy-start.6) | copy-done | bytes 262168
  8.2 0.0 copy-start.8
  8.2 0.0 copy-start.9
  8.2 0.0 copy-start.10
  8.2 0.0 copy-start.12
  8.2 0.0 copy-start.13
  8.2 0.0 copy-start.14
  8.2 0.7 %forward.1 = (f32[8,16,512]{2,1,0:T(8,128)S(1)}, f32[3,8,512]{2,1,0:T(8,128)S(1)}, f32[3,8,512]{2,1,0:T(8,128)S(1)}, f32[12,8,512]{2,1,0:T(8,128)S(1)}) custom-call(f32[8,16,512]{2,1,0:T(8,128)S(1)} %bitcast.11, f32[8,16,512]{2,1,0:T(8,128)S(1)} %bitcast.14, f32[8,16,512]{2,1,0:T(8,128)S(1)} %bitcast.16, f32[8,16,512]{2,1,0:T(8,128)S(1)} %bitcast.18), custom_call_target="tpu_custom_call" | custom-call | tf_op jit(solution)/shard_map/forward/pallas_call | solution.py:27
  9.0 0.0 copy-start.11
  9.0 0.2 copy-done.8
  9.2 0.1 copy-done.9
  9.2 0.1 copy-done.10
  9.3 0.0 copy-done.12
  9.3 0.0 copy-done.13
  9.3 0.0 copy-done.14
  9.3 0.4 copy-done.11
  9.7 0.0 copy-start.3
  9.7 0.0 copy-start.5
  9.7 0.0 copy-start.7
  9.7 0.7 %observe.1 = (f32[8,16,512]{2,1,0:T(8,128)S(1)}, f32[8,16,512]{2,1,0:T(8,128)S(1)}, f32[1,512]{1,0:T(1,128)S(1)}, f32[2,1,512]{2,1,0:T(1,128)S(1)}) custom-call(f32[8,16,512]{2,1,0:T(8,128)S(1)} %bitcast.12, f32[8,16,512]{2,1,0:T(8,128)S(1)} %bitcast.22, f32[8,16,512]{2,1,0:T(8,128)S(1)} %bitcast.24, f32[8,16,512]{2,1,0:T(8,128)S(1)} %bitcast.25, ...), custom_call_target="tpu_custom_call" | custom-call | tf_op jit(solution)/shard_map/observe/pallas_call | solution.py:27
  10.4 0.0 collective-permute-done.1.outer_ref
  10.4 0.0 collective-permute-done.inner_ref
  10.4 0.2 copy-done.3
  10.7 0.1 copy-done.5
  10.7 0.1 copy-done.7
  10.8 0.6 %adjoint.1 = (f32[8,16,512]{2,1,0:T(8,128)S(1)}, f32[5,8,512]{2,1,0:T(8,128)S(1)}, f32[5,8,512]{2,1,0:T(8,128)S(1)}) custom-call(f32[8,16,512]{2,1,0:T(8,128)S(1)} %bitcast.15, f32[8,16,512]{2,1,0:T(8,128)S(1)} %bitcast.17, f32[8,16,512]{2,1,0:T(8,128)S(1)} %bitcast.19, f32[8,16,512]{2,1,0:T(8,128)S(1)} %collective-permute-done.inner_ref, ...), custom_call_target="tpu_custom_call" | custom-call | tf_op jit(solution)/shard_map/adjoint/pallas_call | solution.py:27
  11.5 0.5 %collective-permute-start.4 = (f32[3,4,16,512]{3,2,1,0:T(8,128)S(1)}, f32[3,4,16,512]{3,2,1,0:T(8,128)S(1)}, u32[]{:S(2)}, u32[]{:S(2)}) collective-permute-start(f32[3,4,16,512]{3,2,1,0:T(8,128)S(1)} %share.1), channel_id=1, source_target_pairs={{0,1},{1,0},{2,3},{3,2},{4,5},{5,4},{6,7},{7,6},{8,9},{9,8},{10,11... | collective-permute-start | bytes 1179656 | tf_op jit(solution)/shard_map/ppermute | solution.py:355
  12.1 1.2 %collective-permute-start.2 = (f32[5,8,512]{2,1,0:T(8,128)S(1)}, f32[5,8,512]{2,1,0:T(8,128)S(1)}, u32[]{:S(2)}, u32[]{:S(2)}) collective-permute-start(f32[5,8,512]{2,1,0:T(8,128)S(1)} %get-tuple-element.31.first_ref), channel_id=1, source_target_pairs={{0,4},{4,0},{8,12},{12,8},{1,5},{5,1},{9,13},{13,9},{2,6},{6,2},{1... | collective-permute-start | bytes 245768 | tf_op jit(solution)/shard_map/ppermute | solution.py:355
  13.2 0.2 collective-permute-start.3
  13.4 3.1 %collective-permute-done.2.got_first_ref = f32[5,8,512]{2,1,0:T(8,128)S(1)} collective-permute-done((f32[5,8,512]{2,1,0:T(8,128)S(1)}, f32[5,8,512]{2,1,0:T(8,128)S(1)}, u32[]{:S(2)}, u32[]{:S(2)}) %collective-permute-start.2) | collective-permute-done | bytes 81952 | tf_op jit(solution)/shard_map/ppermute | solution.py:355
  16.5 0.0 collective-permute-done.3.got_second_ref
  16.5 0.1 edges.1
  16.6 0.1 collective-permute-start.5
  16.7 1.3 %collective-permute-done.5.got_fix_ref = f32[2,4,8,512]{3,2,1,0:T(8,128)S(1)} collective-permute-done((f32[2,4,8,512]{3,2,1,0:T(8,128)S(1)}, f32[2,4,8,512]{3,2,1,0:T(8,128)S(1)}, u32[]{:S(2)}, u32[]{:S(2)}) %collective-permute-start.5) | collective-permute-done | bytes 131104 | tf_op jit(solution)/shard_map/ppermute | solution.py:355
  18.0 0.0 collective-permute-done.4.got_ref
  18.1 0.2 pairs.1
  18.2 1.0 %collective-permute-start.6 = (f32[2,4,16,512]{3,2,1,0:T(8,128)S(1)}, f32[2,4,16,512]{3,2,1,0:T(8,128)S(1)}, u32[]{:S(2)}, u32[]{:S(2)}) collective-permute-start(f32[2,4,16,512]{3,2,1,0:T(8,128)S(1)} %get-tuple-element.37), channel_id=1, source_target_pairs={{0,2},{1,3},{2,0},{3,1},{4,6},{5,7},{6,4},{7,5},{8,10},{9,11},{10,... | collective-permute-start | bytes 786440 | tf_op jit(solution)/shard_map/ppermute | solution.py:355
  19.3 7.4 %collective-permute-done.6.got_ref = f32[2,4,16,512]{3,2,1,0:T(8,128)S(1)} collective-permute-done((f32[2,4,16,512]{3,2,1,0:T(8,128)S(1)}, f32[2,4,16,512]{3,2,1,0:T(8,128)S(1)}, u32[]{:S(2)}, u32[]{:S(2)}) %collective-permute-start.6) | collective-permute-done | bytes 262176 | tf_op jit(solution)/shard_map/ppermute | solution.py:355
  26.7 0.0 copy-start.1
  26.7 0.1 dots.1
  26.8 0.1 collective-permute-start.7
  26.9 0.5 %collective-permute-start.8 = (f32[2,8,128]{2,1,0:T(8,128)S(1)}, f32[2,8,128]{2,1,0:T(8,128)S(1)}, u32[]{:S(2)}, u32[]{:S(2)}) collective-permute-start(f32[2,8,128]{2,1,0:T(8,128)S(1)} %get-tuple-element.41), channel_id=1, source_target_pairs={{0,1},{1,0},{2,3},{3,2},{4,5},{5,4},{6,7},{7,6},{8,9},{9,8},{10,11... | collective-permute-start | bytes 24584 | tf_op jit(solution)/shard_map/ppermute | solution.py:355
  27.4 1.0 %collective-permute-done.8 = f32[2,8,128]{2,1,0:T(8,128)S(1)} collective-permute-done((f32[2,8,128]{2,1,0:T(8,128)S(1)}, f32[2,8,128]{2,1,0:T(8,128)S(1)}, u32[]{:S(2)}, u32[]{:S(2)}) %collective-permute-start.8) | collective-permute-done | bytes 8224 | tf_op jit(solution)/shard_map/ppermute | solution.py:355
  28.4 1.0 %collective-permute-start.9 = (f32[2,8,128]{2,1,0:T(8,128)S(1)}, f32[2,8,128]{2,1,0:T(8,128)S(1)}, u32[]{:S(2)}, u32[]{:S(2)}) collective-permute-start(f32[2,8,128]{2,1,0:T(8,128)S(1)} %add.12), channel_id=1, source_target_pairs={{0,2},{1,3},{2,0},{3,1},{4,6},{5,7},{6,4},{7,5},{8,10},{9,11},{10,... | collective-permute-start | bytes 24584 | tf_op jit(solution)/shard_map/ppermute | solution.py:355
  29.4 2.7 %collective-permute-done.9 = f32[2,8,128]{2,1,0:T(8,128)S(1)} collective-permute-done((f32[2,8,128]{2,1,0:T(8,128)S(1)}, f32[2,8,128]{2,1,0:T(8,128)S(1)}, u32[]{:S(2)}, u32[]{:S(2)}) %collective-permute-start.9) | collective-permute-done | bytes 8224 | tf_op jit(solution)/shard_map/ppermute | solution.py:355
  32.1 2.7 %collective-permute-start.10 = (f32[2,8,128]{2,1,0:T(8,128)S(1)}, f32[2,8,128]{2,1,0:T(8,128)S(1)}, u32[]{:S(2)}, u32[]{:S(2)}) collective-permute-start(f32[2,8,128]{2,1,0:T(8,128)S(1)} %add.13), channel_id=1, source_target_pairs={{0,4},{4,0},{8,12},{12,8},{1,5},{5,1},{9,13},{13,9},{2,6},{6,2},{1... | collective-permute-start | bytes 24584 | tf_op jit(solution)/shard_map/ppermute | solution.py:355
  34.7 1.6 %collective-permute-done.10 = f32[2,8,128]{2,1,0:T(8,128)S(1)} collective-permute-done((f32[2,8,128]{2,1,0:T(8,128)S(1)}, f32[2,8,128]{2,1,0:T(8,128)S(1)}, u32[]{:S(2)}, u32[]{:S(2)}) %collective-permute-start.10) | collective-permute-done | bytes 8224 | tf_op jit(solution)/shard_map/ppermute | solution.py:355
  36.4 3.2 %collective-permute-start.11 = (f32[2,8,128]{2,1,0:T(8,128)S(1)}, f32[2,8,128]{2,1,0:T(8,128)S(1)}, u32[]{:S(2)}, u32[]{:S(2)}) collective-permute-start(f32[2,8,128]{2,1,0:T(8,128)S(1)} %add.14), channel_id=1, source_target_pairs={{0,8},{4,12},{8,0},{12,4},{1,9},{5,13},{9,1},{13,5},{2,10},{6,14},... | collective-permute-start | bytes 24584 | tf_op jit(solution)/shard_map/ppermute | solution.py:355
  39.6 1.6 %collective-permute-done.11 = f32[2,8,128]{2,1,0:T(8,128)S(1)} collective-permute-done((f32[2,8,128]{2,1,0:T(8,128)S(1)}, f32[2,8,128]{2,1,0:T(8,128)S(1)}, u32[]{:S(2)}, u32[]{:S(2)}) %collective-permute-start.11) | collective-permute-done | bytes 8224 | tf_op jit(solution)/shard_map/ppermute | solution.py:355
  41.2 0.0 collective-permute-done.7.got_ref
  41.2 0.0 copy-done.1
  41.2 0.9 %update.1 = (f32[8,16,512]{2,1,0:T(8,128)}, f32[8,16,512]{2,1,0:T(8,128)}, f32[1,512]{1,0:T(1,128)}) custom-call(f32[8,16,512]{2,1,0:T(8,128)S(1)} %bitcast.23, f32[8,16,512]{2,1,0:T(8,128)S(1)} %bitcast.13, f32[1,512]{1,0:T(1,128)S(1)} %copy-done.11, f32[1,512]{1,0:T(1,128)S(1)} %get-tuple-element.24.dir_ref, ...), custom_call_target="tpu_custom_call" | custom-call | tf_op jit(solution)/shard_map/update/pallas_call | solution.py:27
  (6 shorter events, 0.1 us)
Async XLA Ops:
  0.6 9.8 %collective-permute-start.1 = (f32[8,16,512]{2,1,0:T(8,128)}, f32[8,16,512]{2,1,0:T(8,128)S(1)}, u32[]{:S(2)}, u32[]{:S(2)}) collective-permute-start(f32[8,16,512]{2,1,0:T(8,128)} %bitcast.20), channel_id=1, source_target_pairs={{0,4},{1,2},{2,1},{3,7},{4,0},{5,6},{6,5},{7,3},{8,12},{9,10},{10,... | collective-permute-start | bytes 786440 | tf_op jit(solution)/shard_map/ppermute | solution.py:393
  3.7 6.7 %collective-permute-start = (f32[8,16,512]{2,1,0:T(8,128)}, f32[8,16,512]{2,1,0:T(8,128)S(1)}, u32[]{:S(2)}, u32[]{:S(2)}) collective-permute-start(f32[8,16,512]{2,1,0:T(8,128)} %bitcast.21), channel_id=1, source_target_pairs={{0,1},{1,0},{2,3},{3,2},{4,5},{5,4},{6,7},{7,6},{8,9},{9,8},{10,11... | collective-permute-start | bytes 786440 | tf_op jit(solution)/shard_map/ppermute | solution.py:355
  4.4 1.0 %copy-start = (f32[1,8,16,512]{3,2,1,0:T(8,128)S(1)}, f32[1,8,16,512]{3,2,1,0:T(8,128)}, u32[]{:S(2)}) copy-start(f32[1,8,16,512]{3,2,1,0:T(8,128)} %param.13) | copy-start | bytes 786436
  5.4 0.9 %copy-start.2 = (f32[1,8,16,512]{3,2,1,0:T(8,128)S(1)}, f32[1,8,16,512]{3,2,1,0:T(8,128)}, u32[]{:S(2)}) copy-start(f32[1,8,16,512]{3,2,1,0:T(8,128)} %param.19) | copy-start | bytes 786436
  6.3 0.9 %copy-start.4 = (f32[1,8,16,512]{3,2,1,0:T(8,128)S(1)}, f32[1,8,16,512]{3,2,1,0:T(8,128)}, u32[]{:S(2)}) copy-start(f32[1,8,16,512]{3,2,1,0:T(8,128)} %param.20) | copy-start | bytes 786436
  7.3 0.9 %copy-start.6 = (f32[1,8,16,512]{3,2,1,0:T(8,128)S(1)}, f32[1,8,16,512]{3,2,1,0:T(8,128)}, u32[]{:S(2)}) copy-start(f32[1,8,16,512]{3,2,1,0:T(8,128)} %param.21) | copy-start | bytes 786436
  8.2 0.9 %copy-start.8 = (f32[1,8,16,512]{3,2,1,0:T(8,128)S(1)}, f32[1,8,16,512]{3,2,1,0:T(8,128)}, u32[]{:S(2)}) copy-start(f32[1,8,16,512]{3,2,1,0:T(8,128)} %param.12) | copy-start | bytes 786436
  8.2 1.0 %copy-start.9 = (f32[1,8,16,512]{3,2,1,0:T(8,128)S(1)}, f32[1,8,16,512]{3,2,1,0:T(8,128)}, u32[]{:S(2)}) copy-start(f32[1,8,16,512]{3,2,1,0:T(8,128)} %param.15) | copy-start | bytes 786436
  8.2 1.1 %copy-start.10 = (f32[1,8,16,512]{3,2,1,0:T(8,128)S(1)}, f32[1,8,16,512]{3,2,1,0:T(8,128)}, u32[]{:S(2)}) copy-start(f32[1,8,16,512]{3,2,1,0:T(8,128)} %param.17) | copy-start | bytes 786436
  8.2 1.1 %copy-start.12 = (s32[1,512]{1,0:T(1,128)S(1)}, s32[1,512]{1,0:T(1,128)}, u32[]{:S(2)}) copy-start(s32[1,512]{1,0:T(1,128)} %cell_ref.1) | copy-start | bytes 6148
  8.2 1.1 %copy-start.13 = (f32[1,512]{1,0:T(1,128)S(1)}, f32[1,512]{1,0:T(1,128)}, u32[]{:S(2)}) copy-start(f32[1,512]{1,0:T(1,128)} %want_ref.1) | copy-start | bytes 6148
  8.2 1.1 %copy-start.14 = (f32[1,512]{1,0:T(1,128)S(1)}, f32[1,512]{1,0:T(1,128)}, u32[]{:S(2)}) copy-start(f32[1,512]{1,0:T(1,128)} %var_ref.1) | copy-start | bytes 6148
  9.0 0.7 %copy-start.11 = (f32[1,512]{1,0:T(1,128)S(1)}, f32[1,512]{1,0:T(1,128)}, u32[]{:S(2)}) copy-start(f32[1,512]{1,0:T(1,128)} %dual_ref.3) | copy-start | bytes 6148
  9.7 0.9 %copy-start.3 = (f32[1,8,16,512]{3,2,1,0:T(8,128)S(1)}, f32[1,8,16,512]{3,2,1,0:T(8,128)}, u32[]{:S(2)}) copy-start(f32[1,8,16,512]{3,2,1,0:T(8,128)} %param.19) | copy-start | bytes 786436
  9.7 1.0 %copy-start.5 = (f32[1,8,16,512]{3,2,1,0:T(8,128)S(1)}, f32[1,8,16,512]{3,2,1,0:T(8,128)}, u32[]{:S(2)}) copy-start(f32[1,8,16,512]{3,2,1,0:T(8,128)} %param.20) | copy-start | bytes 786436
  9.7 1.1 %copy-start.7 = (f32[1,8,16,512]{3,2,1,0:T(8,128)S(1)}, f32[1,8,16,512]{3,2,1,0:T(8,128)}, u32[]{:S(2)}) copy-start(f32[1,8,16,512]{3,2,1,0:T(8,128)} %param.21) | copy-start | bytes 786436
  11.5 6.5 %collective-permute-start.4 = (f32[3,4,16,512]{3,2,1,0:T(8,128)S(1)}, f32[3,4,16,512]{3,2,1,0:T(8,128)S(1)}, u32[]{:S(2)}, u32[]{:S(2)}) collective-permute-start(f32[3,4,16,512]{3,2,1,0:T(8,128)S(1)} %share.1), channel_id=1, source_target_pairs={{0,1},{1,0},{2,3},{3,2},{4,5},{5,4},{6,7},{7,6},{8,9},{9,8},{10,11... | collective-permute-start | bytes 1179656 | tf_op jit(solution)/shard_map/ppermute | solution.py:355
  12.1 4.4 %collective-permute-start.2 = (f32[5,8,512]{2,1,0:T(8,128)S(1)}, f32[5,8,512]{2,1,0:T(8,128)S(1)}, u32[]{:S(2)}, u32[]{:S(2)}) collective-permute-start(f32[5,8,512]{2,1,0:T(8,128)S(1)} %get-tuple-element.31.first_ref), channel_id=1, source_target_pairs={{0,4},{4,0},{8,12},{12,8},{1,5},{5,1},{9,13},{13,9},{2,6},{6,2},{1... | collective-permute-start | bytes 245768 | tf_op jit(solution)/shard_map/ppermute | solution.py:355
  13.2 3.3 %collective-permute-start.3 = (f32[5,8,512]{2,1,0:T(8,128)S(1)}, f32[5,8,512]{2,1,0:T(8,128)S(1)}, u32[]{:S(2)}, u32[]{:S(2)}) collective-permute-start(f32[5,8,512]{2,1,0:T(8,128)S(1)} %get-tuple-element.32.second_ref), channel_id=1, source_target_pairs={{0,1},{1,0},{2,3},{3,2},{4,8},{5,9},{6,10},{7,11},{8,4},{9,5},{10,... | collective-permute-start | bytes 245768 | tf_op jit(solution)/shard_map/ppermute | solution.py:408
  16.6 1.4 %collective-permute-start.5 = (f32[2,4,8,512]{3,2,1,0:T(8,128)S(1)}, f32[2,4,8,512]{3,2,1,0:T(8,128)S(1)}, u32[]{:S(2)}, u32[]{:S(2)}) collective-permute-start(f32[2,4,8,512]{3,2,1,0:T(8,128)S(1)} %pad_maximum_fusion.fix_ref), channel_id=1, source_target_pairs={{0,1},{1,0},{2,3},{3,2},{4,5},{5,4},{6,7},{7,6},{8,9},{9,8},{10,11... | collective-permute-start | bytes 393224 | tf_op jit(solution)/shard_map/ppermute | solution.py:355
  18.2 8.4 %collective-permute-start.6 = (f32[2,4,16,512]{3,2,1,0:T(8,128)S(1)}, f32[2,4,16,512]{3,2,1,0:T(8,128)S(1)}, u32[]{:S(2)}, u32[]{:S(2)}) collective-permute-start(f32[2,4,16,512]{3,2,1,0:T(8,128)S(1)} %get-tuple-element.37), channel_id=1, source_target_pairs={{0,2},{1,3},{2,0},{3,1},{4,6},{5,7},{6,4},{7,5},{8,10},{9,11},{10,... | collective-permute-start | bytes 786440 | tf_op jit(solution)/shard_map/ppermute | solution.py:355
  26.7 14.6 %copy-start.1 = (f32[1,8,16,512]{3,2,1,0:T(8,128)S(1)}, f32[1,8,16,512]{3,2,1,0:T(8,128)}, u32[]{:S(2)}) copy-start(f32[1,8,16,512]{3,2,1,0:T(8,128)} %param.13) | copy-start | bytes 786436
  26.8 14.4 %collective-permute-start.7 = (f32[2,4,16,512]{3,2,1,0:T(8,128)S(1)}, f32[2,4,16,512]{3,2,1,0:T(8,128)S(1)}, u32[]{:S(2)}, u32[]{:S(2)}) collective-permute-start(f32[2,4,16,512]{3,2,1,0:T(8,128)S(1)} %get-tuple-element.40), channel_id=1, source_target_pairs={{0,1},{1,0},{2,3},{3,2},{4,5},{5,4},{6,7},{7,6},{8,9},{9,8},{10,11... | collective-permute-start | bytes 786440 | tf_op jit(solution)/shard_map/ppermute | solution.py:355
  26.9 1.5 %collective-permute-start.8 = (f32[2,8,128]{2,1,0:T(8,128)S(1)}, f32[2,8,128]{2,1,0:T(8,128)S(1)}, u32[]{:S(2)}, u32[]{:S(2)}) collective-permute-start(f32[2,8,128]{2,1,0:T(8,128)S(1)} %get-tuple-element.41), channel_id=1, source_target_pairs={{0,1},{1,0},{2,3},{3,2},{4,5},{5,4},{6,7},{7,6},{8,9},{9,8},{10,11... | collective-permute-start | bytes 24584 | tf_op jit(solution)/shard_map/ppermute | solution.py:355
  28.4 3.7 %collective-permute-start.9 = (f32[2,8,128]{2,1,0:T(8,128)S(1)}, f32[2,8,128]{2,1,0:T(8,128)S(1)}, u32[]{:S(2)}, u32[]{:S(2)}) collective-permute-start(f32[2,8,128]{2,1,0:T(8,128)S(1)} %add.12), channel_id=1, source_target_pairs={{0,2},{1,3},{2,0},{3,1},{4,6},{5,7},{6,4},{7,5},{8,10},{9,11},{10,... | collective-permute-start | bytes 24584 | tf_op jit(solution)/shard_map/ppermute | solution.py:355
  32.1 4.3 %collective-permute-start.10 = (f32[2,8,128]{2,1,0:T(8,128)S(1)}, f32[2,8,128]{2,1,0:T(8,128)S(1)}, u32[]{:S(2)}, u32[]{:S(2)}) collective-permute-start(f32[2,8,128]{2,1,0:T(8,128)S(1)} %add.13), channel_id=1, source_target_pairs={{0,4},{4,0},{8,12},{12,8},{1,5},{5,1},{9,13},{13,9},{2,6},{6,2},{1... | collective-permute-start | bytes 24584 | tf_op jit(solution)/shard_map/ppermute | solution.py:355
  36.4 4.8 %collective-permute-start.11 = (f32[2,8,128]{2,1,0:T(8,128)S(1)}, f32[2,8,128]{2,1,0:T(8,128)S(1)}, u32[]{:S(2)}, u32[]{:S(2)}) collective-permute-start(f32[2,8,128]{2,1,0:T(8,128)S(1)} %add.14), channel_id=1, source_target_pairs={{0,8},{4,12},{8,0},{12,4},{1,9},{5,13},{9,1},{13,5},{2,10},{6,14},... | collective-permute-start | bytes 24584 | tf_op jit(solution)/shard_map/ppermute | solution.py:355

commit v2 on v1

v2 whole, which is shorter than its diff:
```python
import jax
import jax.numpy as jnp
from jax import lax
from jax.experimental import pallas as pl
from jax.experimental.pallas import tpu as pltpu
from jax.sharding import PartitionSpec as P

F32 = jnp.float32
VMEM = pltpu.VMEM
GRANT = 24 * 1024 * 1024


def kernel_call(body, name, inputs, outputs, scratch=()):
    arrays, in_specs = [], []
    for array, home in inputs:
        if home == "far":
            in_specs.append(pl.BlockSpec(memory_space=pltpu.HBM))
            array = pltpu.with_memory_space_constraint(array, pltpu.HBM)
        else:
            in_specs.append(pl.BlockSpec(memory_space=VMEM))
            array = pltpu.with_memory_space_constraint(array, VMEM)
        arrays.append(array)
    out_shape = []
    for shape, home, *dtype in outputs:
        dtype = dtype[0] if dtype else F32
        out_shape.append(
            VMEM(shape, dtype) if home == "near" else jax.ShapeDtypeStruct(shape, dtype)
        )
    return pl.pallas_call(
        body,
        name=name,
        out_shape=out_shape,
        in_specs=in_specs,
        out_specs=[pl.BlockSpec(memory_space=VMEM)] * len(outputs),
        scratch_shapes=list(scratch),
        cost_estimate=pl.CostEstimate(flops=1, bytes_accessed=1, transcendentals=0),
        compiler_params=pltpu.CompilerParams(vmem_limit_bytes=GRANT),
    )(*arrays)


def lanes(row):
    total = row[:, 0:128]
    for col in range(128, row.shape[1], 128):
        total = total + row[:, col : col + 128]
    return total


def iotas(shape):
    return (
        lax.broadcasted_iota(jnp.int32, shape, 0),
        lax.broadcasted_iota(jnp.int32, shape, 1),
    )


def up(field, axis):
    return pltpu.roll(field, field.shape[axis] - 1, axis)


def down(field, axis):
    return pltpu.roll(field, 1, axis)


def taps(a, b, c):
    i, y = iotas(a.shape)
    rows, cols = a.shape
    return (
        1.0 - 4.0 * c,
        jnp.where(i < rows - 1, c - a, 0.0),
        jnp.where(i > 0, c + a, 0.0),
        jnp.where(y < cols - 1, c - b, 0.0),
        jnp.where(y > 0, c + b, 0.0),
    )


def forward(state, coeffs):
    mid, east, west, north, south = coeffs
    return (
        mid * state
        + east * up(state, 0)
        + west * down(state, 0)
        + north * up(state, 1)
        + south * down(state, 1)
    )


def adjoint(state, coeffs):
    mid, east, west, north, south = coeffs
    return (
        mid * state
        + down(east * state, 0)
        + up(west * state, 0)
        + down(north * state, 1)
        + up(south * state, 1)
    )


EDGE = ("mid_low", "mid_high", "north_low", "north_high", "south_low", "south_high")
EDGE += ("west_low", "west_next", "east_high", "east_next", "east_low", "west_high")


def begin_body(count, *refs):
    sources, targets = refs[:count], refs[count : 2 * count]
    moved_ref, high_ref, low_ref, edge_ref, sems = refs[2 * count :]
    copies = [
        pltpu.make_async_copy(source, target, sems.at[n])
        for n, (source, target) in enumerate(zip(sources, targets))
    ]
    for copy in copies:
        copy.start()
    for copy in copies[:4]:
        copy.wait()
    s_ref, a_ref, b_ref, c_ref = targets[:4]
    levels, rows, _ = s_ref.shape
    last = rows - 1
    for lev in range(levels):
        s, a, b, c = s_ref[lev], a_ref[lev], b_ref[lev], c_ref[lev]
        coeffs = taps(a, b, c)
        once = forward(s, coeffs)
        moved_ref[lev] = forward(once, coeffs)
        mid, east, west, north, south = coeffs
        at = pl.ds(lev, 1)
        open_east = c[last : last + 1] - a[last : last + 1]
        open_west = c[0:1] + a[0:1]
        high_ref[0, at] = s[last : last + 1]
        high_ref[1, at] = once[last : last + 1]
        high_ref[2, at] = open_east
        low_ref[0, at] = s[0:1]
        low_ref[1, at] = once[0:1]
        low_ref[2, at] = open_west
        rows_of = {
            "mid_low": mid[0:1],
            "mid_high": mid[last : last + 1],
            "north_low": north[0:1],
            "north_high": north[last : last + 1],
            "south_low": south[0:1],
            "south_high": south[last : last + 1],
            "west_low": open_west,
            "west_next": west[1:2],
            "east_high": open_east,
            "east_next": east[last - 1 : last],
            "east_low": east[0:1],
            "west_high": west[last : last + 1],
        }
        for n, key in enumerate(EDGE):
            edge_ref[n, at] = rows_of[key]
    for copy in copies[4:]:
        copy.wait()


def adjoint_body(a_ref, b_ref, c_ref, later_ref, back_ref):
    for lev in range(a_ref.shape[0]):
        coeffs = taps(a_ref[lev], b_ref[lev], c_ref[lev])
        back_ref[lev] = adjoint(adjoint(later_ref[lev], coeffs), coeffs)


def outer_products(k, later):
    def once(side, at, beside):
        mid, north, south = k["mid_" + side], k["north_" + side], k["south_" + side]
        return mid * at + beside + down(north * at, 1) + up(south * at, 1)

    west, east = k["west_low"], k["east_high"]
    return (
        (west * later[0], west * once("low", later[0], k["west_next"] * later[1])),
        (east * later[3], east * once("high", later[3], k["east_next"] * later[2])),
    )


def outer_rows(ref, levels, wanted):
    rows = ref.shape[1]
    picked = []
    for row in (0, 1, rows - 2, rows - 1):
        value = jnp.concatenate([ref[lev, row : row + 1] for lev in range(levels)], 0)
        picked.append(jnp.where(wanted, value, 0.0))
    return picked


def rims_body(wanted, edge_ref, later_ref, high_ref, low_ref, first_ref, second_ref):
    odd = lax.rem(lax.axis_index("tile"), 2)
    k = {key: edge_ref[n] for n, key in enumerate(EDGE)}
    low, high = outer_products(k, outer_rows(later_ref, edge_ref.shape[1], wanted()))
    lows = [low_ref[n] for n in range(3)] + list(low)
    highs = [high_ref[n] for n in range(3)] + list(high)
    for n in range(5):
        first_ref[n] = jnp.where(odd == 0, highs[n], lows[n])
        second_ref[n] = jnp.where(odd == 0, lows[n], highs[n])


def late_rims_body(edge_ref, later_ref, first_ref, second_ref):
    odd = lax.rem(lax.axis_index("tile"), 2)
    k = {key: edge_ref[n] for n, key in enumerate(EDGE)}
    low, high = outer_products(k, outer_rows(later_ref, edge_ref.shape[1], lax.axis_index("tm") == 1))
    for n in range(2):
        first_ref[n] = jnp.where(odd == 0, high[n], low[n])
        second_ref[n] = jnp.where(odd == 0, low[n], high[n])


def sides(first, second):
    tile, tiles = lax.axis_index("tile"), lax.axis_size("tile")
    odd = lax.rem(tile, 2)
    below, above = jnp.where(odd == 0, second, first), jnp.where(odd == 0, first, second)
    return jnp.where(tile > 0, below, 0.0), jnp.where(tile < tiles - 1, above, 0.0)


def own_sides(first, second):
    odd = lax.rem(lax.axis_index("tile"), 2)
    return jnp.where(odd == 0, second, first), jnp.where(odd == 0, first, second)


def back_fix(k, product, stepped, own_product, toward):
    def across(x, side):
        mid, north, south = k["mid_" + side], k["north_" + side], k["south_" + side]
        return mid * x + down(north * x, 1) + up(south * x, 1)

    return (
        across(product[0], "low") + (stepped[0] + toward[0] * own_product[0]),
        k["east_low"] * product[0],
        k["west_high"] * product[1],
        across(product[1], "high") + (stepped[1] + toward[1] * own_product[1]),
    )


def edges_body(first_ref, second_ref, got_first_ref, got_second_ref, edge_ref, fix_ref):
    k = {key: edge_ref[n] for n, key in enumerate(EDGE)}
    state, stepped, toward, product, product_stepped = (
        sides(got_first_ref[n], got_second_ref[n]) for n in range(5)
    )
    own_state = own_sides(first_ref[0], second_ref[0])
    own_product = own_sides(first_ref[3], second_ref[3])

    def along(x, side):
        mid, north, south = k["mid_" + side], k["north_" + side], k["south_" + side]
        return mid * x + north * up(x, 1) + south * down(x, 1)

    new_low, new_high = k["west_low"] * state[0], k["east_high"] * state[1]
    fix_ref[0] = along(new_low, "low") + k["west_low"] * (stepped[0] + toward[0] * own_state[0])
    fix_ref[1] = k["west_next"] * new_low
    fix_ref[2] = k["east_next"] * new_high
    fix_ref[3] = along(new_high, "high") + k["east_high"] * (stepped[1] + toward[1] * own_state[1])
    for n, row in enumerate(back_fix(k, product, product_stepped, own_product, toward)):
        fix_ref[4 + n] = row


def late_edges_body(
    first_ref, second_ref, got_first_ref, got_second_ref, past_first_ref, past_second_ref,
    edge_ref, fix_ref,
):
    k = {key: edge_ref[n] for n, key in enumerate(EDGE)}
    product, stepped = (sides(got_first_ref[n], got_second_ref[n]) for n in range(2))
    toward = sides(past_first_ref[2], past_second_ref[2])
    own_product = own_sides(first_ref[0], second_ref[0])
    for n, row in enumerate(back_fix(k, product, stepped, own_product, toward)):
        fix_ref[n] = row


def thirds(x):
    one = x.astype(jnp.bfloat16)
    rest = x - one.astype(F32)
    two = rest.astype(jnp.bfloat16)
    return one, two, (rest - two.astype(F32)).astype(jnp.bfloat16)


def observe_body(
    incr_ref, mult_ref, rhs_ref, err_ref, cell_ref, dual_ref, want_ref, var_ref, valid_ref,
    local_ref, held_ref, dir_ref, sums_ref,
):
    levels, rows, cols = incr_ref.shape
    slots = cell_ref.shape[1]
    lines = levels * rows
    cell = cell_ref[...]
    valid = valid_ref[...]
    dual = dual_ref[...]
    line, col = cell // cols, lax.rem(cell, cols)
    at_line = iotas((lines, slots))[0] == line
    at_col = jnp.where(iotas((cols, slots))[0] == col, 1.0, 0.0).astype(jnp.bfloat16)
    weights = thirds(jnp.where(at_line, valid * dual, 0.0))
    spread = lax.dot_general(
        jnp.concatenate(weights, 0), at_col, (((1,), (1,)), ((), ())), preferred_element_type=F32
    )
    fields = thirds(incr_ref[...].reshape(lines, cols))
    picked = jnp.dot(jnp.concatenate(fields, 0), at_col, preferred_element_type=F32)
    picked = picked[:lines] + picked[lines : 2 * lines] + picked[2 * lines :]
    hx = jnp.sum(jnp.where(at_line, picked, 0.0), axis=0, keepdims=True) * valid
    var = var_ref[...]
    res = valid * (want_ref[...] - (var * dual + hx))
    direction = res / var
    dir_ref[...] = direction
    sums_ref[0] = res * direction
    sums_ref[1] = direction * direction
    ht = spread[:lines] + spread[lines : 2 * lines] + spread[2 * lines :]
    mult = mult_ref[...]
    held_ref[...] = mult + ht.reshape(levels, rows, cols)
    local_ref[...] = rhs_ref[...] - (err_ref[...] * mult + incr_ref[...])


def corrected(field, fix):
    rows = field.shape[0]
    i, _ = iotas(field.shape)
    for n, row in enumerate((0, 1, rows - 2, rows - 1)):
        field = field + jnp.where(i == row, fix[n], 0.0)
    return field


def fixes(ref, start, lev):
    return [ref[start + n, pl.ds(lev, 1)] for n in range(4)]


def minus(rows):
    return [-x for x in rows]


def share_body(
    a_ref, b_ref, c_ref, inner_ref, local_ref, moved_ref, held_ref, fix_ref, own_ref, urgent_ref
):
    position = lax.axis_index("tm")
    first, low_pair = lax.rem(position, 2) == 0, position < 2
    for lev in range(a_ref.shape[0]):
        coeffs = taps(a_ref[lev], b_ref[lev], c_ref[lev])
        back = adjoint(adjoint(inner_ref[lev], coeffs), coeffs)
        back = corrected(jnp.where(first, back, 0.0), fixes(fix_ref, 4, lev))
        moved = corrected(moved_ref[lev], fixes(fix_ref, 0, lev))
        local = local_ref[lev]
        residual = held_ref[lev] - back
        own_ref[0, lev] = local
        own_ref[1, lev] = moved
        own_ref[2, lev] = residual
        urgent_ref[lev] = jnp.where(low_pair, local + moved, residual)


def sends_body(own_ref, got_ref, fix_ref, send_ref):
    _, levels, rows, _ = own_ref.shape
    low_pair = lax.axis_index("tm") < 2
    for lev in range(levels):
        mine = jnp.where(low_pair, own_ref[0, lev], own_ref[2, lev])
        send_ref[lev * rows : (lev + 1) * rows] = mine + got_ref[lev]
    for n in range(4):
        start = levels * rows + n * levels
        send_ref[start : start + levels] = fix_ref[n]


def rest_body(own_ref, obs_ref, out_ref):
    levels = own_ref.shape[1]
    low_pair = lax.axis_index("tm") < 2
    for lev in range(levels):
        out_ref[lev] = own_ref[0, lev]
        out_ref[levels + lev] = jnp.where(low_pair, own_ref[2, lev], own_ref[1, lev])
    out_ref[2 * levels] = jnp.zeros(out_ref.shape[1:], F32)
    for n in range(2):
        out_ref[2 * levels, n : n + 1, 0:128] = lanes(obs_ref[n])


def terms_body(
    a_ref, b_ref, c_ref, cross_ref, own_ref, got_ref, rest_ref, fix_ref, terms_ref, known_ref
):
    low_pair = lax.axis_index("tm") < 2
    levels = own_ref.shape[1]
    for lev in range(levels):
        coeffs = taps(a_ref[lev], b_ref[lev], c_ref[lev])
        cross, got = cross_ref[lev], got_ref[lev]
        local, residual = own_ref[0, lev], own_ref[2, lev]
        back = corrected(adjoint(adjoint(cross, coeffs), coeffs), fixes(fix_ref, 0, lev))
        rest0, rest1 = rest_ref[lev], rest_ref[levels + lev]
        terms_ref[0, lev] = jnp.where(low_pair, rest0, residual)
        terms_ref[1, lev] = jnp.where(low_pair, local, residual) + got
        terms_ref[2, lev] = jnp.where(low_pair, residual - back, rest0 + cross)
        terms_ref[3, lev] = jnp.where(low_pair, rest1, local + rest1)
        known_ref[lev] = jnp.where(low_pair, local, residual + got)


def dots_body(terms_ref, got_ref, rest_ref, obs_ref, keep_ref, give_ref, sums_ref):
    _, levels, rows, cols = terms_ref.shape
    low_pair = lax.axis_index("tm") < 2
    numer, denom = jnp.zeros((8, 128), F32), jnp.zeros((8, 128), F32)

    def folded(x):
        total = None
        for r in range(0, rows, 8):
            part = lanes(x[r : r + 8])
            total = part if total is None else total + part
        return total

    for lev in range(levels):
        y0, one, z0, z1 = (terms_ref[n, lev] for n in range(4))
        late = []
        for n in range(4):
            at = levels * rows + n * levels + lev
            late.append(jnp.where(low_pair, 0.0, got_ref[at : at + 1]))
        z0 = corrected(z0, late)
        two = got_ref[lev * rows : (lev + 1) * rows] + z0
        three = two + z1
        numer = numer + folded(y0 * y0 + (one - y0) * one + z0 * two + z1 * three)
        denom = denom + folded(y0 * y0 + one * one + two * two + three * three)
        keep_ref[0, lev] = jnp.where(low_pair, one, three)
        keep_ref[1, lev] = jnp.where(low_pair, two, y0)
        give_ref[lev] = jnp.where(low_pair, three, two)
    for n, total in enumerate((numer, denom)):
        sums_ref[n] = total
        obs = lanes(obs_ref[n]) + rest_ref[2 * levels, n : n + 1, 0:128]
        sums_ref[n, 0:1] = total[0:1] + obs


def update_body(
    mult_ref, incr_ref, dual_ref, dir_ref, keep_ref, known_ref, got_ref, sums_ref,
    new_m_ref, new_i_ref, new_o_ref,
):
    position = lax.axis_index("tm")
    leads, low_pair = lax.rem(position, 2) == 1, position < 2
    total = [
        jnp.sum(jnp.sum(sums_ref[n], axis=0, keepdims=True), axis=1, keepdims=True)
        for n in range(2)
    ]
    step = total[0] / total[1]
    for lev in range(mult_ref.shape[0]):
        known, got = known_ref[lev], got_ref[lev]
        model = jnp.where(leads, keep_ref[0, lev], jnp.where(low_pair, known, got))
        back = jnp.where(leads, keep_ref[1, lev], jnp.where(low_pair, got, known))
        new_m_ref[lev] = mult_ref[lev] + step * model
        new_i_ref[lev] = incr_ref[lev] - step * back
    new_o_ref[...] = dual_ref[...] + step * dir_ref[...]


def exchange(value, partner):
    groups, tiles, peers = (lax.axis_size(x) for x in ("groups", "tile", "tm"))
    pairs = []
    for g in range(groups):
        for t in range(tiles):
            for k in range(peers):
                to_g, to_t, to_k = partner(g, t, k)
                target = (to_g * tiles + to_t) * peers + to_k
                pairs.append(((g * tiles + t) * peers + k, target))
    return lax.ppermute(value, ("groups", "tile", "tm"), pairs)


def swap(value, axis, distance):
    return lax.ppermute(value, axis, [(i, i ^ distance) for i in range(lax.axis_size(axis))])


def aside(g, t, k):
    return (g ^ 1, t, k) if lax.axis_size("groups") % 2 == 0 else (g, t ^ 1, k)


def leaders(value, tile, tm):
    return exchange(
        value, lambda g, t, k: (g, t ^ tile, k ^ tm) if k % 2 else aside(g, t, k)
    )


def next_pair(g, t, k):
    if 0 < k < lax.axis_size("tm") - 1:
        return g, t, (k - 1 if k % 2 == 0 else k + 1)
    return aside(g, t, k)


def second_side(g, t, k):
    if 0 < t < lax.axis_size("tile") - 1:
        return g, (t - 1 if t % 2 == 0 else t + 1), k
    return g, t, k ^ 1


def shifted(value, steps):
    count = lax.axis_size("tm")
    pairs = [(i, i + steps) for i in range(count) if 0 <= i + steps < count]
    return lax.ppermute(value, "tm", pairs)


def scanned(value, direction):
    reach = 1
    while reach < lax.axis_size("tm"):
        value = value + shifted(value, direction * reach)
        reach *= 2
    return value


def reduced(value, axis):
    distance = 1
    while distance < lax.axis_size(axis):
        value = value + swap(value, axis, distance)
        distance *= 2
    return value


def near(*arrays):
    return [(x, "near") for x in arrays]


def shards(
    multiplier, increment, obs_dual, rhs_model, rhs_obs, model_err, obs_err,
    drift_east, drift_north, diffusion, obs_cell, obs_count,
):
    tiles, peers = lax.axis_size("tile"), lax.axis_size("tm")
    levels, rows, cols = multiplier.shape[1:]
    field = ((levels, rows, cols), "near")
    lines = lambda n: ((n, levels, cols), "near")

    inner = swap(multiplier[0], "tm", 1)
    arguments = [increment[0], drift_east[0], drift_north[0], diffusion[0], multiplier[0]]
    arguments += [rhs_model[0], model_err[0], obs_cell, obs_dual, rhs_obs, obs_err]
    count = len(arguments)
    *here, moved, high, low, edge = kernel_call(
        lambda *refs: begin_body(count, *refs),
        "begin",
        [(x, "far") for x in arguments],
        [(x.shape, "near", x.dtype) for x in arguments]
        + [field, lines(3), lines(3), lines(len(EDGE))],
        [pltpu.SemaphoreType.DMA((count,))],
    )
    incr, *coeffs = here[:4]
    mult, rhs, err, cell, dual, want, var = here[4:]
    if peers == 4:
        later, wanted = inner, lambda: lax.rem(lax.axis_index("tm"), 2) == 0
    else:
        later = jnp.where(lax.axis_index("tm") % 2 == 0, inner, exchange(mult, next_pair))
        wanted = lambda: lax.axis_index("tm") < peers - 1
    first, second = kernel_call(
        lambda *refs: rims_body(wanted, *refs),
        "rims",
        near(edge, later, high, low),
        [lines(5), lines(5)],
    )
    got_first = swap(first, "tile", 1)
    got_second = exchange(second, second_side)
    valid = (lax.broadcasted_iota(jnp.int32, obs_cell.shape, 1) < obs_count).astype(F32)
    local, held, dir_obs, obs_sums = kernel_call(
        observe_body,
        "observe",
        near(incr, mult, rhs, err, cell, dual, want, var, valid),
        [field] * 2 + [(obs_dual.shape, "near"), ((2, *obs_dual.shape), "near")],
    )
    fix = kernel_call(
        edges_body, "edges", near(first, second, got_first, got_second, edge), [lines(8)]
    )[0]
    if peers != 4:
        later = jnp.where(lax.axis_index("tm") == peers - 1, 0.0, later)
        back = kernel_call(adjoint_body, "adjoint", near(*coeffs, later), [field])[0]
        return scan_path(
            multiplier, increment, obs_dual, local, moved, held, back, fix, dir_obs, obs_sums
        )
    cross = jnp.where(lax.axis_index("tm") < 2, moved, inner)
    got_cross = leaders(jnp.pad(cross, ((0, 1), (0, 0), (0, 0))), 0, 2)
    own, urgent = kernel_call(
        share_body,
        "share",
        near(*coeffs, inner, local, moved, held, fix),
        [((3, levels, rows, cols), "near"), field],
    )
    got = swap(urgent, "tm", 1)
    send = kernel_call(
        sends_body, "sends", near(own, got, fix), [((levels * rows + 4 * levels, cols), "near")]
    )[0]
    send, got_cross, own = lax.optimization_barrier((send, got_cross, own))
    got_send = leaders(send, 0, 2)
    rest = kernel_call(
        rest_body, "rest", near(own, obs_sums), [((2 * levels + 1, rows, cols), "near")]
    )[0]
    got_rest = swap(rest, "tm", 1)
    late_first, late_second = kernel_call(
        late_rims_body, "late_rims", near(edge, got_cross), [lines(2), lines(2)]
    )
    got_late_first = swap(late_first, "tile", 1)
    got_late_second = exchange(late_second, second_side)
    late_fix = kernel_call(
        late_edges_body,
        "late_edges",
        near(late_first, late_second, got_late_first, got_late_second)
        + near(got_first, got_second, edge),
        [lines(4)],
    )[0]
    terms, known = kernel_call(
        terms_body,
        "terms",
        near(*coeffs, got_cross, own, got, got_rest, late_fix),
        [((4, levels, rows, cols), "near"), field],
    )
    pair = ((2, levels, rows, cols), "near")
    keep, give, sums = kernel_call(
        dots_body, "dots", near(terms, got_send, got_rest, obs_sums), [pair, field, ((2, 8, 128), "near")]
    )
    total = sums + leaders(sums, 0, 2) + leaders(sums, 1, 0) + leaders(sums, 1, 2)
    distance = 2
    while distance < tiles:
        total = total + leaders(total, distance, 0)
        distance *= 2
    give, total = lax.optimization_barrier((give, total))
    got_dir = swap(give, "tm", 1)
    other = swap(total, "tm", 1)
    total = jnp.where(lax.axis_index("tm") % 2 == 1, total, other)
    new_m, new_i, new_o = kernel_call(
        update_body,
        "update",
        near(mult, incr, dual, dir_obs, keep, known, got_dir, total),
        [(mult.shape, "far"), (mult.shape, "far"), (obs_dual.shape, "far")],
    )
    return new_m[None], new_i[None], new_o


def scan_path(multiplier, increment, obs_dual, local, moved, held, back, fix, dir_obs, obs_sums):
    rows = local.shape[1]
    fix = jnp.moveaxis(fix, 0, 1)
    at = jnp.array([0, 1, rows - 2, rows - 1])
    moved = moved.at[:, at].add(fix[:, :4])
    res_incr = -(held - back.at[:, at].add(fix[:, 4:8]))
    res_model = local + shifted(moved, 1)
    dir_model, dir_incr = scanned(res_model, 1), scanned(res_incr, -1)
    numer = jnp.sum(res_model * dir_model) + jnp.sum(res_incr * dir_incr) + jnp.sum(obs_sums[0])
    denom = jnp.sum(dir_model**2) + jnp.sum(dir_incr**2) + jnp.sum(obs_sums[1])
    sums = reduced(reduced(jnp.stack([numer, denom]), "tm"), "tile")
    step = sums[0] / sums[1]
    return (
        multiplier + step * dir_model[None],
        increment + step * dir_incr[None],
        obs_dual + step * dir_obs,
    )


def solution(mesh):
    grid = P(("groups", "tm"), None, "tile", None)
    line = P(("groups", "tm"), "tile")
    return jax.shard_map(
        shards,
        mesh=mesh,
        in_specs=(grid, grid, line, grid, line, grid, line, grid, grid, grid, line, line),
        out_specs=(grid, grid, line),
        check_vma=False,
    )
```

time: 42.4 us -> 33.6 us (0.79)
  waiting for transfers between devices: 18.8 us -> 11.3 us
  local copies, waits for them, and re-layouts: 4.93 us -> 0.02 us
  Pallas kernels: 3.42 us -> 5.88 us
  starting transfers between devices: 13.5 us -> 14.7 us
    ppermute x10 -> x7, waiting for transfers between devices: 18.8 us -> 5 us  [swap(): lax.ppermute(value, axis, [(i, i ^ distance) for i in range(lax.axis_size...]
    ppermute x2 -> x8, waiting for transfers between devices: 0.01 us -> 6.34 us  [exchange(): return lax.ppermute(value, ('groups', 'tile', 'tm'), pairs)]
    unnamed x30 -> x0, local copies, waits for them, and re-layouts: 4.93 us -> none
    ppermute x2 -> x8, starting transfers between devices: 3.25 us -> 7.9 us  [exchange(): return lax.ppermute(value, ('groups', 'tile', 'tm'), pairs)]
    ppermute x10 -> x7, starting transfers between devices: 10.2 us -> 6.85 us  [swap(): lax.ppermute(value, axis, [(i, i ^ distance) for i in range(lax.axis_size...]
    pallas_call x8 -> x12, Pallas kernels: 3.42 us -> 5.88 us  [kernel_call(): pl.pallas_call(body, name=name, out_shape=out_shape, in_specs=in_specs, o...]
  transfers between devices with their start and end apart: 12 -> 15, of which waited for: 7 -> 9; matrix products, arithmetic and copies ran while one was open for 0% -> 0% of each run, Pallas kernels for 4% -> 13%
where the time goes in v2:
time: 33.6 us; the launch traced here: 33.5 us
  starting transfers between devices  14.7 us (44%)
  waiting for transfers between devices  11.3 us (34%)
  Pallas kernels  5.88 us (18%)
  between operations  1.41 us (4%)
    ppermute x8, starting transfers between devices, exchange(): return lax.ppermute(value, ('groups', 'tile', 'tm'), pairs)  7.9 us
    ppermute x7, starting transfers between devices, swap(): lax.ppermute(value, axis, [(i, i ^ distance) for i in range(lax.axis_size...  6.85 us
    ppermute x8, waiting for transfers between devices, exchange(): return lax.ppermute(value, ('groups', 'tile', 'tm'), pairs)  6.34 us
    pallas_call x12, Pallas kernels, kernel_call(): pl.pallas_call(body, name=name, out_shape=out_shape, in_specs=in_specs, o...  5.88 us
    ppermute x7, waiting for transfers between devices, swap(): lax.ppermute(value, axis, [(i, i ^ distance) for i in range(lax.axis_size...  5 us
  transfers between devices with their start and end apart: 15, of which 9 were waited for; matrix products, arithmetic and copies ran while one was open for 0% of the time, Pallas kernels for 13%

profile of v2, /device:TPU:0, one launch (start us, length us, event | category | flops | bytes accessed | tf_op | source)
XLA Modules:
  0.0 33.5 jit_solution(85286348992163265)
XLA Ops:
  0.6 0.5 %collective-permute-start = (f32[8,16,512]{2,1,0:T(8,128)}, f32[8,16,512]{2,1,0:T(8,128)S(1)}, u32[]{:S(2)}, u32[]{:S(2)}) collective-permute-start(f32[8,16,512]{2,1,0:T(8,128)} %bitcast.17), channel_id=1, source_target_pairs={{0,1},{1,0},{2,3},{3,2},{4,5},{5,4},{6,7},{7,6},{8,9},{9,8},{10,11... | collective-permute-start | bytes 786440 | tf_op jit(solution)/shard_map/ppermute | solution.py:434
  1.2 2.0 %begin.1 = (f32[8,16,512]{2,1,0:T(8,128)S(1)}, f32[8,16,512]{2,1,0:T(8,128)S(1)}, f32[8,16,512]{2,1,0:T(8,128)S(1)}, f32[8,16,512]{2,1,0:T(8,128)S(1)}, f32[8,16...) custom-call(f32[8,16,512]{2,1,0:T(8,128)} %bitcast.11, ...), custom_call_target="tpu_custom_call" | custom-call | flops 1 | bytes 1 | tf_op jit(solution)/shard_map/begin/pallas_call | solution.py:29
  3.8 0.0 collective-permute-done.refs_1_.inner_ref
  3.8 0.1 rims.1
  3.9 2.7 %collective-permute-start.1 = (f32[5,8,512]{2,1,0:T(8,128)S(1)}, f32[5,8,512]{2,1,0:T(8,128)S(1)}, u32[]{:S(2)}, u32[]{:S(2)}) collective-permute-start(f32[5,8,512]{2,1,0:T(8,128)S(1)} %get-tuple-element.59.first_ref), channel_id=1, source_target_pairs={{0,4},{4,0},{8,12},{12,8},{1,5},{5,1},{9,13},{13,9},{2,6},{6,2},{1... | collective-permute-start | bytes 245768 | tf_op jit(solution)/shard_map/ppermute | solution.py:434
  6.6 0.2 collective-permute-start.2
  6.9 1.6 %collective-permute-start.4 = (f32[9,16,512]{2,1,0:T(8,128)S(1)}, f32[9,16,512]{2,1,0:T(8,128)S(1)}, u32[]{:S(2)}, u32[]{:S(2)}) collective-permute-start(f32[9,16,512]{2,1,0:T(8,128)S(1)} %pad.4), channel_id=1, source_target_pairs={{0,16},{1,3},{2,18},{3,1},{4,20},{5,7},{6,22},{7,5},{8,24},{9,11},... | collective-permute-start | bytes 884744 | tf_op jit(solution)/shard_map/ppermute | solution.py:430
  8.5 0.7 %observe.1 = (f32[8,16,512]{2,1,0:T(8,128)S(1)}, f32[8,16,512]{2,1,0:T(8,128)S(1)}, f32[1,512]{1,0:T(1,128)S(1)}, f32[2,1,512]{2,1,0:T(1,128)S(1)}) custom-call(f32[8,16,512]{2,1,0:T(8,128)S(1)} %get-tuple-element.42.incr_ref, f32[8,16,512]{2,1,0:T(8,128)S(1)} %get-tuple-element.41.mult_ref, f32[8,16,512]{2,1,0:T(8,128)S(1)} %get-tuple-element.44.rhs_ref, ...), custom_call_target="tpu_custom_call" | custom-call | flops 1 | bytes 1 | tf_op jit(solution)/shard_map/observe/pallas_call | solution.py:29
  9.1 0.5 %collective-permute-done.1.got_first_ref.past_first_ref = f32[5,8,512]{2,1,0:T(8,128)S(1)} collective-permute-done((f32[5,8,512]{2,1,0:T(8,128)S(1)}, f32[5,8,512]{2,1,0:T(8,128)S(1)}, u32[]{:S(2)}, u32[]{:S(2)}) %collective-permute-start.1) | collective-permute-done | bytes 81952 | tf_op jit(solution)/shard_map/ppermute | solution.py:434
  9.7 0.0 collective-permute-done.2.got_second_ref.past_second_ref
  9.7 0.1 edges.1.fix_ref
  9.8 0.7 %share.1 = (f32[3,8,16,512]{3,2,1,0:T(8,128)S(1)}, f32[8,16,512]{2,1,0:T(8,128)S(1)}) custom-call(f32[8,16,512]{2,1,0:T(8,128)S(1)} %get-tuple-element.50.a_ref, f32[8,16,512]{2,1,0:T(8,128)S(1)} %get-tuple-element.51.b_ref, f32[8,16,512]{2,1,0:T(8,128)S(1)} %get-tuple-element.52.c_ref, f32[8,16,512]{2,1,0:T(8,128)S(1)} %collective-permute-done.refs_1_.inner_ref, ...), custom_call_target="tpu_custom_call" | custom-call | flops 1 | bytes 1 | tf_op jit(solution)/shard_map/share/pallas_call | solution.py:29
  10.5 0.1 collective-permute-start.3
  10.6 1.5 %collective-permute-done.3.got_ref = f32[8,16,512]{2,1,0:T(8,128)S(1)} collective-permute-done((f32[8,16,512]{2,1,0:T(8,128)S(1)}, f32[8,16,512]{2,1,0:T(8,128)S(1)}, u32[]{:S(2)}, u32[]{:S(2)}) %collective-permute-start.3) | collective-permute-done | bytes 262176 | tf_op jit(solution)/shard_map/ppermute | solution.py:434
  12.2 1.5 %collective-permute-done.4.later_ref.cross_ref = f32[9,16,512]{2,1,0:T(8,128)S(1)} collective-permute-done((f32[9,16,512]{2,1,0:T(8,128)S(1)}, f32[9,16,512]{2,1,0:T(8,128)S(1)}, u32[]{:S(2)}, u32[]{:S(2)}) %collective-permute-start.4) | collective-permute-done | bytes 294944 | tf_op jit(solution)/shard_map/ppermute | solution.py:430
  13.7 0.1 collective-permute-start.5
  13.8 1.6 %collective-permute-start.8 = (f32[160,512]{1,0:T(8,128)S(1)}, f32[160,512]{1,0:T(8,128)S(1)}, u32[]{:S(2)}, u32[]{:S(2)}) collective-permute-start(f32[160,512]{1,0:T(8,128)S(1)} %sends.1), channel_id=1, source_target_pairs={{0,16},{1,3},{2,18},{3,1},{4,20},{5,7},{6,22},{7,5},{8,24},{9,11},... | collective-permute-start | bytes 983048 | tf_op jit(solution)/shard_map/ppermute | solution.py:430
  15.4 0.1 late_rims.1
  15.5 3.0 %collective-permute-start.6 = (f32[2,8,512]{2,1,0:T(8,128)S(1)}, f32[2,8,512]{2,1,0:T(8,128)S(1)}, u32[]{:S(2)}, u32[]{:S(2)}) collective-permute-start(f32[2,8,512]{2,1,0:T(8,128)S(1)} %get-tuple-element.66.first_ref), channel_id=1, source_target_pairs={{0,4},{4,0},{8,12},{12,8},{1,5},{5,1},{9,13},{13,9},{2,6},{6,2},{1... | collective-permute-start | bytes 98312 | tf_op jit(solution)/shard_map/ppermute | solution.py:434
  18.5 0.0 collective-permute-start.7
  18.5 1.9 %collective-permute-done.6.got_first_ref = f32[2,8,512]{2,1,0:T(8,128)S(1)} collective-permute-done((f32[2,8,512]{2,1,0:T(8,128)S(1)}, f32[2,8,512]{2,1,0:T(8,128)S(1)}, u32[]{:S(2)}, u32[]{:S(2)}) %collective-permute-start.6) | collective-permute-done | bytes 32800 | tf_op jit(solution)/shard_map/ppermute | solution.py:434
  20.4 0.0 collective-permute-done.7.got_second_ref
  20.4 0.1 late_edges.1.fix_ref
  20.5 0.0 collective-permute-done.5.rest_ref
  20.5 0.7 %terms.1 = (f32[4,8,16,512]{3,2,1,0:T(8,128)S(1)}, f32[8,16,512]{2,1,0:T(8,128)S(1)}) custom-call(f32[8,16,512]{2,1,0:T(8,128)S(1)} %get-tuple-element.50.a_ref, f32[8,16,512]{2,1,0:T(8,128)S(1)} %get-tuple-element.51.b_ref, f32[8,16,512]{2,1,0:T(8,128)S(1)} %get-tuple-element.52.c_ref, f32[9,16,512]{2,1,0:T(8,128)S(1)} %collective-permute-done.4.later_ref.cross_ref, ...), custom_call_target="tpu_custom_call" | custom-call | flops 1 | bytes 1 | tf_op jit(solution)/shard_map/terms/pallas_call | solution.py:29
  21.2 0.0 collective-permute-done.8.got_ref
  21.2 0.3 %dots.1 = (f32[2,8,16,512]{3,2,1,0:T(8,128)S(1)}, f32[8,16,512]{2,1,0:T(8,128)S(1)}, f32[2,8,128]{2,1,0:T(8,128)S(1)}) custom-call(f32[4,8,16,512]{3,2,1,0:T(8,128)S(1)} %get-tuple-element.68.terms_ref, f32[160,512]{1,0:T(8,128)S(1)} %collective-permute-done.8.got_ref, f32[17,16,512]{2,1,0:T(8,128)S(1)} %collective-permute-done.5.rest_ref, ...), custom_call_target="tpu_custom_call" | custom-call | flops 1 | bytes 1 | tf_op jit(solution)/shard_map/dots/pallas_call | solution.py:29
  21.6 1.3 %collective-permute-start.11 = (f32[2,8,128]{2,1,0:T(8,128)S(1)}, f32[2,8,128]{2,1,0:T(8,128)S(1)}, u32[]{:S(2)}, u32[]{:S(2)}) collective-permute-start(f32[2,8,128]{2,1,0:T(8,128)S(1)} %get-tuple-element.73), channel_id=1, source_target_pairs={{0,16},{1,7},{2,18},{3,5},{4,20},{5,3},{6,22},{7,1},{8,24},{9,15},... | collective-permute-start | bytes 24584 | tf_op jit(solution)/shard_map/ppermute | solution.py:430
  22.9 0.8 %collective-permute-start.10 = (f32[2,8,128]{2,1,0:T(8,128)S(1)}, f32[2,8,128]{2,1,0:T(8,128)S(1)}, u32[]{:S(2)}, u32[]{:S(2)}) collective-permute-start(f32[2,8,128]{2,1,0:T(8,128)S(1)} %get-tuple-element.73), channel_id=1, source_target_pairs={{0,16},{1,5},{2,18},{3,7},{4,20},{5,1},{6,22},{7,3},{8,24},{9,13},... | collective-permute-start | bytes 24584 | tf_op jit(solution)/shard_map/ppermute | solution.py:430
  23.7 1.2 %collective-permute-start.9 = (f32[2,8,128]{2,1,0:T(8,128)S(1)}, f32[2,8,128]{2,1,0:T(8,128)S(1)}, u32[]{:S(2)}, u32[]{:S(2)}) collective-permute-start(f32[2,8,128]{2,1,0:T(8,128)S(1)} %get-tuple-element.73), channel_id=1, source_target_pairs={{0,16},{1,3},{2,18},{3,1},{4,20},{5,7},{6,22},{7,5},{8,24},{9,11},... | collective-permute-start | bytes 24584 | tf_op jit(solution)/shard_map/ppermute | solution.py:430
  24.9 0.4 %collective-permute-done.11 = f32[2,8,128]{2,1,0:T(8,128)S(1)} collective-permute-done((f32[2,8,128]{2,1,0:T(8,128)S(1)}, f32[2,8,128]{2,1,0:T(8,128)S(1)}, u32[]{:S(2)}, u32[]{:S(2)}) %collective-permute-start.11) | collective-permute-done | bytes 8224 | tf_op jit(solution)/shard_map/ppermute | solution.py:430
  25.3 1.2 %collective-permute-done.10 = f32[2,8,128]{2,1,0:T(8,128)S(1)} collective-permute-done((f32[2,8,128]{2,1,0:T(8,128)S(1)}, f32[2,8,128]{2,1,0:T(8,128)S(1)}, u32[]{:S(2)}, u32[]{:S(2)}) %collective-permute-start.10) | collective-permute-done | bytes 8224 | tf_op jit(solution)/shard_map/ppermute | solution.py:430
  26.5 0.8 %collective-permute-done.9 = f32[2,8,128]{2,1,0:T(8,128)S(1)} collective-permute-done((f32[2,8,128]{2,1,0:T(8,128)S(1)}, f32[2,8,128]{2,1,0:T(8,128)S(1)}, u32[]{:S(2)}, u32[]{:S(2)}) %collective-permute-start.9) | collective-permute-done | bytes 8224 | tf_op jit(solution)/shard_map/ppermute | solution.py:430
  27.3 1.2 %collective-permute-start.12 = (f32[2,8,128]{2,1,0:T(8,128)S(1)}, f32[2,8,128]{2,1,0:T(8,128)S(1)}, u32[]{:S(2)}, u32[]{:S(2)}) collective-permute-start(f32[2,8,128]{2,1,0:T(8,128)S(1)} %add_add_fusion), channel_id=1, source_target_pairs={{0,16},{1,9},{2,18},{3,11},{4,20},{5,13},{6,22},{7,15},{8,24},{9,1... | collective-permute-start | bytes 24584 | tf_op jit(solution)/shard_map/ppermute | solution.py:430
  28.5 2.4 %collective-permute-done.12 = f32[2,8,128]{2,1,0:T(8,128)S(1)} collective-permute-done((f32[2,8,128]{2,1,0:T(8,128)S(1)}, f32[2,8,128]{2,1,0:T(8,128)S(1)}, u32[]{:S(2)}, u32[]{:S(2)}) %collective-permute-start.12) | collective-permute-done | bytes 8224 | tf_op jit(solution)/shard_map/ppermute | solution.py:430
  31.0 0.0 collective-permute-start.13
  31.0 0.5 %collective-permute-start.14 = (f32[2,8,128]{2,1,0:T(8,128)S(1)}, f32[2,8,128]{2,1,0:T(8,128)S(1)}, u32[]{:S(2)}, u32[]{:S(2)}) collective-permute-start(f32[2,8,128]{2,1,0:T(8,128)S(1)} %add.21), channel_id=1, source_target_pairs={{0,1},{1,0},{2,3},{3,2},{4,5},{5,4},{6,7},{7,6},{8,9},{9,8},{10,11... | collective-permute-start | bytes 24584 | tf_op jit(solution)/shard_map/ppermute | solution.py:434
  31.5 1.0 %collective-permute-done.14 = f32[2,8,128]{2,1,0:T(8,128)S(1)} collective-permute-done((f32[2,8,128]{2,1,0:T(8,128)S(1)}, f32[2,8,128]{2,1,0:T(8,128)S(1)}, u32[]{:S(2)}, u32[]{:S(2)}) %collective-permute-start.14) | collective-permute-done | bytes 8224 | tf_op jit(solution)/shard_map/ppermute | solution.py:434
  32.5 0.0 collective-permute-done.13.got_ref
  32.5 0.9 %update.1 = (f32[8,16,512]{2,1,0:T(8,128)}, f32[8,16,512]{2,1,0:T(8,128)}, f32[1,512]{1,0:T(1,128)}) custom-call(f32[8,16,512]{2,1,0:T(8,128)S(1)} %get-tuple-element.41.mult_ref, f32[8,16,512]{2,1,0:T(8,128)S(1)} %get-tuple-element.42.incr_ref, f32[1,512]{1,0:T(1,128)S(1)} %get-tuple-element.43.dual_ref, f32[1,512]{1,0:T(1,128)S(1)} %get-tuple-element.49.dir_ref, ...), custom_call_target="tpu_custom_call" | custom-call | flops 1 | bytes 1 | tf_op jit(solution)/shard_map/update/pallas_call | solution.py:29
  (8 shorter events, 0.2 us)
Async XLA Ops:
  0.6 3.2 %collective-permute-start = (f32[8,16,512]{2,1,0:T(8,128)}, f32[8,16,512]{2,1,0:T(8,128)S(1)}, u32[]{:S(2)}, u32[]{:S(2)}) collective-permute-start(f32[8,16,512]{2,1,0:T(8,128)} %bitcast.17), channel_id=1, source_target_pairs={{0,1},{1,0},{2,3},{3,2},{4,5},{5,4},{6,7},{7,6},{8,9},{9,8},{10,11... | collective-permute-start | bytes 786440 | tf_op jit(solution)/shard_map/ppermute | solution.py:434
  3.9 5.8 %collective-permute-start.1 = (f32[5,8,512]{2,1,0:T(8,128)S(1)}, f32[5,8,512]{2,1,0:T(8,128)S(1)}, u32[]{:S(2)}, u32[]{:S(2)}) collective-permute-start(f32[5,8,512]{2,1,0:T(8,128)S(1)} %get-tuple-element.59.first_ref), channel_id=1, source_target_pairs={{0,4},{4,0},{8,12},{12,8},{1,5},{5,1},{9,13},{13,9},{2,6},{6,2},{1... | collective-permute-start | bytes 245768 | tf_op jit(solution)/shard_map/ppermute | solution.py:434
  6.6 3.1 %collective-permute-start.2 = (f32[5,8,512]{2,1,0:T(8,128)S(1)}, f32[5,8,512]{2,1,0:T(8,128)S(1)}, u32[]{:S(2)}, u32[]{:S(2)}) collective-permute-start(f32[5,8,512]{2,1,0:T(8,128)S(1)} %get-tuple-element.60.second_ref), channel_id=1, source_target_pairs={{0,1},{1,0},{2,3},{3,2},{4,8},{5,9},{6,10},{7,11},{8,4},{9,5},{10,... | collective-permute-start | bytes 245768 | tf_op jit(solution)/shard_map/ppermute | solution.py:430
  6.9 6.8 %collective-permute-start.4 = (f32[9,16,512]{2,1,0:T(8,128)S(1)}, f32[9,16,512]{2,1,0:T(8,128)S(1)}, u32[]{:S(2)}, u32[]{:S(2)}) collective-permute-start(f32[9,16,512]{2,1,0:T(8,128)S(1)} %pad.4), channel_id=1, source_target_pairs={{0,16},{1,3},{2,18},{3,1},{4,20},{5,7},{6,22},{7,5},{8,24},{9,11},... | collective-permute-start | bytes 884744 | tf_op jit(solution)/shard_map/ppermute | solution.py:430
  10.5 1.6 %collective-permute-start.3 = (f32[8,16,512]{2,1,0:T(8,128)S(1)}, f32[8,16,512]{2,1,0:T(8,128)S(1)}, u32[]{:S(2)}, u32[]{:S(2)}) collective-permute-start(f32[8,16,512]{2,1,0:T(8,128)S(1)} %get-tuple-element.62), channel_id=1, source_target_pairs={{0,1},{1,0},{2,3},{3,2},{4,5},{5,4},{6,7},{7,6},{8,9},{9,8},{10,11... | collective-permute-start | bytes 786440 | tf_op jit(solution)/shard_map/ppermute | solution.py:434
  13.7 6.8 %collective-permute-start.5 = (f32[17,16,512]{2,1,0:T(8,128)S(1)}, f32[17,16,512]{2,1,0:T(8,128)S(1)}, u32[]{:S(2)}, u32[]{:S(2)}) collective-permute-start(f32[17,16,512]{2,1,0:T(8,128)S(1)} %rest.1), channel_id=1, source_target_pairs={{0,1},{1,0},{2,3},{3,2},{4,5},{5,4},{6,7},{7,6},{8,9},{9,8},{10,11... | collective-permute-start | bytes 1671176 | tf_op jit(solution)/shard_map/ppermute | solution.py:434
  13.8 7.4 %collective-permute-start.8 = (f32[160,512]{1,0:T(8,128)S(1)}, f32[160,512]{1,0:T(8,128)S(1)}, u32[]{:S(2)}, u32[]{:S(2)}) collective-permute-start(f32[160,512]{1,0:T(8,128)S(1)} %sends.1), channel_id=1, source_target_pairs={{0,16},{1,3},{2,18},{3,1},{4,20},{5,7},{6,22},{7,5},{8,24},{9,11},... | collective-permute-start | bytes 983048 | tf_op jit(solution)/shard_map/ppermute | solution.py:430
  15.5 4.9 %collective-permute-start.6 = (f32[2,8,512]{2,1,0:T(8,128)S(1)}, f32[2,8,512]{2,1,0:T(8,128)S(1)}, u32[]{:S(2)}, u32[]{:S(2)}) collective-permute-start(f32[2,8,512]{2,1,0:T(8,128)S(1)} %get-tuple-element.66.first_ref), channel_id=1, source_target_pairs={{0,4},{4,0},{8,12},{12,8},{1,5},{5,1},{9,13},{13,9},{2,6},{6,2},{1... | collective-permute-start | bytes 98312 | tf_op jit(solution)/shard_map/ppermute | solution.py:434
  18.5 1.9 %collective-permute-start.7 = (f32[2,8,512]{2,1,0:T(8,128)S(1)}, f32[2,8,512]{2,1,0:T(8,128)S(1)}, u32[]{:S(2)}, u32[]{:S(2)}) collective-permute-start(f32[2,8,512]{2,1,0:T(8,128)S(1)} %get-tuple-element.67.second_ref), channel_id=1, source_target_pairs={{0,1},{1,0},{2,3},{3,2},{4,8},{5,9},{6,10},{7,11},{8,4},{9,5},{10,... | collective-permute-start | bytes 98312 | tf_op jit(solution)/shard_map/ppermute | solution.py:430
  21.6 3.7 %collective-permute-start.11 = (f32[2,8,128]{2,1,0:T(8,128)S(1)}, f32[2,8,128]{2,1,0:T(8,128)S(1)}, u32[]{:S(2)}, u32[]{:S(2)}) collective-permute-start(f32[2,8,128]{2,1,0:T(8,128)S(1)} %get-tuple-element.73), channel_id=1, source_target_pairs={{0,16},{1,7},{2,18},{3,5},{4,20},{5,3},{6,22},{7,1},{8,24},{9,15},... | collective-permute-start | bytes 24584 | tf_op jit(solution)/shard_map/ppermute | solution.py:430
  22.9 3.7 %collective-permute-start.10 = (f32[2,8,128]{2,1,0:T(8,128)S(1)}, f32[2,8,128]{2,1,0:T(8,128)S(1)}, u32[]{:S(2)}, u32[]{:S(2)}) collective-permute-start(f32[2,8,128]{2,1,0:T(8,128)S(1)} %get-tuple-element.73), channel_id=1, source_target_pairs={{0,16},{1,5},{2,18},{3,7},{4,20},{5,1},{6,22},{7,3},{8,24},{9,13},... | collective-permute-start | bytes 24584 | tf_op jit(solution)/shard_map/ppermute | solution.py:430
  23.7 3.7 %collective-permute-start.9 = (f32[2,8,128]{2,1,0:T(8,128)S(1)}, f32[2,8,128]{2,1,0:T(8,128)S(1)}, u32[]{:S(2)}, u32[]{:S(2)}) collective-permute-start(f32[2,8,128]{2,1,0:T(8,128)S(1)} %get-tuple-element.73), channel_id=1, source_target_pairs={{0,16},{1,3},{2,18},{3,1},{4,20},{5,7},{6,22},{7,5},{8,24},{9,11},... | collective-permute-start | bytes 24584 | tf_op jit(solution)/shard_map/ppermute | solution.py:430
  27.3 3.7 %collective-permute-start.12 = (f32[2,8,128]{2,1,0:T(8,128)S(1)}, f32[2,8,128]{2,1,0:T(8,128)S(1)}, u32[]{:S(2)}, u32[]{:S(2)}) collective-permute-start(f32[2,8,128]{2,1,0:T(8,128)S(1)} %add_add_fusion), channel_id=1, source_target_pairs={{0,16},{1,9},{2,18},{3,11},{4,20},{5,13},{6,22},{7,15},{8,24},{9,1... | collective-permute-start | bytes 24584 | tf_op jit(solution)/shard_map/ppermute | solution.py:430
  31.0 1.6 %collective-permute-start.13 = (f32[8,16,512]{2,1,0:T(8,128)S(1)}, f32[8,16,512]{2,1,0:T(8,128)S(1)}, u32[]{:S(2)}, u32[]{:S(2)}) collective-permute-start(f32[8,16,512]{2,1,0:T(8,128)S(1)} %get-tuple-element.74), channel_id=1, source_target_pairs={{0,1},{1,0},{2,3},{3,2},{4,5},{5,4},{6,7},{7,6},{8,9},{9,8},{10,11... | collective-permute-start | bytes 786440 | tf_op jit(solution)/shard_map/ppermute | solution.py:434
  31.0 1.5 %collective-permute-start.14 = (f32[2,8,128]{2,1,0:T(8,128)S(1)}, f32[2,8,128]{2,1,0:T(8,128)S(1)}, u32[]{:S(2)}, u32[]{:S(2)}) collective-permute-start(f32[2,8,128]{2,1,0:T(8,128)S(1)} %add.21), channel_id=1, source_target_pairs={{0,1},{1,0},{2,3},{3,2},{4,5},{5,4},{6,7},{7,6},{8,9},{9,8},{10,11... | collective-permute-start | bytes 24584 | tf_op jit(solution)/shard_map/ppermute | solution.py:434

commit v3 on v2

--- a/solution.py
+++ b/solution.py
@@ -8,9 +8,10 @@
 F32 = jnp.float32
 VMEM = pltpu.VMEM
 GRANT = 24 * 1024 * 1024
-
-
-def kernel_call(body, name, inputs, outputs, scratch=()):
+WEIGHT = 3200000000
+
+
+def kernel_call(body, name, inputs, outputs, scratch=(), weight=1):
     arrays, in_specs = [], []
     for array, home in inputs:
         if home == "far":
@@ -33,7 +34,7 @@
         in_specs=in_specs,
         out_specs=[pl.BlockSpec(memory_space=VMEM)] * len(outputs),
         scratch_shapes=list(scratch),
-        cost_estimate=pl.CostEstimate(flops=1, bytes_accessed=1, transcendentals=0),
+        cost_estimate=pl.CostEstimate(flops=weight, bytes_accessed=1, transcendentals=0),
         compiler_params=pltpu.CompilerParams(vmem_limit_bytes=GRANT),
     )(*arrays)
 
@@ -259,37 +260,45 @@
     return one, two, (rest - two.astype(F32)).astype(jnp.bfloat16)
 
 
-def observe_body(
-    incr_ref, mult_ref, rhs_ref, err_ref, cell_ref, dual_ref, want_ref, var_ref, valid_ref,
-    local_ref, held_ref, dir_ref, sums_ref,
+def slot_masks(cell, lines, cols):
+    slots = cell.shape[1]
+    at_line = iotas((lines, slots))[0] == cell // cols
+    at_col = iotas((cols, slots))[0] == lax.rem(cell, cols)
+    return at_line, jnp.where(at_col, 1.0, 0.0).astype(jnp.bfloat16)
+
+
+def spread_body(
+    incr_ref, mult_ref, rhs_ref, err_ref, cell_ref, dual_ref, valid_ref, local_ref, held_ref
 ):
     levels, rows, cols = incr_ref.shape
-    slots = cell_ref.shape[1]
     lines = levels * rows
-    cell = cell_ref[...]
-    valid = valid_ref[...]
-    dual = dual_ref[...]
-    line, col = cell // cols, lax.rem(cell, cols)
-    at_line = iotas((lines, slots))[0] == line
-    at_col = jnp.where(iotas((cols, slots))[0] == col, 1.0, 0.0).astype(jnp.bfloat16)
-    weights = thirds(jnp.where(at_line, valid * dual, 0.0))
+    at_line, at_col = slot_masks(cell_ref[...], lines, cols)
+    weights = thirds(jnp.where(at_line, valid_ref[...] * dual_ref[...], 0.0))
     spread = lax.dot_general(
         jnp.concatenate(weights, 0), at_col, (((1,), (1,)), ((), ())), preferred_element_type=F32
     )
+    ht = spread[:lines] + spread[lines : 2 * lines] + spread[2 * lines :]
+    mult = mult_ref[...]
+    held_ref[...] = mult + ht.reshape(levels, rows, cols)
+    local_ref[...] = rhs_ref[...] - (err_ref[...] * mult + incr_ref[...])
+
+
+def gather_body(
+    incr_ref, cell_ref, dual_ref, want_ref, var_ref, valid_ref, dir_ref, sums_ref
+):
+    levels, rows, cols = incr_ref.shape
+    lines = levels * rows
+    at_line, at_col = slot_masks(cell_ref[...], lines, cols)
     fields = thirds(incr_ref[...].reshape(lines, cols))
     picked = jnp.dot(jnp.concatenate(fields, 0), at_col, preferred_element_type=F32)
     picked = picked[:lines] + picked[lines : 2 * lines] + picked[2 * lines :]
+    valid, var = valid_ref[...], var_ref[...]
     hx = jnp.sum(jnp.where(at_line, picked, 0.0), axis=0, keepdims=True) * valid
-    var = var_ref[...]
-    res = valid * (want_ref[...] - (var * dual + hx))
+    res = valid * (want_ref[...] - (var * dual_ref[...] + hx))
     direction = res / var
     dir_ref[...] = direction
     sums_ref[0] = res * direction
     sums_ref[1] = direction * direction
-    ht = spread[:lines] + spread[lines : 2 * lines] + spread[2 * lines :]
-    mult = mult_ref[...]
-    held_ref[...] = mult + ht.reshape(levels, rows, cols)
-    local_ref[...] = rhs_ref[...] - (err_ref[...] * mult + incr_ref[...])
 
 
 def corrected(field, fix):
@@ -308,18 +317,14 @@
     return [-x for x in rows]
 
 
-def share_body(
-    a_ref, b_ref, c_ref, inner_ref, local_ref, moved_ref, held_ref, fix_ref, own_ref, urgent_ref
-):
+def share_body(local_ref, moved_ref, held_ref, back_ref, fix_ref, own_ref, urgent_ref):
     position = lax.axis_index("tm")
     first, low_pair = lax.rem(position, 2) == 0, position < 2
-    for lev in range(a_ref.shape[0]):
-        coeffs = taps(a_ref[lev], b_ref[lev], c_ref[lev])
-        back = adjoint(adjoint(inner_ref[lev], coeffs), coeffs)
-        back = corrected(jnp.where(first, back, 0.0), fixes(fix_ref, 4, lev))
+    for lev in range(local_ref.shape[0]):
+        back = corrected(back_ref[lev], fixes(fix_ref, 4, lev))
         moved = corrected(moved_ref[lev], fixes(fix_ref, 0, lev))
         local = local_ref[lev]
-        residual = held_ref[lev] - back
+        residual = held_ref[lev] - jnp.where(first, back, 0.0)
         own_ref[0, lev] = local
         own_ref[1, lev] = moved
         own_ref[2, lev] = residual
@@ -337,28 +342,27 @@
         send_ref[start : start + levels] = fix_ref[n]
 
 
-def rest_body(own_ref, obs_ref, out_ref):
+def rest_body(own_ref, obs_ref, local_ref, other_ref):
     levels = own_ref.shape[1]
     low_pair = lax.axis_index("tm") < 2
     for lev in range(levels):
-        out_ref[lev] = own_ref[0, lev]
-        out_ref[levels + lev] = jnp.where(low_pair, own_ref[2, lev], own_ref[1, lev])
-    out_ref[2 * levels] = jnp.zeros(out_ref.shape[1:], F32)
+        local_ref[lev] = own_ref[0, lev]
+        other_ref[lev] = jnp.where(low_pair, own_ref[2, lev], own_ref[1, lev])
+    local_ref[levels] = jnp.zeros(local_ref.shape[1:], F32)
     for n in range(2):
-        out_ref[2 * levels, n : n + 1, 0:128] = lanes(obs_ref[n])
+        local_ref[levels, n : n + 1, 0:128] = lanes(obs_ref[n])
 
 
 def terms_body(
-    a_ref, b_ref, c_ref, cross_ref, own_ref, got_ref, rest_ref, fix_ref, terms_ref, known_ref
+    cross_ref, beyond_ref, own_ref, got_ref, rest_ref, other_ref, fix_ref, terms_ref, known_ref
 ):
     low_pair = lax.axis_index("tm") < 2
     levels = own_ref.shape[1]
     for lev in range(levels):
-        coeffs = taps(a_ref[lev], b_ref[lev], c_ref[lev])
         cross, got = cross_ref[lev], got_ref[lev]
         local, residual = own_ref[0, lev], own_ref[2, lev]
-        back = corrected(adjoint(adjoint(cross, coeffs), coeffs), fixes(fix_ref, 0, lev))
-        rest0, rest1 = rest_ref[lev], rest_ref[levels + lev]
+        back = corrected(beyond_ref[lev], fixes(fix_ref, 0, lev))
+        rest0, rest1 = rest_ref[lev], other_ref[lev]
         terms_ref[0, lev] = jnp.where(low_pair, rest0, residual)
         terms_ref[1, lev] = jnp.where(low_pair, local, residual) + got
         terms_ref[2, lev] = jnp.where(low_pair, residual - back, rest0 + cross)
@@ -394,7 +398,7 @@
         give_ref[lev] = jnp.where(low_pair, three, two)
     for n, total in enumerate((numer, denom)):
         sums_ref[n] = total
-        obs = lanes(obs_ref[n]) + rest_ref[2 * levels, n : n + 1, 0:128]
+        obs = lanes(obs_ref[n]) + rest_ref[levels, n : n + 1, 0:128]
         sums_ref[n, 0:1] = total[0:1] + obs
 
 
@@ -519,11 +523,8 @@
     got_first = swap(first, "tile", 1)
     got_second = exchange(second, second_side)
     valid = (lax.broadcasted_iota(jnp.int32, obs_cell.shape, 1) < obs_count).astype(F32)
-    local, held, dir_obs, obs_sums = kernel_call(
-        observe_body,
-        "observe",
-        near(incr, mult, rhs, err, cell, dual, want, var, valid),
-        [field] * 2 + [(obs_dual.shape, "near"), ((2, *obs_dual.shape), "near")],
+    local, held = kernel_call(
+        spread_body, "spread", near(incr, mult, rhs, err, cell, dual, valid), [field] * 2
     )
     fix = kernel_call(
         edges_body, "edges", near(first, second, got_first, got_second, edge), [lines(8)]
@@ -531,29 +532,42 @@
     if peers != 4:
         later = jnp.where(lax.axis_index("tm") == peers - 1, 0.0, later)
         back = kernel_call(adjoint_body, "adjoint", near(*coeffs, later), [field])[0]
+        dir_obs, obs_sums = kernel_call(
+            gather_body,
+            "gather",
+            near(incr, cell, dual, want, var, valid),
+            [(obs_dual.shape, "near"), ((2, *obs_dual.shape), "near")],
+        )
         return scan_path(
             multiplier, increment, obs_dual, local, moved, held, back, fix, dir_obs, obs_sums
         )
     cross = jnp.where(lax.axis_index("tm") < 2, moved, inner)
     got_cross = leaders(jnp.pad(cross, ((0, 1), (0, 0), (0, 0))), 0, 2)
+    back = kernel_call(adjoint_body, "adjoint", near(*coeffs, inner), [field])[0]
     own, urgent = kernel_call(
         share_body,
         "share",
-        near(*coeffs, inner, local, moved, held, fix),
+        near(local, moved, held, back, fix),
         [((3, levels, rows, cols), "near"), field],
     )
     got = swap(urgent, "tm", 1)
     send = kernel_call(
         sends_body, "sends", near(own, got, fix), [((levels * rows + 4 * levels, cols), "near")]
     )[0]
-    send, got_cross, own = lax.optimization_barrier((send, got_cross, own))
+    send, own, cell = lax.optimization_barrier((send, own, cell))
     got_send = leaders(send, 0, 2)
-    rest = kernel_call(
-        rest_body, "rest", near(own, obs_sums), [((2 * levels + 1, rows, cols), "near")]
-    )[0]
-    got_rest = swap(rest, "tm", 1)
+    dir_obs, obs_sums = kernel_call(
+        gather_body,
+        "gather",
+        near(incr, cell, dual, want, var, valid),
+        [(obs_dual.shape, "near"), ((2, *obs_dual.shape), "near")],
+    )
+    rest, other = kernel_call(
+        rest_body, "rest", near(own, obs_sums), [((levels + 1, rows, cols), "near"), field]
+    )
+    got_rest, got_other = swap(rest, "tm", 1), swap(other, "tm", 1)
     late_first, late_second = kernel_call(
-        late_rims_body, "late_rims", near(edge, got_cross), [lines(2), lines(2)]
+        late_rims_body, "late_rims", near(edge, got_cross), [lines(2), lines(2)], weight=WEIGHT
     )
     got_late_first = swap(late_first, "tile", 1)
     got_late_second = exchange(late_second, second_side)
@@ -564,10 +578,11 @@
         + near(got_first, got_second, edge),
         [lines(4)],
     )[0]
+    beyond = kernel_call(adjoint_body, "beyond", near(*coeffs, got_cross), [field])[0]
     terms, known = kernel_call(
         terms_body,
         "terms",
-        near(*coeffs, got_cross, own, got, got_rest, late_fix),
+        near(got_cross, beyond, own, got, got_rest, got_other, late_fix),
         [((4, levels, rows, cols), "near"), field],
     )
     pair = ((2, levels, rows, cols), "near")

time: 33.6 us -> 31.8 us (0.946)
  waiting for transfers between devices: 11.3 us -> 9.11 us
    ppermute x7 -> x8, waiting for transfers between devices: 5 us -> 3.87 us  [swap(): lax.ppermute(value, axis, [(i, i ^ distance) for i in range(lax.axis_size...]
    ppermute x8, waiting for transfers between devices: 6.34 us -> 5.24 us  [exchange(): return lax.ppermute(value, ('groups', 'tile', 'tm'), pairs)]
    pallas_call x12 -> x15, Pallas kernels: 5.88 us -> 6.21 us  [kernel_call(): pl.pallas_call(body, name=name, out_shape=out_shape, in_specs=in_specs, o...]
    ppermute x7 -> x8, starting transfers between devices: 6.85 us -> 7.1 us  [swap(): lax.ppermute(value, axis, [(i, i ^ distance) for i in range(lax.axis_size...]
  transfers between devices with their start and end apart: 15 -> 16, of which waited for: 9 -> 8; matrix products, arithmetic and copies ran while one was open for 0% -> 0% of each run, Pallas kernels for 13% -> 15%
where the time goes in v3:
time: 31.8 us; the launch traced here: 31.6 us
  starting transfers between devices  14.8 us (47%)
  waiting for transfers between devices  9.11 us (29%)
  Pallas kernels  6.21 us (20%)
  between operations  1.45 us (5%)
    ppermute x8, starting transfers between devices, exchange(): return lax.ppermute(value, ('groups', 'tile', 'tm'), pairs)  7.7 us
    ppermute x8, starting transfers between devices, swap(): lax.ppermute(value, axis, [(i, i ^ distance) for i in range(lax.axis_size...  7.1 us
    pallas_call x15, Pallas kernels, kernel_call(): pl.pallas_call(body, name=name, out_shape=out_shape, in_specs=in_specs, o...  6.21 us
    ppermute x8, waiting for transfers between devices, exchange(): return lax.ppermute(value, ('groups', 'tile', 'tm'), pairs)  5.24 us
    ppermute x8, waiting for transfers between devices, swap(): lax.ppermute(value, axis, [(i, i ^ distance) for i in range(lax.axis_size...  3.87 us
  transfers between devices with their start and end apart: 16, of which 8 were waited for; matrix products, arithmetic and copies ran while one was open for 0% of the time, Pallas kernels for 15%

profile of v3, /device:TPU:0, one launch (start us, length us, event | category | flops | bytes accessed | tf_op | source)
XLA Modules:
  0.0 31.6 jit_solution(17627798727117080413)
XLA Ops:
  0.6 0.5 %collective-permute-start = (f32[8,16,512]{2,1,0:T(8,128)}, f32[8,16,512]{2,1,0:T(8,128)S(1)}, u32[]{:S(2)}, u32[]{:S(2)}) collective-permute-start(f32[8,16,512]{2,1,0:T(8,128)} %bitcast.17), channel_id=1, source_target_pairs={{0,1},{1,0},{2,3},{3,2},{4,5},{5,4},{6,7},{7,6},{8,9},{9,8},{10,11... | collective-permute-start | bytes 786440 | tf_op jit(solution)/shard_map/ppermute | solution.py:438
  1.2 2.0 %begin.1 = (f32[8,16,512]{2,1,0:T(8,128)S(1)}, f32[8,16,512]{2,1,0:T(8,128)S(1)}, f32[8,16,512]{2,1,0:T(8,128)S(1)}, f32[8,16,512]{2,1,0:T(8,128)S(1)}, f32[8,16...) custom-call(f32[8,16,512]{2,1,0:T(8,128)} %bitcast.11, ...), custom_call_target="tpu_custom_call" | custom-call | flops 1 | bytes 1 | tf_op jit(solution)/shard_map/begin/pallas_call | solution.py:30
  3.8 0.0 collective-permute-done.later_ref.refs_1_
  3.8 0.1 rims.1
  3.9 2.7 %collective-permute-start.1 = (f32[5,8,512]{2,1,0:T(8,128)S(1)}, f32[5,8,512]{2,1,0:T(8,128)S(1)}, u32[]{:S(2)}, u32[]{:S(2)}) collective-permute-start(f32[5,8,512]{2,1,0:T(8,128)S(1)} %get-tuple-element.58.first_ref), channel_id=1, source_target_pairs={{0,4},{4,0},{8,12},{12,8},{1,5},{5,1},{9,13},{13,9},{2,6},{6,2},{1... | collective-permute-start | bytes 245768 | tf_op jit(solution)/shard_map/ppermute | solution.py:438
  6.6 0.2 collective-permute-start.2
  6.9 1.6 %collective-permute-start.4 = (f32[9,16,512]{2,1,0:T(8,128)S(1)}, f32[9,16,512]{2,1,0:T(8,128)S(1)}, u32[]{:S(2)}, u32[]{:S(2)}) collective-permute-start(f32[9,16,512]{2,1,0:T(8,128)S(1)} %pad.4), channel_id=1, source_target_pairs={{0,16},{1,3},{2,18},{3,1},{4,20},{5,7},{6,22},{7,5},{8,24},{9,11},... | collective-permute-start | bytes 884744 | tf_op jit(solution)/shard_map/ppermute | solution.py:434
  8.5 0.4 %spread.1 = (f32[8,16,512]{2,1,0:T(8,128)S(1)}, f32[8,16,512]{2,1,0:T(8,128)S(1)}) custom-call(f32[8,16,512]{2,1,0:T(8,128)S(1)} %get-tuple-element.44.incr_ref, f32[8,16,512]{2,1,0:T(8,128)S(1)} %get-tuple-element.43.mult_ref, f32[8,16,512]{2,1,0:T(8,128)S(1)} %get-tuple-element.46.rhs_ref, f32[8,16,512]{2,1,0:T(8,128)S(1)} %get-tuple-element.47.err_ref, ...), custom_call_target="tpu_custom_call" | custom-call | flops 1 | bytes 1 | tf_op jit(solution)/shard_map/spread/pallas_call | solution.py:30
  8.9 0.7 %adjoint.1.back_ref = f32[8,16,512]{2,1,0:T(8,128)S(1)} custom-call(f32[8,16,512]{2,1,0:T(8,128)S(1)} %get-tuple-element.52.a_ref, f32[8,16,512]{2,1,0:T(8,128)S(1)} %get-tuple-element.53.b_ref, f32[8,16,512]{2,1,0:T(8,128)S(1)} %get-tuple-element.54.c_ref, f32[8,16,512]{2,1,0:T(8,128)S(1)} %collective-permute-done.later_ref.refs_1_), custom_call_target="tpu_custom_call" | custom-call | flops 1 | bytes 1 | tf_op jit(solution)/shard_map/adjoint/pallas_call | solution.py:30
  9.6 0.1 collective-permute-done.1.got_first_ref.past_first_ref
  9.7 0.0 collective-permute-done.2.got_second_ref.past_second_ref
  9.7 0.1 edges.1.fix_ref
  9.8 0.1 share.1
  10.0 0.1 collective-permute-start.3
  10.0 1.5 %collective-permute-done.3.got_ref = f32[8,16,512]{2,1,0:T(8,128)S(1)} collective-permute-done((f32[8,16,512]{2,1,0:T(8,128)S(1)}, f32[8,16,512]{2,1,0:T(8,128)S(1)}, u32[]{:S(2)}, u32[]{:S(2)}) %collective-permute-start.3) | collective-permute-done | bytes 262176 | tf_op jit(solution)/shard_map/ppermute | solution.py:438
  11.6 1.7 %collective-permute-start.9 = (f32[160,512]{1,0:T(8,128)S(1)}, f32[160,512]{1,0:T(8,128)S(1)}, u32[]{:S(2)}, u32[]{:S(2)}) collective-permute-start(f32[160,512]{1,0:T(8,128)S(1)} %sends.1), channel_id=1, source_target_pairs={{0,16},{1,3},{2,18},{3,1},{4,20},{5,7},{6,22},{7,5},{8,24},{9,11},... | collective-permute-start | bytes 983048 | tf_op jit(solution)/shard_map/ppermute | solution.py:434
  13.4 0.4 %gather.1 = (f32[1,512]{1,0:T(1,128)S(1)}, f32[2,1,512]{2,1,0:T(1,128)S(1)}) custom-call(f32[8,16,512]{2,1,0:T(8,128)S(1)} %get-tuple-element.44.incr_ref, s32[1,512]{1,0:T(1,128)S(1)} %get-tuple-element.62.cell_ref, f32[1,512]{1,0:T(1,128)S(1)} %get-tuple-element.45.dual_ref, f32[1,512]{1,0:T(1,128)S(1)} %get-tuple-element.63.want_ref, ...), custom_call_target="tpu_custom_call" | custom-call | flops 1 | bytes 1 | tf_op jit(solution)/shard_map/gather/pallas_call | solution.py:30
  13.8 0.1 rest.1
  13.8 0.1 collective-permute-start.6
  13.9 0.5 %collective-permute-start.5 = (f32[9,16,512]{2,1,0:T(8,128)S(1)}, f32[9,16,512]{2,1,0:T(8,128)S(1)}, u32[]{:S(2)}, u32[]{:S(2)}) collective-permute-start(f32[9,16,512]{2,1,0:T(8,128)S(1)} %get-tuple-element.68), channel_id=1, source_target_pairs={{0,1},{1,0},{2,3},{3,2},{4,5},{5,4},{6,7},{7,6},{8,9},{9,8},{10,11... | collective-permute-start | bytes 884744 | tf_op jit(solution)/shard_map/ppermute | solution.py:438
  14.4 0.0 collective-permute-done.4.later_ref.cross_ref
  14.4 0.1 late_rims.1
  14.5 2.8 %collective-permute-start.7 = (f32[2,8,512]{2,1,0:T(8,128)S(1)}, f32[2,8,512]{2,1,0:T(8,128)S(1)}, u32[]{:S(2)}, u32[]{:S(2)}) collective-permute-start(f32[2,8,512]{2,1,0:T(8,128)S(1)} %get-tuple-element.70.first_ref), channel_id=1, source_target_pairs={{0,4},{4,0},{8,12},{12,8},{1,5},{5,1},{9,13},{13,9},{2,6},{6,2},{1... | collective-permute-start | bytes 98312 | tf_op jit(solution)/shard_map/ppermute | solution.py:438
  17.3 0.0 collective-permute-start.8
  17.3 0.7 %beyond.1.beyond_ref = f32[8,16,512]{2,1,0:T(8,128)S(1)} custom-call(f32[8,16,512]{2,1,0:T(8,128)S(1)} %get-tuple-element.52.a_ref, f32[8,16,512]{2,1,0:T(8,128)S(1)} %get-tuple-element.53.b_ref, f32[8,16,512]{2,1,0:T(8,128)S(1)} %get-tuple-element.54.c_ref, f32[9,16,512]{2,1,0:T(8,128)S(1)} %collective-permute-done.4.later_ref.cross_ref), custom_call_target="tpu_custom_call" | custom-call | flops 1 | bytes 1 | tf_op jit(solution)/shard_map/beyond/pallas_call | solution.py:30
  18.0 1.2 %collective-permute-done.7.got_first_ref = f32[2,8,512]{2,1,0:T(8,128)S(1)} collective-permute-done((f32[2,8,512]{2,1,0:T(8,128)S(1)}, f32[2,8,512]{2,1,0:T(8,128)S(1)}, u32[]{:S(2)}, u32[]{:S(2)}) %collective-permute-start.7) | collective-permute-done | bytes 32800 | tf_op jit(solution)/shard_map/ppermute | solution.py:438
  19.2 0.0 collective-permute-done.8.got_second_ref
  19.2 0.1 late_edges.1.fix_ref
  19.3 0.0 collective-permute-done.6.other_ref
  19.3 0.0 collective-permute-done.5.rest_ref
  19.3 0.1 terms.1
  19.4 0.0 collective-permute-done.9.got_ref
  19.5 0.3 dots.1
  19.8 1.1 %collective-permute-start.12 = (f32[2,8,128]{2,1,0:T(8,128)S(1)}, f32[2,8,128]{2,1,0:T(8,128)S(1)}, u32[]{:S(2)}, u32[]{:S(2)}) collective-permute-start(f32[2,8,128]{2,1,0:T(8,128)S(1)} %get-tuple-element.77), channel_id=1, source_target_pairs={{0,16},{1,7},{2,18},{3,5},{4,20},{5,3},{6,22},{7,1},{8,24},{9,15},... | collective-permute-start | bytes 24584 | tf_op jit(solution)/shard_map/ppermute | solution.py:434
  20.9 1.0 %collective-permute-start.11 = (f32[2,8,128]{2,1,0:T(8,128)S(1)}, f32[2,8,128]{2,1,0:T(8,128)S(1)}, u32[]{:S(2)}, u32[]{:S(2)}) collective-permute-start(f32[2,8,128]{2,1,0:T(8,128)S(1)} %get-tuple-element.77), channel_id=1, source_target_pairs={{0,16},{1,5},{2,18},{3,7},{4,20},{5,1},{6,22},{7,3},{8,24},{9,13},... | collective-permute-start | bytes 24584 | tf_op jit(solution)/shard_map/ppermute | solution.py:434
  21.8 1.0 %collective-permute-start.10 = (f32[2,8,128]{2,1,0:T(8,128)S(1)}, f32[2,8,128]{2,1,0:T(8,128)S(1)}, u32[]{:S(2)}, u32[]{:S(2)}) collective-permute-start(f32[2,8,128]{2,1,0:T(8,128)S(1)} %get-tuple-element.77), channel_id=1, source_target_pairs={{0,16},{1,3},{2,18},{3,1},{4,20},{5,7},{6,22},{7,5},{8,24},{9,11},... | collective-permute-start | bytes 24584 | tf_op jit(solution)/shard_map/ppermute | solution.py:434
  22.9 0.6 %collective-permute-done.12 = f32[2,8,128]{2,1,0:T(8,128)S(1)} collective-permute-done((f32[2,8,128]{2,1,0:T(8,128)S(1)}, f32[2,8,128]{2,1,0:T(8,128)S(1)}, u32[]{:S(2)}, u32[]{:S(2)}) %collective-permute-start.12) | collective-permute-done | bytes 8224 | tf_op jit(solution)/shard_map/ppermute | solution.py:434
  23.5 1.0 %collective-permute-done.11 = f32[2,8,128]{2,1,0:T(8,128)S(1)} collective-permute-done((f32[2,8,128]{2,1,0:T(8,128)S(1)}, f32[2,8,128]{2,1,0:T(8,128)S(1)}, u32[]{:S(2)}, u32[]{:S(2)}) %collective-permute-start.11) | collective-permute-done | bytes 8224 | tf_op jit(solution)/shard_map/ppermute | solution.py:434
  24.5 1.0 %collective-permute-done.10 = f32[2,8,128]{2,1,0:T(8,128)S(1)} collective-permute-done((f32[2,8,128]{2,1,0:T(8,128)S(1)}, f32[2,8,128]{2,1,0:T(8,128)S(1)}, u32[]{:S(2)}, u32[]{:S(2)}) %collective-permute-start.10) | collective-permute-done | bytes 8224 | tf_op jit(solution)/shard_map/ppermute | solution.py:434
  25.5 1.0 %collective-permute-start.13 = (f32[2,8,128]{2,1,0:T(8,128)S(1)}, f32[2,8,128]{2,1,0:T(8,128)S(1)}, u32[]{:S(2)}, u32[]{:S(2)}) collective-permute-start(f32[2,8,128]{2,1,0:T(8,128)S(1)} %add_add_fusion), channel_id=1, source_target_pairs={{0,16},{1,9},{2,18},{3,11},{4,20},{5,13},{6,22},{7,15},{8,24},{9,1... | collective-permute-start | bytes 24584 | tf_op jit(solution)/shard_map/ppermute | solution.py:434
  26.5 2.6 %collective-permute-done.13 = f32[2,8,128]{2,1,0:T(8,128)S(1)} collective-permute-done((f32[2,8,128]{2,1,0:T(8,128)S(1)}, f32[2,8,128]{2,1,0:T(8,128)S(1)}, u32[]{:S(2)}, u32[]{:S(2)}) %collective-permute-start.13) | collective-permute-done | bytes 8224 | tf_op jit(solution)/shard_map/ppermute | solution.py:434
  29.2 0.0 collective-permute-start.14
  29.2 0.5 %collective-permute-start.15 = (f32[2,8,128]{2,1,0:T(8,128)S(1)}, f32[2,8,128]{2,1,0:T(8,128)S(1)}, u32[]{:S(2)}, u32[]{:S(2)}) collective-permute-start(f32[2,8,128]{2,1,0:T(8,128)S(1)} %add.21), channel_id=1, source_target_pairs={{0,1},{1,0},{2,3},{3,2},{4,5},{5,4},{6,7},{7,6},{8,9},{9,8},{10,11... | collective-permute-start | bytes 24584 | tf_op jit(solution)/shard_map/ppermute | solution.py:438
  29.7 1.0 %collective-permute-done.15 = f32[2,8,128]{2,1,0:T(8,128)S(1)} collective-permute-done((f32[2,8,128]{2,1,0:T(8,128)S(1)}, f32[2,8,128]{2,1,0:T(8,128)S(1)}, u32[]{:S(2)}, u32[]{:S(2)}) %collective-permute-start.15) | collective-permute-done | bytes 8224 | tf_op jit(solution)/shard_map/ppermute | solution.py:438
  30.7 0.0 collective-permute-done.14.got_ref
  30.7 0.9 %update.1 = (f32[8,16,512]{2,1,0:T(8,128)}, f32[8,16,512]{2,1,0:T(8,128)}, f32[1,512]{1,0:T(1,128)}) custom-call(f32[8,16,512]{2,1,0:T(8,128)S(1)} %get-tuple-element.43.mult_ref, f32[8,16,512]{2,1,0:T(8,128)S(1)} %get-tuple-element.44.incr_ref, f32[1,512]{1,0:T(1,128)S(1)} %get-tuple-element.45.dual_ref, f32[1,512]{1,0:T(1,128)S(1)} %get-tuple-element.65.dir_ref, ...), custom_call_target="tpu_custom_call" | custom-call | flops 1 | bytes 1 | tf_op jit(solution)/shard_map/update/pallas_call | solution.py:30
  (7 shorter events, 0.1 us)
Async XLA Ops:
  0.6 3.2 %collective-permute-start = (f32[8,16,512]{2,1,0:T(8,128)}, f32[8,16,512]{2,1,0:T(8,128)S(1)}, u32[]{:S(2)}, u32[]{:S(2)}) collective-permute-start(f32[8,16,512]{2,1,0:T(8,128)} %bitcast.17), channel_id=1, source_target_pairs={{0,1},{1,0},{2,3},{3,2},{4,5},{5,4},{6,7},{7,6},{8,9},{9,8},{10,11... | collective-permute-start | bytes 786440 | tf_op jit(solution)/shard_map/ppermute | solution.py:438
  3.9 5.8 %collective-permute-start.1 = (f32[5,8,512]{2,1,0:T(8,128)S(1)}, f32[5,8,512]{2,1,0:T(8,128)S(1)}, u32[]{:S(2)}, u32[]{:S(2)}) collective-permute-start(f32[5,8,512]{2,1,0:T(8,128)S(1)} %get-tuple-element.58.first_ref), channel_id=1, source_target_pairs={{0,4},{4,0},{8,12},{12,8},{1,5},{5,1},{9,13},{13,9},{2,6},{6,2},{1... | collective-permute-start | bytes 245768 | tf_op jit(solution)/shard_map/ppermute | solution.py:438
  6.6 3.1 %collective-permute-start.2 = (f32[5,8,512]{2,1,0:T(8,128)S(1)}, f32[5,8,512]{2,1,0:T(8,128)S(1)}, u32[]{:S(2)}, u32[]{:S(2)}) collective-permute-start(f32[5,8,512]{2,1,0:T(8,128)S(1)} %get-tuple-element.59.second_ref), channel_id=1, source_target_pairs={{0,1},{1,0},{2,3},{3,2},{4,8},{5,9},{6,10},{7,11},{8,4},{9,5},{10,... | collective-permute-start | bytes 245768 | tf_op jit(solution)/shard_map/ppermute | solution.py:434
  6.9 7.5 %collective-permute-start.4 = (f32[9,16,512]{2,1,0:T(8,128)S(1)}, f32[9,16,512]{2,1,0:T(8,128)S(1)}, u32[]{:S(2)}, u32[]{:S(2)}) collective-permute-start(f32[9,16,512]{2,1,0:T(8,128)S(1)} %pad.4), channel_id=1, source_target_pairs={{0,16},{1,3},{2,18},{3,1},{4,20},{5,7},{6,22},{7,5},{8,24},{9,11},... | collective-permute-start | bytes 884744 | tf_op jit(solution)/shard_map/ppermute | solution.py:434
  10.0 1.6 %collective-permute-start.3 = (f32[8,16,512]{2,1,0:T(8,128)S(1)}, f32[8,16,512]{2,1,0:T(8,128)S(1)}, u32[]{:S(2)}, u32[]{:S(2)}) collective-permute-start(f32[8,16,512]{2,1,0:T(8,128)S(1)} %get-tuple-element.61), channel_id=1, source_target_pairs={{0,1},{1,0},{2,3},{3,2},{4,5},{5,4},{6,7},{7,6},{8,9},{9,8},{10,11... | collective-permute-start | bytes 786440 | tf_op jit(solution)/shard_map/ppermute | solution.py:438
  11.6 7.8 %collective-permute-start.9 = (f32[160,512]{1,0:T(8,128)S(1)}, f32[160,512]{1,0:T(8,128)S(1)}, u32[]{:S(2)}, u32[]{:S(2)}) collective-permute-start(f32[160,512]{1,0:T(8,128)S(1)} %sends.1), channel_id=1, source_target_pairs={{0,16},{1,3},{2,18},{3,1},{4,20},{5,7},{6,22},{7,5},{8,24},{9,11},... | collective-permute-start | bytes 983048 | tf_op jit(solution)/shard_map/ppermute | solution.py:434
  13.8 5.5 %collective-permute-start.6 = (f32[8,16,512]{2,1,0:T(8,128)S(1)}, f32[8,16,512]{2,1,0:T(8,128)S(1)}, u32[]{:S(2)}, u32[]{:S(2)}) collective-permute-start(f32[8,16,512]{2,1,0:T(8,128)S(1)} %get-tuple-element.69), channel_id=1, source_target_pairs={{0,1},{1,0},{2,3},{3,2},{4,5},{5,4},{6,7},{7,6},{8,9},{9,8},{10,11... | collective-permute-start | bytes 786440 | tf_op jit(solution)/shard_map/ppermute | solution.py:438
  13.9 5.4 %collective-permute-start.5 = (f32[9,16,512]{2,1,0:T(8,128)S(1)}, f32[9,16,512]{2,1,0:T(8,128)S(1)}, u32[]{:S(2)}, u32[]{:S(2)}) collective-permute-start(f32[9,16,512]{2,1,0:T(8,128)S(1)} %get-tuple-element.68), channel_id=1, source_target_pairs={{0,1},{1,0},{2,3},{3,2},{4,5},{5,4},{6,7},{7,6},{8,9},{9,8},{10,11... | collective-permute-start | bytes 884744 | tf_op jit(solution)/shard_map/ppermute | solution.py:438
  14.5 4.7 %collective-permute-start.7 = (f32[2,8,512]{2,1,0:T(8,128)S(1)}, f32[2,8,512]{2,1,0:T(8,128)S(1)}, u32[]{:S(2)}, u32[]{:S(2)}) collective-permute-start(f32[2,8,512]{2,1,0:T(8,128)S(1)} %get-tuple-element.70.first_ref), channel_id=1, source_target_pairs={{0,4},{4,0},{8,12},{12,8},{1,5},{5,1},{9,13},{13,9},{2,6},{6,2},{1... | collective-permute-start | bytes 98312 | tf_op jit(solution)/shard_map/ppermute | solution.py:438
  17.3 1.9 %collective-permute-start.8 = (f32[2,8,512]{2,1,0:T(8,128)S(1)}, f32[2,8,512]{2,1,0:T(8,128)S(1)}, u32[]{:S(2)}, u32[]{:S(2)}) collective-permute-start(f32[2,8,512]{2,1,0:T(8,128)S(1)} %get-tuple-element.71.second_ref), channel_id=1, source_target_pairs={{0,1},{1,0},{2,3},{3,2},{4,8},{5,9},{6,10},{7,11},{8,4},{9,5},{10,... | collective-permute-start | bytes 98312 | tf_op jit(solution)/shard_map/ppermute | solution.py:434
  19.8 3.7 %collective-permute-start.12 = (f32[2,8,128]{2,1,0:T(8,128)S(1)}, f32[2,8,128]{2,1,0:T(8,128)S(1)}, u32[]{:S(2)}, u32[]{:S(2)}) collective-permute-start(f32[2,8,128]{2,1,0:T(8,128)S(1)} %get-tuple-element.77), channel_id=1, source_target_pairs={{0,16},{1,7},{2,18},{3,5},{4,20},{5,3},{6,22},{7,1},{8,24},{9,15},... | collective-permute-start | bytes 24584 | tf_op jit(solution)/shard_map/ppermute | solution.py:434
  20.9 3.7 %collective-permute-start.11 = (f32[2,8,128]{2,1,0:T(8,128)S(1)}, f32[2,8,128]{2,1,0:T(8,128)S(1)}, u32[]{:S(2)}, u32[]{:S(2)}) collective-permute-start(f32[2,8,128]{2,1,0:T(8,128)S(1)} %get-tuple-element.77), channel_id=1, source_target_pairs={{0,16},{1,5},{2,18},{3,7},{4,20},{5,1},{6,22},{7,3},{8,24},{9,13},... | collective-permute-start | bytes 24584 | tf_op jit(solution)/shard_map/ppermute | solution.py:434
  21.8 3.7 %collective-permute-start.10 = (f32[2,8,128]{2,1,0:T(8,128)S(1)}, f32[2,8,128]{2,1,0:T(8,128)S(1)}, u32[]{:S(2)}, u32[]{:S(2)}) collective-permute-start(f32[2,8,128]{2,1,0:T(8,128)S(1)} %get-tuple-element.77), channel_id=1, source_target_pairs={{0,16},{1,3},{2,18},{3,1},{4,20},{5,7},{6,22},{7,5},{8,24},{9,11},... | collective-permute-start | bytes 24584 | tf_op jit(solution)/shard_map/ppermute | solution.py:434
  25.5 3.7 %collective-permute-start.13 = (f32[2,8,128]{2,1,0:T(8,128)S(1)}, f32[2,8,128]{2,1,0:T(8,128)S(1)}, u32[]{:S(2)}, u32[]{:S(2)}) collective-permute-start(f32[2,8,128]{2,1,0:T(8,128)S(1)} %add_add_fusion), channel_id=1, source_target_pairs={{0,16},{1,9},{2,18},{3,11},{4,20},{5,13},{6,22},{7,15},{8,24},{9,1... | collective-permute-start | bytes 24584 | tf_op jit(solution)/shard_map/ppermute | solution.py:434
  29.2 1.6 %collective-permute-start.14 = (f32[8,16,512]{2,1,0:T(8,128)S(1)}, f32[8,16,512]{2,1,0:T(8,128)S(1)}, u32[]{:S(2)}, u32[]{:S(2)}) collective-permute-start(f32[8,16,512]{2,1,0:T(8,128)S(1)} %get-tuple-element.78), channel_id=1, source_target_pairs={{0,1},{1,0},{2,3},{3,2},{4,5},{5,4},{6,7},{7,6},{8,9},{9,8},{10,11... | collective-permute-start | bytes 786440 | tf_op jit(solution)/shard_map/ppermute | solution.py:438
  29.2 1.5 %collective-permute-start.15 = (f32[2,8,128]{2,1,0:T(8,128)S(1)}, f32[2,8,128]{2,1,0:T(8,128)S(1)}, u32[]{:S(2)}, u32[]{:S(2)}) collective-permute-start(f32[2,8,128]{2,1,0:T(8,128)S(1)} %add.21), channel_id=1, source_target_pairs={{0,1},{1,0},{2,3},{3,2},{4,5},{5,4},{6,7},{7,6},{8,9},{9,8},{10,11... | collective-permute-start | bytes 24584 | tf_op jit(solution)/shard_map/ppermute | solution.py:438

commit v4 on v3

--- a/solution.py
+++ b/solution.py
@@ -9,6 +9,7 @@
 VMEM = pltpu.VMEM
 GRANT = 24 * 1024 * 1024
 WEIGHT = 3200000000
+PARTS = 2
 
 
 def kernel_call(body, name, inputs, outputs, scratch=(), weight=1):
@@ -21,9 +22,10 @@
             in_specs.append(pl.BlockSpec(memory_space=VMEM))
             array = pltpu.with_memory_space_constraint(array, VMEM)
         arrays.append(array)
-    out_shape = []
+    out_shape, out_specs = [], []
     for shape, home, *dtype in outputs:
         dtype = dtype[0] if dtype else F32
+        out_specs.append(pl.BlockSpec(memory_space=VMEM))
         out_shape.append(
             VMEM(shape, dtype) if home == "near" else jax.ShapeDtypeStruct(shape, dtype)
         )
@@ -32,7 +34,7 @@
         name=name,
         out_shape=out_shape,
         in_specs=in_specs,
-        out_specs=[pl.BlockSpec(memory_space=VMEM)] * len(outputs),
+        out_specs=out_specs,
         scratch_shapes=list(scratch),
         cost_estimate=pl.CostEstimate(flops=weight, bytes_accessed=1, transcendentals=0),
         compiler_params=pltpu.CompilerParams(vmem_limit_bytes=GRANT),
@@ -102,18 +104,31 @@
 def begin_body(count, *refs):
     sources, targets = refs[:count], refs[count : 2 * count]
     moved_ref, high_ref, low_ref, edge_ref, sems = refs[2 * count :]
-    copies = [
-        pltpu.make_async_copy(source, target, sems.at[n])
-        for n, (source, target) in enumerate(zip(sources, targets))
-    ]
-    for copy in copies:
-        copy.start()
-    for copy in copies[:4]:
-        copy.wait()
     s_ref, a_ref, b_ref, c_ref = targets[:4]
     levels, rows, _ = s_ref.shape
     last = rows - 1
+    cut = levels // PARTS
+    parts = [
+        [
+            pltpu.make_async_copy(
+                sources[n].at[pl.ds(part * cut, cut)],
+                targets[n].at[pl.ds(part * cut, cut)],
+                sems.at[part * 4 + n],
+            )
+            for n in range(4)
+        ]
+        for part in range(PARTS)
+    ]
+    rest = [
+        pltpu.make_async_copy(sources[n], targets[n], sems.at[4 * (PARTS - 1) + n])
+        for n in range(4, count)
+    ]
+    for copy in sum(parts, []) + rest:
+        copy.start()
     for lev in range(levels):
+        if lev % cut == 0:
+            for copy in parts[lev // cut]:
+                copy.wait()
         s, a, b, c = s_ref[lev], a_ref[lev], b_ref[lev], c_ref[lev]
         coeffs = taps(a, b, c)
         once = forward(s, coeffs)
@@ -144,7 +159,7 @@
         }
         for n, key in enumerate(EDGE):
             edge_ref[n, at] = rows_of[key]
-    for copy in copies[4:]:
+    for copy in rest:
         copy.wait()
 
 
@@ -397,9 +412,8 @@
         keep_ref[1, lev] = jnp.where(low_pair, two, y0)
         give_ref[lev] = jnp.where(low_pair, three, two)
     for n, total in enumerate((numer, denom)):
-        sums_ref[n] = total
         obs = lanes(obs_ref[n]) + rest_ref[levels, n : n + 1, 0:128]
-        sums_ref[n, 0:1] = total[0:1] + obs
+        sums_ref[n : n + 1] = jnp.sum(total, axis=0, keepdims=True) + obs
 
 
 def update_body(
@@ -408,11 +422,8 @@
 ):
     position = lax.axis_index("tm")
     leads, low_pair = lax.rem(position, 2) == 1, position < 2
-    total = [
-        jnp.sum(jnp.sum(sums_ref[n], axis=0, keepdims=True), axis=1, keepdims=True)
-        for n in range(2)
-    ]
-    step = total[0] / total[1]
+    total = jnp.sum(sums_ref[...], axis=1, keepdims=True)
+    step = total[0:1] / total[1:2]
     for lev in range(mult_ref.shape[0]):
         known, got = known_ref[lev], got_ref[lev]
         model = jnp.where(leads, keep_ref[0, lev], jnp.where(low_pair, known, got))
@@ -505,7 +516,7 @@
         [(x, "far") for x in arguments],
         [(x.shape, "near", x.dtype) for x in arguments]
         + [field, lines(3), lines(3), lines(len(EDGE))],
-        [pltpu.SemaphoreType.DMA((count,))],
+        [pltpu.SemaphoreType.DMA((count + 4 * (PARTS - 1),))],
     )
     incr, *coeffs = here[:4]
     mult, rhs, err, cell, dual, want, var = here[4:]
@@ -551,17 +562,18 @@
         [((3, levels, rows, cols), "near"), field],
     )
     got = swap(urgent, "tm", 1)
-    send = kernel_call(
-        sends_body, "sends", near(own, got, fix), [((levels * rows + 4 * levels, cols), "near")]
-    )[0]
-    send, own, cell = lax.optimization_barrier((send, own, cell))
-    got_send = leaders(send, 0, 2)
     dir_obs, obs_sums = kernel_call(
         gather_body,
         "gather",
         near(incr, cell, dual, want, var, valid),
         [(obs_dual.shape, "near"), ((2, *obs_dual.shape), "near")],
     )
+    got, obs_sums = lax.optimization_barrier((got, obs_sums))
+    send = kernel_call(
+        sends_body, "sends", near(own, got, fix), [((levels * rows + 4 * levels, cols), "near")]
+    )[0]
+    send, own = lax.optimization_barrier((send, own))
+    got_send = leaders(send, 0, 2)
     rest, other = kernel_call(
         rest_body, "rest", near(own, obs_sums), [((levels + 1, rows, cols), "near"), field]
     )
@@ -587,7 +599,7 @@
     )
     pair = ((2, levels, rows, cols), "near")
     keep, give, sums = kernel_call(
-        dots_body, "dots", near(terms, got_send, got_rest, obs_sums), [pair, field, ((2, 8, 128), "near")]
+        dots_body, "dots", near(terms, got_send, got_rest, obs_sums), [pair, field, ((2, 128), "near")]
     )
     total = sums + leaders(sums, 0, 2) + leaders(sums, 1, 0) + leaders(sums, 1, 2)
     distance = 2

time: 31.8 us -> 31.1 us (0.978)
  waiting for transfers between devices: 9.11 us -> 7.72 us
  starting transfers between devices: 14.8 us -> 15.6 us
    ppermute x8, waiting for transfers between devices: 5.24 us -> 4.26 us  [exchange(): return lax.ppermute(value, ('groups', 'tile', 'tm'), pairs)]
    ppermute x8, starting transfers between devices: 7.7 us -> 8.51 us  [exchange(): return lax.ppermute(value, ('groups', 'tile', 'tm'), pairs)]
    ppermute x8, waiting for transfers between devices: 3.87 us -> 3.46 us  [swap(): lax.ppermute(value, axis, [(i, i ^ distance) for i in range(lax.axis_size...]
where the time goes in v4:
time: 31.1 us; the launch traced here: 30.9 us
  starting transfers between devices  15.6 us (50%)
  waiting for transfers between devices  7.72 us (25%)
  Pallas kernels  6.04 us (19%)
  between operations  1.44 us (5%)
    ppermute x8, starting transfers between devices, exchange(): return lax.ppermute(value, ('groups', 'tile', 'tm'), pairs)  8.51 us
    ppermute x8, starting transfers between devices, swap(): lax.ppermute(value, axis, [(i, i ^ distance) for i in range(lax.axis_size...  7.1 us
    pallas_call x15, Pallas kernels, kernel_call(): pl.pallas_call(body, name=name, out_shape=out_shape, in_specs=in_specs, o...  6.04 us
    ppermute x8, waiting for transfers between devices, exchange(): return lax.ppermute(value, ('groups', 'tile', 'tm'), pairs)  4.26 us
    ppermute x8, waiting for transfers between devices, swap(): lax.ppermute(value, axis, [(i, i ^ distance) for i in range(lax.axis_size...  3.46 us
  transfers between devices with their start and end apart: 16, of which 8 were waited for; matrix products, arithmetic and copies ran while one was open for 0% of the time, Pallas kernels for 15%

profile of v4, /device:TPU:0, one launch (start us, length us, event | category | flops | bytes accessed | tf_op | source)
XLA Modules:
  0.0 30.9 jit_solution(14559947712837308927)
XLA Ops:
  0.6 0.5 %collective-permute-start = (f32[8,16,512]{2,1,0:T(8,128)}, f32[8,16,512]{2,1,0:T(8,128)S(1)}, u32[]{:S(2)}, u32[]{:S(2)}) collective-permute-start(f32[8,16,512]{2,1,0:T(8,128)} %bitcast.17), channel_id=1, source_target_pairs={{0,1},{1,0},{2,3},{3,2},{4,5},{5,4},{6,7},{7,6},{8,9},{9,8},{10,11... | collective-permute-start | bytes 786440 | tf_op jit(solution)/shard_map/ppermute | solution.py:449
  1.2 1.8 %begin.1 = (f32[8,16,512]{2,1,0:T(8,128)S(1)}, f32[8,16,512]{2,1,0:T(8,128)S(1)}, f32[8,16,512]{2,1,0:T(8,128)S(1)}, f32[8,16,512]{2,1,0:T(8,128)S(1)}, f32[8,16...) custom-call(f32[8,16,512]{2,1,0:T(8,128)} %bitcast.11, ...), custom_call_target="tpu_custom_call" | custom-call | flops 1 | bytes 1 | tf_op jit(solution)/shard_map/begin/pallas_call | solution.py:32
  3.7 0.0 collective-permute-done.later_ref.refs_1_
  3.7 0.1 rims.1
  3.8 2.7 %collective-permute-start.2 = (f32[5,8,512]{2,1,0:T(8,128)S(1)}, f32[5,8,512]{2,1,0:T(8,128)S(1)}, u32[]{:S(2)}, u32[]{:S(2)}) collective-permute-start(f32[5,8,512]{2,1,0:T(8,128)S(1)} %get-tuple-element.62.first_ref), channel_id=1, source_target_pairs={{0,4},{4,0},{8,12},{12,8},{1,5},{5,1},{9,13},{13,9},{2,6},{6,2},{1... | collective-permute-start | bytes 245768 | tf_op jit(solution)/shard_map/ppermute | solution.py:449
  6.4 0.2 collective-permute-start.3
  6.7 1.6 %collective-permute-start.1 = (f32[9,16,512]{2,1,0:T(8,128)S(1)}, f32[9,16,512]{2,1,0:T(8,128)S(1)}, u32[]{:S(2)}, u32[]{:S(2)}) collective-permute-start(f32[9,16,512]{2,1,0:T(8,128)S(1)} %pad.4), channel_id=1, source_target_pairs={{0,16},{1,3},{2,18},{3,1},{4,20},{5,7},{6,22},{7,5},{8,24},{9,11},... | collective-permute-start | bytes 884744 | tf_op jit(solution)/shard_map/ppermute | solution.py:445
  8.3 0.4 %spread.1 = (f32[8,16,512]{2,1,0:T(8,128)S(1)}, f32[8,16,512]{2,1,0:T(8,128)S(1)}) custom-call(f32[8,16,512]{2,1,0:T(8,128)S(1)} %get-tuple-element.45.incr_ref, f32[8,16,512]{2,1,0:T(8,128)S(1)} %get-tuple-element.44.mult_ref, f32[8,16,512]{2,1,0:T(8,128)S(1)} %get-tuple-element.55.rhs_ref, f32[8,16,512]{2,1,0:T(8,128)S(1)} %get-tuple-element.56.err_ref, ...), custom_call_target="tpu_custom_call" | custom-call | flops 1 | bytes 1 | tf_op jit(solution)/shard_map/spread/pallas_call | solution.py:32
  8.7 0.7 %adjoint.1.back_ref = f32[8,16,512]{2,1,0:T(8,128)S(1)} custom-call(f32[8,16,512]{2,1,0:T(8,128)S(1)} %get-tuple-element.52.a_ref, f32[8,16,512]{2,1,0:T(8,128)S(1)} %get-tuple-element.53.b_ref, f32[8,16,512]{2,1,0:T(8,128)S(1)} %get-tuple-element.54.c_ref, f32[8,16,512]{2,1,0:T(8,128)S(1)} %collective-permute-done.later_ref.refs_1_), custom_call_target="tpu_custom_call" | custom-call | flops 1 | bytes 1 | tf_op jit(solution)/shard_map/adjoint/pallas_call | solution.py:32
  9.4 0.1 collective-permute-done.2.got_first_ref.past_first_ref
  9.5 0.0 collective-permute-done.3.got_second_ref.past_second_ref
  9.5 0.1 edges.1.fix_ref
  9.7 0.1 share.1
  9.8 0.1 collective-permute-start.4
  9.9 0.4 %gather.1 = (f32[1,512]{1,0:T(1,128)S(1)}, f32[2,1,512]{2,1,0:T(1,128)S(1)}) custom-call(f32[8,16,512]{2,1,0:T(8,128)S(1)} %get-tuple-element.45.incr_ref, s32[1,512]{1,0:T(1,128)S(1)} %get-tuple-element.47.cell_ref, f32[1,512]{1,0:T(1,128)S(1)} %get-tuple-element.46.dual_ref, f32[1,512]{1,0:T(1,128)S(1)} %get-tuple-element.48.want_ref, ...), custom_call_target="tpu_custom_call" | custom-call | flops 1 | bytes 1 | tf_op jit(solution)/shard_map/gather/pallas_call | solution.py:32
  10.3 1.1 %collective-permute-done.4.got_ref = f32[8,16,512]{2,1,0:T(8,128)S(1)} collective-permute-done((f32[8,16,512]{2,1,0:T(8,128)S(1)}, f32[8,16,512]{2,1,0:T(8,128)S(1)}, u32[]{:S(2)}, u32[]{:S(2)}) %collective-permute-start.4) | collective-permute-done | bytes 262176 | tf_op jit(solution)/shard_map/ppermute | solution.py:449
  11.4 1.7 %collective-permute-start.9 = (f32[160,512]{1,0:T(8,128)S(1)}, f32[160,512]{1,0:T(8,128)S(1)}, u32[]{:S(2)}, u32[]{:S(2)}) collective-permute-start(f32[160,512]{1,0:T(8,128)S(1)} %sends.1), channel_id=1, source_target_pairs={{0,16},{1,3},{2,18},{3,1},{4,20},{5,7},{6,22},{7,5},{8,24},{9,11},... | collective-permute-start | bytes 983048 | tf_op jit(solution)/shard_map/ppermute | solution.py:445
  13.2 0.1 collective-permute-start.6
  13.3 0.5 %collective-permute-start.5 = (f32[9,16,512]{2,1,0:T(8,128)S(1)}, f32[9,16,512]{2,1,0:T(8,128)S(1)}, u32[]{:S(2)}, u32[]{:S(2)}) collective-permute-start(f32[9,16,512]{2,1,0:T(8,128)S(1)} %get-tuple-element.70), channel_id=1, source_target_pairs={{0,1},{1,0},{2,3},{3,2},{4,5},{5,4},{6,7},{7,6},{8,9},{9,8},{10,11... | collective-permute-start | bytes 884744 | tf_op jit(solution)/shard_map/ppermute | solution.py:449
  13.8 0.0 collective-permute-done.1.later_ref.cross_ref
  13.8 0.1 late_rims.1
  13.9 2.8 %collective-permute-start.7 = (f32[2,8,512]{2,1,0:T(8,128)S(1)}, f32[2,8,512]{2,1,0:T(8,128)S(1)}, u32[]{:S(2)}, u32[]{:S(2)}) collective-permute-start(f32[2,8,512]{2,1,0:T(8,128)S(1)} %get-tuple-element.72.first_ref), channel_id=1, source_target_pairs={{0,4},{4,0},{8,12},{12,8},{1,5},{5,1},{9,13},{13,9},{2,6},{6,2},{1... | collective-permute-start | bytes 98312 | tf_op jit(solution)/shard_map/ppermute | solution.py:449
  16.7 0.0 collective-permute-start.8
  16.7 0.7 %beyond.1.beyond_ref = f32[8,16,512]{2,1,0:T(8,128)S(1)} custom-call(f32[8,16,512]{2,1,0:T(8,128)S(1)} %get-tuple-element.52.a_ref, f32[8,16,512]{2,1,0:T(8,128)S(1)} %get-tuple-element.53.b_ref, f32[8,16,512]{2,1,0:T(8,128)S(1)} %get-tuple-element.54.c_ref, f32[9,16,512]{2,1,0:T(8,128)S(1)} %collective-permute-done.1.later_ref.cross_ref), custom_call_target="tpu_custom_call" | custom-call | flops 1 | bytes 1 | tf_op jit(solution)/shard_map/beyond/pallas_call | solution.py:32
  17.4 1.2 %collective-permute-done.7.got_first_ref = f32[2,8,512]{2,1,0:T(8,128)S(1)} collective-permute-done((f32[2,8,512]{2,1,0:T(8,128)S(1)}, f32[2,8,512]{2,1,0:T(8,128)S(1)}, u32[]{:S(2)}, u32[]{:S(2)}) %collective-permute-start.7) | collective-permute-done | bytes 32800 | tf_op jit(solution)/shard_map/ppermute | solution.py:449
  18.6 0.0 collective-permute-done.8.got_second_ref
  18.6 0.1 late_edges.1.fix_ref
  18.7 0.0 collective-permute-done.6.other_ref
  18.7 0.0 collective-permute-done.5.rest_ref
  18.7 0.1 terms.1
  18.9 0.0 collective-permute-done.9.got_ref
  18.9 0.3 dots.1
  19.1 1.5 %collective-permute-start.12 = (f32[2,128]{1,0:T(2,128)S(1)}, f32[2,128]{1,0:T(2,128)S(1)}, u32[]{:S(2)}, u32[]{:S(2)}) collective-permute-start(f32[2,128]{1,0:T(2,128)S(1)} %get-tuple-element.79), channel_id=1, source_target_pairs={{0,16},{1,7},{2,18},{3,5},{4,20},{5,3},{6,22},{7,1},{8,24},{9,15},... | collective-permute-start | bytes 3080 | tf_op jit(solution)/shard_map/ppermute | solution.py:445
  20.7 0.6 %collective-permute-start.11 = (f32[2,128]{1,0:T(2,128)S(1)}, f32[2,128]{1,0:T(2,128)S(1)}, u32[]{:S(2)}, u32[]{:S(2)}) collective-permute-start(f32[2,128]{1,0:T(2,128)S(1)} %get-tuple-element.79), channel_id=1, source_target_pairs={{0,16},{1,5},{2,18},{3,7},{4,20},{5,1},{6,22},{7,3},{8,24},{9,13},... | collective-permute-start | bytes 3080 | tf_op jit(solution)/shard_map/ppermute | solution.py:445
  21.2 1.4 %collective-permute-start.10 = (f32[2,128]{1,0:T(2,128)S(1)}, f32[2,128]{1,0:T(2,128)S(1)}, u32[]{:S(2)}, u32[]{:S(2)}) collective-permute-start(f32[2,128]{1,0:T(2,128)S(1)} %get-tuple-element.79), channel_id=1, source_target_pairs={{0,16},{1,3},{2,18},{3,1},{4,20},{5,7},{6,22},{7,5},{8,24},{9,11},... | collective-permute-start | bytes 3080 | tf_op jit(solution)/shard_map/ppermute | solution.py:445
  22.7 0.1 collective-permute-done.12
  22.8 1.4 %collective-permute-done.11 = f32[2,128]{1,0:T(2,128)S(1)} collective-permute-done((f32[2,128]{1,0:T(2,128)S(1)}, f32[2,128]{1,0:T(2,128)S(1)}, u32[]{:S(2)}, u32[]{:S(2)}) %collective-permute-start.11) | collective-permute-done | bytes 1056 | tf_op jit(solution)/shard_map/ppermute | solution.py:445
  24.2 0.6 %collective-permute-done.10 = f32[2,128]{1,0:T(2,128)S(1)} collective-permute-done((f32[2,128]{1,0:T(2,128)S(1)}, f32[2,128]{1,0:T(2,128)S(1)}, u32[]{:S(2)}, u32[]{:S(2)}) %collective-permute-start.10) | collective-permute-done | bytes 1056 | tf_op jit(solution)/shard_map/ppermute | solution.py:445
  24.8 1.4 %collective-permute-start.13 = (f32[2,128]{1,0:T(2,128)S(1)}, f32[2,128]{1,0:T(2,128)S(1)}, u32[]{:S(2)}, u32[]{:S(2)}) collective-permute-start(f32[2,128]{1,0:T(2,128)S(1)} %add_add_fusion), channel_id=1, source_target_pairs={{0,16},{1,9},{2,18},{3,11},{4,20},{5,13},{6,22},{7,15},{8,24},{9,1... | collective-permute-start | bytes 3080 | tf_op jit(solution)/shard_map/ppermute | solution.py:445
  26.3 2.1 %collective-permute-done.13 = f32[2,128]{1,0:T(2,128)S(1)} collective-permute-done((f32[2,128]{1,0:T(2,128)S(1)}, f32[2,128]{1,0:T(2,128)S(1)}, u32[]{:S(2)}, u32[]{:S(2)}) %collective-permute-start.13) | collective-permute-done | bytes 1056 | tf_op jit(solution)/shard_map/ppermute | solution.py:445
  28.4 0.0 collective-permute-start.14
  28.4 0.5 %collective-permute-start.15 = (f32[2,128]{1,0:T(2,128)S(1)}, f32[2,128]{1,0:T(2,128)S(1)}, u32[]{:S(2)}, u32[]{:S(2)}) collective-permute-start(f32[2,128]{1,0:T(2,128)S(1)} %add.21), channel_id=1, source_target_pairs={{0,1},{1,0},{2,3},{3,2},{4,5},{5,4},{6,7},{7,6},{8,9},{9,8},{10,11... | collective-permute-start | bytes 3080 | tf_op jit(solution)/shard_map/ppermute | solution.py:449
  28.9 1.0 %collective-permute-done.15 = f32[2,128]{1,0:T(2,128)S(1)} collective-permute-done((f32[2,128]{1,0:T(2,128)S(1)}, f32[2,128]{1,0:T(2,128)S(1)}, u32[]{:S(2)}, u32[]{:S(2)}) %collective-permute-start.15) | collective-permute-done | bytes 1056 | tf_op jit(solution)/shard_map/ppermute | solution.py:449
  29.9 0.0 collective-permute-done.14.got_ref
  29.9 1.0 %update.1 = (f32[8,16,512]{2,1,0:T(8,128)}, f32[8,16,512]{2,1,0:T(8,128)}, f32[1,512]{1,0:T(1,128)}) custom-call(f32[8,16,512]{2,1,0:T(8,128)S(1)} %get-tuple-element.44.mult_ref, f32[8,16,512]{2,1,0:T(8,128)S(1)} %get-tuple-element.45.incr_ref, f32[1,512]{1,0:T(1,128)S(1)} %get-tuple-element.46.dual_ref, f32[1,512]{1,0:T(1,128)S(1)} %get-tuple-element.50.dir_ref, ...), custom_call_target="tpu_custom_call" | custom-call | flops 1 | bytes 1 | tf_op jit(solution)/shard_map/update/pallas_call | solution.py:32
  (8 shorter events, 0.2 us)
Async XLA Ops:
  0.6 3.0 %collective-permute-start = (f32[8,16,512]{2,1,0:T(8,128)}, f32[8,16,512]{2,1,0:T(8,128)S(1)}, u32[]{:S(2)}, u32[]{:S(2)}) collective-permute-start(f32[8,16,512]{2,1,0:T(8,128)} %bitcast.17), channel_id=1, source_target_pairs={{0,1},{1,0},{2,3},{3,2},{4,5},{5,4},{6,7},{7,6},{8,9},{9,8},{10,11... | collective-permute-start | bytes 786440 | tf_op jit(solution)/shard_map/ppermute | solution.py:449
  3.8 5.8 %collective-permute-start.2 = (f32[5,8,512]{2,1,0:T(8,128)S(1)}, f32[5,8,512]{2,1,0:T(8,128)S(1)}, u32[]{:S(2)}, u32[]{:S(2)}) collective-permute-start(f32[5,8,512]{2,1,0:T(8,128)S(1)} %get-tuple-element.62.first_ref), channel_id=1, source_target_pairs={{0,4},{4,0},{8,12},{12,8},{1,5},{5,1},{9,13},{13,9},{2,6},{6,2},{1... | collective-permute-start | bytes 245768 | tf_op jit(solution)/shard_map/ppermute | solution.py:449
  6.4 3.1 %collective-permute-start.3 = (f32[5,8,512]{2,1,0:T(8,128)S(1)}, f32[5,8,512]{2,1,0:T(8,128)S(1)}, u32[]{:S(2)}, u32[]{:S(2)}) collective-permute-start(f32[5,8,512]{2,1,0:T(8,128)S(1)} %get-tuple-element.63.second_ref), channel_id=1, source_target_pairs={{0,1},{1,0},{2,3},{3,2},{4,8},{5,9},{6,10},{7,11},{8,4},{9,5},{10,... | collective-permute-start | bytes 245768 | tf_op jit(solution)/shard_map/ppermute | solution.py:445
  6.7 7.1 %collective-permute-start.1 = (f32[9,16,512]{2,1,0:T(8,128)S(1)}, f32[9,16,512]{2,1,0:T(8,128)S(1)}, u32[]{:S(2)}, u32[]{:S(2)}) collective-permute-start(f32[9,16,512]{2,1,0:T(8,128)S(1)} %pad.4), channel_id=1, source_target_pairs={{0,16},{1,3},{2,18},{3,1},{4,20},{5,7},{6,22},{7,5},{8,24},{9,11},... | collective-permute-start | bytes 884744 | tf_op jit(solution)/shard_map/ppermute | solution.py:445
  9.8 1.6 %collective-permute-start.4 = (f32[8,16,512]{2,1,0:T(8,128)S(1)}, f32[8,16,512]{2,1,0:T(8,128)S(1)}, u32[]{:S(2)}, u32[]{:S(2)}) collective-permute-start(f32[8,16,512]{2,1,0:T(8,128)S(1)} %get-tuple-element.65), channel_id=1, source_target_pairs={{0,1},{1,0},{2,3},{3,2},{4,5},{5,4},{6,7},{7,6},{8,9},{9,8},{10,11... | collective-permute-start | bytes 786440 | tf_op jit(solution)/shard_map/ppermute | solution.py:449
  11.4 7.4 %collective-permute-start.9 = (f32[160,512]{1,0:T(8,128)S(1)}, f32[160,512]{1,0:T(8,128)S(1)}, u32[]{:S(2)}, u32[]{:S(2)}) collective-permute-start(f32[160,512]{1,0:T(8,128)S(1)} %sends.1), channel_id=1, source_target_pairs={{0,16},{1,3},{2,18},{3,1},{4,20},{5,7},{6,22},{7,5},{8,24},{9,11},... | collective-permute-start | bytes 983048 | tf_op jit(solution)/shard_map/ppermute | solution.py:445
  13.2 5.5 %collective-permute-start.6 = (f32[8,16,512]{2,1,0:T(8,128)S(1)}, f32[8,16,512]{2,1,0:T(8,128)S(1)}, u32[]{:S(2)}, u32[]{:S(2)}) collective-permute-start(f32[8,16,512]{2,1,0:T(8,128)S(1)} %get-tuple-element.71), channel_id=1, source_target_pairs={{0,1},{1,0},{2,3},{3,2},{4,5},{5,4},{6,7},{7,6},{8,9},{9,8},{10,11... | collective-permute-start | bytes 786440 | tf_op jit(solution)/shard_map/ppermute | solution.py:449
  13.3 5.4 %collective-permute-start.5 = (f32[9,16,512]{2,1,0:T(8,128)S(1)}, f32[9,16,512]{2,1,0:T(8,128)S(1)}, u32[]{:S(2)}, u32[]{:S(2)}) collective-permute-start(f32[9,16,512]{2,1,0:T(8,128)S(1)} %get-tuple-element.70), channel_id=1, source_target_pairs={{0,1},{1,0},{2,3},{3,2},{4,5},{5,4},{6,7},{7,6},{8,9},{9,8},{10,11... | collective-permute-start | bytes 884744 | tf_op jit(solution)/shard_map/ppermute | solution.py:449
  13.9 4.7 %collective-permute-start.7 = (f32[2,8,512]{2,1,0:T(8,128)S(1)}, f32[2,8,512]{2,1,0:T(8,128)S(1)}, u32[]{:S(2)}, u32[]{:S(2)}) collective-permute-start(f32[2,8,512]{2,1,0:T(8,128)S(1)} %get-tuple-element.72.first_ref), channel_id=1, source_target_pairs={{0,4},{4,0},{8,12},{12,8},{1,5},{5,1},{9,13},{13,9},{2,6},{6,2},{1... | collective-permute-start | bytes 98312 | tf_op jit(solution)/shard_map/ppermute | solution.py:449
  16.7 1.9 %collective-permute-start.8 = (f32[2,8,512]{2,1,0:T(8,128)S(1)}, f32[2,8,512]{2,1,0:T(8,128)S(1)}, u32[]{:S(2)}, u32[]{:S(2)}) collective-permute-start(f32[2,8,512]{2,1,0:T(8,128)S(1)} %get-tuple-element.73.second_ref), channel_id=1, source_target_pairs={{0,1},{1,0},{2,3},{3,2},{4,8},{5,9},{6,10},{7,11},{8,4},{9,5},{10,... | collective-permute-start | bytes 98312 | tf_op jit(solution)/shard_map/ppermute | solution.py:445
  19.1 3.6 %collective-permute-start.12 = (f32[2,128]{1,0:T(2,128)S(1)}, f32[2,128]{1,0:T(2,128)S(1)}, u32[]{:S(2)}, u32[]{:S(2)}) collective-permute-start(f32[2,128]{1,0:T(2,128)S(1)} %get-tuple-element.79), channel_id=1, source_target_pairs={{0,16},{1,7},{2,18},{3,5},{4,20},{5,3},{6,22},{7,1},{8,24},{9,15},... | collective-permute-start | bytes 3080 | tf_op jit(solution)/shard_map/ppermute | solution.py:445
  20.7 3.6 %collective-permute-start.11 = (f32[2,128]{1,0:T(2,128)S(1)}, f32[2,128]{1,0:T(2,128)S(1)}, u32[]{:S(2)}, u32[]{:S(2)}) collective-permute-start(f32[2,128]{1,0:T(2,128)S(1)} %get-tuple-element.79), channel_id=1, source_target_pairs={{0,16},{1,5},{2,18},{3,7},{4,20},{5,1},{6,22},{7,3},{8,24},{9,13},... | collective-permute-start | bytes 3080 | tf_op jit(solution)/shard_map/ppermute | solution.py:445
  21.2 3.6 %collective-permute-start.10 = (f32[2,128]{1,0:T(2,128)S(1)}, f32[2,128]{1,0:T(2,128)S(1)}, u32[]{:S(2)}, u32[]{:S(2)}) collective-permute-start(f32[2,128]{1,0:T(2,128)S(1)} %get-tuple-element.79), channel_id=1, source_target_pairs={{0,16},{1,3},{2,18},{3,1},{4,20},{5,7},{6,22},{7,5},{8,24},{9,11},... | collective-permute-start | bytes 3080 | tf_op jit(solution)/shard_map/ppermute | solution.py:445
  24.8 3.6 %collective-permute-start.13 = (f32[2,128]{1,0:T(2,128)S(1)}, f32[2,128]{1,0:T(2,128)S(1)}, u32[]{:S(2)}, u32[]{:S(2)}) collective-permute-start(f32[2,128]{1,0:T(2,128)S(1)} %add_add_fusion), channel_id=1, source_target_pairs={{0,16},{1,9},{2,18},{3,11},{4,20},{5,13},{6,22},{7,15},{8,24},{9,1... | collective-permute-start | bytes 3080 | tf_op jit(solution)/shard_map/ppermute | solution.py:445
  28.4 1.5 %collective-permute-start.14 = (f32[8,16,512]{2,1,0:T(8,128)S(1)}, f32[8,16,512]{2,1,0:T(8,128)S(1)}, u32[]{:S(2)}, u32[]{:S(2)}) collective-permute-start(f32[8,16,512]{2,1,0:T(8,128)S(1)} %get-tuple-element.80), channel_id=1, source_target_pairs={{0,1},{1,0},{2,3},{3,2},{4,5},{5,4},{6,7},{7,6},{8,9},{9,8},{10,11... | collective-permute-start | bytes 786440 | tf_op jit(solution)/shard_map/ppermute | solution.py:449
  28.4 1.5 %collective-permute-start.15 = (f32[2,128]{1,0:T(2,128)S(1)}, f32[2,128]{1,0:T(2,128)S(1)}, u32[]{:S(2)}, u32[]{:S(2)}) collective-permute-start(f32[2,128]{1,0:T(2,128)S(1)} %add.21), channel_id=1, source_target_pairs={{0,1},{1,0},{2,3},{3,2},{4,5},{5,4},{6,7},{7,6},{8,9},{9,8},{10,11... | collective-permute-start | bytes 3080 | tf_op jit(solution)/shard_map/ppermute | solution.py:449

commit v5 on v4

--- a/solution.py
+++ b/solution.py
@@ -8,7 +8,7 @@
 F32 = jnp.float32
 VMEM = pltpu.VMEM
 GRANT = 24 * 1024 * 1024
-WEIGHT = 3200000000
+WEIGHT = 2600000000
 PARTS = 2
 
 
@@ -140,9 +140,13 @@
         high_ref[0, at] = s[last : last + 1]
         high_ref[1, at] = once[last : last + 1]
         high_ref[2, at] = open_east
+        high_ref[3, at] = b[last : last + 1]
+        high_ref[4, at] = c[last : last + 1]
         low_ref[0, at] = s[0:1]
         low_ref[1, at] = once[0:1]
         low_ref[2, at] = open_west
+        low_ref[3, at] = b[0:1]
+        low_ref[4, at] = c[0:1]
         rows_of = {
             "mid_low": mid[0:1],
             "mid_high": mid[last : last + 1],
@@ -181,33 +185,34 @@
     )
 
 
-def outer_rows(ref, levels, wanted):
-    rows = ref.shape[1]
-    picked = []
-    for row in (0, 1, rows - 2, rows - 1):
-        value = jnp.concatenate([ref[lev, row : row + 1] for lev in range(levels)], 0)
-        picked.append(jnp.where(wanted, value, 0.0))
-    return picked
-
-
-def rims_body(wanted, edge_ref, later_ref, high_ref, low_ref, first_ref, second_ref):
+def rims_body(four, edge_ref, later_ref, high_ref, low_ref, first_ref, second_ref):
+    position, peers = lax.axis_index("tm"), lax.axis_size("tm")
     odd = lax.rem(lax.axis_index("tile"), 2)
     k = {key: edge_ref[n] for n, key in enumerate(EDGE)}
-    low, high = outer_products(k, outer_rows(later_ref, edge_ref.shape[1], wanted()))
-    lows = [low_ref[n] for n in range(3)] + list(low)
-    highs = [high_ref[n] for n in range(3)] + list(high)
-    for n in range(5):
-        first_ref[n] = jnp.where(odd == 0, highs[n], lows[n])
-        second_ref[n] = jnp.where(odd == 0, lows[n], highs[n])
-
-
-def late_rims_body(edge_ref, later_ref, first_ref, second_ref):
-    odd = lax.rem(lax.axis_index("tile"), 2)
-    k = {key: edge_ref[n] for n, key in enumerate(EDGE)}
-    low, high = outer_products(k, outer_rows(later_ref, edge_ref.shape[1], lax.axis_index("tm") == 1))
-    for n in range(2):
-        first_ref[n] = jnp.where(odd == 0, high[n], low[n])
-        second_ref[n] = jnp.where(odd == 0, low[n], high[n])
+    levels, rows, _ = later_ref.shape
+    later = [
+        jnp.concatenate([later_ref[lev, row : row + 1] for lev in range(levels)], 0)
+        for row in (0, 1, rows - 2, rows - 1)
+    ]
+    products = outer_products(k, later)
+    zero = jnp.zeros(later[0].shape, F32)
+    sent = []
+    for ref, product, outer, inside, beside in (
+        (low_ref, products[0], later[0], later[1], k["west_next"]),
+        (high_ref, products[1], later[3], later[2], k["east_next"]),
+    ):
+        out = [ref[0], ref[1], ref[2], *product, zero]
+        if four:
+            second, final = position == 1, position == peers - 1
+            out[0] = jnp.where(final, outer, out[0])
+            out[1] = jnp.where(final, inside, out[1])
+            out[3] = jnp.where(second, ref[3], out[3])
+            out[4] = jnp.where(second, ref[4], out[4])
+            out[5] = jnp.where(second, beside, zero)
+        sent.append(out)
+    for n, (low, high) in enumerate(zip(*sent)):
+        first_ref[n] = jnp.where(odd == 0, high, low)
+        second_ref[n] = jnp.where(odd == 0, low, high)
 
 
 def sides(first, second):
@@ -235,37 +240,66 @@
     )
 
 
-def edges_body(first_ref, second_ref, got_first_ref, got_second_ref, edge_ref, fix_ref):
+def edges_body(
+    four, first_ref, second_ref, got_first_ref, got_second_ref, edge_ref, fix_ref, late_ref
+):
+    position, peers = lax.axis_index("tm"), lax.axis_size("tm")
     k = {key: edge_ref[n] for n, key in enumerate(EDGE)}
     state, stepped, toward, product, product_stepped = (
         sides(got_first_ref[n], got_second_ref[n]) for n in range(5)
     )
     own_state = own_sides(first_ref[0], second_ref[0])
     own_product = own_sides(first_ref[3], second_ref[3])
+    wanted = lax.rem(position, 2) == 0 if four else position < peers - 1
 
     def along(x, side):
         mid, north, south = k["mid_" + side], k["north_" + side], k["south_" + side]
         return mid * x + north * up(x, 1) + south * down(x, 1)
 
     new_low, new_high = k["west_low"] * state[0], k["east_high"] * state[1]
-    fix_ref[0] = along(new_low, "low") + k["west_low"] * (stepped[0] + toward[0] * own_state[0])
-    fix_ref[1] = k["west_next"] * new_low
-    fix_ref[2] = k["east_next"] * new_high
-    fix_ref[3] = along(new_high, "high") + k["east_high"] * (stepped[1] + toward[1] * own_state[1])
-    for n, row in enumerate(back_fix(k, product, product_stepped, own_product, toward)):
-        fix_ref[4 + n] = row
-
-
-def late_edges_body(
-    first_ref, second_ref, got_first_ref, got_second_ref, past_first_ref, past_second_ref,
-    edge_ref, fix_ref,
-):
+    moved = (
+        along(new_low, "low") + k["west_low"] * (stepped[0] + toward[0] * own_state[0]),
+        k["west_next"] * new_low,
+        k["east_next"] * new_high,
+        along(new_high, "high") + k["east_high"] * (stepped[1] + toward[1] * own_state[1]),
+    )
+    back = back_fix(k, product, product_stepped, own_product, toward)
+    beyond = (state[0], stepped[0], state[1], stepped[1])
+    for n in range(4):
+        fix_ref[n] = moved[n]
+        fix_ref[4 + n] = jnp.where(wanted, back[n], 0.0)
+        late_ref[n] = jnp.where(position < peers // 2, moved[n], beyond[n])
+
+
+def late_body(rows, got_first_ref, got_second_ref, edge_ref, cross_ref, late_ref, fix_ref):
     k = {key: edge_ref[n] for n, key in enumerate(EDGE)}
-    product, stepped = (sides(got_first_ref[n], got_second_ref[n]) for n in range(2))
-    toward = sides(past_first_ref[2], past_second_ref[2])
-    own_product = own_sides(first_ref[0], second_ref[0])
-    for n, row in enumerate(back_fix(k, product, stepped, own_product, toward)):
-        fix_ref[n] = row
+    levels, cols = edge_ref.shape[1:]
+    _, y = iotas((levels, cols))
+    toward, drift, diffuse, beside = (
+        sides(got_first_ref[n], got_second_ref[n]) for n in range(2, 6)
+    )
+    product, stepped, own = [], [], []
+    for side in range(2):
+        near_by, far_off = late_ref[2 * side], late_ref[2 * side + 1]
+        b, c = drift[side], diffuse[side]
+        north, south = jnp.where(y < cols - 1, c - b, 0.0), jnp.where(y > 0, c + b, 0.0)
+        once = (1.0 - 4.0 * c) * near_by + beside[side] * far_off
+        once = once + down(north * near_by, 1) + up(south * near_by, 1)
+        product.append(toward[side] * near_by)
+        stepped.append(toward[side] * once)
+        row = side * (rows - 1)
+        outer = [cross_ref[lev * rows + row : lev * rows + row + 1] for lev in range(levels)]
+        own.append(k[("west_low", "east_high")[side]] * jnp.concatenate(outer, 0))
+    for n, fix in enumerate(back_fix(k, product, stepped, own, toward)):
+        fix_ref[n] = fix
+
+
+def beyond_body(a_ref, b_ref, c_ref, cross_ref, back_ref):
+    levels, rows, _ = a_ref.shape
+    for lev in range(levels):
+        coeffs = taps(a_ref[lev], b_ref[lev], c_ref[lev])
+        cross = cross_ref[lev * rows : (lev + 1) * rows]
+        back_ref[lev] = adjoint(adjoint(cross, coeffs), coeffs)
 
 
 def thirds(x):
@@ -346,41 +380,42 @@
         urgent_ref[lev] = jnp.where(low_pair, local + moved, residual)
 
 
-def sends_body(own_ref, got_ref, fix_ref, send_ref):
-    _, levels, rows, _ = own_ref.shape
+def sends_body(own_ref, got_ref, send_ref):
     low_pair = lax.axis_index("tm") < 2
-    for lev in range(levels):
+    for lev in range(own_ref.shape[1]):
         mine = jnp.where(low_pair, own_ref[0, lev], own_ref[2, lev])
-        send_ref[lev * rows : (lev + 1) * rows] = mine + got_ref[lev]
-    for n in range(4):
-        start = levels * rows + n * levels
-        send_ref[start : start + levels] = fix_ref[n]
-
-
-def rest_body(own_ref, obs_ref, local_ref, other_ref):
+        send_ref[lev] = mine + got_ref[lev]
+
+
+def rest_body(own_ref, obs_ref, *out_refs):
     levels = own_ref.shape[1]
     low_pair = lax.axis_index("tm") < 2
+    blocks = [(ref, n) for ref in out_refs for n in range(ref.shape[0])]
     for lev in range(levels):
-        local_ref[lev] = own_ref[0, lev]
-        other_ref[lev] = jnp.where(low_pair, own_ref[2, lev], own_ref[1, lev])
-    local_ref[levels] = jnp.zeros(local_ref.shape[1:], F32)
-    for n in range(2):
-        local_ref[levels, n : n + 1, 0:128] = lanes(obs_ref[n])
-
-
-def terms_body(
-    cross_ref, beyond_ref, own_ref, got_ref, rest_ref, other_ref, fix_ref, terms_ref, known_ref
-):
+        ref, n = blocks[lev]
+        ref[n] = own_ref[0, lev]
+        ref, n = blocks[levels + lev]
+        ref[n] = jnp.where(low_pair, own_ref[2, lev], own_ref[1, lev])
+    ref, n = blocks[2 * levels]
+    ref[n] = jnp.zeros(ref.shape[1:], F32)
+    for i in range(2):
+        ref[n, i : i + 1, 0:128] = lanes(obs_ref[i])
+
+
+def terms_body(cross_ref, late_ref, beyond_ref, own_ref, got_ref, fix_ref, *refs):
     low_pair = lax.axis_index("tm") < 2
-    levels = own_ref.shape[1]
+    _, levels, rows, _ = own_ref.shape
+    *rest_refs, terms_ref, known_ref = refs
+    blocks = [(ref, n) for ref in rest_refs for n in range(ref.shape[0])]
     for lev in range(levels):
-        cross, got = cross_ref[lev], got_ref[lev]
+        got = got_ref[lev]
         local, residual = own_ref[0, lev], own_ref[2, lev]
         back = corrected(beyond_ref[lev], fixes(fix_ref, 0, lev))
-        rest0, rest1 = rest_ref[lev], other_ref[lev]
+        moved = corrected(cross_ref[lev * rows : (lev + 1) * rows], fixes(late_ref, 0, lev))
+        rest0, rest1 = (ref[n] for ref, n in (blocks[lev], blocks[levels + lev]))
         terms_ref[0, lev] = jnp.where(low_pair, rest0, residual)
         terms_ref[1, lev] = jnp.where(low_pair, local, residual) + got
-        terms_ref[2, lev] = jnp.where(low_pair, residual - back, rest0 + cross)
+        terms_ref[2, lev] = jnp.where(low_pair, residual - back, rest0 + moved)
         terms_ref[3, lev] = jnp.where(low_pair, rest1, local + rest1)
         known_ref[lev] = jnp.where(low_pair, local, residual + got)
 
@@ -399,12 +434,7 @@
 
     for lev in range(levels):
         y0, one, z0, z1 = (terms_ref[n, lev] for n in range(4))
-        late = []
-        for n in range(4):
-            at = levels * rows + n * levels + lev
-            late.append(jnp.where(low_pair, 0.0, got_ref[at : at + 1]))
-        z0 = corrected(z0, late)
-        two = got_ref[lev * rows : (lev + 1) * rows] + z0
+        two = got_ref[lev] + z0
         three = two + z1
         numer = numer + folded(y0 * y0 + (one - y0) * one + z0 * two + z1 * three)
         denom = denom + folded(y0 * y0 + one * one + two * two + three * three)
@@ -412,7 +442,7 @@
         keep_ref[1, lev] = jnp.where(low_pair, two, y0)
         give_ref[lev] = jnp.where(low_pair, three, two)
     for n, total in enumerate((numer, denom)):
-        obs = lanes(obs_ref[n]) + rest_ref[levels, n : n + 1, 0:128]
+        obs = lanes(obs_ref[n]) + rest_ref[rest_ref.shape[0] - 1, n : n + 1, 0:128]
         sums_ref[n : n + 1] = jnp.sum(total, axis=0, keepdims=True) + obs
 
 
@@ -515,21 +545,21 @@
         "begin",
         [(x, "far") for x in arguments],
         [(x.shape, "near", x.dtype) for x in arguments]
-        + [field, lines(3), lines(3), lines(len(EDGE))],
+        + [field, lines(5), lines(5), lines(len(EDGE))],
         [pltpu.SemaphoreType.DMA((count + 4 * (PARTS - 1),))],
     )
     incr, *coeffs = here[:4]
     mult, rhs, err, cell, dual, want, var = here[4:]
-    if peers == 4:
-        later, wanted = inner, lambda: lax.rem(lax.axis_index("tm"), 2) == 0
+    four = peers == 4
+    if four:
+        later = inner
     else:
         later = jnp.where(lax.axis_index("tm") % 2 == 0, inner, exchange(mult, next_pair))
-        wanted = lambda: lax.axis_index("tm") < peers - 1
     first, second = kernel_call(
-        lambda *refs: rims_body(wanted, *refs),
+        lambda *refs: rims_body(four, *refs),
         "rims",
         near(edge, later, high, low),
-        [lines(5), lines(5)],
+        [lines(6), lines(6)],
     )
     got_first = swap(first, "tile", 1)
     got_second = exchange(second, second_side)
@@ -537,10 +567,13 @@
     local, held = kernel_call(
         spread_body, "spread", near(incr, mult, rhs, err, cell, dual, valid), [field] * 2
     )
-    fix = kernel_call(
-        edges_body, "edges", near(first, second, got_first, got_second, edge), [lines(8)]
-    )[0]
-    if peers != 4:
+    fix, late = kernel_call(
+        lambda *refs: edges_body(four, *refs),
+        "edges",
+        near(first, second, got_first, got_second, edge),
+        [lines(8), lines(4)],
+    )
+    if not four:
         later = jnp.where(lax.axis_index("tm") == peers - 1, 0.0, later)
         back = kernel_call(adjoint_body, "adjoint", near(*coeffs, later), [field])[0]
         dir_obs, obs_sums = kernel_call(
@@ -552,8 +585,9 @@
         return scan_path(
             multiplier, increment, obs_dual, local, moved, held, back, fix, dir_obs, obs_sums
         )
-    cross = jnp.where(lax.axis_index("tm") < 2, moved, inner)
-    got_cross = leaders(jnp.pad(cross, ((0, 1), (0, 0), (0, 0))), 0, 2)
+    cross = jnp.where(lax.axis_index("tm") < 2, moved, inner).reshape(levels * rows, cols)
+    got_cross = leaders(jnp.pad(cross, ((0, rows), (0, 0))), 0, 2)
+    got_late = leaders(late, 0, 2)
     back = kernel_call(adjoint_body, "adjoint", near(*coeffs, inner), [field])[0]
     own, urgent = kernel_call(
         share_body,
@@ -562,44 +596,38 @@
         [((3, levels, rows, cols), "near"), field],
     )
     got = swap(urgent, "tm", 1)
+    send = kernel_call(sends_body, "sends", near(own, got), [field])[0]
+    send, own, cell = lax.optimization_barrier((send, own, cell))
+    got_send = leaders(send, 0, 2)
     dir_obs, obs_sums = kernel_call(
         gather_body,
         "gather",
         near(incr, cell, dual, want, var, valid),
         [(obs_dual.shape, "near"), ((2, *obs_dual.shape), "near")],
     )
-    got, obs_sums = lax.optimization_barrier((got, obs_sums))
-    send = kernel_call(
-        sends_body, "sends", near(own, got, fix), [((levels * rows + 4 * levels, cols), "near")]
+    parts = [-(-(2 * levels + 1) // 3)] * 2
+    parts.append(2 * levels + 1 - sum(parts))
+    rest = kernel_call(
+        rest_body, "rest", near(own, obs_sums), [((n, rows, cols), "near") for n in parts]
+    )
+    got_rest = [swap(x, "tm", 1) for x in rest]
+    late_fix = kernel_call(
+        lambda *refs: late_body(rows, *refs),
+        "late",
+        near(got_first, got_second, edge, got_cross, got_late),
+        [lines(4)],
+        weight=WEIGHT,
     )[0]
-    send, own = lax.optimization_barrier((send, own))
-    got_send = leaders(send, 0, 2)
-    rest, other = kernel_call(
-        rest_body, "rest", near(own, obs_sums), [((levels + 1, rows, cols), "near"), field]
-    )
-    got_rest, got_other = swap(rest, "tm", 1), swap(other, "tm", 1)
-    late_first, late_second = kernel_call(
-        late_rims_body, "late_rims", near(edge, got_cross), [lines(2), lines(2)], weight=WEIGHT
-    )
-    got_late_first = swap(late_first, "tile", 1)
-    got_late_second = exchange(late_second, second_side)
-    late_fix = kernel_call(
-        late_edges_body,
-        "late_edges",
-        near(late_first, late_second, got_late_first, got_late_second)
-        + near(got_first, got_second, edge),
-        [lines(4)],
-    )[0]
-    beyond = kernel_call(adjoint_body, "beyond", near(*coeffs, got_cross), [field])[0]
+    beyond = kernel_call(beyond_body, "beyond", near(*coeffs, got_cross), [field])[0]
     terms, known = kernel_call(
         terms_body,
         "terms",
-        near(got_cross, beyond, own, got, got_rest, got_other, late_fix),
+        near(got_cross, got_late, beyond, own, got, late_fix, *got_rest),
         [((4, levels, rows, cols), "near"), field],
     )
     pair = ((2, levels, rows, cols), "near")
     keep, give, sums = kernel_call(
-        dots_body, "dots", near(terms, got_send, got_rest, obs_sums), [pair, field, ((2, 128), "near")]
+        dots_body, "dots", near(terms, got_send, got_rest[-1], obs_sums), [pair, field, ((2, 128), "near")]
     )
     total = sums + leaders(sums, 0, 2) + leaders(sums, 1, 0) + leaders(sums, 1, 2)
     distance = 2

time: 31.1 us -> 30.7 us (0.987)
  starting transfers between devices: 15.6 us -> 14.5 us
  waiting for transfers between devices: 7.72 us -> 8.54 us
    ppermute x8, starting transfers between devices: 7.1 us -> 4.41 us  [swap(): lax.ppermute(value, axis, [(i, i ^ distance) for i in range(lax.axis_size...]
    ppermute x8, waiting for transfers between devices: 4.26 us -> 5.8 us  [exchange(): return lax.ppermute(value, ('groups', 'tile', 'tm'), pairs)]
    ppermute x8, starting transfers between devices: 8.51 us -> 10 us  [exchange(): return lax.ppermute(value, ('groups', 'tile', 'tm'), pairs)]
    ppermute x8, waiting for transfers between devices: 3.46 us -> 2.73 us  [swap(): lax.ppermute(value, axis, [(i, i ^ distance) for i in range(lax.axis_size...]
    pallas_call x15 -> x14, Pallas kernels: 6.04 us -> 5.93 us  [kernel_call(): pl.pallas_call(body, name=name, out_shape=out_shape, in_specs=in_specs, o...]
  transfers between devices with their start and end apart: 16 -> 16, of which waited for: 8 -> 10; matrix products, arithmetic and copies ran while one was open for 0% -> 0% of each run, Pallas kernels for 15% -> 15%
where the time goes in v5:
time: 30.7 us; the launch traced here: 30.4 us
  starting transfers between devices  14.5 us (47%)
  waiting for transfers between devices  8.54 us (28%)
  Pallas kernels  5.93 us (19%)
  between operations  1.41 us (5%)
    ppermute x8, starting transfers between devices, exchange(): return lax.ppermute(value, ('groups', 'tile', 'tm'), pairs)  10 us
    pallas_call x14, Pallas kernels, kernel_call(): pl.pallas_call(body, name=name, out_shape=out_shape, in_specs=in_specs, o...  5.93 us
    ppermute x8, waiting for transfers between devices, exchange(): return lax.ppermute(value, ('groups', 'tile', 'tm'), pairs)  5.8 us
    ppermute x8, starting transfers between devices, swap(): lax.ppermute(value, axis, [(i, i ^ distance) for i in range(lax.axis_size...  4.41 us
    ppermute x8, waiting for transfers between devices, swap(): lax.ppermute(value, axis, [(i, i ^ distance) for i in range(lax.axis_size...  2.73 us
  transfers between devices with their start and end apart: 16, of which 10 were waited for; matrix products, arithmetic and copies ran while one was open for 0% of the time, Pallas kernels for 15%

profile of v5, /device:TPU:0, one launch (start us, length us, event | category | flops | bytes accessed | tf_op | source)
XLA Modules:
  0.0 30.4 jit_solution(6131802092604419135)
XLA Ops:
  0.6 0.5 %collective-permute-start = (f32[8,16,512]{2,1,0:T(8,128)}, f32[8,16,512]{2,1,0:T(8,128)S(1)}, u32[]{:S(2)}, u32[]{:S(2)}) collective-permute-start(f32[8,16,512]{2,1,0:T(8,128)} %bitcast.19), channel_id=1, source_target_pairs={{0,1},{1,0},{2,3},{3,2},{4,5},{5,4},{6,7},{7,6},{8,9},{9,8},{10,11... | collective-permute-start | bytes 786440 | tf_op jit(solution)/shard_map/ppermute | solution.py:479
  1.2 1.9 %begin.1 = (f32[8,16,512]{2,1,0:T(8,128)S(1)}, f32[8,16,512]{2,1,0:T(8,128)S(1)}, f32[8,16,512]{2,1,0:T(8,128)S(1)}, f32[8,16,512]{2,1,0:T(8,128)S(1)}, f32[8,16...) custom-call(f32[8,16,512]{2,1,0:T(8,128)} %bitcast.13, ...), custom_call_target="tpu_custom_call" | custom-call | flops 1 | bytes 1 | tf_op jit(solution)/shard_map/begin/pallas_call | solution.py:32
  3.7 0.0 collective-permute-done.later_ref.refs_1_
  3.7 0.1 rims.1
  3.8 2.7 %collective-permute-start.1 = (f32[6,8,512]{2,1,0:T(8,128)S(1)}, f32[6,8,512]{2,1,0:T(8,128)S(1)}, u32[]{:S(2)}, u32[]{:S(2)}) collective-permute-start(f32[6,8,512]{2,1,0:T(8,128)S(1)} %get-tuple-element.59.refs_0_), channel_id=1, source_target_pairs={{0,4},{4,0},{8,12},{12,8},{1,5},{5,1},{9,13},{13,9},{2,6},{6,2},{1... | collective-permute-start | bytes 294920 | tf_op jit(solution)/shard_map/ppermute | solution.py:479
  6.5 0.2 collective-permute-start.2
  6.7 1.6 %collective-permute-start.4 = (f32[144,512]{1,0:T(8,128)S(1)}, f32[144,512]{1,0:T(8,128)S(1)}, u32[]{:S(2)}, u32[]{:S(2)}) collective-permute-start(f32[144,512]{1,0:T(8,128)S(1)} %pad.4), channel_id=1, source_target_pairs={{0,16},{1,3},{2,18},{3,1},{4,20},{5,7},{6,22},{7,5},{8,24},{9,11},... | collective-permute-start | bytes 884744 | tf_op jit(solution)/shard_map/ppermute | solution.py:475
  8.3 0.4 %spread.1 = (f32[8,16,512]{2,1,0:T(8,128)S(1)}, f32[8,16,512]{2,1,0:T(8,128)S(1)}) custom-call(f32[8,16,512]{2,1,0:T(8,128)S(1)} %get-tuple-element.45.incr_ref, f32[8,16,512]{2,1,0:T(8,128)S(1)} %get-tuple-element.44.mult_ref, f32[8,16,512]{2,1,0:T(8,128)S(1)} %get-tuple-element.47.rhs_ref, f32[8,16,512]{2,1,0:T(8,128)S(1)} %get-tuple-element.48.err_ref, ...), custom_call_target="tpu_custom_call" | custom-call | flops 1 | bytes 1 | tf_op jit(solution)/shard_map/spread/pallas_call | solution.py:32
  8.7 0.7 %adjoint.1.back_ref = f32[8,16,512]{2,1,0:T(8,128)S(1)} custom-call(f32[8,16,512]{2,1,0:T(8,128)S(1)} %get-tuple-element.53.a_ref, f32[8,16,512]{2,1,0:T(8,128)S(1)} %get-tuple-element.54.b_ref, f32[8,16,512]{2,1,0:T(8,128)S(1)} %get-tuple-element.55.c_ref, f32[8,16,512]{2,1,0:T(8,128)S(1)} %collective-permute-done.later_ref.refs_1_), custom_call_target="tpu_custom_call" | custom-call | flops 1 | bytes 1 | tf_op jit(solution)/shard_map/adjoint/pallas_call | solution.py:32
  9.4 0.5 %collective-permute-done.1.refs_2_.refs_0_ = f32[6,8,512]{2,1,0:T(8,128)S(1)} collective-permute-done((f32[6,8,512]{2,1,0:T(8,128)S(1)}, f32[6,8,512]{2,1,0:T(8,128)S(1)}, u32[]{:S(2)}, u32[]{:S(2)}) %collective-permute-start.1) | collective-permute-done | bytes 98336 | tf_op jit(solution)/shard_map/ppermute | solution.py:479
  9.9 0.0 collective-permute-done.2.refs_3_.refs_1_
  9.9 0.1 edges.1
  10.0 0.1 share.1
  10.2 0.1 collective-permute-start.3
  10.2 1.7 %collective-permute-start.5 = (f32[4,8,512]{2,1,0:T(8,128)S(1)}, f32[4,8,512]{2,1,0:T(8,128)S(1)}, u32[]{:S(2)}, u32[]{:S(2)}) collective-permute-start(f32[4,8,512]{2,1,0:T(8,128)S(1)} %get-tuple-element.68), channel_id=1, source_target_pairs={{0,16},{1,3},{2,18},{3,1},{4,20},{5,7},{6,22},{7,5},{8,24},{9,11},... | collective-permute-start | bytes 196616 | tf_op jit(solution)/shard_map/ppermute | solution.py:475
  12.0 0.0 collective-permute-done.3.got_ref
  12.0 1.5 %collective-permute-start.9 = (f32[8,16,512]{2,1,0:T(8,128)S(1)}, f32[8,16,512]{2,1,0:T(8,128)S(1)}, u32[]{:S(2)}, u32[]{:S(2)}) collective-permute-start(f32[8,16,512]{2,1,0:T(8,128)S(1)} %sends.1), channel_id=1, source_target_pairs={{0,16},{1,3},{2,18},{3,1},{4,20},{5,7},{6,22},{7,5},{8,24},{9,11},... | collective-permute-start | bytes 786440 | tf_op jit(solution)/shard_map/ppermute | solution.py:475
  13.6 0.0 collective-permute-done.4.cross_ref.refs_3_
  13.6 0.7 %beyond.1.beyond_ref = f32[8,16,512]{2,1,0:T(8,128)S(1)} custom-call(f32[8,16,512]{2,1,0:T(8,128)S(1)} %get-tuple-element.53.a_ref, f32[8,16,512]{2,1,0:T(8,128)S(1)} %get-tuple-element.54.b_ref, f32[8,16,512]{2,1,0:T(8,128)S(1)} %get-tuple-element.55.c_ref, f32[144,512]{1,0:T(8,128)S(1)} %collective-permute-done.4.cross_ref.refs_3_), custom_call_target="tpu_custom_call" | custom-call | flops 1 | bytes 1 | tf_op jit(solution)/shard_map/beyond/pallas_call | solution.py:32
  14.3 0.4 %gather.1 = (f32[1,512]{1,0:T(1,128)S(1)}, f32[2,1,512]{2,1,0:T(1,128)S(1)}) custom-call(f32[8,16,512]{2,1,0:T(8,128)S(1)} %get-tuple-element.45.incr_ref, s32[1,512]{1,0:T(1,128)S(1)} %get-tuple-element.64.cell_ref, f32[1,512]{1,0:T(1,128)S(1)} %get-tuple-element.46.dual_ref, f32[1,512]{1,0:T(1,128)S(1)} %get-tuple-element.65.want_ref, ...), custom_call_target="tpu_custom_call" | custom-call | flops 1 | bytes 1 | tf_op jit(solution)/shard_map/gather/pallas_call | solution.py:32
  14.7 0.1 rest.1
  14.7 0.1 collective-permute-start.8
  14.8 0.5 %collective-permute-start.6 = (f32[6,16,512]{2,1,0:T(8,128)S(1)}, f32[6,16,512]{2,1,0:T(8,128)S(1)}, u32[]{:S(2)}, u32[]{:S(2)}) collective-permute-start(f32[6,16,512]{2,1,0:T(8,128)S(1)} %get-tuple-element.71), channel_id=1, source_target_pairs={{0,1},{1,0},{2,3},{3,2},{4,5},{5,4},{6,7},{7,6},{8,9},{9,8},{10,11... | collective-permute-start | bytes 589832 | tf_op jit(solution)/shard_map/ppermute | solution.py:479
  15.3 0.1 collective-permute-start.7
  15.4 0.0 collective-permute-done.5.refs_4_.late_ref
  15.4 0.1 late.1.fix_ref
  15.5 0.7 %collective-permute-done.8.refs_2_.rest_ref = f32[5,16,512]{2,1,0:T(8,128)S(1)} collective-permute-done((f32[5,16,512]{2,1,0:T(8,128)S(1)}, f32[5,16,512]{2,1,0:T(8,128)S(1)}, u32[]{:S(2)}, u32[]{:S(2)}) %collective-permute-start.8) | collective-permute-done | bytes 163872 | tf_op jit(solution)/shard_map/ppermute | solution.py:479
  16.2 0.3 collective-permute-done.6.refs_0_
  16.5 0.3 collective-permute-done.7.refs_1_
  16.7 0.2 terms.1
  16.9 1.6 %collective-permute-done.9.got_ref = f32[8,16,512]{2,1,0:T(8,128)S(1)} collective-permute-done((f32[8,16,512]{2,1,0:T(8,128)S(1)}, f32[8,16,512]{2,1,0:T(8,128)S(1)}, u32[]{:S(2)}, u32[]{:S(2)}) %collective-permute-start.9) | collective-permute-done | bytes 262176 | tf_op jit(solution)/shard_map/ppermute | solution.py:475
  18.5 0.2 dots.1
  18.7 1.5 %collective-permute-start.12 = (f32[2,128]{1,0:T(2,128)S(1)}, f32[2,128]{1,0:T(2,128)S(1)}, u32[]{:S(2)}, u32[]{:S(2)}) collective-permute-start(f32[2,128]{1,0:T(2,128)S(1)} %get-tuple-element.79), channel_id=1, source_target_pairs={{0,16},{1,7},{2,18},{3,5},{4,20},{5,3},{6,22},{7,1},{8,24},{9,15},... | collective-permute-start | bytes 3080 | tf_op jit(solution)/shard_map/ppermute | solution.py:475
  20.2 0.6 %collective-permute-start.11 = (f32[2,128]{1,0:T(2,128)S(1)}, f32[2,128]{1,0:T(2,128)S(1)}, u32[]{:S(2)}, u32[]{:S(2)}) collective-permute-start(f32[2,128]{1,0:T(2,128)S(1)} %get-tuple-element.79), channel_id=1, source_target_pairs={{0,16},{1,5},{2,18},{3,7},{4,20},{5,1},{6,22},{7,3},{8,24},{9,13},... | collective-permute-start | bytes 3080 | tf_op jit(solution)/shard_map/ppermute | solution.py:475
  20.8 1.5 %collective-permute-start.10 = (f32[2,128]{1,0:T(2,128)S(1)}, f32[2,128]{1,0:T(2,128)S(1)}, u32[]{:S(2)}, u32[]{:S(2)}) collective-permute-start(f32[2,128]{1,0:T(2,128)S(1)} %get-tuple-element.79), channel_id=1, source_target_pairs={{0,16},{1,3},{2,18},{3,1},{4,20},{5,7},{6,22},{7,5},{8,24},{9,11},... | collective-permute-start | bytes 3080 | tf_op jit(solution)/shard_map/ppermute | solution.py:475
  22.2 0.1 collective-permute-done.12
  22.3 1.5 %collective-permute-done.11 = f32[2,128]{1,0:T(2,128)S(1)} collective-permute-done((f32[2,128]{1,0:T(2,128)S(1)}, f32[2,128]{1,0:T(2,128)S(1)}, u32[]{:S(2)}, u32[]{:S(2)}) %collective-permute-start.11) | collective-permute-done | bytes 1056 | tf_op jit(solution)/shard_map/ppermute | solution.py:475
  23.8 0.6 %collective-permute-done.10 = f32[2,128]{1,0:T(2,128)S(1)} collective-permute-done((f32[2,128]{1,0:T(2,128)S(1)}, f32[2,128]{1,0:T(2,128)S(1)}, u32[]{:S(2)}, u32[]{:S(2)}) %collective-permute-start.10) | collective-permute-done | bytes 1056 | tf_op jit(solution)/shard_map/ppermute | solution.py:475
  24.3 1.5 %collective-permute-start.13 = (f32[2,128]{1,0:T(2,128)S(1)}, f32[2,128]{1,0:T(2,128)S(1)}, u32[]{:S(2)}, u32[]{:S(2)}) collective-permute-start(f32[2,128]{1,0:T(2,128)S(1)} %add_add_fusion), channel_id=1, source_target_pairs={{0,16},{1,9},{2,18},{3,11},{4,20},{5,13},{6,22},{7,15},{8,24},{9,1... | collective-permute-start | bytes 3080 | tf_op jit(solution)/shard_map/ppermute | solution.py:475
  25.8 2.1 %collective-permute-done.13 = f32[2,128]{1,0:T(2,128)S(1)} collective-permute-done((f32[2,128]{1,0:T(2,128)S(1)}, f32[2,128]{1,0:T(2,128)S(1)}, u32[]{:S(2)}, u32[]{:S(2)}) %collective-permute-start.13) | collective-permute-done | bytes 1056 | tf_op jit(solution)/shard_map/ppermute | solution.py:475
  27.9 0.0 collective-permute-start.14
  27.9 0.5 %collective-permute-start.15 = (f32[2,128]{1,0:T(2,128)S(1)}, f32[2,128]{1,0:T(2,128)S(1)}, u32[]{:S(2)}, u32[]{:S(2)}) collective-permute-start(f32[2,128]{1,0:T(2,128)S(1)} %add.21), channel_id=1, source_target_pairs={{0,1},{1,0},{2,3},{3,2},{4,5},{5,4},{6,7},{7,6},{8,9},{9,8},{10,11... | collective-permute-start | bytes 3080 | tf_op jit(solution)/shard_map/ppermute | solution.py:479
  28.4 1.0 %collective-permute-done.15 = f32[2,128]{1,0:T(2,128)S(1)} collective-permute-done((f32[2,128]{1,0:T(2,128)S(1)}, f32[2,128]{1,0:T(2,128)S(1)}, u32[]{:S(2)}, u32[]{:S(2)}) %collective-permute-start.15) | collective-permute-done | bytes 1056 | tf_op jit(solution)/shard_map/ppermute | solution.py:479
  29.5 0.0 collective-permute-done.14.got_ref
  29.5 1.0 %update.1 = (f32[8,16,512]{2,1,0:T(8,128)}, f32[8,16,512]{2,1,0:T(8,128)}, f32[1,512]{1,0:T(1,128)}) custom-call(f32[8,16,512]{2,1,0:T(8,128)S(1)} %get-tuple-element.44.mult_ref, f32[8,16,512]{2,1,0:T(8,128)S(1)} %get-tuple-element.45.incr_ref, f32[1,512]{1,0:T(1,128)S(1)} %get-tuple-element.46.dual_ref, f32[1,512]{1,0:T(1,128)S(1)} %get-tuple-element.67.dir_ref, ...), custom_call_target="tpu_custom_call" | custom-call | flops 1 | bytes 1 | tf_op jit(solution)/shard_map/update/pallas_call | solution.py:32
  (7 shorter events, 0.1 us)
Async XLA Ops:
  0.6 3.0 %collective-permute-start = (f32[8,16,512]{2,1,0:T(8,128)}, f32[8,16,512]{2,1,0:T(8,128)S(1)}, u32[]{:S(2)}, u32[]{:S(2)}) collective-permute-start(f32[8,16,512]{2,1,0:T(8,128)} %bitcast.19), channel_id=1, source_target_pairs={{0,1},{1,0},{2,3},{3,2},{4,5},{5,4},{6,7},{7,6},{8,9},{9,8},{10,11... | collective-permute-start | bytes 786440 | tf_op jit(solution)/shard_map/ppermute | solution.py:479
  3.8 6.1 %collective-permute-start.1 = (f32[6,8,512]{2,1,0:T(8,128)S(1)}, f32[6,8,512]{2,1,0:T(8,128)S(1)}, u32[]{:S(2)}, u32[]{:S(2)}) collective-permute-start(f32[6,8,512]{2,1,0:T(8,128)S(1)} %get-tuple-element.59.refs_0_), channel_id=1, source_target_pairs={{0,4},{4,0},{8,12},{12,8},{1,5},{5,1},{9,13},{13,9},{2,6},{6,2},{1... | collective-permute-start | bytes 294920 | tf_op jit(solution)/shard_map/ppermute | solution.py:479
  6.5 3.4 %collective-permute-start.2 = (f32[6,8,512]{2,1,0:T(8,128)S(1)}, f32[6,8,512]{2,1,0:T(8,128)S(1)}, u32[]{:S(2)}, u32[]{:S(2)}) collective-permute-start(f32[6,8,512]{2,1,0:T(8,128)S(1)} %get-tuple-element.60.refs_1_), channel_id=1, source_target_pairs={{0,1},{1,0},{2,3},{3,2},{4,8},{5,9},{6,10},{7,11},{8,4},{9,5},{10,... | collective-permute-start | bytes 294920 | tf_op jit(solution)/shard_map/ppermute | solution.py:475
  6.7 6.8 %collective-permute-start.4 = (f32[144,512]{1,0:T(8,128)S(1)}, f32[144,512]{1,0:T(8,128)S(1)}, u32[]{:S(2)}, u32[]{:S(2)}) collective-permute-start(f32[144,512]{1,0:T(8,128)S(1)} %pad.4), channel_id=1, source_target_pairs={{0,16},{1,3},{2,18},{3,1},{4,20},{5,7},{6,22},{7,5},{8,24},{9,11},... | collective-permute-start | bytes 884744 | tf_op jit(solution)/shard_map/ppermute | solution.py:475
  10.2 1.8 %collective-permute-start.3 = (f32[8,16,512]{2,1,0:T(8,128)S(1)}, f32[8,16,512]{2,1,0:T(8,128)S(1)}, u32[]{:S(2)}, u32[]{:S(2)}) collective-permute-start(f32[8,16,512]{2,1,0:T(8,128)S(1)} %get-tuple-element.63), channel_id=1, source_target_pairs={{0,1},{1,0},{2,3},{3,2},{4,5},{5,4},{6,7},{7,6},{8,9},{9,8},{10,11... | collective-permute-start | bytes 786440 | tf_op jit(solution)/shard_map/ppermute | solution.py:479
  10.2 5.1 %collective-permute-start.5 = (f32[4,8,512]{2,1,0:T(8,128)S(1)}, f32[4,8,512]{2,1,0:T(8,128)S(1)}, u32[]{:S(2)}, u32[]{:S(2)}) collective-permute-start(f32[4,8,512]{2,1,0:T(8,128)S(1)} %get-tuple-element.68), channel_id=1, source_target_pairs={{0,16},{1,3},{2,18},{3,1},{4,20},{5,7},{6,22},{7,5},{8,24},{9,11},... | collective-permute-start | bytes 196616 | tf_op jit(solution)/shard_map/ppermute | solution.py:475
  12.0 6.4 %collective-permute-start.9 = (f32[8,16,512]{2,1,0:T(8,128)S(1)}, f32[8,16,512]{2,1,0:T(8,128)S(1)}, u32[]{:S(2)}, u32[]{:S(2)}) collective-permute-start(f32[8,16,512]{2,1,0:T(8,128)S(1)} %sends.1), channel_id=1, source_target_pairs={{0,16},{1,3},{2,18},{3,1},{4,20},{5,7},{6,22},{7,5},{8,24},{9,11},... | collective-permute-start | bytes 786440 | tf_op jit(solution)/shard_map/ppermute | solution.py:475
  14.7 1.5 %collective-permute-start.8 = (f32[5,16,512]{2,1,0:T(8,128)S(1)}, f32[5,16,512]{2,1,0:T(8,128)S(1)}, u32[]{:S(2)}, u32[]{:S(2)}) collective-permute-start(f32[5,16,512]{2,1,0:T(8,128)S(1)} %get-tuple-element.73), channel_id=1, source_target_pairs={{0,1},{1,0},{2,3},{3,2},{4,5},{5,4},{6,7},{7,6},{8,9},{9,8},{10,11... | collective-permute-start | bytes 491528 | tf_op jit(solution)/shard_map/ppermute | solution.py:479
  14.8 1.7 %collective-permute-start.6 = (f32[6,16,512]{2,1,0:T(8,128)S(1)}, f32[6,16,512]{2,1,0:T(8,128)S(1)}, u32[]{:S(2)}, u32[]{:S(2)}) collective-permute-start(f32[6,16,512]{2,1,0:T(8,128)S(1)} %get-tuple-element.71), channel_id=1, source_target_pairs={{0,1},{1,0},{2,3},{3,2},{4,5},{5,4},{6,7},{7,6},{8,9},{9,8},{10,11... | collective-permute-start | bytes 589832 | tf_op jit(solution)/shard_map/ppermute | solution.py:479
  15.3 1.4 %collective-permute-start.7 = (f32[6,16,512]{2,1,0:T(8,128)S(1)}, f32[6,16,512]{2,1,0:T(8,128)S(1)}, u32[]{:S(2)}, u32[]{:S(2)}) collective-permute-start(f32[6,16,512]{2,1,0:T(8,128)S(1)} %get-tuple-element.72), channel_id=1, source_target_pairs={{0,1},{1,0},{2,3},{3,2},{4,5},{5,4},{6,7},{7,6},{8,9},{9,8},{10,11... | collective-permute-start | bytes 589832 | tf_op jit(solution)/shard_map/ppermute | solution.py:479
  18.7 3.6 %collective-permute-start.12 = (f32[2,128]{1,0:T(2,128)S(1)}, f32[2,128]{1,0:T(2,128)S(1)}, u32[]{:S(2)}, u32[]{:S(2)}) collective-permute-start(f32[2,128]{1,0:T(2,128)S(1)} %get-tuple-element.79), channel_id=1, source_target_pairs={{0,16},{1,7},{2,18},{3,5},{4,20},{5,3},{6,22},{7,1},{8,24},{9,15},... | collective-permute-start | bytes 3080 | tf_op jit(solution)/shard_map/ppermute | solution.py:475
  20.2 3.6 %collective-permute-start.11 = (f32[2,128]{1,0:T(2,128)S(1)}, f32[2,128]{1,0:T(2,128)S(1)}, u32[]{:S(2)}, u32[]{:S(2)}) collective-permute-start(f32[2,128]{1,0:T(2,128)S(1)} %get-tuple-element.79), channel_id=1, source_target_pairs={{0,16},{1,5},{2,18},{3,7},{4,20},{5,1},{6,22},{7,3},{8,24},{9,13},... | collective-permute-start | bytes 3080 | tf_op jit(solution)/shard_map/ppermute | solution.py:475
  20.8 3.6 %collective-permute-start.10 = (f32[2,128]{1,0:T(2,128)S(1)}, f32[2,128]{1,0:T(2,128)S(1)}, u32[]{:S(2)}, u32[]{:S(2)}) collective-permute-start(f32[2,128]{1,0:T(2,128)S(1)} %get-tuple-element.79), channel_id=1, source_target_pairs={{0,16},{1,3},{2,18},{3,1},{4,20},{5,7},{6,22},{7,5},{8,24},{9,11},... | collective-permute-start | bytes 3080 | tf_op jit(solution)/shard_map/ppermute | solution.py:475
  24.3 3.6 %collective-permute-start.13 = (f32[2,128]{1,0:T(2,128)S(1)}, f32[2,128]{1,0:T(2,128)S(1)}, u32[]{:S(2)}, u32[]{:S(2)}) collective-permute-start(f32[2,128]{1,0:T(2,128)S(1)} %add_add_fusion), channel_id=1, source_target_pairs={{0,16},{1,9},{2,18},{3,11},{4,20},{5,13},{6,22},{7,15},{8,24},{9,1... | collective-permute-start | bytes 3080 | tf_op jit(solution)/shard_map/ppermute | solution.py:475
  27.9 1.5 %collective-permute-start.14 = (f32[8,16,512]{2,1,0:T(8,128)S(1)}, f32[8,16,512]{2,1,0:T(8,128)S(1)}, u32[]{:S(2)}, u32[]{:S(2)}) collective-permute-start(f32[8,16,512]{2,1,0:T(8,128)S(1)} %get-tuple-element.80), channel_id=1, source_target_pairs={{0,1},{1,0},{2,3},{3,2},{4,5},{5,4},{6,7},{7,6},{8,9},{9,8},{10,11... | collective-permute-start | bytes 786440 | tf_op jit(solution)/shard_map/ppermute | solution.py:479
  27.9 1.5 %collective-permute-start.15 = (f32[2,128]{1,0:T(2,128)S(1)}, f32[2,128]{1,0:T(2,128)S(1)}, u32[]{:S(2)}, u32[]{:S(2)}) collective-permute-start(f32[2,128]{1,0:T(2,128)S(1)} %add.21), channel_id=1, source_target_pairs={{0,1},{1,0},{2,3},{3,2},{4,5},{5,4},{6,7},{7,6},{8,9},{9,8},{10,11... | collective-permute-start | bytes 3080 | tf_op jit(solution)/shard_map/ppermute | solution.py:479

commit v6 on v5

--- a/solution.py
+++ b/solution.py
@@ -240,17 +240,13 @@
     )
 
 
-def edges_body(
-    four, first_ref, second_ref, got_first_ref, got_second_ref, edge_ref, fix_ref, late_ref
-):
-    position, peers = lax.axis_index("tm"), lax.axis_size("tm")
+def edges_of(first_ref, second_ref, got_first_ref, got_second_ref, edge_ref):
     k = {key: edge_ref[n] for n, key in enumerate(EDGE)}
     state, stepped, toward, product, product_stepped = (
         sides(got_first_ref[n], got_second_ref[n]) for n in range(5)
     )
     own_state = own_sides(first_ref[0], second_ref[0])
     own_product = own_sides(first_ref[3], second_ref[3])
-    wanted = lax.rem(position, 2) == 0 if four else position < peers - 1
 
     def along(x, side):
         mid, north, south = k["mid_" + side], k["north_" + side], k["south_" + side]
@@ -264,11 +260,16 @@
         along(new_high, "high") + k["east_high"] * (stepped[1] + toward[1] * own_state[1]),
     )
     back = back_fix(k, product, product_stepped, own_product, toward)
-    beyond = (state[0], stepped[0], state[1], stepped[1])
+    return moved, back, (state[0], stepped[0], state[1], stepped[1])
+
+
+def edges_body(*refs):
+    *in_refs, fix_ref = refs
+    moved, back, _ = edges_of(*in_refs)
+    wanted = lax.axis_index("tm") < lax.axis_size("tm") - 1
     for n in range(4):
         fix_ref[n] = moved[n]
         fix_ref[4 + n] = jnp.where(wanted, back[n], 0.0)
-        late_ref[n] = jnp.where(position < peers // 2, moved[n], beyond[n])
 
 
 def late_body(rows, got_first_ref, got_second_ref, edge_ref, cross_ref, late_ref, fix_ref):
@@ -366,12 +367,20 @@
     return [-x for x in rows]
 
 
-def share_body(local_ref, moved_ref, held_ref, back_ref, fix_ref, own_ref, urgent_ref):
+def share_body(
+    first_ref, second_ref, got_first_ref, got_second_ref, edge_ref,
+    local_ref, moved_ref, held_ref, back_ref, own_ref, urgent_ref, late_ref,
+):
     position = lax.axis_index("tm")
     first, low_pair = lax.rem(position, 2) == 0, position < 2
+    fix_moved, fix_back, beyond = edges_of(
+        first_ref, second_ref, got_first_ref, got_second_ref, edge_ref
+    )
+    for n in range(4):
+        late_ref[n] = jnp.where(low_pair, fix_moved[n], beyond[n])
     for lev in range(local_ref.shape[0]):
-        back = corrected(back_ref[lev], fixes(fix_ref, 4, lev))
-        moved = corrected(moved_ref[lev], fixes(fix_ref, 0, lev))
+        back = corrected(back_ref[lev], [x[lev : lev + 1] for x in fix_back])
+        moved = corrected(moved_ref[lev], [x[lev : lev + 1] for x in fix_moved])
         local = local_ref[lev]
         residual = held_ref[lev] - jnp.where(first, back, 0.0)
         own_ref[0, lev] = local
@@ -567,13 +576,9 @@
     local, held = kernel_call(
         spread_body, "spread", near(incr, mult, rhs, err, cell, dual, valid), [field] * 2
     )
-    fix, late = kernel_call(
-        lambda *refs: edges_body(four, *refs),
-        "edges",
-        near(first, second, got_first, got_second, edge),
-        [lines(8), lines(4)],
-    )
+    rims = near(first, second, got_first, got_second, edge)
     if not four:
+        fix = kernel_call(edges_body, "edges", rims, [lines(8)])[0]
         later = jnp.where(lax.axis_index("tm") == peers - 1, 0.0, later)
         back = kernel_call(adjoint_body, "adjoint", near(*coeffs, later), [field])[0]
         dir_obs, obs_sums = kernel_call(
@@ -587,14 +592,14 @@
         )
     cross = jnp.where(lax.axis_index("tm") < 2, moved, inner).reshape(levels * rows, cols)
     got_cross = leaders(jnp.pad(cross, ((0, rows), (0, 0))), 0, 2)
-    got_late = leaders(late, 0, 2)
     back = kernel_call(adjoint_body, "adjoint", near(*coeffs, inner), [field])[0]
-    own, urgent = kernel_call(
+    own, urgent, late = kernel_call(
         share_body,
         "share",
-        near(local, moved, held, back, fix),
-        [((3, levels, rows, cols), "near"), field],
-    )
+        rims + near(local, moved, held, back),
+        [((3, levels, rows, cols), "near"), field, lines(4)],
+    )
+    got_late = leaders(late, 0, 2)
     got = swap(urgent, "tm", 1)
     send = kernel_call(sends_body, "sends", near(own, got), [field])[0]
     send, own, cell = lax.optimization_barrier((send, own, cell))
@@ -634,7 +639,6 @@
     while distance < tiles:
         total = total + leaders(total, distance, 0)
         distance *= 2
-    give, total = lax.optimization_barrier((give, total))
     got_dir = swap(give, "tm", 1)
     other = swap(total, "tm", 1)
     total = jnp.where(lax.axis_index("tm") % 2 == 1, total, other)

time: 30.7 us -> 30.4 us (level)
  starting transfers between devices: 14.5 us -> 14 us
    ppermute x8, starting transfers between devices: 4.41 us -> 3.91 us  [swap(): lax.ppermute(value, axis, [(i, i ^ distance) for i in range(lax.axis_size...]
    pallas_call x14 -> x13, Pallas kernels: 5.93 us -> 5.92 us  [kernel_call(): pl.pallas_call(body, name=name, out_shape=out_shape, in_specs=in_specs, o...]
  transfers between devices with their start and end apart: 16 -> 16, of which waited for: 10 -> 10; matrix products, arithmetic and copies ran while one was open for 0% -> 0% of each run, Pallas kernels for 15% -> 16%
where the time goes in v6:
time: 30.4 us; the launch traced here: 30 us
  starting transfers between devices  14 us (46%)
  waiting for transfers between devices  8.65 us (28%)
  Pallas kernels  5.92 us (19%)
  between operations  1.41 us (5%)
    ppermute x8, starting transfers between devices, exchange(): return lax.ppermute(value, ('groups', 'tile', 'tm'), pairs)  10 us
    pallas_call x13, Pallas kernels, kernel_call(): pl.pallas_call(body, name=name, out_shape=out_shape, in_specs=in_specs, o...  5.92 us
    ppermute x8, waiting for transfers between devices, exchange(): return lax.ppermute(value, ('groups', 'tile', 'tm'), pairs)  5.8 us
    ppermute x8, starting transfers between devices, swap(): lax.ppermute(value, axis, [(i, i ^ distance) for i in range(lax.axis_size...  3.91 us
    ppermute x8, waiting for transfers between devices, swap(): lax.ppermute(value, axis, [(i, i ^ distance) for i in range(lax.axis_size...  2.84 us
  transfers between devices with their start and end apart: 16, of which 10 were waited for; matrix products, arithmetic and copies ran while one was open for 0% of the time, Pallas kernels for 16%

profile of v6, /device:TPU:0, one launch (start us, length us, event | category | flops | bytes accessed | tf_op | source)
XLA Modules:
  0.0 30.0 jit_solution(5432733951354636526)
XLA Ops:
  0.6 0.5 %collective-permute-start = (f32[8,16,512]{2,1,0:T(8,128)}, f32[8,16,512]{2,1,0:T(8,128)S(1)}, u32[]{:S(2)}, u32[]{:S(2)}) collective-permute-start(f32[8,16,512]{2,1,0:T(8,128)} %bitcast.19), channel_id=1, source_target_pairs={{0,1},{1,0},{2,3},{3,2},{4,5},{5,4},{6,7},{7,6},{8,9},{9,8},{10,11... | collective-permute-start | bytes 786440 | tf_op jit(solution)/shard_map/ppermute | solution.py:488
  1.2 1.9 %begin.1 = (f32[8,16,512]{2,1,0:T(8,128)S(1)}, f32[8,16,512]{2,1,0:T(8,128)S(1)}, f32[8,16,512]{2,1,0:T(8,128)S(1)}, f32[8,16,512]{2,1,0:T(8,128)S(1)}, f32[8,16...) custom-call(f32[8,16,512]{2,1,0:T(8,128)} %bitcast.13, ...), custom_call_target="tpu_custom_call" | custom-call | flops 1 | bytes 1 | tf_op jit(solution)/shard_map/begin/pallas_call | solution.py:32
  3.7 0.0 collective-permute-done.refs_1_.later_ref
  3.7 0.1 rims.1
  3.8 2.7 %collective-permute-start.1 = (f32[6,8,512]{2,1,0:T(8,128)S(1)}, f32[6,8,512]{2,1,0:T(8,128)S(1)}, u32[]{:S(2)}, u32[]{:S(2)}) collective-permute-start(f32[6,8,512]{2,1,0:T(8,128)S(1)} %get-tuple-element.47.first_ref), channel_id=1, source_target_pairs={{0,4},{4,0},{8,12},{12,8},{1,5},{5,1},{9,13},{13,9},{2,6},{6,2},{1... | collective-permute-start | bytes 294920 | tf_op jit(solution)/shard_map/ppermute | solution.py:488
  6.5 0.2 collective-permute-start.2
  6.7 1.6 %collective-permute-start.4 = (f32[144,512]{1,0:T(8,128)S(1)}, f32[144,512]{1,0:T(8,128)S(1)}, u32[]{:S(2)}, u32[]{:S(2)}) collective-permute-start(f32[144,512]{1,0:T(8,128)S(1)} %pad.4), channel_id=1, source_target_pairs={{0,16},{1,3},{2,18},{3,1},{4,20},{5,7},{6,22},{7,5},{8,24},{9,11},... | collective-permute-start | bytes 884744 | tf_op jit(solution)/shard_map/ppermute | solution.py:484
  8.3 0.4 %spread.1 = (f32[8,16,512]{2,1,0:T(8,128)S(1)}, f32[8,16,512]{2,1,0:T(8,128)S(1)}) custom-call(f32[8,16,512]{2,1,0:T(8,128)S(1)} %get-tuple-element.42.incr_ref, f32[8,16,512]{2,1,0:T(8,128)S(1)} %get-tuple-element.41.mult_ref, f32[8,16,512]{2,1,0:T(8,128)S(1)} %get-tuple-element.49.rhs_ref, f32[8,16,512]{2,1,0:T(8,128)S(1)} %get-tuple-element.50.err_ref, ...), custom_call_target="tpu_custom_call" | custom-call | flops 1 | bytes 1 | tf_op jit(solution)/shard_map/spread/pallas_call | solution.py:32
  8.7 0.7 %adjoint.1.back_ref = f32[8,16,512]{2,1,0:T(8,128)S(1)} custom-call(f32[8,16,512]{2,1,0:T(8,128)S(1)} %get-tuple-element.55.a_ref, f32[8,16,512]{2,1,0:T(8,128)S(1)} %get-tuple-element.56.b_ref, f32[8,16,512]{2,1,0:T(8,128)S(1)} %get-tuple-element.57.c_ref, f32[8,16,512]{2,1,0:T(8,128)S(1)} %collective-permute-done.refs_1_.later_ref), custom_call_target="tpu_custom_call" | custom-call | flops 1 | bytes 1 | tf_op jit(solution)/shard_map/adjoint/pallas_call | solution.py:32
  9.4 0.5 %collective-permute-done.1.got_first_ref.refs_0_ = f32[6,8,512]{2,1,0:T(8,128)S(1)} collective-permute-done((f32[6,8,512]{2,1,0:T(8,128)S(1)}, f32[6,8,512]{2,1,0:T(8,128)S(1)}, u32[]{:S(2)}, u32[]{:S(2)}) %collective-permute-start.1) | collective-permute-done | bytes 98336 | tf_op jit(solution)/shard_map/ppermute | solution.py:488
  9.9 0.0 collective-permute-done.2.got_second_ref.refs_1_
  9.9 0.2 share.1
  10.2 0.1 collective-permute-start.3
  10.2 1.7 %collective-permute-start.5 = (f32[4,8,512]{2,1,0:T(8,128)S(1)}, f32[4,8,512]{2,1,0:T(8,128)S(1)}, u32[]{:S(2)}, u32[]{:S(2)}) collective-permute-start(f32[4,8,512]{2,1,0:T(8,128)S(1)} %get-tuple-element.64), channel_id=1, source_target_pairs={{0,16},{1,3},{2,18},{3,1},{4,20},{5,7},{6,22},{7,5},{8,24},{9,11},... | collective-permute-start | bytes 196616 | tf_op jit(solution)/shard_map/ppermute | solution.py:484
  12.0 0.0 collective-permute-done.3.got_ref
  12.0 1.5 %collective-permute-start.9 = (f32[8,16,512]{2,1,0:T(8,128)S(1)}, f32[8,16,512]{2,1,0:T(8,128)S(1)}, u32[]{:S(2)}, u32[]{:S(2)}) collective-permute-start(f32[8,16,512]{2,1,0:T(8,128)S(1)} %sends.1), channel_id=1, source_target_pairs={{0,16},{1,3},{2,18},{3,1},{4,20},{5,7},{6,22},{7,5},{8,24},{9,11},... | collective-permute-start | bytes 786440 | tf_op jit(solution)/shard_map/ppermute | solution.py:484
  13.5 0.0 collective-permute-done.4.cross_ref.refs_3_
  13.6 0.7 %beyond.1.beyond_ref = f32[8,16,512]{2,1,0:T(8,128)S(1)} custom-call(f32[8,16,512]{2,1,0:T(8,128)S(1)} %get-tuple-element.55.a_ref, f32[8,16,512]{2,1,0:T(8,128)S(1)} %get-tuple-element.56.b_ref, f32[8,16,512]{2,1,0:T(8,128)S(1)} %get-tuple-element.57.c_ref, f32[144,512]{1,0:T(8,128)S(1)} %collective-permute-done.4.cross_ref.refs_3_), custom_call_target="tpu_custom_call" | custom-call | flops 1 | bytes 1 | tf_op jit(solution)/shard_map/beyond/pallas_call | solution.py:32
  14.3 0.4 %gather.1 = (f32[1,512]{1,0:T(1,128)S(1)}, f32[2,1,512]{2,1,0:T(1,128)S(1)}) custom-call(f32[8,16,512]{2,1,0:T(8,128)S(1)} %get-tuple-element.42.incr_ref, s32[1,512]{1,0:T(1,128)S(1)} %get-tuple-element.60.cell_ref, f32[1,512]{1,0:T(1,128)S(1)} %get-tuple-element.43.dual_ref, f32[1,512]{1,0:T(1,128)S(1)} %get-tuple-element.61.want_ref, ...), custom_call_target="tpu_custom_call" | custom-call | flops 1 | bytes 1 | tf_op jit(solution)/shard_map/gather/pallas_call | solution.py:32
  14.7 0.1 rest.1
  14.7 0.1 collective-permute-start.8
  14.8 0.5 %collective-permute-start.6 = (f32[6,16,512]{2,1,0:T(8,128)S(1)}, f32[6,16,512]{2,1,0:T(8,128)S(1)}, u32[]{:S(2)}, u32[]{:S(2)}) collective-permute-start(f32[6,16,512]{2,1,0:T(8,128)S(1)} %get-tuple-element.67), channel_id=1, source_target_pairs={{0,1},{1,0},{2,3},{3,2},{4,5},{5,4},{6,7},{7,6},{8,9},{9,8},{10,11... | collective-permute-start | bytes 589832 | tf_op jit(solution)/shard_map/ppermute | solution.py:488
  15.3 0.1 collective-permute-start.7
  15.4 0.0 collective-permute-done.5.refs_4_.late_ref
  15.4 0.1 late.1.fix_ref
  15.5 0.7 %collective-permute-done.8.refs_2_.rest_ref = f32[5,16,512]{2,1,0:T(8,128)S(1)} collective-permute-done((f32[5,16,512]{2,1,0:T(8,128)S(1)}, f32[5,16,512]{2,1,0:T(8,128)S(1)}, u32[]{:S(2)}, u32[]{:S(2)}) %collective-permute-start.8) | collective-permute-done | bytes 163872 | tf_op jit(solution)/shard_map/ppermute | solution.py:488
  16.2 0.3 collective-permute-done.6.refs_0_
  16.5 0.3 collective-permute-done.7.refs_1_
  16.7 0.2 terms.1
  16.9 1.6 %collective-permute-done.9.got_ref = f32[8,16,512]{2,1,0:T(8,128)S(1)} collective-permute-done((f32[8,16,512]{2,1,0:T(8,128)S(1)}, f32[8,16,512]{2,1,0:T(8,128)S(1)}, u32[]{:S(2)}, u32[]{:S(2)}) %collective-permute-start.9) | collective-permute-done | bytes 262176 | tf_op jit(solution)/shard_map/ppermute | solution.py:484
  18.5 0.2 dots.1
  18.7 1.5 %collective-permute-start.13 = (f32[2,128]{1,0:T(2,128)S(1)}, f32[2,128]{1,0:T(2,128)S(1)}, u32[]{:S(2)}, u32[]{:S(2)}) collective-permute-start(f32[2,128]{1,0:T(2,128)S(1)} %get-tuple-element.75), channel_id=1, source_target_pairs={{0,16},{1,7},{2,18},{3,5},{4,20},{5,3},{6,22},{7,1},{8,24},{9,15},... | collective-permute-start | bytes 3080 | tf_op jit(solution)/shard_map/ppermute | solution.py:484
  20.2 0.6 %collective-permute-start.12 = (f32[2,128]{1,0:T(2,128)S(1)}, f32[2,128]{1,0:T(2,128)S(1)}, u32[]{:S(2)}, u32[]{:S(2)}) collective-permute-start(f32[2,128]{1,0:T(2,128)S(1)} %get-tuple-element.75), channel_id=1, source_target_pairs={{0,16},{1,5},{2,18},{3,7},{4,20},{5,1},{6,22},{7,3},{8,24},{9,13},... | collective-permute-start | bytes 3080 | tf_op jit(solution)/shard_map/ppermute | solution.py:484
  20.8 1.5 %collective-permute-start.11 = (f32[2,128]{1,0:T(2,128)S(1)}, f32[2,128]{1,0:T(2,128)S(1)}, u32[]{:S(2)}, u32[]{:S(2)}) collective-permute-start(f32[2,128]{1,0:T(2,128)S(1)} %get-tuple-element.75), channel_id=1, source_target_pairs={{0,16},{1,3},{2,18},{3,1},{4,20},{5,7},{6,22},{7,5},{8,24},{9,11},... | collective-permute-start | bytes 3080 | tf_op jit(solution)/shard_map/ppermute | solution.py:484
  22.2 0.0 collective-permute-start.10
  22.2 0.1 collective-permute-done.13
  22.3 1.5 %collective-permute-done.12 = f32[2,128]{1,0:T(2,128)S(1)} collective-permute-done((f32[2,128]{1,0:T(2,128)S(1)}, f32[2,128]{1,0:T(2,128)S(1)}, u32[]{:S(2)}, u32[]{:S(2)}) %collective-permute-start.12) | collective-permute-done | bytes 1056 | tf_op jit(solution)/shard_map/ppermute | solution.py:484
  23.8 0.6 %collective-permute-done.11 = f32[2,128]{1,0:T(2,128)S(1)} collective-permute-done((f32[2,128]{1,0:T(2,128)S(1)}, f32[2,128]{1,0:T(2,128)S(1)}, u32[]{:S(2)}, u32[]{:S(2)}) %collective-permute-start.11) | collective-permute-done | bytes 1056 | tf_op jit(solution)/shard_map/ppermute | solution.py:484
  24.3 1.5 %collective-permute-start.14 = (f32[2,128]{1,0:T(2,128)S(1)}, f32[2,128]{1,0:T(2,128)S(1)}, u32[]{:S(2)}, u32[]{:S(2)}) collective-permute-start(f32[2,128]{1,0:T(2,128)S(1)} %add_add_fusion), channel_id=1, source_target_pairs={{0,16},{1,9},{2,18},{3,11},{4,20},{5,13},{6,22},{7,15},{8,24},{9,1... | collective-permute-start | bytes 3080 | tf_op jit(solution)/shard_map/ppermute | solution.py:484
  25.8 2.1 %collective-permute-done.14 = f32[2,128]{1,0:T(2,128)S(1)} collective-permute-done((f32[2,128]{1,0:T(2,128)S(1)}, f32[2,128]{1,0:T(2,128)S(1)}, u32[]{:S(2)}, u32[]{:S(2)}) %collective-permute-start.14) | collective-permute-done | bytes 1056 | tf_op jit(solution)/shard_map/ppermute | solution.py:484
  27.9 0.0 collective-permute-start.15
  27.9 1.1 %collective-permute-done.15 = f32[2,128]{1,0:T(2,128)S(1)} collective-permute-done((f32[2,128]{1,0:T(2,128)S(1)}, f32[2,128]{1,0:T(2,128)S(1)}, u32[]{:S(2)}, u32[]{:S(2)}) %collective-permute-start.15) | collective-permute-done | bytes 1056 | tf_op jit(solution)/shard_map/ppermute | solution.py:488
  29.1 0.0 collective-permute-done.10.got_ref
  29.1 1.0 %update.1 = (f32[8,16,512]{2,1,0:T(8,128)}, f32[8,16,512]{2,1,0:T(8,128)}, f32[1,512]{1,0:T(1,128)}) custom-call(f32[8,16,512]{2,1,0:T(8,128)S(1)} %get-tuple-element.41.mult_ref, f32[8,16,512]{2,1,0:T(8,128)S(1)} %get-tuple-element.42.incr_ref, f32[1,512]{1,0:T(1,128)S(1)} %get-tuple-element.43.dual_ref, f32[1,512]{1,0:T(1,128)S(1)} %get-tuple-element.63.dir_ref, ...), custom_call_target="tpu_custom_call" | custom-call | flops 1 | bytes 1 | tf_op jit(solution)/shard_map/update/pallas_call | solution.py:32
  (7 shorter events, 0.1 us)
Async XLA Ops:
  0.6 3.0 %collective-permute-start = (f32[8,16,512]{2,1,0:T(8,128)}, f32[8,16,512]{2,1,0:T(8,128)S(1)}, u32[]{:S(2)}, u32[]{:S(2)}) collective-permute-start(f32[8,16,512]{2,1,0:T(8,128)} %bitcast.19), channel_id=1, source_target_pairs={{0,1},{1,0},{2,3},{3,2},{4,5},{5,4},{6,7},{7,6},{8,9},{9,8},{10,11... | collective-permute-start | bytes 786440 | tf_op jit(solution)/shard_map/ppermute | solution.py:488
  3.8 6.1 %collective-permute-start.1 = (f32[6,8,512]{2,1,0:T(8,128)S(1)}, f32[6,8,512]{2,1,0:T(8,128)S(1)}, u32[]{:S(2)}, u32[]{:S(2)}) collective-permute-start(f32[6,8,512]{2,1,0:T(8,128)S(1)} %get-tuple-element.47.first_ref), channel_id=1, source_target_pairs={{0,4},{4,0},{8,12},{12,8},{1,5},{5,1},{9,13},{13,9},{2,6},{6,2},{1... | collective-permute-start | bytes 294920 | tf_op jit(solution)/shard_map/ppermute | solution.py:488
  6.5 3.4 %collective-permute-start.2 = (f32[6,8,512]{2,1,0:T(8,128)S(1)}, f32[6,8,512]{2,1,0:T(8,128)S(1)}, u32[]{:S(2)}, u32[]{:S(2)}) collective-permute-start(f32[6,8,512]{2,1,0:T(8,128)S(1)} %get-tuple-element.48.second_ref), channel_id=1, source_target_pairs={{0,1},{1,0},{2,3},{3,2},{4,8},{5,9},{6,10},{7,11},{8,4},{9,5},{10,... | collective-permute-start | bytes 294920 | tf_op jit(solution)/shard_map/ppermute | solution.py:484
  6.7 6.8 %collective-permute-start.4 = (f32[144,512]{1,0:T(8,128)S(1)}, f32[144,512]{1,0:T(8,128)S(1)}, u32[]{:S(2)}, u32[]{:S(2)}) collective-permute-start(f32[144,512]{1,0:T(8,128)S(1)} %pad.4), channel_id=1, source_target_pairs={{0,16},{1,3},{2,18},{3,1},{4,20},{5,7},{6,22},{7,5},{8,24},{9,11},... | collective-permute-start | bytes 884744 | tf_op jit(solution)/shard_map/ppermute | solution.py:484
  10.2 1.8 %collective-permute-start.3 = (f32[8,16,512]{2,1,0:T(8,128)S(1)}, f32[8,16,512]{2,1,0:T(8,128)S(1)}, u32[]{:S(2)}, u32[]{:S(2)}) collective-permute-start(f32[8,16,512]{2,1,0:T(8,128)S(1)} %get-tuple-element.59), channel_id=1, source_target_pairs={{0,1},{1,0},{2,3},{3,2},{4,5},{5,4},{6,7},{7,6},{8,9},{9,8},{10,11... | collective-permute-start | bytes 786440 | tf_op jit(solution)/shard_map/ppermute | solution.py:488
  10.2 5.1 %collective-permute-start.5 = (f32[4,8,512]{2,1,0:T(8,128)S(1)}, f32[4,8,512]{2,1,0:T(8,128)S(1)}, u32[]{:S(2)}, u32[]{:S(2)}) collective-permute-start(f32[4,8,512]{2,1,0:T(8,128)S(1)} %get-tuple-element.64), channel_id=1, source_target_pairs={{0,16},{1,3},{2,18},{3,1},{4,20},{5,7},{6,22},{7,5},{8,24},{9,11},... | collective-permute-start | bytes 196616 | tf_op jit(solution)/shard_map/ppermute | solution.py:484
  12.0 6.4 %collective-permute-start.9 = (f32[8,16,512]{2,1,0:T(8,128)S(1)}, f32[8,16,512]{2,1,0:T(8,128)S(1)}, u32[]{:S(2)}, u32[]{:S(2)}) collective-permute-start(f32[8,16,512]{2,1,0:T(8,128)S(1)} %sends.1), channel_id=1, source_target_pairs={{0,16},{1,3},{2,18},{3,1},{4,20},{5,7},{6,22},{7,5},{8,24},{9,11},... | collective-permute-start | bytes 786440 | tf_op jit(solution)/shard_map/ppermute | solution.py:484
  14.7 1.5 %collective-permute-start.8 = (f32[5,16,512]{2,1,0:T(8,128)S(1)}, f32[5,16,512]{2,1,0:T(8,128)S(1)}, u32[]{:S(2)}, u32[]{:S(2)}) collective-permute-start(f32[5,16,512]{2,1,0:T(8,128)S(1)} %get-tuple-element.69), channel_id=1, source_target_pairs={{0,1},{1,0},{2,3},{3,2},{4,5},{5,4},{6,7},{7,6},{8,9},{9,8},{10,11... | collective-permute-start | bytes 491528 | tf_op jit(solution)/shard_map/ppermute | solution.py:488
  14.8 1.7 %collective-permute-start.6 = (f32[6,16,512]{2,1,0:T(8,128)S(1)}, f32[6,16,512]{2,1,0:T(8,128)S(1)}, u32[]{:S(2)}, u32[]{:S(2)}) collective-permute-start(f32[6,16,512]{2,1,0:T(8,128)S(1)} %get-tuple-element.67), channel_id=1, source_target_pairs={{0,1},{1,0},{2,3},{3,2},{4,5},{5,4},{6,7},{7,6},{8,9},{9,8},{10,11... | collective-permute-start | bytes 589832 | tf_op jit(solution)/shard_map/ppermute | solution.py:488
  15.3 1.4 %collective-permute-start.7 = (f32[6,16,512]{2,1,0:T(8,128)S(1)}, f32[6,16,512]{2,1,0:T(8,128)S(1)}, u32[]{:S(2)}, u32[]{:S(2)}) collective-permute-start(f32[6,16,512]{2,1,0:T(8,128)S(1)} %get-tuple-element.68), channel_id=1, source_target_pairs={{0,1},{1,0},{2,3},{3,2},{4,5},{5,4},{6,7},{7,6},{8,9},{9,8},{10,11... | collective-permute-start | bytes 589832 | tf_op jit(solution)/shard_map/ppermute | solution.py:488
  18.7 3.6 %collective-permute-start.13 = (f32[2,128]{1,0:T(2,128)S(1)}, f32[2,128]{1,0:T(2,128)S(1)}, u32[]{:S(2)}, u32[]{:S(2)}) collective-permute-start(f32[2,128]{1,0:T(2,128)S(1)} %get-tuple-element.75), channel_id=1, source_target_pairs={{0,16},{1,7},{2,18},{3,5},{4,20},{5,3},{6,22},{7,1},{8,24},{9,15},... | collective-permute-start | bytes 3080 | tf_op jit(solution)/shard_map/ppermute | solution.py:484
  20.2 3.6 %collective-permute-start.12 = (f32[2,128]{1,0:T(2,128)S(1)}, f32[2,128]{1,0:T(2,128)S(1)}, u32[]{:S(2)}, u32[]{:S(2)}) collective-permute-start(f32[2,128]{1,0:T(2,128)S(1)} %get-tuple-element.75), channel_id=1, source_target_pairs={{0,16},{1,5},{2,18},{3,7},{4,20},{5,1},{6,22},{7,3},{8,24},{9,13},... | collective-permute-start | bytes 3080 | tf_op jit(solution)/shard_map/ppermute | solution.py:484
  20.8 3.6 %collective-permute-start.11 = (f32[2,128]{1,0:T(2,128)S(1)}, f32[2,128]{1,0:T(2,128)S(1)}, u32[]{:S(2)}, u32[]{:S(2)}) collective-permute-start(f32[2,128]{1,0:T(2,128)S(1)} %get-tuple-element.75), channel_id=1, source_target_pairs={{0,16},{1,3},{2,18},{3,1},{4,20},{5,7},{6,22},{7,5},{8,24},{9,11},... | collective-permute-start | bytes 3080 | tf_op jit(solution)/shard_map/ppermute | solution.py:484
  22.2 6.8 %collective-permute-start.10 = (f32[8,16,512]{2,1,0:T(8,128)S(1)}, f32[8,16,512]{2,1,0:T(8,128)S(1)}, u32[]{:S(2)}, u32[]{:S(2)}) collective-permute-start(f32[8,16,512]{2,1,0:T(8,128)S(1)} %get-tuple-element.74), channel_id=1, source_target_pairs={{0,1},{1,0},{2,3},{3,2},{4,5},{5,4},{6,7},{7,6},{8,9},{9,8},{10,11... | collective-permute-start | bytes 786440 | tf_op jit(solution)/shard_map/ppermute | solution.py:488
  24.3 3.6 %collective-permute-start.14 = (f32[2,128]{1,0:T(2,128)S(1)}, f32[2,128]{1,0:T(2,128)S(1)}, u32[]{:S(2)}, u32[]{:S(2)}) collective-permute-start(f32[2,128]{1,0:T(2,128)S(1)} %add_add_fusion), channel_id=1, source_target_pairs={{0,16},{1,9},{2,18},{3,11},{4,20},{5,13},{6,22},{7,15},{8,24},{9,1... | collective-permute-start | bytes 3080 | tf_op jit(solution)/shard_map/ppermute | solution.py:484
  27.9 1.1 %collective-permute-start.15 = (f32[2,128]{1,0:T(2,128)S(1)}, f32[2,128]{1,0:T(2,128)S(1)}, u32[]{:S(2)}, u32[]{:S(2)}) collective-permute-start(f32[2,128]{1,0:T(2,128)S(1)} %add.22), channel_id=1, source_target_pairs={{0,1},{1,0},{2,3},{3,2},{4,5},{5,4},{6,7},{7,6},{8,9},{9,8},{10,11... | collective-permute-start | bytes 3080 | tf_op jit(solution)/shard_map/ppermute | solution.py:488

commit v7 on v6

--- a/solution.py
+++ b/solution.py
@@ -103,7 +103,7 @@
 
 def begin_body(count, *refs):
     sources, targets = refs[:count], refs[count : 2 * count]
-    moved_ref, high_ref, low_ref, edge_ref, sems = refs[2 * count :]
+    once_ref, high_ref, low_ref, edge_ref, sems = refs[2 * count :]
     s_ref, a_ref, b_ref, c_ref = targets[:4]
     levels, rows, _ = s_ref.shape
     last = rows - 1
@@ -132,7 +132,7 @@
         s, a, b, c = s_ref[lev], a_ref[lev], b_ref[lev], c_ref[lev]
         coeffs = taps(a, b, c)
         once = forward(s, coeffs)
-        moved_ref[lev] = forward(once, coeffs)
+        once_ref[lev] = once
         mid, east, west, north, south = coeffs
         at = pl.ds(lev, 1)
         open_east = c[last : last + 1] - a[last : last + 1]
@@ -167,6 +167,12 @@
         copy.wait()
 
 
+def forward_body(a_ref, b_ref, c_ref, once_ref, moved_ref):
+    for lev in range(a_ref.shape[0]):
+        coeffs = taps(a_ref[lev], b_ref[lev], c_ref[lev])
+        moved_ref[lev] = forward(once_ref[lev], coeffs)
+
+
 def adjoint_body(a_ref, b_ref, c_ref, later_ref, back_ref):
     for lev in range(a_ref.shape[0]):
         coeffs = taps(a_ref[lev], b_ref[lev], c_ref[lev])
@@ -549,7 +555,7 @@
     arguments = [increment[0], drift_east[0], drift_north[0], diffusion[0], multiplier[0]]
     arguments += [rhs_model[0], model_err[0], obs_cell, obs_dual, rhs_obs, obs_err]
     count = len(arguments)
-    *here, moved, high, low, edge = kernel_call(
+    *here, once, high, low, edge = kernel_call(
         lambda *refs: begin_body(count, *refs),
         "begin",
         [(x, "far") for x in arguments],
@@ -576,6 +582,8 @@
     local, held = kernel_call(
         spread_body, "spread", near(incr, mult, rhs, err, cell, dual, valid), [field] * 2
     )
+    once, first = lax.optimization_barrier((once, first))
+    moved = kernel_call(forward_body, "forward", near(*coeffs, once), [field])[0]
     rims = near(first, second, got_first, got_second, edge)
     if not four:
         fix = kernel_call(edges_body, "edges", rims, [lines(8)])[0]

time: 30.4 us -> 30.2 us (level)
    pallas_call x13 -> x14, Pallas kernels: 5.92 us -> 5.95 us  [kernel_call(): pl.pallas_call(body, name=name, out_shape=out_shape, in_specs=in_specs, o...]
  transfers between devices with their start and end apart: 16 -> 16, of which waited for: 10 -> 11; matrix products, arithmetic and copies ran while one was open for 0% -> 0% of each run, Pallas kernels for 16% -> 16%
where the time goes in v7:
time: 30.2 us; the launch traced here: 29.8 us
  starting transfers between devices  14 us (46%)
  waiting for transfers between devices  8.41 us (28%)
  Pallas kernels  5.95 us (20%)
  between operations  1.42 us (5%)
    ppermute x8, starting transfers between devices, exchange(): return lax.ppermute(value, ('groups', 'tile', 'tm'), pairs)  10 us
    pallas_call x14, Pallas kernels, kernel_call(): pl.pallas_call(body, name=name, out_shape=out_shape, in_specs=in_specs, o...  5.95 us
    ppermute x8, waiting for transfers between devices, exchange(): return lax.ppermute(value, ('groups', 'tile', 'tm'), pairs)  5.8 us
    ppermute x8, starting transfers between devices, swap(): lax.ppermute(value, axis, [(i, i ^ distance) for i in range(lax.axis_size...  3.91 us
    ppermute x8, waiting for transfers between devices, swap(): lax.ppermute(value, axis, [(i, i ^ distance) for i in range(lax.axis_size...  2.6 us
  transfers between devices with their start and end apart: 16, of which 11 were waited for; matrix products, arithmetic and copies ran while one was open for 0% of the time, Pallas kernels for 16%

profile of v7, /device:TPU:0, one launch (start us, length us, event | category | flops | bytes accessed | tf_op | source)
XLA Modules:
  0.0 29.8 jit_solution(2498720457469637141)
XLA Ops:
  0.6 0.5 %collective-permute-start = (f32[8,16,512]{2,1,0:T(8,128)}, f32[8,16,512]{2,1,0:T(8,128)S(1)}, u32[]{:S(2)}, u32[]{:S(2)}) collective-permute-start(f32[8,16,512]{2,1,0:T(8,128)} %bitcast.19), channel_id=1, source_target_pairs={{0,1},{1,0},{2,3},{3,2},{4,5},{5,4},{6,7},{7,6},{8,9},{9,8},{10,11... | collective-permute-start | bytes 786440 | tf_op jit(solution)/shard_map/ppermute | solution.py:494
  1.2 1.7 %begin.1 = (f32[8,16,512]{2,1,0:T(8,128)S(1)}, f32[8,16,512]{2,1,0:T(8,128)S(1)}, f32[8,16,512]{2,1,0:T(8,128)S(1)}, f32[8,16,512]{2,1,0:T(8,128)S(1)}, f32[8,16...) custom-call(f32[8,16,512]{2,1,0:T(8,128)} %bitcast.13, ...), custom_call_target="tpu_custom_call" | custom-call | flops 1 | bytes 1 | tf_op jit(solution)/shard_map/begin/pallas_call | solution.py:32
  3.5 0.0 collective-permute-done.refs_1_.later_ref
  3.5 0.1 rims.1
  3.6 2.7 %collective-permute-start.1 = (f32[6,8,512]{2,1,0:T(8,128)S(1)}, f32[6,8,512]{2,1,0:T(8,128)S(1)}, u32[]{:S(2)}, u32[]{:S(2)}) collective-permute-start(f32[6,8,512]{2,1,0:T(8,128)S(1)} %get-tuple-element.51.first_ref), channel_id=1, source_target_pairs={{0,4},{4,0},{8,12},{12,8},{1,5},{5,1},{9,13},{13,9},{2,6},{6,2},{1... | collective-permute-start | bytes 294920 | tf_op jit(solution)/shard_map/ppermute | solution.py:494
  6.3 0.2 collective-permute-start.2
  6.5 0.2 forward.1.moved_ref
  6.8 1.6 %collective-permute-start.4 = (f32[144,512]{1,0:T(8,128)S(1)}, f32[144,512]{1,0:T(8,128)S(1)}, u32[]{:S(2)}, u32[]{:S(2)}) collective-permute-start(f32[144,512]{1,0:T(8,128)S(1)} %pad.4), channel_id=1, source_target_pairs={{0,16},{1,3},{2,18},{3,1},{4,20},{5,7},{6,22},{7,5},{8,24},{9,11},... | collective-permute-start | bytes 884744 | tf_op jit(solution)/shard_map/ppermute | solution.py:490
  8.4 0.4 %spread.1 = (f32[8,16,512]{2,1,0:T(8,128)S(1)}, f32[8,16,512]{2,1,0:T(8,128)S(1)}) custom-call(f32[8,16,512]{2,1,0:T(8,128)S(1)} %get-tuple-element.44.incr_ref, f32[8,16,512]{2,1,0:T(8,128)S(1)} %get-tuple-element.43.mult_ref, f32[8,16,512]{2,1,0:T(8,128)S(1)} %get-tuple-element.53.rhs_ref, f32[8,16,512]{2,1,0:T(8,128)S(1)} %get-tuple-element.54.err_ref, ...), custom_call_target="tpu_custom_call" | custom-call | flops 1 | bytes 1 | tf_op jit(solution)/shard_map/spread/pallas_call | solution.py:32
  8.8 0.7 %adjoint.1.back_ref = f32[8,16,512]{2,1,0:T(8,128)S(1)} custom-call(f32[8,16,512]{2,1,0:T(8,128)S(1)} %get-tuple-element.57.a_ref, f32[8,16,512]{2,1,0:T(8,128)S(1)} %get-tuple-element.58.b_ref, f32[8,16,512]{2,1,0:T(8,128)S(1)} %get-tuple-element.59.c_ref, f32[8,16,512]{2,1,0:T(8,128)S(1)} %collective-permute-done.refs_1_.later_ref), custom_call_target="tpu_custom_call" | custom-call | flops 1 | bytes 1 | tf_op jit(solution)/shard_map/adjoint/pallas_call | solution.py:32
  9.5 0.2 collective-permute-done.1.got_first_ref.refs_0_
  9.7 0.0 collective-permute-done.2.got_second_ref.refs_1_
  9.7 0.2 share.1
  10.0 0.1 collective-permute-start.3
  10.0 1.7 %collective-permute-start.5 = (f32[4,8,512]{2,1,0:T(8,128)S(1)}, f32[4,8,512]{2,1,0:T(8,128)S(1)}, u32[]{:S(2)}, u32[]{:S(2)}) collective-permute-start(f32[4,8,512]{2,1,0:T(8,128)S(1)} %get-tuple-element.68), channel_id=1, source_target_pairs={{0,16},{1,3},{2,18},{3,1},{4,20},{5,7},{6,22},{7,5},{8,24},{9,11},... | collective-permute-start | bytes 196616 | tf_op jit(solution)/shard_map/ppermute | solution.py:490
  11.8 0.0 collective-permute-done.3.got_ref
  11.8 1.5 %collective-permute-start.9 = (f32[8,16,512]{2,1,0:T(8,128)S(1)}, f32[8,16,512]{2,1,0:T(8,128)S(1)}, u32[]{:S(2)}, u32[]{:S(2)}) collective-permute-start(f32[8,16,512]{2,1,0:T(8,128)S(1)} %sends.1), channel_id=1, source_target_pairs={{0,16},{1,3},{2,18},{3,1},{4,20},{5,7},{6,22},{7,5},{8,24},{9,11},... | collective-permute-start | bytes 786440 | tf_op jit(solution)/shard_map/ppermute | solution.py:490
  13.4 0.2 collective-permute-done.4.cross_ref.refs_3_
  13.6 0.7 %beyond.1.beyond_ref = f32[8,16,512]{2,1,0:T(8,128)S(1)} custom-call(f32[8,16,512]{2,1,0:T(8,128)S(1)} %get-tuple-element.57.a_ref, f32[8,16,512]{2,1,0:T(8,128)S(1)} %get-tuple-element.58.b_ref, f32[8,16,512]{2,1,0:T(8,128)S(1)} %get-tuple-element.59.c_ref, f32[144,512]{1,0:T(8,128)S(1)} %collective-permute-done.4.cross_ref.refs_3_), custom_call_target="tpu_custom_call" | custom-call | flops 1 | bytes 1 | tf_op jit(solution)/shard_map/beyond/pallas_call | solution.py:32
  14.3 0.4 %gather.1 = (f32[1,512]{1,0:T(1,128)S(1)}, f32[2,1,512]{2,1,0:T(1,128)S(1)}) custom-call(f32[8,16,512]{2,1,0:T(8,128)S(1)} %get-tuple-element.44.incr_ref, s32[1,512]{1,0:T(1,128)S(1)} %get-tuple-element.64.cell_ref, f32[1,512]{1,0:T(1,128)S(1)} %get-tuple-element.45.dual_ref, f32[1,512]{1,0:T(1,128)S(1)} %get-tuple-element.65.want_ref, ...), custom_call_target="tpu_custom_call" | custom-call | flops 1 | bytes 1 | tf_op jit(solution)/shard_map/gather/pallas_call | solution.py:32
  14.7 0.1 rest.1
  14.7 0.1 collective-permute-start.8
  14.8 0.5 %collective-permute-start.6 = (f32[6,16,512]{2,1,0:T(8,128)S(1)}, f32[6,16,512]{2,1,0:T(8,128)S(1)}, u32[]{:S(2)}, u32[]{:S(2)}) collective-permute-start(f32[6,16,512]{2,1,0:T(8,128)S(1)} %get-tuple-element.71), channel_id=1, source_target_pairs={{0,1},{1,0},{2,3},{3,2},{4,5},{5,4},{6,7},{7,6},{8,9},{9,8},{10,11... | collective-permute-start | bytes 589832 | tf_op jit(solution)/shard_map/ppermute | solution.py:494
  15.3 0.1 collective-permute-start.7
  15.4 0.0 collective-permute-done.5.refs_4_.late_ref
  15.4 0.1 late.1.fix_ref
  15.5 0.7 %collective-permute-done.8.refs_2_.rest_ref = f32[5,16,512]{2,1,0:T(8,128)S(1)} collective-permute-done((f32[5,16,512]{2,1,0:T(8,128)S(1)}, f32[5,16,512]{2,1,0:T(8,128)S(1)}, u32[]{:S(2)}, u32[]{:S(2)}) %collective-permute-start.8) | collective-permute-done | bytes 163872 | tf_op jit(solution)/shard_map/ppermute | solution.py:494
  16.2 0.3 collective-permute-done.6.refs_0_
  16.5 0.3 collective-permute-done.7.refs_1_
  16.7 0.2 terms.1
  16.9 1.4 %collective-permute-done.9.got_ref = f32[8,16,512]{2,1,0:T(8,128)S(1)} collective-permute-done((f32[8,16,512]{2,1,0:T(8,128)S(1)}, f32[8,16,512]{2,1,0:T(8,128)S(1)}, u32[]{:S(2)}, u32[]{:S(2)}) %collective-permute-start.9) | collective-permute-done | bytes 262176 | tf_op jit(solution)/shard_map/ppermute | solution.py:490
  18.3 0.2 dots.1
  18.5 1.5 %collective-permute-start.13 = (f32[2,128]{1,0:T(2,128)S(1)}, f32[2,128]{1,0:T(2,128)S(1)}, u32[]{:S(2)}, u32[]{:S(2)}) collective-permute-start(f32[2,128]{1,0:T(2,128)S(1)} %get-tuple-element.79), channel_id=1, source_target_pairs={{0,16},{1,7},{2,18},{3,5},{4,20},{5,3},{6,22},{7,1},{8,24},{9,15},... | collective-permute-start | bytes 3080 | tf_op jit(solution)/shard_map/ppermute | solution.py:490
  20.0 0.6 %collective-permute-start.12 = (f32[2,128]{1,0:T(2,128)S(1)}, f32[2,128]{1,0:T(2,128)S(1)}, u32[]{:S(2)}, u32[]{:S(2)}) collective-permute-start(f32[2,128]{1,0:T(2,128)S(1)} %get-tuple-element.79), channel_id=1, source_target_pairs={{0,16},{1,5},{2,18},{3,7},{4,20},{5,1},{6,22},{7,3},{8,24},{9,13},... | collective-permute-start | bytes 3080 | tf_op jit(solution)/shard_map/ppermute | solution.py:490
  20.6 1.5 %collective-permute-start.11 = (f32[2,128]{1,0:T(2,128)S(1)}, f32[2,128]{1,0:T(2,128)S(1)}, u32[]{:S(2)}, u32[]{:S(2)}) collective-permute-start(f32[2,128]{1,0:T(2,128)S(1)} %get-tuple-element.79), channel_id=1, source_target_pairs={{0,16},{1,3},{2,18},{3,1},{4,20},{5,7},{6,22},{7,5},{8,24},{9,11},... | collective-permute-start | bytes 3080 | tf_op jit(solution)/shard_map/ppermute | solution.py:490
  22.0 0.0 collective-permute-start.10
  22.0 0.1 collective-permute-done.13
  22.1 1.5 %collective-permute-done.12 = f32[2,128]{1,0:T(2,128)S(1)} collective-permute-done((f32[2,128]{1,0:T(2,128)S(1)}, f32[2,128]{1,0:T(2,128)S(1)}, u32[]{:S(2)}, u32[]{:S(2)}) %collective-permute-start.12) | collective-permute-done | bytes 1056 | tf_op jit(solution)/shard_map/ppermute | solution.py:490
  23.6 0.6 %collective-permute-done.11 = f32[2,128]{1,0:T(2,128)S(1)} collective-permute-done((f32[2,128]{1,0:T(2,128)S(1)}, f32[2,128]{1,0:T(2,128)S(1)}, u32[]{:S(2)}, u32[]{:S(2)}) %collective-permute-start.11) | collective-permute-done | bytes 1056 | tf_op jit(solution)/shard_map/ppermute | solution.py:490
  24.1 1.5 %collective-permute-start.14 = (f32[2,128]{1,0:T(2,128)S(1)}, f32[2,128]{1,0:T(2,128)S(1)}, u32[]{:S(2)}, u32[]{:S(2)}) collective-permute-start(f32[2,128]{1,0:T(2,128)S(1)} %add_add_fusion), channel_id=1, source_target_pairs={{0,16},{1,9},{2,18},{3,11},{4,20},{5,13},{6,22},{7,15},{8,24},{9,1... | collective-permute-start | bytes 3080 | tf_op jit(solution)/shard_map/ppermute | solution.py:490
  25.6 2.1 %collective-permute-done.14 = f32[2,128]{1,0:T(2,128)S(1)} collective-permute-done((f32[2,128]{1,0:T(2,128)S(1)}, f32[2,128]{1,0:T(2,128)S(1)}, u32[]{:S(2)}, u32[]{:S(2)}) %collective-permute-start.14) | collective-permute-done | bytes 1056 | tf_op jit(solution)/shard_map/ppermute | solution.py:490
  27.7 0.0 collective-permute-start.15
  27.7 1.1 %collective-permute-done.15 = f32[2,128]{1,0:T(2,128)S(1)} collective-permute-done((f32[2,128]{1,0:T(2,128)S(1)}, f32[2,128]{1,0:T(2,128)S(1)}, u32[]{:S(2)}, u32[]{:S(2)}) %collective-permute-start.15) | collective-permute-done | bytes 1056 | tf_op jit(solution)/shard_map/ppermute | solution.py:494
  28.9 0.0 collective-permute-done.10.got_ref
  28.9 1.0 %update.1 = (f32[8,16,512]{2,1,0:T(8,128)}, f32[8,16,512]{2,1,0:T(8,128)}, f32[1,512]{1,0:T(1,128)}) custom-call(f32[8,16,512]{2,1,0:T(8,128)S(1)} %get-tuple-element.43.mult_ref, f32[8,16,512]{2,1,0:T(8,128)S(1)} %get-tuple-element.44.incr_ref, f32[1,512]{1,0:T(1,128)S(1)} %get-tuple-element.45.dual_ref, f32[1,512]{1,0:T(1,128)S(1)} %get-tuple-element.67.dir_ref, ...), custom_call_target="tpu_custom_call" | custom-call | flops 1 | bytes 1 | tf_op jit(solution)/shard_map/update/pallas_call | solution.py:32
  (7 shorter events, 0.1 us)
Async XLA Ops:
  0.6 2.8 %collective-permute-start = (f32[8,16,512]{2,1,0:T(8,128)}, f32[8,16,512]{2,1,0:T(8,128)S(1)}, u32[]{:S(2)}, u32[]{:S(2)}) collective-permute-start(f32[8,16,512]{2,1,0:T(8,128)} %bitcast.19), channel_id=1, source_target_pairs={{0,1},{1,0},{2,3},{3,2},{4,5},{5,4},{6,7},{7,6},{8,9},{9,8},{10,11... | collective-permute-start | bytes 786440 | tf_op jit(solution)/shard_map/ppermute | solution.py:494
  3.6 6.1 %collective-permute-start.1 = (f32[6,8,512]{2,1,0:T(8,128)S(1)}, f32[6,8,512]{2,1,0:T(8,128)S(1)}, u32[]{:S(2)}, u32[]{:S(2)}) collective-permute-start(f32[6,8,512]{2,1,0:T(8,128)S(1)} %get-tuple-element.51.first_ref), channel_id=1, source_target_pairs={{0,4},{4,0},{8,12},{12,8},{1,5},{5,1},{9,13},{13,9},{2,6},{6,2},{1... | collective-permute-start | bytes 294920 | tf_op jit(solution)/shard_map/ppermute | solution.py:494
  6.3 3.4 %collective-permute-start.2 = (f32[6,8,512]{2,1,0:T(8,128)S(1)}, f32[6,8,512]{2,1,0:T(8,128)S(1)}, u32[]{:S(2)}, u32[]{:S(2)}) collective-permute-start(f32[6,8,512]{2,1,0:T(8,128)S(1)} %get-tuple-element.52.second_ref), channel_id=1, source_target_pairs={{0,1},{1,0},{2,3},{3,2},{4,8},{5,9},{6,10},{7,11},{8,4},{9,5},{10,... | collective-permute-start | bytes 294920 | tf_op jit(solution)/shard_map/ppermute | solution.py:490
  6.8 6.8 %collective-permute-start.4 = (f32[144,512]{1,0:T(8,128)S(1)}, f32[144,512]{1,0:T(8,128)S(1)}, u32[]{:S(2)}, u32[]{:S(2)}) collective-permute-start(f32[144,512]{1,0:T(8,128)S(1)} %pad.4), channel_id=1, source_target_pairs={{0,16},{1,3},{2,18},{3,1},{4,20},{5,7},{6,22},{7,5},{8,24},{9,11},... | collective-permute-start | bytes 884744 | tf_op jit(solution)/shard_map/ppermute | solution.py:490
  10.0 1.8 %collective-permute-start.3 = (f32[8,16,512]{2,1,0:T(8,128)S(1)}, f32[8,16,512]{2,1,0:T(8,128)S(1)}, u32[]{:S(2)}, u32[]{:S(2)}) collective-permute-start(f32[8,16,512]{2,1,0:T(8,128)S(1)} %get-tuple-element.63), channel_id=1, source_target_pairs={{0,1},{1,0},{2,3},{3,2},{4,5},{5,4},{6,7},{7,6},{8,9},{9,8},{10,11... | collective-permute-start | bytes 786440 | tf_op jit(solution)/shard_map/ppermute | solution.py:494
  10.0 5.3 %collective-permute-start.5 = (f32[4,8,512]{2,1,0:T(8,128)S(1)}, f32[4,8,512]{2,1,0:T(8,128)S(1)}, u32[]{:S(2)}, u32[]{:S(2)}) collective-permute-start(f32[4,8,512]{2,1,0:T(8,128)S(1)} %get-tuple-element.68), channel_id=1, source_target_pairs={{0,16},{1,3},{2,18},{3,1},{4,20},{5,7},{6,22},{7,5},{8,24},{9,11},... | collective-permute-start | bytes 196616 | tf_op jit(solution)/shard_map/ppermute | solution.py:490
  11.8 6.4 %collective-permute-start.9 = (f32[8,16,512]{2,1,0:T(8,128)S(1)}, f32[8,16,512]{2,1,0:T(8,128)S(1)}, u32[]{:S(2)}, u32[]{:S(2)}) collective-permute-start(f32[8,16,512]{2,1,0:T(8,128)S(1)} %sends.1), channel_id=1, source_target_pairs={{0,16},{1,3},{2,18},{3,1},{4,20},{5,7},{6,22},{7,5},{8,24},{9,11},... | collective-permute-start | bytes 786440 | tf_op jit(solution)/shard_map/ppermute | solution.py:490
  14.7 1.5 %collective-permute-start.8 = (f32[5,16,512]{2,1,0:T(8,128)S(1)}, f32[5,16,512]{2,1,0:T(8,128)S(1)}, u32[]{:S(2)}, u32[]{:S(2)}) collective-permute-start(f32[5,16,512]{2,1,0:T(8,128)S(1)} %get-tuple-element.73), channel_id=1, source_target_pairs={{0,1},{1,0},{2,3},{3,2},{4,5},{5,4},{6,7},{7,6},{8,9},{9,8},{10,11... | collective-permute-start | bytes 491528 | tf_op jit(solution)/shard_map/ppermute | solution.py:494
  14.8 1.7 %collective-permute-start.6 = (f32[6,16,512]{2,1,0:T(8,128)S(1)}, f32[6,16,512]{2,1,0:T(8,128)S(1)}, u32[]{:S(2)}, u32[]{:S(2)}) collective-permute-start(f32[6,16,512]{2,1,0:T(8,128)S(1)} %get-tuple-element.71), channel_id=1, source_target_pairs={{0,1},{1,0},{2,3},{3,2},{4,5},{5,4},{6,7},{7,6},{8,9},{9,8},{10,11... | collective-permute-start | bytes 589832 | tf_op jit(solution)/shard_map/ppermute | solution.py:494
  15.3 1.4 %collective-permute-start.7 = (f32[6,16,512]{2,1,0:T(8,128)S(1)}, f32[6,16,512]{2,1,0:T(8,128)S(1)}, u32[]{:S(2)}, u32[]{:S(2)}) collective-permute-start(f32[6,16,512]{2,1,0:T(8,128)S(1)} %get-tuple-element.72), channel_id=1, source_target_pairs={{0,1},{1,0},{2,3},{3,2},{4,5},{5,4},{6,7},{7,6},{8,9},{9,8},{10,11... | collective-permute-start | bytes 589832 | tf_op jit(solution)/shard_map/ppermute | solution.py:494
  18.5 3.6 %collective-permute-start.13 = (f32[2,128]{1,0:T(2,128)S(1)}, f32[2,128]{1,0:T(2,128)S(1)}, u32[]{:S(2)}, u32[]{:S(2)}) collective-permute-start(f32[2,128]{1,0:T(2,128)S(1)} %get-tuple-element.79), channel_id=1, source_target_pairs={{0,16},{1,7},{2,18},{3,5},{4,20},{5,3},{6,22},{7,1},{8,24},{9,15},... | collective-permute-start | bytes 3080 | tf_op jit(solution)/shard_map/ppermute | solution.py:490
  20.0 3.6 %collective-permute-start.12 = (f32[2,128]{1,0:T(2,128)S(1)}, f32[2,128]{1,0:T(2,128)S(1)}, u32[]{:S(2)}, u32[]{:S(2)}) collective-permute-start(f32[2,128]{1,0:T(2,128)S(1)} %get-tuple-element.79), channel_id=1, source_target_pairs={{0,16},{1,5},{2,18},{3,7},{4,20},{5,1},{6,22},{7,3},{8,24},{9,13},... | collective-permute-start | bytes 3080 | tf_op jit(solution)/shard_map/ppermute | solution.py:490
  20.6 3.6 %collective-permute-start.11 = (f32[2,128]{1,0:T(2,128)S(1)}, f32[2,128]{1,0:T(2,128)S(1)}, u32[]{:S(2)}, u32[]{:S(2)}) collective-permute-start(f32[2,128]{1,0:T(2,128)S(1)} %get-tuple-element.79), channel_id=1, source_target_pairs={{0,16},{1,3},{2,18},{3,1},{4,20},{5,7},{6,22},{7,5},{8,24},{9,11},... | collective-permute-start | bytes 3080 | tf_op jit(solution)/shard_map/ppermute | solution.py:490
  22.0 6.8 %collective-permute-start.10 = (f32[8,16,512]{2,1,0:T(8,128)S(1)}, f32[8,16,512]{2,1,0:T(8,128)S(1)}, u32[]{:S(2)}, u32[]{:S(2)}) collective-permute-start(f32[8,16,512]{2,1,0:T(8,128)S(1)} %get-tuple-element.78), channel_id=1, source_target_pairs={{0,1},{1,0},{2,3},{3,2},{4,5},{5,4},{6,7},{7,6},{8,9},{9,8},{10,11... | collective-permute-start | bytes 786440 | tf_op jit(solution)/shard_map/ppermute | solution.py:494
  24.1 3.6 %collective-permute-start.14 = (f32[2,128]{1,0:T(2,128)S(1)}, f32[2,128]{1,0:T(2,128)S(1)}, u32[]{:S(2)}, u32[]{:S(2)}) collective-permute-start(f32[2,128]{1,0:T(2,128)S(1)} %add_add_fusion), channel_id=1, source_target_pairs={{0,16},{1,9},{2,18},{3,11},{4,20},{5,13},{6,22},{7,15},{8,24},{9,1... | collective-permute-start | bytes 3080 | tf_op jit(solution)/shard_map/ppermute | solution.py:490
  27.7 1.1 %collective-permute-start.15 = (f32[2,128]{1,0:T(2,128)S(1)}, f32[2,128]{1,0:T(2,128)S(1)}, u32[]{:S(2)}, u32[]{:S(2)}) collective-permute-start(f32[2,128]{1,0:T(2,128)S(1)} %add.22), channel_id=1, source_target_pairs={{0,1},{1,0},{2,3},{3,2},{4,5},{5,4},{6,7},{7,6},{8,9},{9,8},{10,11... | collective-permute-start | bytes 3080 | tf_op jit(solution)/shard_map/ppermute | solution.py:494

commit v8 on v7

--- a/solution.py
+++ b/solution.py
@@ -193,7 +193,7 @@
 
 def rims_body(four, edge_ref, later_ref, high_ref, low_ref, first_ref, second_ref):
     position, peers = lax.axis_index("tm"), lax.axis_size("tm")
-    odd = lax.rem(lax.axis_index("tile"), 2)
+    odd = lax.rem(lax.axis_index("tile") + 1, 2)
     k = {key: edge_ref[n] for n, key in enumerate(EDGE)}
     levels, rows, _ = later_ref.shape
     later = [
@@ -223,13 +223,13 @@
 
 def sides(first, second):
     tile, tiles = lax.axis_index("tile"), lax.axis_size("tile")
-    odd = lax.rem(tile, 2)
+    odd = lax.rem(tile + 1, 2)
     below, above = jnp.where(odd == 0, second, first), jnp.where(odd == 0, first, second)
     return jnp.where(tile > 0, below, 0.0), jnp.where(tile < tiles - 1, above, 0.0)
 
 
 def own_sides(first, second):
-    odd = lax.rem(lax.axis_index("tile"), 2)
+    odd = lax.rem(lax.axis_index("tile") + 1, 2)
     return jnp.where(odd == 0, second, first), jnp.where(odd == 0, first, second)
 
 
@@ -369,10 +369,6 @@
     return [ref[start + n, pl.ds(lev, 1)] for n in range(4)]
 
 
-def minus(rows):
-    return [-x for x in rows]
-
-
 def share_body(
     first_ref, second_ref, got_first_ref, got_second_ref, edge_ref,
     local_ref, moved_ref, held_ref, back_ref, own_ref, urgent_ref, late_ref,
@@ -576,14 +572,17 @@
         near(edge, later, high, low),
         [lines(6), lines(6)],
     )
-    got_first = swap(first, "tile", 1)
-    got_second = exchange(second, second_side)
+    got_front = exchange(second, lambda g, t, k: (g, t ^ 1, k) if t % 4 < 2 else (g, t, k ^ 1))
+    once, second = lax.optimization_barrier((once, second))
+    moved = kernel_call(forward_body, "forward", near(*coeffs, once), [field])[0]
+    moved, first, second, incr = lax.optimization_barrier((moved, first, second, incr))
+    got_first = exchange(first, second_side)
+    got_back = exchange(second, lambda g, t, k: (g, t, k ^ 1) if t % 4 < 2 else (g, t ^ 1, k))
+    got_second = jnp.where(lax.axis_index("tile") % 4 < 2, got_front, got_back)
     valid = (lax.broadcasted_iota(jnp.int32, obs_cell.shape, 1) < obs_count).astype(F32)
     local, held = kernel_call(
         spread_body, "spread", near(incr, mult, rhs, err, cell, dual, valid), [field] * 2
     )
-    once, first = lax.optimization_barrier((once, first))
-    moved = kernel_call(forward_body, "forward", near(*coeffs, once), [field])[0]
     rims = near(first, second, got_first, got_second, edge)
     if not four:
         fix = kernel_call(edges_body, "edges", rims, [lines(8)])[0]

time: 30.2 us -> 30 us (level)
    ppermute x8 -> x10, starting transfers between devices: 10 us -> 12.9 us  [exchange(): return lax.ppermute(value, ('groups', 'tile', 'tm'), pairs)]
    ppermute x8 -> x7, starting transfers between devices: 3.91 us -> 1.24 us  [swap(): lax.ppermute(value, axis, [(i, i ^ distance) for i in range(lax.axis_size...]
    ppermute x8 -> x7, waiting for transfers between devices: 2.6 us -> 2.39 us  [swap(): lax.ppermute(value, axis, [(i, i ^ distance) for i in range(lax.axis_size...]
    ppermute x8 -> x10, waiting for transfers between devices: 5.8 us -> 5.77 us  [exchange(): return lax.ppermute(value, ('groups', 'tile', 'tm'), pairs)]
  transfers between devices with their start and end apart: 16 -> 17, of which waited for: 11 -> 10; matrix products, arithmetic and copies ran while one was open for 0% -> 0% of each run, Pallas kernels for 16% -> 16%
where the time goes in v8:
time: 30 us; the launch traced here: 29.9 us
  starting transfers between devices  14.2 us (47%)
  waiting for transfers between devices  8.16 us (27%)
  Pallas kernels  5.99 us (20%)
  between operations  1.46 us (5%)
    ppermute x10, starting transfers between devices, exchange(): return lax.ppermute(value, ('groups', 'tile', 'tm'), pairs)  12.9 us
    pallas_call x14, Pallas kernels, kernel_call(): pl.pallas_call(body, name=name, out_shape=out_shape, in_specs=in_specs, o...  5.99 us
    ppermute x10, waiting for transfers between devices, exchange(): return lax.ppermute(value, ('groups', 'tile', 'tm'), pairs)  5.77 us
    ppermute x7, waiting for transfers between devices, swap(): lax.ppermute(value, axis, [(i, i ^ distance) for i in range(lax.axis_size...  2.39 us
    ppermute x7, starting transfers between devices, swap(): lax.ppermute(value, axis, [(i, i ^ distance) for i in range(lax.axis_size...  1.24 us
  transfers between devices with their start and end apart: 17, of which 10 were waited for; matrix products, arithmetic and copies ran while one was open for 0% of the time, Pallas kernels for 16%

profile of v8, /device:TPU:0, one launch (start us, length us, event | category | flops | bytes accessed | tf_op | source)
XLA Modules:
  0.0 29.9 jit_solution(16721581567067305863)
XLA Ops:
  0.6 0.5 %collective-permute-start = (f32[8,16,512]{2,1,0:T(8,128)}, f32[8,16,512]{2,1,0:T(8,128)S(1)}, u32[]{:S(2)}, u32[]{:S(2)}) collective-permute-start(f32[8,16,512]{2,1,0:T(8,128)} %bitcast.19), channel_id=1, source_target_pairs={{0,1},{1,0},{2,3},{3,2},{4,5},{5,4},{6,7},{7,6},{8,9},{9,8},{10,11... | collective-permute-start | bytes 786440 | tf_op jit(solution)/shard_map/ppermute | solution.py:490
  1.2 1.7 %begin.1 = (f32[8,16,512]{2,1,0:T(8,128)S(1)}, f32[8,16,512]{2,1,0:T(8,128)S(1)}, f32[8,16,512]{2,1,0:T(8,128)S(1)}, f32[8,16,512]{2,1,0:T(8,128)S(1)}, f32[8,16...) custom-call(f32[8,16,512]{2,1,0:T(8,128)} %bitcast.13, ...), custom_call_target="tpu_custom_call" | custom-call | flops 1 | bytes 1 | tf_op jit(solution)/shard_map/begin/pallas_call | solution.py:32
  3.5 0.0 collective-permute-done.refs_1_.later_ref
  3.5 0.1 rims.1
  3.6 2.7 %collective-permute-start.2 = (f32[6,8,512]{2,1,0:T(8,128)S(1)}, f32[6,8,512]{2,1,0:T(8,128)S(1)}, u32[]{:S(2)}, u32[]{:S(2)}) collective-permute-start(f32[6,8,512]{2,1,0:T(8,128)S(1)} %get-tuple-element.63.second_ref), channel_id=1, source_target_pairs={{0,4},{1,5},{2,6},{3,7},{4,0},{5,1},{6,2},{7,3},{8,9},{9,8},{10,11... | collective-permute-start | bytes 294920 | tf_op jit(solution)/shard_map/ppermute | solution.py:486
  6.3 0.2 forward.1.moved_ref
  6.5 0.3 collective-permute-start.1
  6.8 0.3 %collective-permute-start.3 = (f32[6,8,512]{2,1,0:T(8,128)S(1)}, f32[6,8,512]{2,1,0:T(8,128)S(1)}, u32[]{:S(2)}, u32[]{:S(2)}) collective-permute-start(f32[6,8,512]{2,1,0:T(8,128)S(1)} %get-tuple-element.63.second_ref), channel_id=1, source_target_pairs={{0,1},{1,0},{2,3},{3,2},{4,5},{5,4},{6,7},{7,6},{8,12},{9,13},{10,... | collective-permute-start | bytes 294920 | tf_op jit(solution)/shard_map/ppermute | solution.py:486
  7.2 1.6 %collective-permute-start.5 = (f32[144,512]{1,0:T(8,128)S(1)}, f32[144,512]{1,0:T(8,128)S(1)}, u32[]{:S(2)}, u32[]{:S(2)}) collective-permute-start(f32[144,512]{1,0:T(8,128)S(1)} %pad.4), channel_id=1, source_target_pairs={{0,16},{1,3},{2,18},{3,1},{4,20},{5,7},{6,22},{7,5},{8,24},{9,11},... | collective-permute-start | bytes 884744 | tf_op jit(solution)/shard_map/ppermute | solution.py:486
  8.7 0.4 %spread.1 = (f32[8,16,512]{2,1,0:T(8,128)S(1)}, f32[8,16,512]{2,1,0:T(8,128)S(1)}) custom-call(f32[8,16,512]{2,1,0:T(8,128)S(1)} %get-tuple-element.60.incr_ref, f32[8,16,512]{2,1,0:T(8,128)S(1)} %get-tuple-element.47.mult_ref, f32[8,16,512]{2,1,0:T(8,128)S(1)} %get-tuple-element.64.rhs_ref, f32[8,16,512]{2,1,0:T(8,128)S(1)} %get-tuple-element.65.err_ref, ...), custom_call_target="tpu_custom_call" | custom-call | flops 1 | bytes 1 | tf_op jit(solution)/shard_map/spread/pallas_call | solution.py:32
  9.2 0.7 %adjoint.1.back_ref = f32[8,16,512]{2,1,0:T(8,128)S(1)} custom-call(f32[8,16,512]{2,1,0:T(8,128)S(1)} %get-tuple-element.48.a_ref, f32[8,16,512]{2,1,0:T(8,128)S(1)} %get-tuple-element.49.b_ref, f32[8,16,512]{2,1,0:T(8,128)S(1)} %get-tuple-element.50.c_ref, f32[8,16,512]{2,1,0:T(8,128)S(1)} %collective-permute-done.refs_1_.later_ref), custom_call_target="tpu_custom_call" | custom-call | flops 1 | bytes 1 | tf_op jit(solution)/shard_map/adjoint/pallas_call | solution.py:32
  9.9 0.0 collective-permute-done.3
  9.9 0.0 collective-permute-done.2
  9.9 0.0 collective-permute-done.1.got_first_ref.refs_0_
  9.9 0.3 share.1
  10.2 0.1 collective-permute-start.4
  10.3 1.6 %collective-permute-start.6 = (f32[4,8,512]{2,1,0:T(8,128)S(1)}, f32[4,8,512]{2,1,0:T(8,128)S(1)}, u32[]{:S(2)}, u32[]{:S(2)}) collective-permute-start(f32[4,8,512]{2,1,0:T(8,128)S(1)} %get-tuple-element.76), channel_id=1, source_target_pairs={{0,16},{1,3},{2,18},{3,1},{4,20},{5,7},{6,22},{7,5},{8,24},{9,11},... | collective-permute-start | bytes 196616 | tf_op jit(solution)/shard_map/ppermute | solution.py:486
  11.8 0.0 collective-permute-done.4.got_ref
  11.9 1.5 %collective-permute-start.10 = (f32[8,16,512]{2,1,0:T(8,128)S(1)}, f32[8,16,512]{2,1,0:T(8,128)S(1)}, u32[]{:S(2)}, u32[]{:S(2)}) collective-permute-start(f32[8,16,512]{2,1,0:T(8,128)S(1)} %sends.1), channel_id=1, source_target_pairs={{0,16},{1,3},{2,18},{3,1},{4,20},{5,7},{6,22},{7,5},{8,24},{9,11},... | collective-permute-start | bytes 786440 | tf_op jit(solution)/shard_map/ppermute | solution.py:486
  13.4 0.5 %collective-permute-done.5.cross_ref.refs_3_ = f32[144,512]{1,0:T(8,128)S(1)} collective-permute-done((f32[144,512]{1,0:T(8,128)S(1)}, f32[144,512]{1,0:T(8,128)S(1)}, u32[]{:S(2)}, u32[]{:S(2)}) %collective-permute-start.5) | collective-permute-done | bytes 294944 | tf_op jit(solution)/shard_map/ppermute | solution.py:486
  14.0 0.7 %beyond.1.beyond_ref = f32[8,16,512]{2,1,0:T(8,128)S(1)} custom-call(f32[8,16,512]{2,1,0:T(8,128)S(1)} %get-tuple-element.48.a_ref, f32[8,16,512]{2,1,0:T(8,128)S(1)} %get-tuple-element.49.b_ref, f32[8,16,512]{2,1,0:T(8,128)S(1)} %get-tuple-element.50.c_ref, f32[144,512]{1,0:T(8,128)S(1)} %collective-permute-done.5.cross_ref.refs_3_), custom_call_target="tpu_custom_call" | custom-call | flops 1 | bytes 1 | tf_op jit(solution)/shard_map/beyond/pallas_call | solution.py:32
  14.7 0.4 %gather.1 = (f32[1,512]{1,0:T(1,128)S(1)}, f32[2,1,512]{2,1,0:T(1,128)S(1)}) custom-call(f32[8,16,512]{2,1,0:T(8,128)S(1)} %get-tuple-element.60.incr_ref, s32[1,512]{1,0:T(1,128)S(1)} %get-tuple-element.72.cell_ref, f32[1,512]{1,0:T(1,128)S(1)} %get-tuple-element.61.dual_ref, f32[1,512]{1,0:T(1,128)S(1)} %get-tuple-element.73.want_ref, ...), custom_call_target="tpu_custom_call" | custom-call | flops 1 | bytes 1 | tf_op jit(solution)/shard_map/gather/pallas_call | solution.py:32
  15.1 0.1 rest.1
  15.1 0.1 collective-permute-start.9
  15.2 0.5 %collective-permute-start.7 = (f32[6,16,512]{2,1,0:T(8,128)S(1)}, f32[6,16,512]{2,1,0:T(8,128)S(1)}, u32[]{:S(2)}, u32[]{:S(2)}) collective-permute-start(f32[6,16,512]{2,1,0:T(8,128)S(1)} %get-tuple-element.79), channel_id=1, source_target_pairs={{0,1},{1,0},{2,3},{3,2},{4,5},{5,4},{6,7},{7,6},{8,9},{9,8},{10,11... | collective-permute-start | bytes 589832 | tf_op jit(solution)/shard_map/ppermute | solution.py:490
  15.7 0.1 collective-permute-start.8
  15.8 0.0 collective-permute-done.6.refs_4_.late_ref
  15.8 0.1 late.1.fix_ref
  15.9 0.7 %collective-permute-done.9.refs_2_.rest_ref = f32[5,16,512]{2,1,0:T(8,128)S(1)} collective-permute-done((f32[5,16,512]{2,1,0:T(8,128)S(1)}, f32[5,16,512]{2,1,0:T(8,128)S(1)}, u32[]{:S(2)}, u32[]{:S(2)}) %collective-permute-start.9) | collective-permute-done | bytes 163872 | tf_op jit(solution)/shard_map/ppermute | solution.py:490
  16.6 0.3 collective-permute-done.7.refs_0_
  16.9 0.3 collective-permute-done.8.refs_1_
  17.1 0.2 terms.1
  17.3 1.0 %collective-permute-done.10.got_ref = f32[8,16,512]{2,1,0:T(8,128)S(1)} collective-permute-done((f32[8,16,512]{2,1,0:T(8,128)S(1)}, f32[8,16,512]{2,1,0:T(8,128)S(1)}, u32[]{:S(2)}, u32[]{:S(2)}) %collective-permute-start.10) | collective-permute-done | bytes 262176 | tf_op jit(solution)/shard_map/ppermute | solution.py:486
  18.3 0.2 dots.1
  18.5 1.5 %collective-permute-start.14 = (f32[2,128]{1,0:T(2,128)S(1)}, f32[2,128]{1,0:T(2,128)S(1)}, u32[]{:S(2)}, u32[]{:S(2)}) collective-permute-start(f32[2,128]{1,0:T(2,128)S(1)} %get-tuple-element.87), channel_id=1, source_target_pairs={{0,16},{1,7},{2,18},{3,5},{4,20},{5,3},{6,22},{7,1},{8,24},{9,15},... | collective-permute-start | bytes 3080 | tf_op jit(solution)/shard_map/ppermute | solution.py:486
  20.0 0.6 %collective-permute-start.13 = (f32[2,128]{1,0:T(2,128)S(1)}, f32[2,128]{1,0:T(2,128)S(1)}, u32[]{:S(2)}, u32[]{:S(2)}) collective-permute-start(f32[2,128]{1,0:T(2,128)S(1)} %get-tuple-element.87), channel_id=1, source_target_pairs={{0,16},{1,5},{2,18},{3,7},{4,20},{5,1},{6,22},{7,3},{8,24},{9,13},... | collective-permute-start | bytes 3080 | tf_op jit(solution)/shard_map/ppermute | solution.py:486
  20.6 1.5 %collective-permute-start.12 = (f32[2,128]{1,0:T(2,128)S(1)}, f32[2,128]{1,0:T(2,128)S(1)}, u32[]{:S(2)}, u32[]{:S(2)}) collective-permute-start(f32[2,128]{1,0:T(2,128)S(1)} %get-tuple-element.87), channel_id=1, source_target_pairs={{0,16},{1,3},{2,18},{3,1},{4,20},{5,7},{6,22},{7,5},{8,24},{9,11},... | collective-permute-start | bytes 3080 | tf_op jit(solution)/shard_map/ppermute | solution.py:486
  22.1 0.0 collective-permute-start.11
  22.1 0.1 collective-permute-done.14
  22.2 1.5 %collective-permute-done.13 = f32[2,128]{1,0:T(2,128)S(1)} collective-permute-done((f32[2,128]{1,0:T(2,128)S(1)}, f32[2,128]{1,0:T(2,128)S(1)}, u32[]{:S(2)}, u32[]{:S(2)}) %collective-permute-start.13) | collective-permute-done | bytes 1056 | tf_op jit(solution)/shard_map/ppermute | solution.py:486
  23.6 0.6 %collective-permute-done.12 = f32[2,128]{1,0:T(2,128)S(1)} collective-permute-done((f32[2,128]{1,0:T(2,128)S(1)}, f32[2,128]{1,0:T(2,128)S(1)}, u32[]{:S(2)}, u32[]{:S(2)}) %collective-permute-start.12) | collective-permute-done | bytes 1056 | tf_op jit(solution)/shard_map/ppermute | solution.py:486
  24.2 1.5 %collective-permute-start.15 = (f32[2,128]{1,0:T(2,128)S(1)}, f32[2,128]{1,0:T(2,128)S(1)}, u32[]{:S(2)}, u32[]{:S(2)}) collective-permute-start(f32[2,128]{1,0:T(2,128)S(1)} %add_add_fusion), channel_id=1, source_target_pairs={{0,16},{1,9},{2,18},{3,11},{4,20},{5,13},{6,22},{7,15},{8,24},{9,1... | collective-permute-start | bytes 3080 | tf_op jit(solution)/shard_map/ppermute | solution.py:486
  25.6 2.1 %collective-permute-done.15 = f32[2,128]{1,0:T(2,128)S(1)} collective-permute-done((f32[2,128]{1,0:T(2,128)S(1)}, f32[2,128]{1,0:T(2,128)S(1)}, u32[]{:S(2)}, u32[]{:S(2)}) %collective-permute-start.15) | collective-permute-done | bytes 1056 | tf_op jit(solution)/shard_map/ppermute | solution.py:486
  27.8 0.0 collective-permute-start.16
  27.8 1.1 %collective-permute-done.16 = f32[2,128]{1,0:T(2,128)S(1)} collective-permute-done((f32[2,128]{1,0:T(2,128)S(1)}, f32[2,128]{1,0:T(2,128)S(1)}, u32[]{:S(2)}, u32[]{:S(2)}) %collective-permute-start.16) | collective-permute-done | bytes 1056 | tf_op jit(solution)/shard_map/ppermute | solution.py:490
  28.9 0.0 collective-permute-done.11.got_ref
  28.9 1.0 %update.1 = (f32[8,16,512]{2,1,0:T(8,128)}, f32[8,16,512]{2,1,0:T(8,128)}, f32[1,512]{1,0:T(1,128)}) custom-call(f32[8,16,512]{2,1,0:T(8,128)S(1)} %get-tuple-element.47.mult_ref, f32[8,16,512]{2,1,0:T(8,128)S(1)} %get-tuple-element.60.incr_ref, f32[1,512]{1,0:T(1,128)S(1)} %get-tuple-element.61.dual_ref, f32[1,512]{1,0:T(1,128)S(1)} %get-tuple-element.75.dir_ref, ...), custom_call_target="tpu_custom_call" | custom-call | flops 1 | bytes 1 | tf_op jit(solution)/shard_map/update/pallas_call | solution.py:32
  (8 shorter events, 0.1 us)
Async XLA Ops:
  0.6 2.9 %collective-permute-start = (f32[8,16,512]{2,1,0:T(8,128)}, f32[8,16,512]{2,1,0:T(8,128)S(1)}, u32[]{:S(2)}, u32[]{:S(2)}) collective-permute-start(f32[8,16,512]{2,1,0:T(8,128)} %bitcast.19), channel_id=1, source_target_pairs={{0,1},{1,0},{2,3},{3,2},{4,5},{5,4},{6,7},{7,6},{8,9},{9,8},{10,11... | collective-permute-start | bytes 786440 | tf_op jit(solution)/shard_map/ppermute | solution.py:490
  3.6 6.3 %collective-permute-start.2 = (f32[6,8,512]{2,1,0:T(8,128)S(1)}, f32[6,8,512]{2,1,0:T(8,128)S(1)}, u32[]{:S(2)}, u32[]{:S(2)}) collective-permute-start(f32[6,8,512]{2,1,0:T(8,128)S(1)} %get-tuple-element.63.second_ref), channel_id=1, source_target_pairs={{0,4},{1,5},{2,6},{3,7},{4,0},{5,1},{6,2},{7,3},{8,9},{9,8},{10,11... | collective-permute-start | bytes 294920 | tf_op jit(solution)/shard_map/ppermute | solution.py:486
  6.5 3.4 %collective-permute-start.1 = (f32[6,8,512]{2,1,0:T(8,128)S(1)}, f32[6,8,512]{2,1,0:T(8,128)S(1)}, u32[]{:S(2)}, u32[]{:S(2)}) collective-permute-start(f32[6,8,512]{2,1,0:T(8,128)S(1)} %get-tuple-element.62.first_ref), channel_id=1, source_target_pairs={{0,1},{1,0},{2,3},{3,2},{4,8},{5,9},{6,10},{7,11},{8,4},{9,5},{10,... | collective-permute-start | bytes 294920 | tf_op jit(solution)/shard_map/ppermute | solution.py:486
  6.8 3.1 %collective-permute-start.3 = (f32[6,8,512]{2,1,0:T(8,128)S(1)}, f32[6,8,512]{2,1,0:T(8,128)S(1)}, u32[]{:S(2)}, u32[]{:S(2)}) collective-permute-start(f32[6,8,512]{2,1,0:T(8,128)S(1)} %get-tuple-element.63.second_ref), channel_id=1, source_target_pairs={{0,1},{1,0},{2,3},{3,2},{4,5},{5,4},{6,7},{7,6},{8,12},{9,13},{10,... | collective-permute-start | bytes 294920 | tf_op jit(solution)/shard_map/ppermute | solution.py:486
  7.2 6.8 %collective-permute-start.5 = (f32[144,512]{1,0:T(8,128)S(1)}, f32[144,512]{1,0:T(8,128)S(1)}, u32[]{:S(2)}, u32[]{:S(2)}) collective-permute-start(f32[144,512]{1,0:T(8,128)S(1)} %pad.4), channel_id=1, source_target_pairs={{0,16},{1,3},{2,18},{3,1},{4,20},{5,7},{6,22},{7,5},{8,24},{9,11},... | collective-permute-start | bytes 884744 | tf_op jit(solution)/shard_map/ppermute | solution.py:486
  10.2 1.7 %collective-permute-start.4 = (f32[8,16,512]{2,1,0:T(8,128)S(1)}, f32[8,16,512]{2,1,0:T(8,128)S(1)}, u32[]{:S(2)}, u32[]{:S(2)}) collective-permute-start(f32[8,16,512]{2,1,0:T(8,128)S(1)} %get-tuple-element.71), channel_id=1, source_target_pairs={{0,1},{1,0},{2,3},{3,2},{4,5},{5,4},{6,7},{7,6},{8,9},{9,8},{10,11... | collective-permute-start | bytes 786440 | tf_op jit(solution)/shard_map/ppermute | solution.py:490
  10.3 5.5 %collective-permute-start.6 = (f32[4,8,512]{2,1,0:T(8,128)S(1)}, f32[4,8,512]{2,1,0:T(8,128)S(1)}, u32[]{:S(2)}, u32[]{:S(2)}) collective-permute-start(f32[4,8,512]{2,1,0:T(8,128)S(1)} %get-tuple-element.76), channel_id=1, source_target_pairs={{0,16},{1,3},{2,18},{3,1},{4,20},{5,7},{6,22},{7,5},{8,24},{9,11},... | collective-permute-start | bytes 196616 | tf_op jit(solution)/shard_map/ppermute | solution.py:486
  11.9 6.4 %collective-permute-start.10 = (f32[8,16,512]{2,1,0:T(8,128)S(1)}, f32[8,16,512]{2,1,0:T(8,128)S(1)}, u32[]{:S(2)}, u32[]{:S(2)}) collective-permute-start(f32[8,16,512]{2,1,0:T(8,128)S(1)} %sends.1), channel_id=1, source_target_pairs={{0,16},{1,3},{2,18},{3,1},{4,20},{5,7},{6,22},{7,5},{8,24},{9,11},... | collective-permute-start | bytes 786440 | tf_op jit(solution)/shard_map/ppermute | solution.py:486
  15.1 1.5 %collective-permute-start.9 = (f32[5,16,512]{2,1,0:T(8,128)S(1)}, f32[5,16,512]{2,1,0:T(8,128)S(1)}, u32[]{:S(2)}, u32[]{:S(2)}) collective-permute-start(f32[5,16,512]{2,1,0:T(8,128)S(1)} %get-tuple-element.81), channel_id=1, source_target_pairs={{0,1},{1,0},{2,3},{3,2},{4,5},{5,4},{6,7},{7,6},{8,9},{9,8},{10,11... | collective-permute-start | bytes 491528 | tf_op jit(solution)/shard_map/ppermute | solution.py:490
  15.2 1.7 %collective-permute-start.7 = (f32[6,16,512]{2,1,0:T(8,128)S(1)}, f32[6,16,512]{2,1,0:T(8,128)S(1)}, u32[]{:S(2)}, u32[]{:S(2)}) collective-permute-start(f32[6,16,512]{2,1,0:T(8,128)S(1)} %get-tuple-element.79), channel_id=1, source_target_pairs={{0,1},{1,0},{2,3},{3,2},{4,5},{5,4},{6,7},{7,6},{8,9},{9,8},{10,11... | collective-permute-start | bytes 589832 | tf_op jit(solution)/shard_map/ppermute | solution.py:490
  15.7 1.4 %collective-permute-start.8 = (f32[6,16,512]{2,1,0:T(8,128)S(1)}, f32[6,16,512]{2,1,0:T(8,128)S(1)}, u32[]{:S(2)}, u32[]{:S(2)}) collective-permute-start(f32[6,16,512]{2,1,0:T(8,128)S(1)} %get-tuple-element.80), channel_id=1, source_target_pairs={{0,1},{1,0},{2,3},{3,2},{4,5},{5,4},{6,7},{7,6},{8,9},{9,8},{10,11... | collective-permute-start | bytes 589832 | tf_op jit(solution)/shard_map/ppermute | solution.py:490
  18.5 3.6 %collective-permute-start.14 = (f32[2,128]{1,0:T(2,128)S(1)}, f32[2,128]{1,0:T(2,128)S(1)}, u32[]{:S(2)}, u32[]{:S(2)}) collective-permute-start(f32[2,128]{1,0:T(2,128)S(1)} %get-tuple-element.87), channel_id=1, source_target_pairs={{0,16},{1,7},{2,18},{3,5},{4,20},{5,3},{6,22},{7,1},{8,24},{9,15},... | collective-permute-start | bytes 3080 | tf_op jit(solution)/shard_map/ppermute | solution.py:486
  20.0 3.6 %collective-permute-start.13 = (f32[2,128]{1,0:T(2,128)S(1)}, f32[2,128]{1,0:T(2,128)S(1)}, u32[]{:S(2)}, u32[]{:S(2)}) collective-permute-start(f32[2,128]{1,0:T(2,128)S(1)} %get-tuple-element.87), channel_id=1, source_target_pairs={{0,16},{1,5},{2,18},{3,7},{4,20},{5,1},{6,22},{7,3},{8,24},{9,13},... | collective-permute-start | bytes 3080 | tf_op jit(solution)/shard_map/ppermute | solution.py:486
  20.6 3.6 %collective-permute-start.12 = (f32[2,128]{1,0:T(2,128)S(1)}, f32[2,128]{1,0:T(2,128)S(1)}, u32[]{:S(2)}, u32[]{:S(2)}) collective-permute-start(f32[2,128]{1,0:T(2,128)S(1)} %get-tuple-element.87), channel_id=1, source_target_pairs={{0,16},{1,3},{2,18},{3,1},{4,20},{5,7},{6,22},{7,5},{8,24},{9,11},... | collective-permute-start | bytes 3080 | tf_op jit(solution)/shard_map/ppermute | solution.py:486
  22.1 6.8 %collective-permute-start.11 = (f32[8,16,512]{2,1,0:T(8,128)S(1)}, f32[8,16,512]{2,1,0:T(8,128)S(1)}, u32[]{:S(2)}, u32[]{:S(2)}) collective-permute-start(f32[8,16,512]{2,1,0:T(8,128)S(1)} %get-tuple-element.86), channel_id=1, source_target_pairs={{0,1},{1,0},{2,3},{3,2},{4,5},{5,4},{6,7},{7,6},{8,9},{9,8},{10,11... | collective-permute-start | bytes 786440 | tf_op jit(solution)/shard_map/ppermute | solution.py:490
  24.2 3.6 %collective-permute-start.15 = (f32[2,128]{1,0:T(2,128)S(1)}, f32[2,128]{1,0:T(2,128)S(1)}, u32[]{:S(2)}, u32[]{:S(2)}) collective-permute-start(f32[2,128]{1,0:T(2,128)S(1)} %add_add_fusion), channel_id=1, source_target_pairs={{0,16},{1,9},{2,18},{3,11},{4,20},{5,13},{6,22},{7,15},{8,24},{9,1... | collective-permute-start | bytes 3080 | tf_op jit(solution)/shard_map/ppermute | solution.py:486
  27.8 1.1 %collective-permute-start.16 = (f32[2,128]{1,0:T(2,128)S(1)}, f32[2,128]{1,0:T(2,128)S(1)}, u32[]{:S(2)}, u32[]{:S(2)}) collective-permute-start(f32[2,128]{1,0:T(2,128)S(1)} %add.26), channel_id=1, source_target_pairs={{0,1},{1,0},{2,3},{3,2},{4,5},{5,4},{6,7},{7,6},{8,9},{9,8},{10,11... | collective-permute-start | bytes 3080 | tf_op jit(solution)/shard_map/ppermute | solution.py:490

commit v9 on v8

--- a/solution.py
+++ b/solution.py
@@ -431,30 +431,47 @@
         known_ref[lev] = jnp.where(low_pair, local, residual + got)
 
 
-def dots_body(terms_ref, got_ref, rest_ref, obs_ref, keep_ref, give_ref, sums_ref):
-    _, levels, rows, cols = terms_ref.shape
+def folded(x):
+    total = None
+    for r in range(0, x.shape[0], 8):
+        part = lanes(x[r : r + 8])
+        total = part if total is None else total + part
+    return total
+
+
+def early_body(terms_ref, rest_ref, obs_ref, sums_ref):
+    levels, last = terms_ref.shape[1], rest_ref.shape[0] - 1
+    numer, denom = jnp.zeros((8, 128), F32), jnp.zeros((8, 128), F32)
+    for lev in range(levels):
+        y0, one = terms_ref[0, lev], terms_ref[1, lev]
+        numer = numer + folded(y0 * y0 + (one - y0) * one)
+        denom = denom + folded(y0 * y0 + one * one)
+    for n, total in enumerate((numer, denom)):
+        obs = lanes(obs_ref[n]) + rest_ref[last, n : n + 1, 0:128]
+        sums_ref[n : n + 1] = jnp.sum(total, axis=0, keepdims=True) + obs
+
+
+def dots_body(terms_ref, got_ref, early_ref, sums_ref):
+    numer, denom = jnp.zeros((8, 128), F32), jnp.zeros((8, 128), F32)
+    for lev in range(got_ref.shape[0]):
+        z0, z1 = terms_ref[2, lev], terms_ref[3, lev]
+        two = got_ref[lev] + z0
+        three = two + z1
+        numer = numer + folded(z0 * two + z1 * three)
+        denom = denom + folded(two * two + three * three)
+    for n, total in enumerate((numer, denom)):
+        sums_ref[n : n + 1] = early_ref[n : n + 1] + jnp.sum(total, axis=0, keepdims=True)
+
+
+def directions_body(terms_ref, got_ref, keep_ref, give_ref):
     low_pair = lax.axis_index("tm") < 2
-    numer, denom = jnp.zeros((8, 128), F32), jnp.zeros((8, 128), F32)
-
-    def folded(x):
-        total = None
-        for r in range(0, rows, 8):
-            part = lanes(x[r : r + 8])
-            total = part if total is None else total + part
-        return total
-
-    for lev in range(levels):
+    for lev in range(got_ref.shape[0]):
         y0, one, z0, z1 = (terms_ref[n, lev] for n in range(4))
         two = got_ref[lev] + z0
         three = two + z1
-        numer = numer + folded(y0 * y0 + (one - y0) * one + z0 * two + z1 * three)
-        denom = denom + folded(y0 * y0 + one * one + two * two + three * three)
         keep_ref[0, lev] = jnp.where(low_pair, one, three)
         keep_ref[1, lev] = jnp.where(low_pair, two, y0)
         give_ref[lev] = jnp.where(low_pair, three, two)
-    for n, total in enumerate((numer, denom)):
-        obs = lanes(obs_ref[n]) + rest_ref[rest_ref.shape[0] - 1, n : n + 1, 0:128]
-        sums_ref[n : n + 1] = jnp.sum(total, axis=0, keepdims=True) + obs
 
 
 def update_body(
@@ -638,8 +655,12 @@
         [((4, levels, rows, cols), "near"), field],
     )
     pair = ((2, levels, rows, cols), "near")
-    keep, give, sums = kernel_call(
-        dots_body, "dots", near(terms, got_send, got_rest[-1], obs_sums), [pair, field, ((2, 128), "near")]
+    line = ((2, 128), "near")
+    early = kernel_call(early_body, "early", near(terms, got_rest[-1], obs_sums), [line])[0]
+    sums = kernel_call(dots_body, "dots", near(terms, got_send, early), [line])[0]
+    terms, got_send, sums = lax.optimization_barrier((terms, got_send, sums))
+    keep, give = kernel_call(
+        directions_body, "directions", near(terms, got_send), [pair, field]
     )
     total = sums + leaders(sums, 0, 2) + leaders(sums, 1, 0) + leaders(sums, 1, 2)
     distance = 2

time: 30 us -> 29.9 us (level)
    pallas_call x14 -> x16, Pallas kernels: 5.99 us -> 6.03 us  [kernel_call(): pl.pallas_call(body, name=name, out_shape=out_shape, in_specs=in_specs, o...]
  transfers between devices with their start and end apart: 17 -> 17, of which waited for: 10 -> 9; matrix products, arithmetic and copies ran while one was open for 0% -> 0% of each run, Pallas kernels for 16% -> 16%
where the time goes in v9:
time: 29.9 us; the launch traced here: 29.8 us
  starting transfers between devices  14.2 us (47%)
  waiting for transfers between devices  7.94 us (27%)
  Pallas kernels  6.03 us (20%)
  between operations  1.49 us (5%)
    ppermute x10, starting transfers between devices, exchange(): return lax.ppermute(value, ('groups', 'tile', 'tm'), pairs)  12.9 us
    pallas_call x16, Pallas kernels, kernel_call(): pl.pallas_call(body, name=name, out_shape=out_shape, in_specs=in_specs, o...  6.03 us
    ppermute x10, waiting for transfers between devices, exchange(): return lax.ppermute(value, ('groups', 'tile', 'tm'), pairs)  5.56 us
    ppermute x7, waiting for transfers between devices, swap(): lax.ppermute(value, axis, [(i, i ^ distance) for i in range(lax.axis_size...  2.39 us
    ppermute x7, starting transfers between devices, swap(): lax.ppermute(value, axis, [(i, i ^ distance) for i in range(lax.axis_size...  1.31 us
  transfers between devices with their start and end apart: 17, of which 9 were waited for; matrix products, arithmetic and copies ran while one was open for 0% of the time, Pallas kernels for 16%

profile of v9, /device:TPU:0, one launch (start us, length us, event | category | flops | bytes accessed | tf_op | source)
XLA Modules:
  0.0 29.8 jit_solution(9253349589211483852)
XLA Ops:
  0.6 0.5 %collective-permute-start = (f32[8,16,512]{2,1,0:T(8,128)}, f32[8,16,512]{2,1,0:T(8,128)S(1)}, u32[]{:S(2)}, u32[]{:S(2)}) collective-permute-start(f32[8,16,512]{2,1,0:T(8,128)} %bitcast.19), channel_id=1, source_target_pairs={{0,1},{1,0},{2,3},{3,2},{4,5},{5,4},{6,7},{7,6},{8,9},{9,8},{10,11... | collective-permute-start | bytes 786440 | tf_op jit(solution)/shard_map/ppermute | solution.py:507
  1.2 1.7 %begin.1 = (f32[8,16,512]{2,1,0:T(8,128)S(1)}, f32[8,16,512]{2,1,0:T(8,128)S(1)}, f32[8,16,512]{2,1,0:T(8,128)S(1)}, f32[8,16,512]{2,1,0:T(8,128)S(1)}, f32[8,16...) custom-call(f32[8,16,512]{2,1,0:T(8,128)} %bitcast.13, ...), custom_call_target="tpu_custom_call" | custom-call | flops 1 | bytes 1 | tf_op jit(solution)/shard_map/begin/pallas_call | solution.py:32
  3.5 0.0 collective-permute-done.refs_1_.later_ref
  3.5 0.1 rims.1
  3.6 2.7 %collective-permute-start.2 = (f32[6,8,512]{2,1,0:T(8,128)S(1)}, f32[6,8,512]{2,1,0:T(8,128)S(1)}, u32[]{:S(2)}, u32[]{:S(2)}) collective-permute-start(f32[6,8,512]{2,1,0:T(8,128)S(1)} %get-tuple-element.65.second_ref), channel_id=1, source_target_pairs={{0,4},{1,5},{2,6},{3,7},{4,0},{5,1},{6,2},{7,3},{8,9},{9,8},{10,11... | collective-permute-start | bytes 294920 | tf_op jit(solution)/shard_map/ppermute | solution.py:503
  6.3 0.2 forward.1.moved_ref
  6.5 0.3 collective-permute-start.1
  6.8 0.3 %collective-permute-start.3 = (f32[6,8,512]{2,1,0:T(8,128)S(1)}, f32[6,8,512]{2,1,0:T(8,128)S(1)}, u32[]{:S(2)}, u32[]{:S(2)}) collective-permute-start(f32[6,8,512]{2,1,0:T(8,128)S(1)} %get-tuple-element.65.second_ref), channel_id=1, source_target_pairs={{0,1},{1,0},{2,3},{3,2},{4,5},{5,4},{6,7},{7,6},{8,12},{9,13},{10,... | collective-permute-start | bytes 294920 | tf_op jit(solution)/shard_map/ppermute | solution.py:503
  7.2 1.6 %collective-permute-start.5 = (f32[144,512]{1,0:T(8,128)S(1)}, f32[144,512]{1,0:T(8,128)S(1)}, u32[]{:S(2)}, u32[]{:S(2)}) collective-permute-start(f32[144,512]{1,0:T(8,128)S(1)} %pad.4), channel_id=1, source_target_pairs={{0,16},{1,3},{2,18},{3,1},{4,20},{5,7},{6,22},{7,5},{8,24},{9,11},... | collective-permute-start | bytes 884744 | tf_op jit(solution)/shard_map/ppermute | solution.py:503
  8.7 0.4 %spread.1 = (f32[8,16,512]{2,1,0:T(8,128)S(1)}, f32[8,16,512]{2,1,0:T(8,128)S(1)}) custom-call(f32[8,16,512]{2,1,0:T(8,128)S(1)} %get-tuple-element.62.incr_ref, f32[8,16,512]{2,1,0:T(8,128)S(1)} %get-tuple-element.49.mult_ref, f32[8,16,512]{2,1,0:T(8,128)S(1)} %get-tuple-element.66.rhs_ref, f32[8,16,512]{2,1,0:T(8,128)S(1)} %get-tuple-element.67.err_ref, ...), custom_call_target="tpu_custom_call" | custom-call | flops 1 | bytes 1 | tf_op jit(solution)/shard_map/spread/pallas_call | solution.py:32
  9.2 0.7 %adjoint.1.back_ref = f32[8,16,512]{2,1,0:T(8,128)S(1)} custom-call(f32[8,16,512]{2,1,0:T(8,128)S(1)} %get-tuple-element.50.a_ref, f32[8,16,512]{2,1,0:T(8,128)S(1)} %get-tuple-element.51.b_ref, f32[8,16,512]{2,1,0:T(8,128)S(1)} %get-tuple-element.52.c_ref, f32[8,16,512]{2,1,0:T(8,128)S(1)} %collective-permute-done.refs_1_.later_ref), custom_call_target="tpu_custom_call" | custom-call | flops 1 | bytes 1 | tf_op jit(solution)/shard_map/adjoint/pallas_call | solution.py:32
  9.9 0.0 collective-permute-done.3
  9.9 0.0 collective-permute-done.2
  9.9 0.0 collective-permute-done.1.got_first_ref.refs_0_
  9.9 0.3 share.1
  10.2 0.1 collective-permute-start.4
  10.3 1.6 %collective-permute-start.6 = (f32[4,8,512]{2,1,0:T(8,128)S(1)}, f32[4,8,512]{2,1,0:T(8,128)S(1)}, u32[]{:S(2)}, u32[]{:S(2)}) collective-permute-start(f32[4,8,512]{2,1,0:T(8,128)S(1)} %get-tuple-element.78), channel_id=1, source_target_pairs={{0,16},{1,3},{2,18},{3,1},{4,20},{5,7},{6,22},{7,5},{8,24},{9,11},... | collective-permute-start | bytes 196616 | tf_op jit(solution)/shard_map/ppermute | solution.py:503
  11.8 0.0 collective-permute-done.4.got_ref
  11.9 1.5 %collective-permute-start.10 = (f32[8,16,512]{2,1,0:T(8,128)S(1)}, f32[8,16,512]{2,1,0:T(8,128)S(1)}, u32[]{:S(2)}, u32[]{:S(2)}) collective-permute-start(f32[8,16,512]{2,1,0:T(8,128)S(1)} %sends.1), channel_id=1, source_target_pairs={{0,16},{1,3},{2,18},{3,1},{4,20},{5,7},{6,22},{7,5},{8,24},{9,11},... | collective-permute-start | bytes 786440 | tf_op jit(solution)/shard_map/ppermute | solution.py:503
  13.4 0.5 %collective-permute-done.5.cross_ref.refs_3_ = f32[144,512]{1,0:T(8,128)S(1)} collective-permute-done((f32[144,512]{1,0:T(8,128)S(1)}, f32[144,512]{1,0:T(8,128)S(1)}, u32[]{:S(2)}, u32[]{:S(2)}) %collective-permute-start.5) | collective-permute-done | bytes 294944 | tf_op jit(solution)/shard_map/ppermute | solution.py:503
  14.0 0.7 %beyond.1.beyond_ref = f32[8,16,512]{2,1,0:T(8,128)S(1)} custom-call(f32[8,16,512]{2,1,0:T(8,128)S(1)} %get-tuple-element.50.a_ref, f32[8,16,512]{2,1,0:T(8,128)S(1)} %get-tuple-element.51.b_ref, f32[8,16,512]{2,1,0:T(8,128)S(1)} %get-tuple-element.52.c_ref, f32[144,512]{1,0:T(8,128)S(1)} %collective-permute-done.5.cross_ref.refs_3_), custom_call_target="tpu_custom_call" | custom-call | flops 1 | bytes 1 | tf_op jit(solution)/shard_map/beyond/pallas_call | solution.py:32
  14.7 0.4 %gather.1 = (f32[1,512]{1,0:T(1,128)S(1)}, f32[2,1,512]{2,1,0:T(1,128)S(1)}) custom-call(f32[8,16,512]{2,1,0:T(8,128)S(1)} %get-tuple-element.62.incr_ref, s32[1,512]{1,0:T(1,128)S(1)} %get-tuple-element.74.cell_ref, f32[1,512]{1,0:T(1,128)S(1)} %get-tuple-element.63.dual_ref, f32[1,512]{1,0:T(1,128)S(1)} %get-tuple-element.75.want_ref, ...), custom_call_target="tpu_custom_call" | custom-call | flops 1 | bytes 1 | tf_op jit(solution)/shard_map/gather/pallas_call | solution.py:32
  15.1 0.1 rest.1
  15.1 0.1 collective-permute-start.9
  15.2 0.5 %collective-permute-start.7 = (f32[6,16,512]{2,1,0:T(8,128)S(1)}, f32[6,16,512]{2,1,0:T(8,128)S(1)}, u32[]{:S(2)}, u32[]{:S(2)}) collective-permute-start(f32[6,16,512]{2,1,0:T(8,128)S(1)} %get-tuple-element.81), channel_id=1, source_target_pairs={{0,1},{1,0},{2,3},{3,2},{4,5},{5,4},{6,7},{7,6},{8,9},{9,8},{10,11... | collective-permute-start | bytes 589832 | tf_op jit(solution)/shard_map/ppermute | solution.py:507
  15.7 0.1 collective-permute-start.8
  15.8 0.0 collective-permute-done.6.refs_4_.late_ref
  15.8 0.1 late.1.fix_ref
  15.9 0.7 %collective-permute-done.9.refs_2_.rest_ref = f32[5,16,512]{2,1,0:T(8,128)S(1)} collective-permute-done((f32[5,16,512]{2,1,0:T(8,128)S(1)}, f32[5,16,512]{2,1,0:T(8,128)S(1)}, u32[]{:S(2)}, u32[]{:S(2)}) %collective-permute-start.9) | collective-permute-done | bytes 163872 | tf_op jit(solution)/shard_map/ppermute | solution.py:507
  16.6 0.3 collective-permute-done.7.refs_0_
  16.9 0.3 collective-permute-done.8.refs_1_
  17.1 0.2 terms.1
  17.3 0.1 early.1.early_ref
  17.4 0.9 %collective-permute-done.10.got_ref = f32[8,16,512]{2,1,0:T(8,128)S(1)} collective-permute-done((f32[8,16,512]{2,1,0:T(8,128)S(1)}, f32[8,16,512]{2,1,0:T(8,128)S(1)}, u32[]{:S(2)}, u32[]{:S(2)}) %collective-permute-start.10) | collective-permute-done | bytes 262176 | tf_op jit(solution)/shard_map/ppermute | solution.py:503
  18.3 0.1 dots.1
  18.4 1.5 %collective-permute-start.14 = (f32[2,128]{1,0:T(2,128)S(1)}, f32[2,128]{1,0:T(2,128)S(1)}, u32[]{:S(2)}, u32[]{:S(2)}) collective-permute-start(f32[2,128]{1,0:T(2,128)S(1)} %dots.1), channel_id=1, source_target_pairs={{0,16},{1,7},{2,18},{3,5},{4,20},{5,3},{6,22},{7,1},{8,24},{9,15},... | collective-permute-start | bytes 3080 | tf_op jit(solution)/shard_map/ppermute | solution.py:503
  20.0 0.6 %collective-permute-start.13 = (f32[2,128]{1,0:T(2,128)S(1)}, f32[2,128]{1,0:T(2,128)S(1)}, u32[]{:S(2)}, u32[]{:S(2)}) collective-permute-start(f32[2,128]{1,0:T(2,128)S(1)} %dots.1), channel_id=1, source_target_pairs={{0,16},{1,5},{2,18},{3,7},{4,20},{5,1},{6,22},{7,3},{8,24},{9,13},... | collective-permute-start | bytes 3080 | tf_op jit(solution)/shard_map/ppermute | solution.py:503
  20.5 1.5 %collective-permute-start.12 = (f32[2,128]{1,0:T(2,128)S(1)}, f32[2,128]{1,0:T(2,128)S(1)}, u32[]{:S(2)}, u32[]{:S(2)}) collective-permute-start(f32[2,128]{1,0:T(2,128)S(1)} %dots.1), channel_id=1, source_target_pairs={{0,16},{1,3},{2,18},{3,1},{4,20},{5,7},{6,22},{7,5},{8,24},{9,11},... | collective-permute-start | bytes 3080 | tf_op jit(solution)/shard_map/ppermute | solution.py:503
  22.0 0.1 directions.1
  22.1 0.1 collective-permute-start.11
  22.1 0.0 collective-permute-done.14
  22.1 1.4 %collective-permute-done.13 = f32[2,128]{1,0:T(2,128)S(1)} collective-permute-done((f32[2,128]{1,0:T(2,128)S(1)}, f32[2,128]{1,0:T(2,128)S(1)}, u32[]{:S(2)}, u32[]{:S(2)}) %collective-permute-start.13) | collective-permute-done | bytes 1056 | tf_op jit(solution)/shard_map/ppermute | solution.py:503
  23.5 0.6 %collective-permute-done.12 = f32[2,128]{1,0:T(2,128)S(1)} collective-permute-done((f32[2,128]{1,0:T(2,128)S(1)}, f32[2,128]{1,0:T(2,128)S(1)}, u32[]{:S(2)}, u32[]{:S(2)}) %collective-permute-start.12) | collective-permute-done | bytes 1056 | tf_op jit(solution)/shard_map/ppermute | solution.py:503
  24.1 1.5 %collective-permute-start.15 = (f32[2,128]{1,0:T(2,128)S(1)}, f32[2,128]{1,0:T(2,128)S(1)}, u32[]{:S(2)}, u32[]{:S(2)}) collective-permute-start(f32[2,128]{1,0:T(2,128)S(1)} %add_add_fusion), channel_id=1, source_target_pairs={{0,16},{1,9},{2,18},{3,11},{4,20},{5,13},{6,22},{7,15},{8,24},{9,1... | collective-permute-start | bytes 3080 | tf_op jit(solution)/shard_map/ppermute | solution.py:503
  25.6 2.1 %collective-permute-done.15 = f32[2,128]{1,0:T(2,128)S(1)} collective-permute-done((f32[2,128]{1,0:T(2,128)S(1)}, f32[2,128]{1,0:T(2,128)S(1)}, u32[]{:S(2)}, u32[]{:S(2)}) %collective-permute-start.15) | collective-permute-done | bytes 1056 | tf_op jit(solution)/shard_map/ppermute | solution.py:503
  27.7 0.0 collective-permute-start.16
  27.7 1.1 %collective-permute-done.16 = f32[2,128]{1,0:T(2,128)S(1)} collective-permute-done((f32[2,128]{1,0:T(2,128)S(1)}, f32[2,128]{1,0:T(2,128)S(1)}, u32[]{:S(2)}, u32[]{:S(2)}) %collective-permute-start.16) | collective-permute-done | bytes 1056 | tf_op jit(solution)/shard_map/ppermute | solution.py:507
  28.8 0.0 collective-permute-done.11.got_ref
  28.8 1.0 %update.1 = (f32[8,16,512]{2,1,0:T(8,128)}, f32[8,16,512]{2,1,0:T(8,128)}, f32[1,512]{1,0:T(1,128)}) custom-call(f32[8,16,512]{2,1,0:T(8,128)S(1)} %get-tuple-element.49.mult_ref, f32[8,16,512]{2,1,0:T(8,128)S(1)} %get-tuple-element.62.incr_ref, f32[1,512]{1,0:T(1,128)S(1)} %get-tuple-element.63.dual_ref, f32[1,512]{1,0:T(1,128)S(1)} %get-tuple-element.77.dir_ref, ...), custom_call_target="tpu_custom_call" | custom-call | flops 1 | bytes 1 | tf_op jit(solution)/shard_map/update/pallas_call | solution.py:32
  (8 shorter events, 0.1 us)
Async XLA Ops:
  0.6 2.9 %collective-permute-start = (f32[8,16,512]{2,1,0:T(8,128)}, f32[8,16,512]{2,1,0:T(8,128)S(1)}, u32[]{:S(2)}, u32[]{:S(2)}) collective-permute-start(f32[8,16,512]{2,1,0:T(8,128)} %bitcast.19), channel_id=1, source_target_pairs={{0,1},{1,0},{2,3},{3,2},{4,5},{5,4},{6,7},{7,6},{8,9},{9,8},{10,11... | collective-permute-start | bytes 786440 | tf_op jit(solution)/shard_map/ppermute | solution.py:507
  3.6 6.3 %collective-permute-start.2 = (f32[6,8,512]{2,1,0:T(8,128)S(1)}, f32[6,8,512]{2,1,0:T(8,128)S(1)}, u32[]{:S(2)}, u32[]{:S(2)}) collective-permute-start(f32[6,8,512]{2,1,0:T(8,128)S(1)} %get-tuple-element.65.second_ref), channel_id=1, source_target_pairs={{0,4},{1,5},{2,6},{3,7},{4,0},{5,1},{6,2},{7,3},{8,9},{9,8},{10,11... | collective-permute-start | bytes 294920 | tf_op jit(solution)/shard_map/ppermute | solution.py:503
  6.5 3.4 %collective-permute-start.1 = (f32[6,8,512]{2,1,0:T(8,128)S(1)}, f32[6,8,512]{2,1,0:T(8,128)S(1)}, u32[]{:S(2)}, u32[]{:S(2)}) collective-permute-start(f32[6,8,512]{2,1,0:T(8,128)S(1)} %get-tuple-element.64.first_ref), channel_id=1, source_target_pairs={{0,1},{1,0},{2,3},{3,2},{4,8},{5,9},{6,10},{7,11},{8,4},{9,5},{10,... | collective-permute-start | bytes 294920 | tf_op jit(solution)/shard_map/ppermute | solution.py:503
  6.8 3.1 %collective-permute-start.3 = (f32[6,8,512]{2,1,0:T(8,128)S(1)}, f32[6,8,512]{2,1,0:T(8,128)S(1)}, u32[]{:S(2)}, u32[]{:S(2)}) collective-permute-start(f32[6,8,512]{2,1,0:T(8,128)S(1)} %get-tuple-element.65.second_ref), channel_id=1, source_target_pairs={{0,1},{1,0},{2,3},{3,2},{4,5},{5,4},{6,7},{7,6},{8,12},{9,13},{10,... | collective-permute-start | bytes 294920 | tf_op jit(solution)/shard_map/ppermute | solution.py:503
  7.2 6.8 %collective-permute-start.5 = (f32[144,512]{1,0:T(8,128)S(1)}, f32[144,512]{1,0:T(8,128)S(1)}, u32[]{:S(2)}, u32[]{:S(2)}) collective-permute-start(f32[144,512]{1,0:T(8,128)S(1)} %pad.4), channel_id=1, source_target_pairs={{0,16},{1,3},{2,18},{3,1},{4,20},{5,7},{6,22},{7,5},{8,24},{9,11},... | collective-permute-start | bytes 884744 | tf_op jit(solution)/shard_map/ppermute | solution.py:503
  10.2 1.7 %collective-permute-start.4 = (f32[8,16,512]{2,1,0:T(8,128)S(1)}, f32[8,16,512]{2,1,0:T(8,128)S(1)}, u32[]{:S(2)}, u32[]{:S(2)}) collective-permute-start(f32[8,16,512]{2,1,0:T(8,128)S(1)} %get-tuple-element.73), channel_id=1, source_target_pairs={{0,1},{1,0},{2,3},{3,2},{4,5},{5,4},{6,7},{7,6},{8,9},{9,8},{10,11... | collective-permute-start | bytes 786440 | tf_op jit(solution)/shard_map/ppermute | solution.py:507
  10.3 5.5 %collective-permute-start.6 = (f32[4,8,512]{2,1,0:T(8,128)S(1)}, f32[4,8,512]{2,1,0:T(8,128)S(1)}, u32[]{:S(2)}, u32[]{:S(2)}) collective-permute-start(f32[4,8,512]{2,1,0:T(8,128)S(1)} %get-tuple-element.78), channel_id=1, source_target_pairs={{0,16},{1,3},{2,18},{3,1},{4,20},{5,7},{6,22},{7,5},{8,24},{9,11},... | collective-permute-start | bytes 196616 | tf_op jit(solution)/shard_map/ppermute | solution.py:503
  11.9 6.4 %collective-permute-start.10 = (f32[8,16,512]{2,1,0:T(8,128)S(1)}, f32[8,16,512]{2,1,0:T(8,128)S(1)}, u32[]{:S(2)}, u32[]{:S(2)}) collective-permute-start(f32[8,16,512]{2,1,0:T(8,128)S(1)} %sends.1), channel_id=1, source_target_pairs={{0,16},{1,3},{2,18},{3,1},{4,20},{5,7},{6,22},{7,5},{8,24},{9,11},... | collective-permute-start | bytes 786440 | tf_op jit(solution)/shard_map/ppermute | solution.py:503
  15.1 1.5 %collective-permute-start.9 = (f32[5,16,512]{2,1,0:T(8,128)S(1)}, f32[5,16,512]{2,1,0:T(8,128)S(1)}, u32[]{:S(2)}, u32[]{:S(2)}) collective-permute-start(f32[5,16,512]{2,1,0:T(8,128)S(1)} %get-tuple-element.83), channel_id=1, source_target_pairs={{0,1},{1,0},{2,3},{3,2},{4,5},{5,4},{6,7},{7,6},{8,9},{9,8},{10,11... | collective-permute-start | bytes 491528 | tf_op jit(solution)/shard_map/ppermute | solution.py:507
  15.2 1.7 %collective-permute-start.7 = (f32[6,16,512]{2,1,0:T(8,128)S(1)}, f32[6,16,512]{2,1,0:T(8,128)S(1)}, u32[]{:S(2)}, u32[]{:S(2)}) collective-permute-start(f32[6,16,512]{2,1,0:T(8,128)S(1)} %get-tuple-element.81), channel_id=1, source_target_pairs={{0,1},{1,0},{2,3},{3,2},{4,5},{5,4},{6,7},{7,6},{8,9},{9,8},{10,11... | collective-permute-start | bytes 589832 | tf_op jit(solution)/shard_map/ppermute | solution.py:507
  15.7 1.4 %collective-permute-start.8 = (f32[6,16,512]{2,1,0:T(8,128)S(1)}, f32[6,16,512]{2,1,0:T(8,128)S(1)}, u32[]{:S(2)}, u32[]{:S(2)}) collective-permute-start(f32[6,16,512]{2,1,0:T(8,128)S(1)} %get-tuple-element.82), channel_id=1, source_target_pairs={{0,1},{1,0},{2,3},{3,2},{4,5},{5,4},{6,7},{7,6},{8,9},{9,8},{10,11... | collective-permute-start | bytes 589832 | tf_op jit(solution)/shard_map/ppermute | solution.py:507
  18.4 3.7 %collective-permute-start.14 = (f32[2,128]{1,0:T(2,128)S(1)}, f32[2,128]{1,0:T(2,128)S(1)}, u32[]{:S(2)}, u32[]{:S(2)}) collective-permute-start(f32[2,128]{1,0:T(2,128)S(1)} %dots.1), channel_id=1, source_target_pairs={{0,16},{1,7},{2,18},{3,5},{4,20},{5,3},{6,22},{7,1},{8,24},{9,15},... | collective-permute-start | bytes 3080 | tf_op jit(solution)/shard_map/ppermute | solution.py:503
  20.0 3.6 %collective-permute-start.13 = (f32[2,128]{1,0:T(2,128)S(1)}, f32[2,128]{1,0:T(2,128)S(1)}, u32[]{:S(2)}, u32[]{:S(2)}) collective-permute-start(f32[2,128]{1,0:T(2,128)S(1)} %dots.1), channel_id=1, source_target_pairs={{0,16},{1,5},{2,18},{3,7},{4,20},{5,1},{6,22},{7,3},{8,24},{9,13},... | collective-permute-start | bytes 3080 | tf_op jit(solution)/shard_map/ppermute | solution.py:503
  20.5 3.6 %collective-permute-start.12 = (f32[2,128]{1,0:T(2,128)S(1)}, f32[2,128]{1,0:T(2,128)S(1)}, u32[]{:S(2)}, u32[]{:S(2)}) collective-permute-start(f32[2,128]{1,0:T(2,128)S(1)} %dots.1), channel_id=1, source_target_pairs={{0,16},{1,3},{2,18},{3,1},{4,20},{5,7},{6,22},{7,5},{8,24},{9,11},... | collective-permute-start | bytes 3080 | tf_op jit(solution)/shard_map/ppermute | solution.py:503
  22.1 6.8 %collective-permute-start.11 = (f32[8,16,512]{2,1,0:T(8,128)S(1)}, f32[8,16,512]{2,1,0:T(8,128)S(1)}, u32[]{:S(2)}, u32[]{:S(2)}) collective-permute-start(f32[8,16,512]{2,1,0:T(8,128)S(1)} %get-tuple-element.90), channel_id=1, source_target_pairs={{0,1},{1,0},{2,3},{3,2},{4,5},{5,4},{6,7},{7,6},{8,9},{9,8},{10,11... | collective-permute-start | bytes 786440 | tf_op jit(solution)/shard_map/ppermute | solution.py:507
  24.1 3.6 %collective-permute-start.15 = (f32[2,128]{1,0:T(2,128)S(1)}, f32[2,128]{1,0:T(2,128)S(1)}, u32[]{:S(2)}, u32[]{:S(2)}) collective-permute-start(f32[2,128]{1,0:T(2,128)S(1)} %add_add_fusion), channel_id=1, source_target_pairs={{0,16},{1,9},{2,18},{3,11},{4,20},{5,13},{6,22},{7,15},{8,24},{9,1... | collective-permute-start | bytes 3080 | tf_op jit(solution)/shard_map/ppermute | solution.py:503
  27.7 1.1 %collective-permute-start.16 = (f32[2,128]{1,0:T(2,128)S(1)}, f32[2,128]{1,0:T(2,128)S(1)}, u32[]{:S(2)}, u32[]{:S(2)}) collective-permute-start(f32[2,128]{1,0:T(2,128)S(1)} %add.26), channel_id=1, source_target_pairs={{0,1},{1,0},{2,3},{3,2},{4,5},{5,4},{6,7},{7,6},{8,9},{9,8},{10,11... | collective-permute-start | bytes 3080 | tf_op jit(solution)/shard_map/ppermute | solution.py:507

commit v10 on v8

--- a/solution.py
+++ b/solution.py
@@ -495,9 +495,14 @@
 
 
 def leaders(value, tile, tm):
-    return exchange(
-        value, lambda g, t, k: (g, t ^ tile, k ^ tm) if k % 2 else aside(g, t, k)
-    )
+    few = value.shape[0] == 2
+
+    def partner(g, t, k):
+        if k % 2:
+            return g, t ^ tile, k ^ tm
+        return (g, t, k ^ 2) if few else aside(g, t, k)
+
+    return exchange(value, partner)
 
 
 def next_pair(g, t, k):

time: 30 us -> 30 us (level)
  transfers between devices with their start and end apart: 17 -> 17, of which waited for: 10 -> 9; matrix products, arithmetic and copies ran while one was open for 0% -> 0% of each run, Pallas kernels for 16% -> 16%
where the time goes in v10:
time: 30 us; the launch traced here: 29.9 us
  starting transfers between devices  14.3 us (48%)
  waiting for transfers between devices  8.04 us (27%)
  Pallas kernels  5.99 us (20%)
  between operations  1.46 us (5%)
    ppermute x10, starting transfers between devices, exchange(): return lax.ppermute(value, ('groups', 'tile', 'tm'), pairs)  13 us
    pallas_call x14, Pallas kernels, kernel_call(): pl.pallas_call(body, name=name, out_shape=out_shape, in_specs=in_specs, o...  5.99 us
    ppermute x10, waiting for transfers between devices, exchange(): return lax.ppermute(value, ('groups', 'tile', 'tm'), pairs)  5.65 us
    ppermute x7, waiting for transfers between devices, swap(): lax.ppermute(value, axis, [(i, i ^ distance) for i in range(lax.axis_size...  2.39 us
    ppermute x7, starting transfers between devices, swap(): lax.ppermute(value, axis, [(i, i ^ distance) for i in range(lax.axis_size...  1.24 us
  transfers between devices with their start and end apart: 17, of which 9 were waited for; matrix products, arithmetic and copies ran while one was open for 0% of the time, Pallas kernels for 16%

profile of v10, /device:TPU:0, one launch (start us, length us, event | category | flops | bytes accessed | tf_op | source)
XLA Modules:
  0.0 29.9 jit_solution(3310190147912111441)
XLA Ops:
  0.6 0.5 %collective-permute-start = (f32[8,16,512]{2,1,0:T(8,128)}, f32[8,16,512]{2,1,0:T(8,128)S(1)}, u32[]{:S(2)}, u32[]{:S(2)}) collective-permute-start(f32[8,16,512]{2,1,0:T(8,128)} %bitcast.19), channel_id=1, source_target_pairs={{0,1},{1,0},{2,3},{3,2},{4,5},{5,4},{6,7},{7,6},{8,9},{9,8},{10,11... | collective-permute-start | bytes 786440 | tf_op jit(solution)/shard_map/ppermute | solution.py:490
  1.2 1.7 %begin.1 = (f32[8,16,512]{2,1,0:T(8,128)S(1)}, f32[8,16,512]{2,1,0:T(8,128)S(1)}, f32[8,16,512]{2,1,0:T(8,128)S(1)}, f32[8,16,512]{2,1,0:T(8,128)S(1)}, f32[8,16...) custom-call(f32[8,16,512]{2,1,0:T(8,128)} %bitcast.13, ...), custom_call_target="tpu_custom_call" | custom-call | flops 1 | bytes 1 | tf_op jit(solution)/shard_map/begin/pallas_call | solution.py:32
  3.5 0.0 collective-permute-done.refs_1_.later_ref
  3.5 0.1 rims.1
  3.6 2.7 %collective-permute-start.2 = (f32[6,8,512]{2,1,0:T(8,128)S(1)}, f32[6,8,512]{2,1,0:T(8,128)S(1)}, u32[]{:S(2)}, u32[]{:S(2)}) collective-permute-start(f32[6,8,512]{2,1,0:T(8,128)S(1)} %get-tuple-element.63.second_ref), channel_id=1, source_target_pairs={{0,4},{1,5},{2,6},{3,7},{4,0},{5,1},{6,2},{7,3},{8,9},{9,8},{10,11... | collective-permute-start | bytes 294920 | tf_op jit(solution)/shard_map/ppermute | solution.py:486
  6.3 0.2 forward.1.moved_ref
  6.5 0.3 collective-permute-start.1
  6.8 0.3 %collective-permute-start.3 = (f32[6,8,512]{2,1,0:T(8,128)S(1)}, f32[6,8,512]{2,1,0:T(8,128)S(1)}, u32[]{:S(2)}, u32[]{:S(2)}) collective-permute-start(f32[6,8,512]{2,1,0:T(8,128)S(1)} %get-tuple-element.63.second_ref), channel_id=1, source_target_pairs={{0,1},{1,0},{2,3},{3,2},{4,5},{5,4},{6,7},{7,6},{8,12},{9,13},{10,... | collective-permute-start | bytes 294920 | tf_op jit(solution)/shard_map/ppermute | solution.py:486
  7.2 1.6 %collective-permute-start.5 = (f32[144,512]{1,0:T(8,128)S(1)}, f32[144,512]{1,0:T(8,128)S(1)}, u32[]{:S(2)}, u32[]{:S(2)}) collective-permute-start(f32[144,512]{1,0:T(8,128)S(1)} %pad.4), channel_id=1, source_target_pairs={{0,16},{1,3},{2,18},{3,1},{4,20},{5,7},{6,22},{7,5},{8,24},{9,11},... | collective-permute-start | bytes 884744 | tf_op jit(solution)/shard_map/ppermute | solution.py:486
  8.7 0.4 %spread.1 = (f32[8,16,512]{2,1,0:T(8,128)S(1)}, f32[8,16,512]{2,1,0:T(8,128)S(1)}) custom-call(f32[8,16,512]{2,1,0:T(8,128)S(1)} %get-tuple-element.60.incr_ref, f32[8,16,512]{2,1,0:T(8,128)S(1)} %get-tuple-element.47.mult_ref, f32[8,16,512]{2,1,0:T(8,128)S(1)} %get-tuple-element.64.rhs_ref, f32[8,16,512]{2,1,0:T(8,128)S(1)} %get-tuple-element.65.err_ref, ...), custom_call_target="tpu_custom_call" | custom-call | flops 1 | bytes 1 | tf_op jit(solution)/shard_map/spread/pallas_call | solution.py:32
  9.2 0.7 %adjoint.1.back_ref = f32[8,16,512]{2,1,0:T(8,128)S(1)} custom-call(f32[8,16,512]{2,1,0:T(8,128)S(1)} %get-tuple-element.48.a_ref, f32[8,16,512]{2,1,0:T(8,128)S(1)} %get-tuple-element.49.b_ref, f32[8,16,512]{2,1,0:T(8,128)S(1)} %get-tuple-element.50.c_ref, f32[8,16,512]{2,1,0:T(8,128)S(1)} %collective-permute-done.refs_1_.later_ref), custom_call_target="tpu_custom_call" | custom-call | flops 1 | bytes 1 | tf_op jit(solution)/shard_map/adjoint/pallas_call | solution.py:32
  9.9 0.0 collective-permute-done.3
  9.9 0.0 collective-permute-done.2
  9.9 0.0 collective-permute-done.1.got_first_ref.refs_0_
  9.9 0.3 share.1
  10.2 0.1 collective-permute-start.4
  10.3 1.6 %collective-permute-start.6 = (f32[4,8,512]{2,1,0:T(8,128)S(1)}, f32[4,8,512]{2,1,0:T(8,128)S(1)}, u32[]{:S(2)}, u32[]{:S(2)}) collective-permute-start(f32[4,8,512]{2,1,0:T(8,128)S(1)} %get-tuple-element.76), channel_id=1, source_target_pairs={{0,16},{1,3},{2,18},{3,1},{4,20},{5,7},{6,22},{7,5},{8,24},{9,11},... | collective-permute-start | bytes 196616 | tf_op jit(solution)/shard_map/ppermute | solution.py:486
  11.8 0.0 collective-permute-done.4.got_ref
  11.9 1.5 %collective-permute-start.10 = (f32[8,16,512]{2,1,0:T(8,128)S(1)}, f32[8,16,512]{2,1,0:T(8,128)S(1)}, u32[]{:S(2)}, u32[]{:S(2)}) collective-permute-start(f32[8,16,512]{2,1,0:T(8,128)S(1)} %sends.1), channel_id=1, source_target_pairs={{0,16},{1,3},{2,18},{3,1},{4,20},{5,7},{6,22},{7,5},{8,24},{9,11},... | collective-permute-start | bytes 786440 | tf_op jit(solution)/shard_map/ppermute | solution.py:486
  13.4 0.5 %collective-permute-done.5.cross_ref.refs_3_ = f32[144,512]{1,0:T(8,128)S(1)} collective-permute-done((f32[144,512]{1,0:T(8,128)S(1)}, f32[144,512]{1,0:T(8,128)S(1)}, u32[]{:S(2)}, u32[]{:S(2)}) %collective-permute-start.5) | collective-permute-done | bytes 294944 | tf_op jit(solution)/shard_map/ppermute | solution.py:486
  14.0 0.7 %beyond.1.beyond_ref = f32[8,16,512]{2,1,0:T(8,128)S(1)} custom-call(f32[8,16,512]{2,1,0:T(8,128)S(1)} %get-tuple-element.48.a_ref, f32[8,16,512]{2,1,0:T(8,128)S(1)} %get-tuple-element.49.b_ref, f32[8,16,512]{2,1,0:T(8,128)S(1)} %get-tuple-element.50.c_ref, f32[144,512]{1,0:T(8,128)S(1)} %collective-permute-done.5.cross_ref.refs_3_), custom_call_target="tpu_custom_call" | custom-call | flops 1 | bytes 1 | tf_op jit(solution)/shard_map/beyond/pallas_call | solution.py:32
  14.7 0.4 %gather.1 = (f32[1,512]{1,0:T(1,128)S(1)}, f32[2,1,512]{2,1,0:T(1,128)S(1)}) custom-call(f32[8,16,512]{2,1,0:T(8,128)S(1)} %get-tuple-element.60.incr_ref, s32[1,512]{1,0:T(1,128)S(1)} %get-tuple-element.72.cell_ref, f32[1,512]{1,0:T(1,128)S(1)} %get-tuple-element.61.dual_ref, f32[1,512]{1,0:T(1,128)S(1)} %get-tuple-element.73.want_ref, ...), custom_call_target="tpu_custom_call" | custom-call | flops 1 | bytes 1 | tf_op jit(solution)/shard_map/gather/pallas_call | solution.py:32
  15.1 0.1 rest.1
  15.1 0.1 collective-permute-start.9
  15.2 0.5 %collective-permute-start.7 = (f32[6,16,512]{2,1,0:T(8,128)S(1)}, f32[6,16,512]{2,1,0:T(8,128)S(1)}, u32[]{:S(2)}, u32[]{:S(2)}) collective-permute-start(f32[6,16,512]{2,1,0:T(8,128)S(1)} %get-tuple-element.79), channel_id=1, source_target_pairs={{0,1},{1,0},{2,3},{3,2},{4,5},{5,4},{6,7},{7,6},{8,9},{9,8},{10,11... | collective-permute-start | bytes 589832 | tf_op jit(solution)/shard_map/ppermute | solution.py:490
  15.7 0.1 collective-permute-start.8
  15.8 0.0 collective-permute-done.6.refs_4_.late_ref
  15.8 0.1 late.1.fix_ref
  15.9 0.7 %collective-permute-done.9.refs_2_.rest_ref = f32[5,16,512]{2,1,0:T(8,128)S(1)} collective-permute-done((f32[5,16,512]{2,1,0:T(8,128)S(1)}, f32[5,16,512]{2,1,0:T(8,128)S(1)}, u32[]{:S(2)}, u32[]{:S(2)}) %collective-permute-start.9) | collective-permute-done | bytes 163872 | tf_op jit(solution)/shard_map/ppermute | solution.py:490
  16.6 0.3 collective-permute-done.7.refs_0_
  16.9 0.3 collective-permute-done.8.refs_1_
  17.1 0.2 terms.1
  17.3 1.0 %collective-permute-done.10.got_ref = f32[8,16,512]{2,1,0:T(8,128)S(1)} collective-permute-done((f32[8,16,512]{2,1,0:T(8,128)S(1)}, f32[8,16,512]{2,1,0:T(8,128)S(1)}, u32[]{:S(2)}, u32[]{:S(2)}) %collective-permute-start.10) | collective-permute-done | bytes 262176 | tf_op jit(solution)/shard_map/ppermute | solution.py:486
  18.3 0.2 dots.1
  18.5 1.6 %collective-permute-start.14 = (f32[2,128]{1,0:T(2,128)S(1)}, f32[2,128]{1,0:T(2,128)S(1)}, u32[]{:S(2)}, u32[]{:S(2)}) collective-permute-start(f32[2,128]{1,0:T(2,128)S(1)} %get-tuple-element.87), channel_id=1, source_target_pairs={{0,2},{1,7},{2,0},{3,5},{4,6},{5,3},{6,4},{7,1},{8,10},{9,15},{10,... | collective-permute-start | bytes 3080 | tf_op jit(solution)/shard_map/ppermute | solution.py:486
  20.1 0.5 %collective-permute-start.13 = (f32[2,128]{1,0:T(2,128)S(1)}, f32[2,128]{1,0:T(2,128)S(1)}, u32[]{:S(2)}, u32[]{:S(2)}) collective-permute-start(f32[2,128]{1,0:T(2,128)S(1)} %get-tuple-element.87), channel_id=1, source_target_pairs={{0,2},{1,5},{2,0},{3,7},{4,6},{5,1},{6,4},{7,3},{8,10},{9,13},{10,... | collective-permute-start | bytes 3080 | tf_op jit(solution)/shard_map/ppermute | solution.py:486
  20.6 1.5 %collective-permute-start.12 = (f32[2,128]{1,0:T(2,128)S(1)}, f32[2,128]{1,0:T(2,128)S(1)}, u32[]{:S(2)}, u32[]{:S(2)}) collective-permute-start(f32[2,128]{1,0:T(2,128)S(1)} %get-tuple-element.87), channel_id=1, source_target_pairs={{0,2},{1,3},{2,0},{3,1},{4,6},{5,7},{6,4},{7,5},{8,10},{9,11},{10,... | collective-permute-start | bytes 3080 | tf_op jit(solution)/shard_map/ppermute | solution.py:486
  22.1 0.0 collective-permute-start.11
  22.1 0.0 collective-permute-done.14
  22.2 1.5 %collective-permute-done.13 = f32[2,128]{1,0:T(2,128)S(1)} collective-permute-done((f32[2,128]{1,0:T(2,128)S(1)}, f32[2,128]{1,0:T(2,128)S(1)}, u32[]{:S(2)}, u32[]{:S(2)}) %collective-permute-start.13) | collective-permute-done | bytes 1056 | tf_op jit(solution)/shard_map/ppermute | solution.py:486
  23.7 0.5 %collective-permute-done.12 = f32[2,128]{1,0:T(2,128)S(1)} collective-permute-done((f32[2,128]{1,0:T(2,128)S(1)}, f32[2,128]{1,0:T(2,128)S(1)}, u32[]{:S(2)}, u32[]{:S(2)}) %collective-permute-start.12) | collective-permute-done | bytes 1056 | tf_op jit(solution)/shard_map/ppermute | solution.py:486
  24.2 1.5 %collective-permute-start.15 = (f32[2,128]{1,0:T(2,128)S(1)}, f32[2,128]{1,0:T(2,128)S(1)}, u32[]{:S(2)}, u32[]{:S(2)}) collective-permute-start(f32[2,128]{1,0:T(2,128)S(1)} %add_add_fusion), channel_id=1, source_target_pairs={{0,2},{1,9},{2,0},{3,11},{4,6},{5,13},{6,4},{7,15},{8,10},{9,1},{1... | collective-permute-start | bytes 3080 | tf_op jit(solution)/shard_map/ppermute | solution.py:486
  25.7 2.1 %collective-permute-done.15 = f32[2,128]{1,0:T(2,128)S(1)} collective-permute-done((f32[2,128]{1,0:T(2,128)S(1)}, f32[2,128]{1,0:T(2,128)S(1)}, u32[]{:S(2)}, u32[]{:S(2)}) %collective-permute-start.15) | collective-permute-done | bytes 1056 | tf_op jit(solution)/shard_map/ppermute | solution.py:486
  27.8 0.0 collective-permute-start.16
  27.8 1.1 %collective-permute-done.16 = f32[2,128]{1,0:T(2,128)S(1)} collective-permute-done((f32[2,128]{1,0:T(2,128)S(1)}, f32[2,128]{1,0:T(2,128)S(1)}, u32[]{:S(2)}, u32[]{:S(2)}) %collective-permute-start.16) | collective-permute-done | bytes 1056 | tf_op jit(solution)/shard_map/ppermute | solution.py:490
  28.9 0.0 collective-permute-done.11.got_ref
  28.9 1.0 %update.1 = (f32[8,16,512]{2,1,0:T(8,128)}, f32[8,16,512]{2,1,0:T(8,128)}, f32[1,512]{1,0:T(1,128)}) custom-call(f32[8,16,512]{2,1,0:T(8,128)S(1)} %get-tuple-element.47.mult_ref, f32[8,16,512]{2,1,0:T(8,128)S(1)} %get-tuple-element.60.incr_ref, f32[1,512]{1,0:T(1,128)S(1)} %get-tuple-element.61.dual_ref, f32[1,512]{1,0:T(1,128)S(1)} %get-tuple-element.75.dir_ref, ...), custom_call_target="tpu_custom_call" | custom-call | flops 1 | bytes 1 | tf_op jit(solution)/shard_map/update/pallas_call | solution.py:32
  (8 shorter events, 0.1 us)
Async XLA Ops:
  0.6 2.9 %collective-permute-start = (f32[8,16,512]{2,1,0:T(8,128)}, f32[8,16,512]{2,1,0:T(8,128)S(1)}, u32[]{:S(2)}, u32[]{:S(2)}) collective-permute-start(f32[8,16,512]{2,1,0:T(8,128)} %bitcast.19), channel_id=1, source_target_pairs={{0,1},{1,0},{2,3},{3,2},{4,5},{5,4},{6,7},{7,6},{8,9},{9,8},{10,11... | collective-permute-start | bytes 786440 | tf_op jit(solution)/shard_map/ppermute | solution.py:490
  3.6 6.3 %collective-permute-start.2 = (f32[6,8,512]{2,1,0:T(8,128)S(1)}, f32[6,8,512]{2,1,0:T(8,128)S(1)}, u32[]{:S(2)}, u32[]{:S(2)}) collective-permute-start(f32[6,8,512]{2,1,0:T(8,128)S(1)} %get-tuple-element.63.second_ref), channel_id=1, source_target_pairs={{0,4},{1,5},{2,6},{3,7},{4,0},{5,1},{6,2},{7,3},{8,9},{9,8},{10,11... | collective-permute-start | bytes 294920 | tf_op jit(solution)/shard_map/ppermute | solution.py:486
  6.5 3.4 %collective-permute-start.1 = (f32[6,8,512]{2,1,0:T(8,128)S(1)}, f32[6,8,512]{2,1,0:T(8,128)S(1)}, u32[]{:S(2)}, u32[]{:S(2)}) collective-permute-start(f32[6,8,512]{2,1,0:T(8,128)S(1)} %get-tuple-element.62.first_ref), channel_id=1, source_target_pairs={{0,1},{1,0},{2,3},{3,2},{4,8},{5,9},{6,10},{7,11},{8,4},{9,5},{10,... | collective-permute-start | bytes 294920 | tf_op jit(solution)/shard_map/ppermute | solution.py:486
  6.8 3.1 %collective-permute-start.3 = (f32[6,8,512]{2,1,0:T(8,128)S(1)}, f32[6,8,512]{2,1,0:T(8,128)S(1)}, u32[]{:S(2)}, u32[]{:S(2)}) collective-permute-start(f32[6,8,512]{2,1,0:T(8,128)S(1)} %get-tuple-element.63.second_ref), channel_id=1, source_target_pairs={{0,1},{1,0},{2,3},{3,2},{4,5},{5,4},{6,7},{7,6},{8,12},{9,13},{10,... | collective-permute-start | bytes 294920 | tf_op jit(solution)/shard_map/ppermute | solution.py:486
  7.2 6.8 %collective-permute-start.5 = (f32[144,512]{1,0:T(8,128)S(1)}, f32[144,512]{1,0:T(8,128)S(1)}, u32[]{:S(2)}, u32[]{:S(2)}) collective-permute-start(f32[144,512]{1,0:T(8,128)S(1)} %pad.4), channel_id=1, source_target_pairs={{0,16},{1,3},{2,18},{3,1},{4,20},{5,7},{6,22},{7,5},{8,24},{9,11},... | collective-permute-start | bytes 884744 | tf_op jit(solution)/shard_map/ppermute | solution.py:486
  10.2 1.7 %collective-permute-start.4 = (f32[8,16,512]{2,1,0:T(8,128)S(1)}, f32[8,16,512]{2,1,0:T(8,128)S(1)}, u32[]{:S(2)}, u32[]{:S(2)}) collective-permute-start(f32[8,16,512]{2,1,0:T(8,128)S(1)} %get-tuple-element.71), channel_id=1, source_target_pairs={{0,1},{1,0},{2,3},{3,2},{4,5},{5,4},{6,7},{7,6},{8,9},{9,8},{10,11... | collective-permute-start | bytes 786440 | tf_op jit(solution)/shard_map/ppermute | solution.py:490
  10.3 5.5 %collective-permute-start.6 = (f32[4,8,512]{2,1,0:T(8,128)S(1)}, f32[4,8,512]{2,1,0:T(8,128)S(1)}, u32[]{:S(2)}, u32[]{:S(2)}) collective-permute-start(f32[4,8,512]{2,1,0:T(8,128)S(1)} %get-tuple-element.76), channel_id=1, source_target_pairs={{0,16},{1,3},{2,18},{3,1},{4,20},{5,7},{6,22},{7,5},{8,24},{9,11},... | collective-permute-start | bytes 196616 | tf_op jit(solution)/shard_map/ppermute | solution.py:486
  11.9 6.4 %collective-permute-start.10 = (f32[8,16,512]{2,1,0:T(8,128)S(1)}, f32[8,16,512]{2,1,0:T(8,128)S(1)}, u32[]{:S(2)}, u32[]{:S(2)}) collective-permute-start(f32[8,16,512]{2,1,0:T(8,128)S(1)} %sends.1), channel_id=1, source_target_pairs={{0,16},{1,3},{2,18},{3,1},{4,20},{5,7},{6,22},{7,5},{8,24},{9,11},... | collective-permute-start | bytes 786440 | tf_op jit(solution)/shard_map/ppermute | solution.py:486
  15.1 1.5 %collective-permute-start.9 = (f32[5,16,512]{2,1,0:T(8,128)S(1)}, f32[5,16,512]{2,1,0:T(8,128)S(1)}, u32[]{:S(2)}, u32[]{:S(2)}) collective-permute-start(f32[5,16,512]{2,1,0:T(8,128)S(1)} %get-tuple-element.81), channel_id=1, source_target_pairs={{0,1},{1,0},{2,3},{3,2},{4,5},{5,4},{6,7},{7,6},{8,9},{9,8},{10,11... | collective-permute-start | bytes 491528 | tf_op jit(solution)/shard_map/ppermute | solution.py:490
  15.2 1.7 %collective-permute-start.7 = (f32[6,16,512]{2,1,0:T(8,128)S(1)}, f32[6,16,512]{2,1,0:T(8,128)S(1)}, u32[]{:S(2)}, u32[]{:S(2)}) collective-permute-start(f32[6,16,512]{2,1,0:T(8,128)S(1)} %get-tuple-element.79), channel_id=1, source_target_pairs={{0,1},{1,0},{2,3},{3,2},{4,5},{5,4},{6,7},{7,6},{8,9},{9,8},{10,11... | collective-permute-start | bytes 589832 | tf_op jit(solution)/shard_map/ppermute | solution.py:490
  15.7 1.4 %collective-permute-start.8 = (f32[6,16,512]{2,1,0:T(8,128)S(1)}, f32[6,16,512]{2,1,0:T(8,128)S(1)}, u32[]{:S(2)}, u32[]{:S(2)}) collective-permute-start(f32[6,16,512]{2,1,0:T(8,128)S(1)} %get-tuple-element.80), channel_id=1, source_target_pairs={{0,1},{1,0},{2,3},{3,2},{4,5},{5,4},{6,7},{7,6},{8,9},{9,8},{10,11... | collective-permute-start | bytes 589832 | tf_op jit(solution)/shard_map/ppermute | solution.py:490
  18.5 3.6 %collective-permute-start.14 = (f32[2,128]{1,0:T(2,128)S(1)}, f32[2,128]{1,0:T(2,128)S(1)}, u32[]{:S(2)}, u32[]{:S(2)}) collective-permute-start(f32[2,128]{1,0:T(2,128)S(1)} %get-tuple-element.87), channel_id=1, source_target_pairs={{0,2},{1,7},{2,0},{3,5},{4,6},{5,3},{6,4},{7,1},{8,10},{9,15},{10,... | collective-permute-start | bytes 3080 | tf_op jit(solution)/shard_map/ppermute | solution.py:486
  20.1 3.6 %collective-permute-start.13 = (f32[2,128]{1,0:T(2,128)S(1)}, f32[2,128]{1,0:T(2,128)S(1)}, u32[]{:S(2)}, u32[]{:S(2)}) collective-permute-start(f32[2,128]{1,0:T(2,128)S(1)} %get-tuple-element.87), channel_id=1, source_target_pairs={{0,2},{1,5},{2,0},{3,7},{4,6},{5,1},{6,4},{7,3},{8,10},{9,13},{10,... | collective-permute-start | bytes 3080 | tf_op jit(solution)/shard_map/ppermute | solution.py:486
  20.6 3.6 %collective-permute-start.12 = (f32[2,128]{1,0:T(2,128)S(1)}, f32[2,128]{1,0:T(2,128)S(1)}, u32[]{:S(2)}, u32[]{:S(2)}) collective-permute-start(f32[2,128]{1,0:T(2,128)S(1)} %get-tuple-element.87), channel_id=1, source_target_pairs={{0,2},{1,3},{2,0},{3,1},{4,6},{5,7},{6,4},{7,5},{8,10},{9,11},{10,... | collective-permute-start | bytes 3080 | tf_op jit(solution)/shard_map/ppermute | solution.py:486
  22.1 6.8 %collective-permute-start.11 = (f32[8,16,512]{2,1,0:T(8,128)S(1)}, f32[8,16,512]{2,1,0:T(8,128)S(1)}, u32[]{:S(2)}, u32[]{:S(2)}) collective-permute-start(f32[8,16,512]{2,1,0:T(8,128)S(1)} %get-tuple-element.86), channel_id=1, source_target_pairs={{0,1},{1,0},{2,3},{3,2},{4,5},{5,4},{6,7},{7,6},{8,9},{9,8},{10,11... | collective-permute-start | bytes 786440 | tf_op jit(solution)/shard_map/ppermute | solution.py:490
  24.2 3.6 %collective-permute-start.15 = (f32[2,128]{1,0:T(2,128)S(1)}, f32[2,128]{1,0:T(2,128)S(1)}, u32[]{:S(2)}, u32[]{:S(2)}) collective-permute-start(f32[2,128]{1,0:T(2,128)S(1)} %add_add_fusion), channel_id=1, source_target_pairs={{0,2},{1,9},{2,0},{3,11},{4,6},{5,13},{6,4},{7,15},{8,10},{9,1},{1... | collective-permute-start | bytes 3080 | tf_op jit(solution)/shard_map/ppermute | solution.py:486
  27.8 1.1 %collective-permute-start.16 = (f32[2,128]{1,0:T(2,128)S(1)}, f32[2,128]{1,0:T(2,128)S(1)}, u32[]{:S(2)}, u32[]{:S(2)}) collective-permute-start(f32[2,128]{1,0:T(2,128)S(1)} %add.26), channel_id=1, source_target_pairs={{0,1},{1,0},{2,3},{3,2},{4,5},{5,4},{6,7},{7,6},{8,9},{9,8},{10,11... | collective-permute-start | bytes 3080 | tf_op jit(solution)/shard_map/ppermute | solution.py:490
